TPU v7x, 32 devices: a whole 2x2x4 slice. The times are simulated.
32 devices in a mesh: prompt: 8 (over z, core), comp: 4 (over y, x).
Axes of the slice: x: 2, y: 2, z: 4, core: 2. Of those that a mesh axis runs over, the one named last changes fastest.
Arguments:
- prompt_inner: bfloat16 [2048, 16384], P('prompt', 'comp'), may hold values from -0.59765625 to 0.59765625
- prompt_proj: bfloat16 [2048, 4096], P('prompt'), may hold values from -0.8984375 to 0.8984375
- prompt_step: float32 [256, 2048], P('comp', 'prompt')
- completion_inner: bfloat16 [8, 256, 16384], P('comp', None, 'prompt'), may hold values from -0.59765625 to 0.59765625
- completion_gate: bfloat16 [8, 256, 16384], P('comp', None, 'prompt'), may hold values from -12 to 12
- completion_projections: bfloat16 [8, 256, 4096], P('comp'), may hold values from -0.8984375 to 0.8984375
- sample_step: float32 [256, 8, 256], P('prompt', 'comp')
- sample_length: int32 [8], P('comp'), may hold values from 1 to 256, as said below
- decay_log: float32 [256], replicated
- conv_inner: bfloat16 [4, 16384], replicated, may hold values from -3 to 3
- conv_proj: bfloat16 [4, 4096], replicated, may hold values from -3 to 3
- norm_gain: float32 [16384], P('prompt'), may hold values from 0.5 to 1.5
Outputs:
- sample_out: bfloat16 [8, 256, 16384], P('comp', None, 'prompt')
Inputs may be any that keep to these rules, and one draw needn't show every extreme that they name: `sample_length`: some completion slot is full.
All inputs are finite; a program needn't handle non-finite values.
Results may differ from a plain program's by a relative error of at most 0.014.
Values may be sent and summed in bfloat16 or wider, within the bound.
No kernel may reach another device: no remote copies, remote signals or barrier semaphores. Data moves between devices by JAX's collectives and lax.ppermute only.
A program may use at most 128 MiB of HBM per device.

v0:
```python
import jax
import jax.numpy as jnp
from jax import lax
from jax.sharding import PartitionSpec as P

STATE_HEADS = 256
HEAD_WIDTH = 64
STATE_WIDTH = 256
STATE_GROUPS = 8
CONV = 4
BLOCK = 128


EPS = 1e-05
HIGHEST = lax.Precision.HIGHEST


def from_behind(block, axis, distance):
    devices = range(lax.axis_size(axis))
    route = [(i - distance, i) for i in devices if i - distance in devices]
    return lax.ppermute(block, axis, route)


def carried_in(array, axis, combine, identity):
    peers, position = (lax.axis_size(axis), lax.axis_index(axis))
    everything = jax.tree.map(
        lambda part, kind: lax.all_gather(part.astype(kind), axis),
        array,
        (jnp.bfloat16, jnp.bfloat16),
    )
    start = jax.tree.map(
        lambda part, zero: jnp.broadcast_to(jnp.asarray(zero, part.dtype), part.shape),
        array,
        identity,
    )

    def hop(k, before):
        reached = k < position
        new = combine(
            before, jax.tree.map(lambda part, own: part[k].astype(own.dtype), everything, array)
        )
        return jax.tree.map(lambda a, b: jnp.where(reached, a, b), new, before)

    return lax.fori_loop(0, peers, hop, start)


def from_root(array, axis, root):
    mine = lax.axis_index(axis) == root
    return lax.psum(jnp.where(mine, array, jnp.zeros_like(array)), axis)


def from_partner(block, axis, stride):
    count = lax.axis_size(axis)
    route = []
    for low in range(count):
        high = low | 1 << stride
        if high != low and high < count:
            route += [(low, high), (high, low)]
    return lax.ppermute(block, axis, route)


def causal_conv(source, kernel, leading):
    padded = jnp.concatenate([leading, source], axis=0).astype(jnp.float32)
    kernel_wide = kernel.astype(jnp.float32)
    row_count = source.shape[0]
    summed = jnp.zeros(source.shape, jnp.float32)
    for offset in range(kernel.shape[0]):
        summed = summed + kernel_wide[offset] * padded[offset : offset + row_count]
    return jax.nn.silu(summed).astype(jnp.bfloat16)


def block_scan(state_in, inner_blk, b_blk, c_blk, step_blk, rate_vals):
    cumul = jnp.cumsum(-rate_vals[:, :, None] * step_blk, axis=2)
    scores = jnp.einsum("ign,jgn->gij", c_blk, b_blk, preferred_element_type=jnp.float32)
    spread_log = cumul[:, :, :, None] - cumul[:, :, None, :]
    length_q = step_blk.shape[2]
    causal = jnp.arange(length_q)[:, None] >= jnp.arange(length_q)[None, :]
    decay_mat = jnp.exp(jnp.where(causal, spread_log, -jnp.inf))
    mixer_w = (scores[:, None] * decay_mat * step_blk[:, :, None, :]).astype(jnp.bfloat16)
    intra_part = jnp.einsum(
        "gkij,jgkd->igkd", mixer_w, inner_blk, preferred_element_type=jnp.float32
    )
    readout = jnp.einsum("ign,gkdn->igkd", c_blk.astype(jnp.float32), state_in, precision=HIGHEST)
    inter_part = jnp.transpose(jnp.exp(cumul), (2, 0, 1))[..., None] * readout
    weights = jnp.exp(cumul[:, :, -1:] - cumul) * step_blk
    packed = (inner_blk.astype(jnp.float32) * jnp.transpose(weights, (2, 0, 1))[..., None]).astype(
        jnp.bfloat16
    )
    fresh_part = jnp.einsum("jgn,jgkd->gkdn", b_blk, packed, preferred_element_type=jnp.float32)
    return (
        intra_part + inter_part,
        jnp.exp(cumul[:, :, -1])[..., None, None] * state_in + fresh_part,
    )


def local(
    prompt_inner,
    prompt_proj,
    prompt_step,
    completion_inner,
    completion_gate,
    completion_projections,
    sample_step,
    sample_length,
    decay_log,
    conv_inner,
    conv_proj,
    norm_gain,
):
    prompt_count = lax.axis_size("prompt")
    prompt_idx = lax.axis_index("prompt")
    column_idx = lax.axis_index("comp")
    heads_group = STATE_HEADS // STATE_GROUPS
    heads_col = prompt_step.shape[0]
    heads_row = sample_step.shape[0]
    state_feats = STATE_GROUPS * STATE_WIDTH
    lag_rows = CONV - 1
    rows_prompt = prompt_inner.shape[0]
    prev_inner, prev_proj = from_behind(
        (
            prompt_inner[rows_prompt - lag_rows :],
            prompt_proj[rows_prompt - lag_rows :, :state_feats],
        ),
        "prompt",
        1,
    )
    col_start = column_idx * heads_col
    conv_col = lax.dynamic_slice_in_dim(
        conv_inner, col_start * HEAD_WIDTH, heads_col * HEAD_WIDTH, 1
    )
    inner_conv = causal_conv(prompt_inner, conv_col, prev_inner)
    b_conv = causal_conv(prompt_proj[:, :state_feats], conv_proj[:, :state_feats], prev_proj)
    rate_col = jnp.exp(lax.dynamic_slice_in_dim(decay_log, col_start, heads_col, 0))
    step_col = jax.nn.softplus(prompt_step)
    cumul = jnp.cumsum(-rate_col[:, None] * step_col, axis=1)
    local_log = cumul[:, -1]
    weight_col = jnp.exp(local_log[:, None] - cumul) * step_col
    group_span = max(1, heads_col // heads_group)
    per_group = heads_col // group_span
    group_start = col_start // heads_group
    b_select = lax.dynamic_slice_in_dim(
        b_conv.reshape(rows_prompt, STATE_GROUPS, STATE_WIDTH), group_start, group_span, 1
    ).astype(jnp.float32)
    scaled = (
        inner_conv.astype(jnp.float32).reshape(rows_prompt, heads_col, HEAD_WIDTH)
        * jnp.transpose(weight_col)[:, :, None]
    )
    scaled = scaled.reshape(rows_prompt, group_span, per_group, HEAD_WIDTH)
    local_state = jnp.einsum("tgn,tghd->ghdn", b_select, scaled, precision=HIGHEST).reshape(
        heads_col, HEAD_WIDTH, STATE_WIDTH
    )
    own_inner = prompt_inner[rows_prompt - lag_rows :].astype(jnp.float32)
    own_proj = prompt_proj[rows_prompt - lag_rows :].astype(jnp.float32)
    last_index = prompt_count - 1
    head_start = prompt_idx * heads_row
    owner = head_start // heads_col
    head_offset = head_start - owner * heads_col

    def combine(earlier, later):
        return (earlier[0] + later[0], earlier[1] * jnp.exp(later[0])[:, None, None] + later[1])

    before = carried_in(
        (local_log, local_state),
        "prompt",
        combine,
        (jnp.zeros_like(local_log), jnp.zeros_like(local_state)),
    )
    through = combine(before, (local_log, local_state))[1]
    final_state, tail_inner, tail_proj = (
        from_root(through.astype(jnp.bfloat16), "prompt", last_index).astype(through.dtype),
        from_root(own_inner.astype(jnp.bfloat16), "prompt", last_index).astype(own_inner.dtype),
        from_root(own_proj.astype(jnp.bfloat16), "prompt", last_index).astype(own_proj.dtype),
    )
    moved_state, moved_inner = (
        from_root(final_state.astype(jnp.bfloat16), "comp", owner).astype(final_state.dtype),
        from_root(tail_inner.astype(jnp.bfloat16), "comp", owner).astype(tail_inner.dtype),
    )
    start_state = lax.dynamic_slice_in_dim(moved_state, head_offset, heads_row, 0)
    lead_inner = lax.dynamic_slice_in_dim(
        moved_inner, head_offset * HEAD_WIDTH, heads_row * HEAD_WIDTH, 1
    ).astype(jnp.bfloat16)
    group_row = head_start // heads_group
    b_start = group_row * STATE_WIDTH
    c_start = state_feats + group_row * STATE_WIDTH
    proj_select = jnp.concatenate(
        [
            lax.dynamic_slice_in_dim(completion_projections, b_start, STATE_WIDTH, 2),
            lax.dynamic_slice_in_dim(completion_projections, c_start, STATE_WIDTH, 2),
        ],
        axis=2,
    )
    kernel_select = jnp.concatenate(
        [
            lax.dynamic_slice_in_dim(conv_proj, b_start, STATE_WIDTH, 1),
            lax.dynamic_slice_in_dim(conv_proj, c_start, STATE_WIDTH, 1),
        ],
        axis=1,
    )
    lead_wide = tail_proj.astype(jnp.bfloat16)
    lead_select = jnp.concatenate(
        [
            lax.dynamic_slice_in_dim(lead_wide, b_start, STATE_WIDTH, 1),
            lax.dynamic_slice_in_dim(lead_wide, c_start, STATE_WIDTH, 1),
        ],
        axis=1,
    )
    conv_row = lax.dynamic_slice_in_dim(
        conv_inner, head_start * HEAD_WIDTH, heads_row * HEAD_WIDTH, 1
    )
    rate_row = jnp.exp(lax.dynamic_slice_in_dim(decay_log, head_start, heads_row, 0))
    step_row = jax.nn.softplus(sample_step)
    slot_count = completion_inner.shape[0]
    sample_len = completion_inner.shape[1]
    block_count = sample_len // BLOCK

    def advance(carry, block_in):
        block_out, carry_next = block_scan(
            carry, block_in[0], block_in[1], block_in[2], block_in[3], rate_row[None]
        )
        return (carry_next, block_out)

    gated_list = []
    square_list = []
    for slot in range(slot_count):
        slot_conv = causal_conv(completion_inner[slot], conv_row, lead_inner)
        proj_conv = causal_conv(proj_select[slot], kernel_select, lead_select)
        inner_blocks = slot_conv.reshape(block_count, BLOCK, 1, heads_row, HEAD_WIDTH)
        b_blocks = proj_conv[:, :STATE_WIDTH].reshape(block_count, BLOCK, 1, STATE_WIDTH)
        c_blocks = proj_conv[:, STATE_WIDTH:].reshape(block_count, BLOCK, 1, STATE_WIDTH)
        step_blocks = jnp.transpose(
            step_row[:, slot].reshape(heads_row, block_count, BLOCK), (1, 0, 2)
        )[:, None]
        block_inputs = (inner_blocks, b_blocks, c_blocks, step_blocks)
        _, block_outs = lax.scan(advance, start_state[None], block_inputs)
        ssm_out = block_outs.reshape(sample_len, heads_row * HEAD_WIDTH)
        gated = ssm_out * jax.nn.silu(completion_gate[slot].astype(jnp.float32))
        gated_list.append(gated)
        square_list.append(jnp.sum(gated * gated, axis=1))
    square_all = jnp.stack(square_list)
    partner_bits = (prompt_count // STATE_GROUPS).bit_length() - 1
    for bit_number in range(partner_bits):
        square_all = square_all + from_partner(square_all, "prompt", bit_number)
    scale_all = lax.rsqrt(square_all / (heads_group * HEAD_WIDTH) + EPS)
    gated_all = jnp.stack(gated_list)
    result = gated_all * scale_all[:, :, None] * norm_gain[None, None, :]
    live_rows = jnp.arange(sample_len)[None, :] < sample_length[:, None]
    return jnp.where(live_rows[:, :, None], result, 0.0).astype(jnp.bfloat16)


def solution(mesh):
    placed = (
        P("prompt", "comp"),
        P("prompt", None),
        P("comp", "prompt"),
        P("comp", None, "prompt"),
        P("comp", None, "prompt"),
        P("comp", None, None),
        P("prompt", "comp", None),
        P("comp"),
        P(),
        P(),
        P(),
        P("prompt"),
    )
    return jax.shard_map(
        local, mesh=mesh, in_specs=placed, out_specs=P("comp", None, "prompt"), check_vma=False
    )
```

profile of v0, /device:TPU:0, one launch (start us, length us, event | category | flops | bytes accessed | tf_op | source)
XLA Modules:
  0.0 467.2 jit_solution(6643406092231926650)
XLA Ops:
  11.6 5.4 %collective-permute-start.1 = (bf16[3,2048]{0,1:T(8,128)(2,1)}, bf16[3,2048]{0,1:T(8,128)(2,1)}, u32[]{:S(2)}, u32[]{:S(2)}) collective-permute-start(bf16[3,2048]{0,1:T(8,128)(2,1)} %copy.81), channel_id=1, source_target_pairs={{0,4},{4,8},{8,12},{12,16},{16,20},{20,24},{24,28},{1,5},{5,9},{9,... | collective-permute-start | bytes 36872 | tf_op jit(solution)/shard_map/ppermute | solution.py:21
  35.8 6.3 %multiply_convert_fusion.6 = bf16[256,4096]{0,1:T(8,128)(2,1)S(1)} fusion(f32[259,4096]{0,1:T(8,128)S(1)} %maximum_convert_fusion, f32[4096]{0:T(1024)S(1)} %bitcast.314, f32[4096]{0:T(1024)S(1)} %bitcast.315, f32[4096]{0:T(1024)S(1)} %bitcast.316, f32[4096]{0:T(1024)S(1)} %bitcast.313), kind=kLoop, calls=%fused_computation.101 | loop fusion | flops 12582912 | bytes 18939904 | tf_op jit(solution)/shard_map/convert_element_type | solution.py:69
  42.2 5.9 %fusion.124 = (bf16[2,32,64,256]{3,2,1,0:T(8,128)(2,1)}, f32[2,32,64,256]{3,2,1,0:T(8,128)}) fusion(bf16[256,8,256]{0,2,1:T(8,128)(2,1)} %bitcast.310, s32[]{:T(128)S(6)} %select_n.132, bf16[256,2,32,64]{0,3,2,1:T(8,128)(2,1)S(1)} %bitcast.290, f32[256,2,32]{0,2,1:T(8,128)S(1)} %bitcast.312), kind=kOutput, calls=%fused_computation.212 | convolution fusion | flops 3224371200 | bytes 8716292 | tf_op jit(solution)/shard_map/tgn,tghd->ghdn/dot_general | solution.py:149
  50.5 28.2 %all-reduce.1 = (bf16[512]{0:T(512)(128)(2,1)S(1)}, bf16[3,4096]{1,0:T(4,128)(2,1)S(1)}, bf16[3,4096]{1,0:T(4,128)(2,1)S(1)}) all-reduce(bf16[512]{0:T(512)(128)(2,1)S(1)} %dynamic-update-slice, bf16[3,4096]{1,0:T(4,128)(2,1)S(1)} %get-tuple-element.411, ...), channel_id=2, replica_groups=mesh['prompt'=8,'comp'=4] {'prompt'}, use_global_device_ids=true, to_apply=%add | all-reduce | flops 25088 | bytes 100352
  78.8 16.2 %psum.38 = bf16[3,4096]{1,0:T(4,128)(2,1)S(1)} all-reduce(bf16[3,4096]{1,0:T(4,128)(2,1)S(1)} %broadcast_select_fusion.2), channel_id=1, replica_groups=mesh['prompt'=8,'comp'=4] {'comp'}, use_global_device_ids=true, to_apply=%region_7.8 | all-reduce | flops 12288 | bytes 49152 | tf_op jit(solution)/shard_map/psum | solution.py:49
  101.2 4.9 %fusion.96 = (f32[259,2048]{0,1:T(8,128)S(1)}, f32[259,2048]{0,1:T(8,128)}) fusion(bf16[3,2048]{0,1:T(8,128)(2,1)} %copy.85, bf16[256,2048]{0,1:T(8,128)(2,1)} %bitcast.300, bf16[256,2048]{0,1:T(8,128)(2,1)} %bitcast.301), kind=kLoop, calls=%fused_computation.140 | loop fusion | flops 3713024 | bytes 6352896 | tf_op jit(solution)/shard_map/convert_element_type | solution.py:63
  106.1 93.9 %all-gather.3.cloned.1.call-done = bf16[8,64,64,256]{3,2,1,0:T(8,128)(2,1)} async-done(((bf16[1,64,64,256]{3,2,1,0:T(8,128)(2,1)}), bf16[8,64,64,256]{3,2,1,0:T(8,128)(2,1)}) %all-gather.3.cloned.1.call-update) | async-done | bytes 16777232 | tf_op jit(solution)/shard_map/all_gather | solution.py:27
  200.0 46.5 %while.44 = (s32[]{:T(128)}, f32[64,64,256]{2,1,0:T(8,128)}, s32[]{:T(128)}, bf16[8,64]{1,0:T(8,128)(2,1)S(1)}, bf16[8,64,64,256]{3,2,1,0:T(8,128)(2,1)}, /*index=5*/s32[]{:T(128)}, s32[]{:T(128)}) while((s32[]{:T(128)}, f32[64,64,256]{2,1,0:T(8,128)}, s32[]{:T(128)}, bf16[8,64]{1,0:T(8,128)(2,1)S(1)}, ...), condition=%wide.region_3.4_spmd.clone, body=%wide.region_2.3_spmd.clone.sunk | while | flops 5242948 | bytes 10486505 | solution.py:44
  200.0 4.7 %fusion.166 = f32[64,64,256]{2,1,0:T(8,128)} fusion(f32[64,64,256]{2,1,0:T(8,128)} %get-tuple-element.598, bf16[8,64,64,256]{3,2,1,0:T(8,128)(2,1)} %get-tuple-element.608, s32[]{:T(128)} %get-tuple-element.597, f32[64]{0:T(128)S(1)} %exponential_bitcast_fusion.8, pred[]{:T(512)S(6)} %compare.9, pred[]{:T(512)S(6)} %lt.94), kind=kLoop, calls=%fused_computation.1.clone.1 | loop fusion | flops 5242880 | bytes 10486022 | tf_op jit(solution)/shard_map/while/body/eval_jaxpr/jit(_where)/select_n | solution.py:42
  204.7 6.0 %fusion.166 = f32[64,64,256]{2,1,0:T(8,128)} fusion(f32[64,64,256]{2,1,0:T(8,128)} %get-tuple-element.598, bf16[8,64,64,256]{3,2,1,0:T(8,128)(2,1)} %get-tuple-element.608, s32[]{:T(128)} %get-tuple-element.597, f32[64]{0:T(128)S(1)} %exponential_bitcast_fusion.8, pred[]{:T(512)S(6)} %compare.9, pred[]{:T(512)S(6)} %lt.94), kind=kLoop, calls=%fused_computation.1.clone.1 | loop fusion | flops 5242880 | bytes 10486022 | tf_op jit(solution)/shard_map/while/body/eval_jaxpr/jit(_where)/select_n | solution.py:42
  210.7 6.0 %fusion.166 = f32[64,64,256]{2,1,0:T(8,128)} fusion(f32[64,64,256]{2,1,0:T(8,128)} %get-tuple-element.598, bf16[8,64,64,256]{3,2,1,0:T(8,128)(2,1)} %get-tuple-element.608, s32[]{:T(128)} %get-tuple-element.597, f32[64]{0:T(128)S(1)} %exponential_bitcast_fusion.8, pred[]{:T(512)S(6)} %compare.9, pred[]{:T(512)S(6)} %lt.94), kind=kLoop, calls=%fused_computation.1.clone.1 | loop fusion | flops 5242880 | bytes 10486022 | tf_op jit(solution)/shard_map/while/body/eval_jaxpr/jit(_where)/select_n | solution.py:42
  216.6 6.0 %fusion.166 = f32[64,64,256]{2,1,0:T(8,128)} fusion(f32[64,64,256]{2,1,0:T(8,128)} %get-tuple-element.598, bf16[8,64,64,256]{3,2,1,0:T(8,128)(2,1)} %get-tuple-element.608, s32[]{:T(128)} %get-tuple-element.597, f32[64]{0:T(128)S(1)} %exponential_bitcast_fusion.8, pred[]{:T(512)S(6)} %compare.9, pred[]{:T(512)S(6)} %lt.94), kind=kLoop, calls=%fused_computation.1.clone.1 | loop fusion | flops 5242880 | bytes 10486022 | tf_op jit(solution)/shard_map/while/body/eval_jaxpr/jit(_where)/select_n | solution.py:42
  222.6 6.0 %fusion.166 = f32[64,64,256]{2,1,0:T(8,128)} fusion(f32[64,64,256]{2,1,0:T(8,128)} %get-tuple-element.598, bf16[8,64,64,256]{3,2,1,0:T(8,128)(2,1)} %get-tuple-element.608, s32[]{:T(128)} %get-tuple-element.597, f32[64]{0:T(128)S(1)} %exponential_bitcast_fusion.8, pred[]{:T(512)S(6)} %compare.9, pred[]{:T(512)S(6)} %lt.94), kind=kLoop, calls=%fused_computation.1.clone.1 | loop fusion | flops 5242880 | bytes 10486022 | tf_op jit(solution)/shard_map/while/body/eval_jaxpr/jit(_where)/select_n | solution.py:42
  228.6 6.0 %fusion.166 = f32[64,64,256]{2,1,0:T(8,128)} fusion(f32[64,64,256]{2,1,0:T(8,128)} %get-tuple-element.598, bf16[8,64,64,256]{3,2,1,0:T(8,128)(2,1)} %get-tuple-element.608, s32[]{:T(128)} %get-tuple-element.597, f32[64]{0:T(128)S(1)} %exponential_bitcast_fusion.8, pred[]{:T(512)S(6)} %compare.9, pred[]{:T(512)S(6)} %lt.94), kind=kLoop, calls=%fused_computation.1.clone.1 | loop fusion | flops 5242880 | bytes 10486022 | tf_op jit(solution)/shard_map/while/body/eval_jaxpr/jit(_where)/select_n | solution.py:42
  234.5 6.0 %fusion.166 = f32[64,64,256]{2,1,0:T(8,128)} fusion(f32[64,64,256]{2,1,0:T(8,128)} %get-tuple-element.598, bf16[8,64,64,256]{3,2,1,0:T(8,128)(2,1)} %get-tuple-element.608, s32[]{:T(128)} %get-tuple-element.597, f32[64]{0:T(128)S(1)} %exponential_bitcast_fusion.8, pred[]{:T(512)S(6)} %compare.9, pred[]{:T(512)S(6)} %lt.94), kind=kLoop, calls=%fused_computation.1.clone.1 | loop fusion | flops 5242880 | bytes 10486022 | tf_op jit(solution)/shard_map/while/body/eval_jaxpr/jit(_where)/select_n | solution.py:42
  240.5 6.0 %fusion.166 = f32[64,64,256]{2,1,0:T(8,128)} fusion(f32[64,64,256]{2,1,0:T(8,128)} %get-tuple-element.598, bf16[8,64,64,256]{3,2,1,0:T(8,128)(2,1)} %get-tuple-element.608, s32[]{:T(128)} %get-tuple-element.597, f32[64]{0:T(128)S(1)} %exponential_bitcast_fusion.8, pred[]{:T(512)S(6)} %compare.9, pred[]{:T(512)S(6)} %lt.94), kind=kLoop, calls=%fused_computation.1.clone.1 | loop fusion | flops 5242880 | bytes 10486022 | tf_op jit(solution)/shard_map/while/body/eval_jaxpr/jit(_where)/select_n | solution.py:42
  246.5 5.4 %fusion.85 = bf16[64,64,256]{2,1,0:T(8,128)(2,1)} fusion(f32[2,32,64,256]{3,2,1,0:T(8,128)} %get-tuple-element.450, f32[64,64,256]{2,1,0:T(8,128)} %get-tuple-element.287, f32[64]{0:T(128)S(1)} %exp.180, pred[]{:T(512)S(6)} %eq.10), kind=kLoop, calls=%fused_computation.108 | loop fusion | flops 4194304 | bytes 10486017 | tf_op jit(solution)/shard_map/jit(_where)/select_n | solution.py:49
  251.9 10.4 %multiply_convert_fusion.8 = (bf16[256,2048]{0,1:T(8,128)(2,1)}, bf16[256,2048]{0,1:T(8,128)(2,1)}) fusion(f32[259,2048]{0,1:T(8,128)S(1)} %get-tuple-element.415, f32[2048]{0:T(1024)S(1)} %bitcast.320, f32[2048]{0:T(1024)S(1)} %bitcast.321, f32[2048]{0:T(1024)S(1)} %bitcast.322, f32[2048]{0:T(1024)S(1)} %bitcast.319, f32[259,2048]{0,1:T(8,128)} %get-tuple-element.416), kind=kLoop, calls=%fused_computation.133 | loop fusion | flops 12582912 | bytes 18907136 | tf_op jit(solution)/shard_map/convert_element_type | solution.py:69
  282.0 33.3 %all-reduce.5.cloned.1.call-done = bf16[64,64,256]{2,1,0:T(8,128)(2,1)} async-done(((bf16[64,64,256]{2,1,0:T(8,128)(2,1)}), bf16[64,64,256]{2,1,0:T(8,128)(2,1)}) %all-reduce.5.cloned.1.call-update) | async-done | bytes 2097168 | tf_op jit(solution)/shard_map/psum | solution.py:49
  323.7 64.1 %all-reduce.7.cloned.1.call-done = bf16[64,64,256]{2,1,0:T(8,128)(2,1)} async-done(((bf16[64,64,256]{2,1,0:T(8,128)(2,1)}), bf16[64,64,256]{2,1,0:T(8,128)(2,1)}) %all-reduce.7.cloned.1.call-update) | async-done | bytes 2097168 | tf_op jit(solution)/shard_map/psum | solution.py:49
  393.0 21.6 %while.42 = (s32[]{:T(128)}, f32[1,32,64,256]{3,2,1,0:T(8,128)S(1)}, f32[2,128,1,32,64]{1,4,3,2,0:T(8,128)}, f32[1,32,1]{1,2,0:T(1,128)}, f32[2,1,32,128]{3,0,2,...) while((s32[]{:T(128)}, ...), condition=%wide.region_11.12_spmd, body=%wide.region_9.11_spmd.sunk | while | flops 1020551168 | bytes 32723960 | solution.py:234
  414.6 4.8 %copy.88 = f32[2,128,1,32,64]{1,0,2,4,3:T(2,128)} copy(f32[2,128,1,32,64]{1,4,3,2,0:T(8,128)} %get-tuple-element.288) | data formatting | bytes 4194304 | tf_op jit(solution)/shard_map/while | solution.py:234
  422.5 11.8 %while.43 = (s32[]{:T(128)}, f32[1,32,64,256]{3,2,1,0:T(8,128)S(1)}, f32[2,128,1,32,64]{1,4,3,2,0:T(8,128)}, f32[1,32,1]{1,2,0:T(1,128)S(1)}, f32[2,1,32,128]{3,...) while((s32[]{:T(128)}, ...), condition=%wide.region_14.15_spmd, body=%wide.region_12.14_spmd.sunk | while | flops 1020551168 | bytes 27939240 | solution.py:234
  448.9 7.1 %fusion.82 = bf16[2,256,2048]{1,0,2:T(2,128)(2,1)S(1)} fusion(f32[1,256,2048]{1,0,2:T(1,128)S(1)} %fusion.84, f32[1,256,2048]{1,0,2:T(1,128)S(1)} %fusion.83, pred[2,256]{1,0:T(4,128)(4,1)S(1)} %copy-done.24, f32[2048]{0:T(1024)S(1)} %copy-done.23, f32[2,256]{1,0:T(2,128)S(1)} %fusion.114), kind=kLoop, calls=%fused_computation.102 | loop fusion | flops 5242880 | bytes 6302208 | tf_op jit(solution)/shard_map/convert_element_type | solution.py:247
  (204 shorter events, 120.2 us)
Async XLA Ops:
  6.5 193.5 %all-gather.3.cloned.1.call-start = ((), (), s32[]{:S(2)}) async-start(), calls=%async_computation | async-start | bytes 18874368 | tf_op jit(solution)/shard_map/all_gather | solution.py:27
  7.4 26.6 %collective-permute-start = (bf16[3,4096]{1,0:T(4,128)(2,1)S(1)}, bf16[3,4096]{1,0:T(4,128)(2,1)S(1)}, u32[]{:S(2)}, u32[]{:S(2)}) collective-permute-start(bf16[3,4096]{1,0:T(4,128)(2,1)S(1)} %get-tuple-element.412), channel_id=1, source_target_pairs={{0,4},{4,8},{8,12},{12,16},{16,20},{20,24},{24,28},{1,5},{5,9},{9,... | collective-permute-start | bytes 73736 | tf_op jit(solution)/shard_map/ppermute | solution.py:21
  11.6 16.5 %collective-permute-start.1 = (bf16[3,2048]{0,1:T(8,128)(2,1)}, bf16[3,2048]{0,1:T(8,128)(2,1)}, u32[]{:S(2)}, u32[]{:S(2)}) collective-permute-start(bf16[3,2048]{0,1:T(8,128)(2,1)} %copy.81), channel_id=1, source_target_pairs={{0,4},{4,8},{8,12},{12,16},{16,20},{20,24},{24,28},{1,5},{5,9},{9,... | collective-permute-start | bytes 36872 | tf_op jit(solution)/shard_map/ppermute | solution.py:21
  48.1 267.2 %all-reduce.5.cloned.1.call-start = ((), (), s32[]{:S(2)}) async-start(), calls=%async_computation.1 | async-start | bytes 4194304 | tf_op jit(solution)/shard_map/psum | solution.py:49
  251.9 136.0 %all-reduce.7.cloned.1.call-start = ((), (), s32[]{:S(2)}) async-start(), calls=%async_computation.2 | async-start | bytes 4194304 | tf_op jit(solution)/shard_map/psum | solution.py:49
  269.4 3.3 copy-start.3
  269.4 3.3 copy-start.18
  277.9 3.4 copy-start.5
  319.0 2.5 copy-start.21
  396.6 3.8 copy-start.17
  396.6 4.0 copy-start.7
  396.6 4.0 copy-start.13
  396.6 4.0 copy-start.20
  407.5 3.8 copy-start.17
  407.5 4.0 copy-start.7
  407.5 4.0 copy-start.13
  407.5 4.0 copy-start.20
  414.6 4.8 %copy-start.9 = (f32[2,128,1,32,64]{1,4,3,2,0:T(8,128)S(1)}, f32[2,128,1,32,64]{1,4,3,2,0:T(8,128)}, u32[]{:S(2)}) copy-start(f32[2,128,1,32,64]{1,4,3,2,0:T(8,128)} %get-tuple-element.288) | copy-start | bytes 6291460
  414.6 4.8 %copy-start.16 = (f32[1,256,2048]{1,0,2:T(1,128)S(1)}, f32[1,256,2048]{1,0,2:T(1,128)}, u32[]{:S(2)}) copy-start(f32[1,256,2048]{1,0,2:T(1,128)} %convert_element_type.235) | copy-start | bytes 6291460
  434.3 3.5 copy-start.12
  434.3 3.5 copy-start.15
  440.0 4.4 copy-start.6
  444.4 4.5 copy-start.23
  444.5 4.5 copy-start.24
  (17 other events, 27.5 us)
Sparse Core Ops, SparseCore 0:
  48.2 151.6 all-gather.2
  252.0 63.2 all-reduce.4
  318.5 69.2 all-reduce.6
where the time goes:
time: 469 us; the launch traced here: 467 us
  waiting for transfers between devices  191 us (41%)
  other arithmetic  126 us (27%)
  local copies, waits for them, and re-layouts  63 us (13%)
  blocking collectives  44.5 us (9%)
  matrix products  19.6 us (4%)
  between operations  14.3 us (3%)
  starting transfers between devices  7.83 us (2%)
    psum x2, waiting for transfers between devices, from_root(): return lax.psum(jnp.where(mine, array, jnp.zeros_like(array)), axis)  97.4 us
    all_gather x1, waiting for transfers between devices, carried_in(): lax.all_gather(part.astype(kind), axis)  93.9 us
    select_n x8, other arithmetic, hop(): return jax.tree.map(lambda a, b: jnp.where(reached, a, b), new, before)  46.4 us
    unnamed x1, blocking collectives  28.2 us
    convert_element_type x4, other arithmetic, causal_conv(): return jax.nn.silu(summed).astype(jnp.bfloat16)  21.2 us
    unnamed x51, local copies, waits for them, and re-layouts  19.9 us
    psum x1, blocking collectives, from_root(): return lax.psum(jnp.where(mine, array, jnp.zeros_like(array)), axis)  16.2 us
    while x4, local copies, waits for them, and re-layouts, local(): _, block_outs = lax.scan(advance, start_state[None], block_inputs)  9.78 us
  transfers between devices with their start and end apart: 5, of which 3 were waited for; matrix products, arithmetic and copies ran while one was open for 14% of the time, Pallas kernels for 0%

commit v1 on v0

--- a/solution.py
+++ b/solution.py
@@ -1,6 +1,8 @@
 import jax
 import jax.numpy as jnp
 from jax import lax
+from jax.experimental import pallas as pl
+from jax.experimental.pallas import tpu as pltpu
 from jax.sharding import PartitionSpec as P
 
 STATE_HEADS = 256
@@ -93,7 +95,7 @@
     )
 
 
-def local(
+def any_shape(
     prompt_inner,
     prompt_proj,
     prompt_step,
@@ -247,6 +249,468 @@
     return jnp.where(live_rows[:, :, None], result, 0.0).astype(jnp.bfloat16)
 
 
+LOG2E = 1.4426950408889634
+AXES = ("prompt", "comp")
+CHUNKS = 2
+TAIL = 16
+VMEM_BYTES = 48 * 1024 * 1024
+
+
+def routed(block, route):
+    columns = lax.axis_size("comp")
+    pairs = []
+    for row in range(lax.axis_size("prompt")):
+        for column in range(columns):
+            target = route(row // 2, row % 2, column)
+            if target is not None:
+                plane, core, to = target
+                pairs.append((row * columns + column, (2 * plane + core) * columns + to))
+    return lax.ppermute(block, AXES, pairs)
+
+
+def half_silu(value):
+    return 0.5 * value * (1.0 + jnp.tanh(0.5 * value))
+
+
+def conv_rows(padded, taps, lead, block):
+    rows = block.shape[0]
+    width = block.shape[1]
+    padded[0:8, 0:width] = lead.astype(jnp.float32)[TAIL - 8 :]
+    padded[8 : 8 + rows, 0:width] = block.astype(jnp.float32)
+    wide = taps.astype(jnp.float32)
+    total = wide[0:1] * padded[5 : 5 + rows, 0:width]
+    for tap in range(1, CONV):
+        total = total + wide[tap : tap + 1] * padded[5 + tap : 5 + tap + rows, 0:width]
+    return half_silu(total)
+
+
+def spread_heads(first, heads, width):
+    row = lax.broadcasted_iota(jnp.int32, (heads, width), 0)
+    col = lax.broadcasted_iota(jnp.int32, (heads, width), 1)
+    return row == first + col // HEAD_WIDTH
+
+
+def contract(lhs, rhs, dims, precision=None):
+    return lax.dot_general(
+        lhs, rhs, (dims, ((), ())), preferred_element_type=jnp.float32, precision=precision
+    )
+
+
+def softplus(value):
+    return jnp.maximum(value, 0.0) + jnp.log1p(jnp.exp(-jnp.abs(value)))
+
+
+def prompt_weights_kernel(
+    place, own_b, other_b, halo_b, taps, own_step, other_step, decay, w_out, b_out, log_out, padded
+):
+    core = place[2]
+    rows, heads = own_b.shape[0], own_step.shape[0]
+    first_own = core == 0
+    rate = jnp.exp(decay[...])
+    dt_own, dt_other = softplus(own_step[...]), softplus(other_step[...])
+    row = lax.broadcasted_iota(jnp.int32, (rows, rows), 0)
+    col = lax.broadcasted_iota(jnp.int32, (rows, rows), 1)
+    later = (col > row).astype(jnp.float32)
+    same = (col == row).astype(jnp.float32)
+    ones = jnp.ones((8, rows), jnp.float32)
+    last = ((1,), (1,))
+    sum_own = contract(ones, dt_own, last, HIGHEST)[0:1]
+    sum_other = contract(ones, dt_other, last, HIGHEST)[0:1]
+    after_own = contract(later, dt_own, last, HIGHEST) + jnp.where(first_own, sum_other, 0.0)
+    after_other = contract(later, dt_other, last, HIGHEST) + jnp.where(first_own, 0.0, sum_own)
+    w_out[0:rows] = jnp.exp(-rate * after_own) * contract(same, dt_own, last, HIGHEST)
+    w_out[rows:] = jnp.exp(-rate * after_other) * contract(same, dt_other, last, HIGHEST)
+    total = jnp.broadcast_to(-rate * (sum_own + sum_other), (8, heads))
+    spread = spread_heads(0, heads, heads * HEAD_WIDTH).astype(jnp.float32)
+    wide = contract(total, spread, ((1,), (0,)), HIGHEST)
+    high = wide.astype(jnp.bfloat16)
+    rest = wide - high.astype(jnp.float32)
+    mid = rest.astype(jnp.bfloat16)
+    low = (rest - mid.astype(jnp.float32)).astype(jnp.bfloat16)
+    which = lax.broadcasted_iota(jnp.int32, wide.shape, 0)
+    parts = jnp.where(
+        which == 0,
+        high.astype(jnp.float32),
+        jnp.where(which == 1, mid.astype(jnp.float32), jnp.where(which == 2, low.astype(jnp.float32), 0.0)),
+    )
+    log_out[...] = jnp.concatenate([parts, jnp.zeros_like(parts)], axis=0).astype(jnp.bfloat16)
+    own_last, other_last, halo = own_b[rows - TAIL :], other_b[rows - TAIL :], halo_b[...]
+    lead_own = jnp.where(first_own, halo.astype(jnp.float32), other_last.astype(jnp.float32))
+    lead_other = jnp.where(first_own, own_last.astype(jnp.float32), halo.astype(jnp.float32))
+    conv_own = conv_rows(padded, taps[...], lead_own, own_b[...])
+    b_out[:, 0:rows] = jnp.transpose(conv_own).astype(jnp.bfloat16)
+    conv_other = conv_rows(padded, taps[...], lead_other, other_b[...])
+    b_out[:, rows:] = jnp.transpose(conv_other).astype(jnp.bfloat16)
+
+
+def prompt_state_kernel(
+    chunk, parts, place, own, other, halo, taps, weights, b_turned, logs, *rest
+):
+    outs, padded = rest[:parts], rest[parts]
+    column, core = place[1], place[2]
+    first_own = core == 0
+    rows = own.shape[0]
+    width = outs[0].shape[1]
+    part_width = own.shape[1] // parts
+    heads = weights.shape[1]
+    state = b_turned.shape[0]
+    w = weights[...].astype(jnp.bfloat16)
+    for step in range(parts):
+        part = column ^ step
+        start = part * part_width + chunk * width
+        cols = pl.ds(pl.multiple_of(start, width), width)
+        spread = spread_heads(start // HEAD_WIDTH, heads, width).astype(jnp.bfloat16)
+        w_wide = contract(w, spread, ((1,), (0,)))
+        own_x, other_x, halo_x = own[:, cols], other[:, cols], halo[:, cols]
+        own_last, other_last = own_x[rows - TAIL :], other_x[rows - TAIL :]
+        lead_own = jnp.where(first_own, halo_x.astype(jnp.float32), other_last.astype(jnp.float32))
+        lead_other = jnp.where(first_own, own_last.astype(jnp.float32), halo_x.astype(jnp.float32))
+        x_own = conv_rows(padded, taps[:, cols], lead_own, own_x) * w_wide[0:rows]
+        x_other = conv_rows(padded, taps[:, cols], lead_other, other_x) * w_wide[rows:]
+        mine = contract(b_turned[:, 0:rows], x_own.astype(jnp.bfloat16), ((1,), (0,)))
+        theirs = contract(b_turned[:, rows:], x_other.astype(jnp.bfloat16), ((1,), (0,)))
+        outs[step][0:state] = (mine + theirs).astype(jnp.bfloat16)
+        outs[step][state:] = logs[:, cols]
+
+
+def join_state_kernel(place, *refs):
+    arrived, out = refs[:-1], refs[-1]
+    plane = place[0]
+    state = out.shape[0]
+    totals = []
+    for ref in arrived:
+        rows = ref[state:].astype(jnp.float32)
+        totals.append(rows[0:1] + rows[1:2] + rows[2:3])
+    joined = None
+    for step, ref in enumerate(arrived):
+        after = jnp.zeros_like(totals[0])
+        for other in range(len(arrived)):
+            if other != step:
+                after = after + jnp.where((plane ^ other) > (plane ^ step), totals[other], 0.0)
+        term = jnp.exp(after) * ref[0:state].astype(jnp.float32)
+        joined = term if joined is None else joined + term
+    out[...] = joined.astype(jnp.bfloat16)
+
+
+def completion_kernel(
+    place, inner, gate, b_in, c_in, lead, lead_b, lead_c, taps, taps_b, taps_c, step,
+    decay_row, decay_col, fixed_out, factor_out, c_out, padded, diag_low, rows_high,
+):
+    rows = inner.shape[1]
+    width = inner.shape[2]
+    heads = step.shape[1]
+    half = rows // 2
+
+    @pl.when(pl.program_id(1) == 0)
+    def _():
+        b = conv_rows(padded, taps_b[...], lead_b[...], b_in[0]).astype(jnp.bfloat16)
+        c = conv_rows(padded, taps_c[...], lead_c[...], c_in[0]).astype(jnp.bfloat16)
+        c_out[0] = c
+        scores = contract(c, b, ((1,), (1,)))
+        row = lax.broadcasted_iota(jnp.int32, (rows, rows), 0)
+        col = lax.broadcasted_iota(jnp.int32, (rows, rows), 1)
+        scores = jnp.where(row >= col, scores, 0.0)
+        diag_low[...] = scores[0:half, 0:half]
+        rows_high[...] = scores[half:]
+
+    x = conv_rows(padded, taps[...], lead[...], inner[0])
+    x = x.astype(jnp.bfloat16)
+    dt = softplus(step[0])
+    row = lax.broadcasted_iota(jnp.int32, (rows, rows), 0)
+    col = lax.broadcasted_iota(jnp.int32, (rows, rows), 1)
+    upto = (col <= row).astype(jnp.float32)
+    before = (row <= col).astype(jnp.float32)
+    cum_col = contract(upto, dt, ((1,), (1,)), HIGHEST) * (-LOG2E * jnp.exp(decay_row[0]))
+    cum_row = contract(dt, before, ((1,), (0,)), HIGHEST) * (-LOG2E * jnp.exp(decay_col[...]))
+    log_dt = jnp.log(dt) * LOG2E
+    base_row = cum_row - log_dt
+    silu_gate = half_silu(gate[0].astype(jnp.float32))
+    spread = spread_heads(0, heads, width).astype(jnp.bfloat16)
+    decay_wide = contract(jnp.exp2(cum_col).astype(jnp.bfloat16), spread, ((1,), (0,)))
+    factor_out[0] = (decay_wide * silu_gate).astype(jnp.bfloat16)
+    low, high = diag_low[...], rows_high[...]
+    pair = 2 * HEAD_WIDTH
+    lane = lax.broadcasted_iota(jnp.int32, (rows, pair), 1)
+    for first in range(0, heads, 2):
+        at = first * HEAD_WIDTH
+        x_pair = x[:, at : at + pair]
+        zero = jnp.zeros_like(x_pair)
+        left = jnp.where(lane < HEAD_WIDTH, x_pair, zero)
+        right = jnp.where(lane < HEAD_WIDTH, zero, x_pair)
+        lows, highs = [], []
+        for h in (first, first + 1):
+            cc = cum_col[:, h : h + 1]
+            rr, ll = base_row[h : h + 1], log_dt[h : h + 1]
+            grown = jnp.minimum(cc[0:half] - rr[:, 0:half], ll[:, 0:half])
+            lows.append((low * jnp.exp2(grown)).astype(jnp.bfloat16))
+            grown = jnp.minimum(cc[half:] - rr, ll)
+            highs.append((high * jnp.exp2(grown)).astype(jnp.bfloat16))
+        y_low = contract(
+            jnp.concatenate(lows, axis=1),
+            jnp.concatenate([left[0:half], right[0:half]], axis=0),
+            ((1,), (0,)),
+        )
+        y_high = contract(
+            jnp.concatenate(highs, axis=1), jnp.concatenate([left, right], axis=0), ((1,), (0,))
+        )
+        fixed_out[0, 0:half, at : at + pair] = (
+            y_low * silu_gate[0:half, at : at + pair]
+        ).astype(jnp.bfloat16)
+        fixed_out[0, half:, at : at + pair] = (
+            y_high * silu_gate[half:, at : at + pair]
+        ).astype(jnp.bfloat16)
+
+
+def finish_kernel(parts, chunks, place, live, c_ref, fixed, factor, gain, *refs):
+    states, out, gated = refs[: parts * chunks], refs[-2], refs[-1]
+    column = place[1]
+    slot = pl.program_id(0)
+    rows, features = out.shape[1], out.shape[2]
+    width = states[0].shape[1]
+    part_width = features // parts
+    c = c_ref[0]
+    squares = jnp.zeros((rows, 1), jnp.float32)
+    for chunk in range(chunks):
+        for step in range(parts):
+            start = (column ^ step) * part_width + chunk * width
+            cols = pl.ds(pl.multiple_of(start, width), width)
+            read = contract(c, states[chunk * parts + step][...], ((1,), (0,)))
+            value = fixed[0, :, cols].astype(jnp.float32) + read * factor[0, :, cols].astype(
+                jnp.float32
+            )
+            gated[:, cols] = value
+            squares = squares + jnp.sum(value * value, axis=1, keepdims=True)
+    scale = lax.rsqrt(squares / features + EPS)
+    alive = lax.broadcasted_iota(jnp.int32, (rows, 1), 0) < live[slot]
+    scale = jnp.where(alive, scale, 0.0)
+    out[0] = (gated[...] * scale * gain[...]).astype(jnp.bfloat16)
+
+
+def run(kernel, name, place, out_shape, in_specs, out_specs, operands, grid=(1,), scratch=(), scalars=1):
+    return pl.pallas_call(
+        kernel,
+        out_shape=out_shape,
+        grid_spec=pltpu.PrefetchScalarGridSpec(
+            num_scalar_prefetch=scalars,
+            grid=grid,
+            in_specs=in_specs,
+            out_specs=out_specs,
+            scratch_shapes=scratch,
+        ),
+        compiler_params=pltpu.CompilerParams(
+            dimension_semantics=("arbitrary",) * len(grid), vmem_limit_bytes=VMEM_BYTES
+        ),
+        name=name,
+    )(*place, *operands)
+
+
+def matched(
+    prompt_inner,
+    prompt_proj,
+    prompt_step,
+    completion_inner,
+    completion_gate,
+    completion_projections,
+    sample_step,
+    sample_length,
+    decay_log,
+    conv_inner,
+    conv_proj,
+    norm_gain,
+):
+    parts = lax.axis_size("comp")
+    row, column = lax.axis_index("prompt"), lax.axis_index("comp")
+    plane, core = row // 2, row % 2
+    group = 2 * column + core
+    rows = prompt_inner.shape[0]
+    heads = sample_step.shape[0]
+    features = heads * HEAD_WIDTH
+    place = jnp.stack([plane, column, core, row]).astype(jnp.int32)
+    bf16, f32 = jnp.bfloat16, jnp.float32
+
+    def take(array, start, size, axis):
+        return lax.dynamic_slice_in_dim(array, start, size, axis)
+
+    swap = lambda z, k, c: (z, 1 - k, c)
+    other_inner = routed(take(prompt_inner, (1 - core) * features, features, 1), swap)
+    other_b = routed(take(prompt_proj, (2 * column + 1 - core) * STATE_WIDTH, STATE_WIDTH, 1), swap)
+    other_step = routed(take(prompt_step, (1 - core) * heads, heads, 0), swap)
+    own_step = take(prompt_step, core * heads, heads, 0)
+
+    last_inner, last_proj = prompt_inner[rows - TAIL :], prompt_proj[rows - TAIL :]
+    planes = lax.axis_size("prompt") // 2
+    halo, tail = None, None
+    for to in range(2):
+        inner_to = last_inner[:, to * features : (to + 1) * features]
+        b_to = take(last_proj, (2 * column + to) * STATE_WIDTH, STATE_WIDTH, 1)
+        c_to = take(last_proj, (STATE_GROUPS + 2 * column + to) * STATE_WIDTH, STATE_WIDTH, 1)
+        near = routed(
+            jnp.concatenate([inner_to, b_to], axis=1),
+            lambda z, k, c: (z + 1, to, c) if k == 1 and z + 1 < planes else None,
+        )
+        far = routed(
+            jnp.concatenate([inner_to, b_to, c_to], axis=1),
+            lambda z, k, c: (c, to, c) if k == 1 and z + 1 == planes else None,
+        )
+        halo = near if halo is None else halo + near
+        tail = far if tail is None else tail + far
+    first_tail = tail
+    for step in range(1, parts):
+        tail = tail + routed(first_tail, lambda z, k, c: (z, k, z ^ step) if c == z else None)
+
+    whole = lambda shape: pl.BlockSpec(shape, lambda *_: (0,) * len(shape))
+    decay_group = take(decay_log, group * heads, heads, 0)[None]
+    weights, b_turned, logs = run(
+        prompt_weights_kernel,
+        "prompt_weights",
+        (place,),
+        (
+            jax.ShapeDtypeStruct((2 * rows, heads), f32),
+            jax.ShapeDtypeStruct((STATE_WIDTH, 2 * rows), bf16),
+            jax.ShapeDtypeStruct((TAIL, features), bf16),
+        ),
+        [
+            pl.BlockSpec((rows, STATE_WIDTH), lambda i, s: (0, 2 * s[1] + s[2])),
+            whole((rows, STATE_WIDTH)),
+            pl.BlockSpec((TAIL, STATE_WIDTH), lambda i, s: (0, features // STATE_WIDTH)),
+            pl.BlockSpec((CONV, STATE_WIDTH), lambda i, s: (0, 2 * s[1] + s[2])),
+            whole((heads, rows)),
+            whole((heads, rows)),
+            whole((1, heads)),
+        ],
+        (whole((2 * rows, heads)), whole((STATE_WIDTH, 2 * rows)), whole((TAIL, features))),
+        (prompt_proj, other_b, halo, conv_proj, own_step, other_step, decay_group),
+        scratch=[pltpu.VMEM((rows + 8, STATE_WIDTH), f32)],
+    )
+    width = features // parts // CHUNKS
+    message = jax.ShapeDtypeStruct((STATE_WIDTH + TAIL, width), bf16)
+    joined = []
+    for chunk in range(CHUNKS):
+        sent = run(
+            lambda *refs, chunk=chunk: prompt_state_kernel(chunk, parts, *refs),
+            "prompt_state",
+            (place,),
+            (message,) * parts,
+            [
+                pl.BlockSpec((rows, features), lambda i, s: (0, s[2])),
+                whole((rows, features)),
+                pl.BlockSpec((TAIL, features), lambda i, s: (0, 0)),
+                pl.BlockSpec((CONV, features), lambda i, s: (0, 2 * s[1] + s[2])),
+                whole((2 * rows, heads)),
+                whole((STATE_WIDTH, 2 * rows)),
+                whole((TAIL, features)),
+            ],
+            (whole(message.shape),) * parts,
+            (prompt_inner, other_inner, halo, conv_inner, weights, b_turned, logs),
+            scratch=[pltpu.VMEM((rows + 8, width), f32)],
+        )
+        held = [sent[0]] + [
+            routed(sent[step], lambda z, k, c: (z, k, c ^ step)) for step in range(1, parts)
+        ]
+        ready = [lax.select_n(column ^ plane ^ step, *held) for step in range(parts)]
+        arrived = [ready[0]] + [
+            routed(ready[step], lambda z, k, c: (z ^ step, k, c)) for step in range(1, parts)
+        ]
+        state = run(
+            join_state_kernel,
+            "join_state",
+            (place,),
+            jax.ShapeDtypeStruct((STATE_WIDTH, width), bf16),
+            [whole(message.shape)] * parts,
+            whole((STATE_WIDTH, width)),
+            arrived,
+        )
+        joined += [state] + [
+            routed(state, lambda z, k, c: (z, k, c ^ step)) for step in range(1, parts)
+        ]
+
+    slots, positions = completion_inner.shape[:2]
+    block_heads = 8
+    block = block_heads * HEAD_WIDTH
+    blocks = heads // block_heads
+    decay_own = take(decay_log, row * heads, heads, 0)
+    cols_at = features // block
+    c_at = STATE_GROUPS
+    fixed, factor, c_rows = run(
+        completion_kernel,
+        "completion_blocks",
+        (place,),
+        (
+            jax.ShapeDtypeStruct((slots, positions, features), bf16),
+            jax.ShapeDtypeStruct((slots, positions, features), bf16),
+            jax.ShapeDtypeStruct((slots, positions, STATE_WIDTH), bf16),
+        ),
+        [
+            pl.BlockSpec((1, positions, block), lambda i, j, s: (i, 0, j)),
+            pl.BlockSpec((1, positions, block), lambda i, j, s: (i, 0, j)),
+            pl.BlockSpec((1, positions, STATE_WIDTH), lambda i, j, s: (i, 0, s[3])),
+            pl.BlockSpec((1, positions, STATE_WIDTH), lambda i, j, s: (i, 0, c_at + s[3])),
+            pl.BlockSpec((TAIL, block), lambda i, j, s: (0, j)),
+            pl.BlockSpec((TAIL, STATE_WIDTH), lambda i, j, s: (0, features // STATE_WIDTH)),
+            pl.BlockSpec((TAIL, STATE_WIDTH), lambda i, j, s: (0, features // STATE_WIDTH + 1)),
+            pl.BlockSpec((CONV, block), lambda i, j, s: (0, s[3] * cols_at + j)),
+            pl.BlockSpec((CONV, STATE_WIDTH), lambda i, j, s: (0, s[3])),
+            pl.BlockSpec((CONV, STATE_WIDTH), lambda i, j, s: (0, c_at + s[3])),
+            pl.BlockSpec((1, block_heads, positions), lambda i, j, s: (i, j, 0)),
+            pl.BlockSpec((1, 1, block_heads), lambda i, j, s: (j, 0, 0)),
+            pl.BlockSpec((block_heads, 1), lambda i, j, s: (j, 0)),
+        ],
+        (
+            pl.BlockSpec((1, positions, block), lambda i, j, s: (i, 0, j)),
+            pl.BlockSpec((1, positions, block), lambda i, j, s: (i, 0, j)),
+            pl.BlockSpec((1, positions, STATE_WIDTH), lambda i, j, s: (i, 0, 0)),
+        ),
+        (
+            completion_inner,
+            completion_gate,
+            completion_projections,
+            completion_projections,
+            tail,
+            tail,
+            tail,
+            conv_inner,
+            conv_proj,
+            conv_proj,
+            jnp.transpose(sample_step, (1, 0, 2)),
+            decay_own.reshape(blocks, 1, block_heads),
+            decay_own[:, None],
+        ),
+        grid=(slots, blocks),
+        scratch=[
+            pltpu.VMEM((positions + 8, block), f32),
+            pltpu.VMEM((positions // 2, positions // 2), f32),
+            pltpu.VMEM((positions // 2, positions), f32),
+        ],
+    )
+    return run(
+        lambda *refs: finish_kernel(parts, CHUNKS, *refs),
+        "finish",
+        (place, sample_length),
+        jax.ShapeDtypeStruct((slots, positions, features), bf16),
+        [
+            pl.BlockSpec((1, positions, STATE_WIDTH), lambda i, s, n: (i, 0, 0)),
+            pl.BlockSpec((1, positions, features), lambda i, s, n: (i, 0, 0)),
+            pl.BlockSpec((1, positions, features), lambda i, s, n: (i, 0, 0)),
+            whole((1, features)),
+        ]
+        + [whole((STATE_WIDTH, width))] * (parts * CHUNKS),
+        pl.BlockSpec((1, positions, features), lambda i, s, n: (i, 0, 0)),
+        [c_rows, fixed, factor, norm_gain[None]] + joined,
+        grid=(slots,),
+        scratch=[pltpu.VMEM((positions, features), f32)],
+        scalars=2,
+    )
+
+
+def local(*arrays):
+    columns, prompts = lax.axis_size("comp"), lax.axis_size("prompt")
+    heads_col, heads_row = arrays[2].shape[0], arrays[6].shape[0]
+    one_group = heads_row == STATE_HEADS // STATE_GROUPS and heads_col == 2 * heads_row
+    if one_group and prompts == 2 * columns and columns & (columns - 1) == 0:
+        return matched(*arrays)
+    return any_shape(*arrays)
+
+
 def solution(mesh):
     placed = (
         P("prompt", "comp"),

time: 469 us -> 105 us (0.22)
  waiting for transfers between devices: 191 us -> 14.2 us
  other arithmetic: 126 us -> 6.73 us
  local copies, waits for them, and re-layouts: 63 us -> 14 us
  blocking collectives: 44.5 us -> 0 us
  Pallas kernels: 0 us -> 30.5 us
  starting transfers between devices: 7.83 us -> 37.5 us
  matrix products: 19.6 us -> 0 us
  between operations: 14.3 us -> 0.41 us
    psum x2 -> x0, waiting for transfers between devices: 97.4 us -> none  [from_root(): return lax.psum(jnp.where(mine, array, jnp.zeros_like(array)), axis)]
    all_gather x1 -> x0, waiting for transfers between devices: 93.9 us -> none  [carried_in(): lax.all_gather(part.astype(kind), axis)]
    select_n x14 -> x2, other arithmetic: 55.9 us -> 1.18 us  [matched(): lax.select_n(column ^ plane ^ step, *held)]
    convert_element_type x16 -> x0, other arithmetic: 45.5 us -> none  [the longest x4 21.2 us: causal_conv(): return jax.nn.silu(summed).astype(jnp.bfloat16)]
    pallas_call x0 -> x7, Pallas kernels: none -> 30.5 us  [run(): pl.pallas_call(kernel, out_shape=out_shape, grid_spec=pltpu.PrefetchScala...]
    ppermute x2 -> x28, starting transfers between devices: 7.74 us -> 37.5 us  [routed(): return lax.ppermute(block, AXES, pairs)]
    unnamed x1 -> x0, blocking collectives: 28.2 us -> none
    dot_general x17 -> x0, matrix products: 19.6 us -> none  [the longest x4 5.99 us: block_scan(): jnp.einsum('ign,gkdn->igkd', c_blk.astype(jnp.float32), state_in, precisi...]
  transfers between devices with their start and end apart: 5 -> 28, of which waited for: 3 -> 4; matrix products, arithmetic and copies ran while one was open for 14% -> 12% of each run, Pallas kernels for 0% -> 23%
where the time goes in v1:
time: 105 us; the launch traced here: 103 us
  starting transfers between devices  37.5 us (36%)
  Pallas kernels  30.5 us (29%)
  waiting for transfers between devices  14.2 us (14%)
  local copies, waits for them, and re-layouts  14 us (13%)
  other arithmetic  6.73 us (6%)
    ppermute x28, starting transfers between devices, routed(): return lax.ppermute(block, AXES, pairs)  37.5 us
    pallas_call x7, Pallas kernels, run(): pl.pallas_call(kernel, out_shape=out_shape, grid_spec=pltpu.PrefetchScala...  30.5 us
    ppermute x28, waiting for transfers between devices, routed(): return lax.ppermute(block, AXES, pairs)  14.2 us
    unnamed x41, local copies, waits for them, and re-layouts  6.9 us
    dynamic_slice x4, local copies, waits for them, and re-layouts, take(): return lax.dynamic_slice_in_dim(array, start, size, axis)  5.39 us
    concatenate x2, other arithmetic, matched(): jnp.concatenate([inner_to, b_to], axis=1)  2.96 us
  transfers between devices with their start and end apart: 28, of which 4 were waited for; matrix products, arithmetic and copies ran while one was open for 12% of the time, Pallas kernels for 23%

profile of v1, /device:TPU:0, one launch (start us, length us, event | category | flops | bytes accessed | tf_op | source)
XLA Modules:
  0.0 103.3 jit_solution(12245827308356384228)
XLA Ops:
  1.4 2.3 %constant_dynamic-slice_fusion.3 = bf16[256,2048]{1,0:T(8,128)(2,1)} fusion(bf16[256,4096]{1,0:T(8,128)(2,1)} %refs_1_.4, s32[]{:T(128)S(6)} %select_n.220), kind=kLoop, calls=%fused_computation.17 | loop fusion | bytes 2097156 | tf_op jit(solution)/shard_map/dynamic_slice | solution.py:532
  5.0 1.5 %pad_maximum_fusion.2 = bf16[16,2304]{1,0:T(8,128)(2,1)} fusion(bf16[16,256]{1,0:T(8,128)(2,1)S(1)} %get-tuple-element.46, bf16[16,2048]{1,0:T(8,128)(2,1)} %get-tuple-element.34), kind=kLoop, calls=%fused_computation.11 | loop fusion | flops 147456 | bytes 147456 | tf_op jit(solution)/shard_map/concatenate | solution.py:548
  7.2 1.5 %pad_maximum_fusion.3 = bf16[16,2304]{1,0:T(8,128)(2,1)} fusion(bf16[16,256]{1,0:T(8,128)(2,1)S(1)} %get-tuple-element.43, bf16[16,2048]{1,0:T(8,128)(2,1)} %get-tuple-element.33), kind=kLoop, calls=%fused_computation.12 | loop fusion | flops 147456 | bytes 147456 | tf_op jit(solution)/shard_map/concatenate | solution.py:548
  9.9 1.6 %constant_dynamic-slice_fusion.2 = bf16[256,256]{1,0:T(8,128)(2,1)} fusion(bf16[256,4096]{1,0:T(8,128)(2,1)} %own_b.1, s32[]{:T(128)S(6)} %select_n.221), kind=kLoop, calls=%fused_computation.16 | loop fusion | bytes 262148 | tf_op jit(solution)/shard_map/dynamic_slice | solution.py:532
  11.5 7.0 %collective-permute-start.8 = (bf16[256,256]{1,0:T(8,128)(2,1)}, bf16[256,256]{1,0:T(8,128)(2,1)}, u32[]{:S(2)}, u32[]{:S(2)}) collective-permute-start(bf16[256,256]{1,0:T(8,128)(2,1)} %constant_dynamic-slice_fusion.2), channel_id=1, source_target_pairs={{0,4},{1,5},{2,6},{3,7},{4,0},{5,1},{6,2},{7,3},{8,12},{9,13},{10,... | collective-permute-start | bytes 393224 | tf_op jit(solution)/shard_map/ppermute | solution.py:268
  21.6 1.6 %copy-done.1 = bf16[256,4096]{1,0:T(8,128)(2,1)S(1)} copy-done((bf16[256,4096]{1,0:T(8,128)(2,1)S(1)}, bf16[256,4096]{1,0:T(8,128)(2,1)}, u32[]{:S(2)}) %copy-start.1) | copy-done | bytes 2097176
  23.9 2.9 %prompt_weights.1 = (f32[512,32]{1,0:T(8,128)S(1)}, bf16[256,512]{1,0:T(8,128)(2,1)S(1)}, bf16[16,2048]{1,0:T(8,128)(2,1)S(1)}) custom-call(s32[4]{0:T(128)S(1)} %pad_add_fusion.place.refs_0_, bf16[256,4096]{1,0:T(8,128)(2,1)S(1)} %copy-done.1, bf16[256,256]{1,0:T(8,128)(2,1)} %collective-permute-done.8.other_b, bf16[16,2304]{1,0:T(8,128)(2,1)S(1)} %add.80.halo_b.refs_3_, ...), custom_call_target="tpu_custom_call" | custom-call | tf_op jit(solution)/shard_map/prompt_weights/pallas_call | solution.py:490
  26.9 3.6 %prompt_state.3 = (bf16[272,256]{1,0:T(8,128)(2,1)S(1)}, bf16[272,256]{1,0:T(8,128)(2,1)}, bf16[272,256]{1,0:T(8,128)(2,1)}, bf16[272,256]{1,0:T(8,128)(2,1)}) custom-call(s32[4]{0:T(128)S(1)} %pad_add_fusion.place.refs_0_, bf16[256,4096]{1,0:T(8,128)(2,1)S(1)} %copy-done, bf16[256,2048]{1,0:T(8,128)(2,1)S(1)} %collective-permute-done.5.refs_2_, ...), custom_call_target="tpu_custom_call" | custom-call | tf_op jit(solution)/shard_map/prompt_state/pallas_call | solution.py:490
  31.9 1.5 %collective-permute-start.19 = (bf16[272,256]{1,0:T(8,128)(2,1)}, bf16[272,256]{1,0:T(8,128)(2,1)}, u32[]{:S(2)}, u32[]{:S(2)}) collective-permute-start(bf16[272,256]{1,0:T(8,128)(2,1)} %get-tuple-element.30), channel_id=1, source_target_pairs={{0,1},{1,0},{2,3},{3,2},{4,5},{5,4},{6,7},{7,6},{8,9},{9,8},{10,11... | collective-permute-start | bytes 417800 | tf_op jit(solution)/shard_map/ppermute | solution.py:268
  33.4 1.5 %collective-permute-start.20 = (bf16[272,256]{1,0:T(8,128)(2,1)}, bf16[272,256]{1,0:T(8,128)(2,1)}, u32[]{:S(2)}, u32[]{:S(2)}) collective-permute-start(bf16[272,256]{1,0:T(8,128)(2,1)} %get-tuple-element.31), channel_id=1, source_target_pairs={{0,2},{1,3},{2,0},{3,1},{4,6},{5,7},{6,4},{7,5},{8,10},{9,11},{10,... | collective-permute-start | bytes 417800 | tf_op jit(solution)/shard_map/ppermute | solution.py:268
  39.2 3.0 %prompt_state.2 = (bf16[272,256]{1,0:T(8,128)(2,1)S(1)}, bf16[272,256]{1,0:T(8,128)(2,1)S(1)}, bf16[272,256]{1,0:T(8,128)(2,1)S(1)}, bf16[272,256]{1,0:T(8,128)(2,1)S(1)}) custom-call(s32[4]{0:T(128)S(1)} %pad_add_fusion.place.refs_0_, bf16[256,4096]{1,0:T(8,128)(2,1)S(1)} %copy-done, bf16[256,2048]{1,0:T(8,128)(2,1)S(1)} %collective-permute-done.5.refs_2_, ...), custom_call_target="tpu_custom_call" | custom-call | tf_op jit(solution)/shard_map/prompt_state/pallas_call | solution.py:490
  42.2 1.5 %collective-permute-start.10 = (bf16[272,256]{1,0:T(8,128)(2,1)S(1)}, bf16[272,256]{1,0:T(8,128)(2,1)S(1)}, u32[]{:S(2)}, u32[]{:S(2)}) collective-permute-start(bf16[272,256]{1,0:T(8,128)(2,1)S(1)} %get-tuple-element.26), channel_id=1, source_target_pairs={{0,1},{1,0},{2,3},{3,2},{4,5},{5,4},{6,7},{7,6},{8,9},{9,8},{10,11... | collective-permute-start | bytes 417800 | tf_op jit(solution)/shard_map/ppermute | solution.py:268
  43.8 1.5 %collective-permute-start.11 = (bf16[272,256]{1,0:T(8,128)(2,1)S(1)}, bf16[272,256]{1,0:T(8,128)(2,1)S(1)}, u32[]{:S(2)}, u32[]{:S(2)}) collective-permute-start(bf16[272,256]{1,0:T(8,128)(2,1)S(1)} %get-tuple-element.27), channel_id=1, source_target_pairs={{0,2},{1,3},{2,0},{3,1},{4,6},{5,7},{6,4},{7,5},{8,10},{9,11},{10,... | collective-permute-start | bytes 417800 | tf_op jit(solution)/shard_map/ppermute | solution.py:268
  47.0 1.4 %collective-permute-done.10 = bf16[272,256]{1,0:T(8,128)(2,1)S(1)} collective-permute-done((bf16[272,256]{1,0:T(8,128)(2,1)S(1)}, bf16[272,256]{1,0:T(8,128)(2,1)S(1)}, u32[]{:S(2)}, u32[]{:S(2)}) %collective-permute-start.10) | collective-permute-done | bytes 139296 | tf_op jit(solution)/shard_map/ppermute | solution.py:268
  49.4 2.4 %collective-permute-done.11 = bf16[272,256]{1,0:T(8,128)(2,1)S(1)} collective-permute-done((bf16[272,256]{1,0:T(8,128)(2,1)S(1)}, bf16[272,256]{1,0:T(8,128)(2,1)S(1)}, u32[]{:S(2)}, u32[]{:S(2)}) %collective-permute-start.11) | collective-permute-done | bytes 139296 | tf_op jit(solution)/shard_map/ppermute | solution.py:268
  55.4 3.0 %collective-permute-start.14 = (bf16[272,256]{1,0:T(8,128)(2,1)S(1)}, bf16[272,256]{1,0:T(8,128)(2,1)S(1)}, u32[]{:S(2)}, u32[]{:S(2)}) collective-permute-start(bf16[272,256]{1,0:T(8,128)(2,1)S(1)} %get-tuple-element.40), channel_id=1, source_target_pairs={{0,16},{1,17},{2,18},{3,19},{4,20},{5,21},{6,22},{7,23},{8,24},{9,... | collective-permute-start | bytes 417800 | tf_op jit(solution)/shard_map/ppermute | solution.py:268
  58.4 9.0 %collective-permute-done.23.refs_2_ = bf16[272,256]{1,0:T(8,128)(2,1)S(1)} collective-permute-done((bf16[272,256]{1,0:T(8,128)(2,1)S(1)}, bf16[272,256]{1,0:T(8,128)(2,1)S(1)}, u32[]{:S(2)}, u32[]{:S(2)}) %collective-permute-start.23) | collective-permute-done | bytes 139296 | tf_op jit(solution)/shard_map/ppermute | solution.py:268
  68.9 3.4 %collective-permute-start.27 = (bf16[256,256]{1,0:T(8,128)(2,1)S(1)}, bf16[256,256]{1,0:T(8,128)(2,1)S(1)}, u32[]{:S(2)}, u32[]{:S(2)}) collective-permute-start(bf16[256,256]{1,0:T(8,128)(2,1)S(1)} %join_state.3.refs_10_), channel_id=1, source_target_pairs={{0,3},{1,2},{2,1},{3,0},{4,7},{5,6},{6,5},{7,4},{8,11},{9,10},{10,... | collective-permute-start | bytes 393224 | tf_op jit(solution)/shard_map/ppermute | solution.py:268
  73.2 1.9 %collective-permute-start.4 = (bf16[16,2560]{1,0:T(8,128)(2,1)S(1)}, bf16[16,2560]{1,0:T(8,128)(2,1)S(1)}, u32[]{:S(2)}, u32[]{:S(2)}) collective-permute-start(bf16[16,2560]{1,0:T(8,128)(2,1)S(1)} %add.74), channel_id=1, source_target_pairs={{0,3},{4,7},{9,10},{13,14},{18,17},{22,21},{27,24},{31,28}} | collective-permute-start | bytes 245768 | tf_op jit(solution)/shard_map/ppermute | solution.py:268
  75.1 1.7 %collective-permute-start.3 = (bf16[16,2560]{1,0:T(8,128)(2,1)S(1)}, bf16[16,2560]{1,0:T(8,128)(2,1)S(1)}, u32[]{:S(2)}, u32[]{:S(2)}) collective-permute-start(bf16[16,2560]{1,0:T(8,128)(2,1)S(1)} %add.74), channel_id=1, source_target_pairs={{0,2},{4,6},{9,11},{13,15},{18,16},{22,20},{27,25},{31,29}} | collective-permute-start | bytes 245768 | tf_op jit(solution)/shard_map/ppermute | solution.py:268
  76.9 1.5 %collective-permute-start.2 = (bf16[16,2560]{1,0:T(8,128)(2,1)S(1)}, bf16[16,2560]{1,0:T(8,128)(2,1)S(1)}, u32[]{:S(2)}, u32[]{:S(2)}) collective-permute-start(bf16[16,2560]{1,0:T(8,128)(2,1)S(1)} %add.74), channel_id=1, source_target_pairs={{0,1},{4,5},{9,8},{13,12},{18,19},{22,23},{27,26},{31,30}} | collective-permute-start | bytes 245768 | tf_op jit(solution)/shard_map/ppermute | solution.py:268
  79.4 3.4 %collective-permute-start.18 = (bf16[256,256]{1,0:T(8,128)(2,1)S(1)}, bf16[256,256]{1,0:T(8,128)(2,1)S(1)}, u32[]{:S(2)}, u32[]{:S(2)}) collective-permute-start(bf16[256,256]{1,0:T(8,128)(2,1)S(1)} %join_state.2.refs_6_), channel_id=1, source_target_pairs={{0,3},{1,2},{2,1},{3,0},{4,7},{5,6},{6,5},{7,4},{8,11},{9,10},{10,... | collective-permute-start | bytes 393224 | tf_op jit(solution)/shard_map/ppermute | solution.py:268
  83.5 16.3 %completion_blocks.1 = (bf16[2,256,2048]{2,1,0:T(8,128)(2,1)S(1)}, bf16[2,256,2048]{2,1,0:T(8,128)(2,1)S(1)}, bf16[2,256,256]{2,1,0:T(8,128)(2,1)S(1)}) custom-call(s32[4]{0:T(128)S(1)} %pad_add_fusion.place.refs_0_, bf16[2,256,2048]{2,1,0:T(8,128)(2,1)} %inner.1, bf16[2,256,2048]{2,1,0:T(8,128)(2,1)} %gate.1, bf16[2,256,4096]{2,1,0:T(8,128)(2,1)} %c_in.1, ...), custom_call_target="tpu_custom_call" | custom-call | tf_op jit(solution)/shard_map/completion_blocks/pallas_call | solution.py:490
  99.9 3.4 %finish.1 = bf16[2,256,2048]{2,1,0:T(8,128)(2,1)} custom-call(s32[4]{0:T(128)S(1)} %pad_add_fusion.place.refs_0_, s32[2]{0:T(128)S(1)} %copy-done.13, bf16[2,256,256]{2,1,0:T(8,128)(2,1)S(1)} %get-tuple-element.19.refs_2_, bf16[2,256,2048]{2,1,0:T(8,128)(2,1)S(1)} %get-tuple-element.20.refs_3_, bf16[2,256,2048]{2,1,0:T(8,128)(2,1)S(1)} %get-tuple-element.21.refs_4_, ...), custom_call_target="tpu_custom_call" | custom-call | tf_op jit(solution)/shard_map/finish/pallas_call | solution.py:490
  (100 shorter events, 24.6 us)
Async XLA Ops:
  0.9 20.0 %collective-permute-start.9 = (f32[32,256]{1,0:T(8,128)S(1)}, f32[32,256]{1,0:T(8,128)S(1)}, u32[]{:S(2)}, u32[]{:S(2)}) collective-permute-start(f32[32,256]{1,0:T(8,128)S(1)} %get-tuple-element.47), channel_id=1, source_target_pairs={{0,4},{1,5},{2,6},{3,7},{4,0},{5,1},{6,2},{7,3},{8,12},{9,13},{10,... | collective-permute-start | bytes 98312 | tf_op jit(solution)/shard_map/ppermute | solution.py:268
  3.7 23.2 %collective-permute-start.5 = (bf16[256,2048]{1,0:T(8,128)(2,1)}, bf16[256,2048]{1,0:T(8,128)(2,1)S(1)}, u32[]{:S(2)}, u32[]{:S(2)}) collective-permute-start(bf16[256,2048]{1,0:T(8,128)(2,1)} %constant_dynamic-slice_fusion.3), channel_id=1, source_target_pairs={{0,4},{1,5},{2,6},{3,7},{4,0},{5,1},{6,2},{7,3},{8,12},{9,13},{10,... | collective-permute-start | bytes 3145736 | tf_op jit(solution)/shard_map/ppermute | solution.py:268
  6.5 12.8 %collective-permute-start.6 = (bf16[16,2304]{1,0:T(8,128)(2,1)}, bf16[16,2304]{1,0:T(8,128)(2,1)S(1)}, u32[]{:S(2)}, u32[]{:S(2)}) collective-permute-start(bf16[16,2304]{1,0:T(8,128)(2,1)} %pad_maximum_fusion.2), channel_id=1, source_target_pairs={{4,8},{5,9},{6,10},{7,11},{12,16},{13,17},{14,18},{15,19},{20,24},... | collective-permute-start | bytes 221192 | tf_op jit(solution)/shard_map/ppermute | solution.py:268
  8.7 11.3 %collective-permute-start.7 = (bf16[16,2304]{1,0:T(8,128)(2,1)}, bf16[16,2304]{1,0:T(8,128)(2,1)}, u32[]{:S(2)}, u32[]{:S(2)}) collective-permute-start(bf16[16,2304]{1,0:T(8,128)(2,1)} %pad_maximum_fusion.3), channel_id=1, source_target_pairs={{4,12},{5,13},{6,14},{7,15},{12,20},{13,21},{14,22},{15,23},{20,28... | collective-permute-start | bytes 221192 | tf_op jit(solution)/shard_map/ppermute | solution.py:268
  11.5 10.1 %collective-permute-start.8 = (bf16[256,256]{1,0:T(8,128)(2,1)}, bf16[256,256]{1,0:T(8,128)(2,1)}, u32[]{:S(2)}, u32[]{:S(2)}) collective-permute-start(bf16[256,256]{1,0:T(8,128)(2,1)} %constant_dynamic-slice_fusion.2), channel_id=1, source_target_pairs={{0,4},{1,5},{2,6},{3,7},{4,0},{5,1},{6,2},{7,3},{8,12},{9,13},{10,... | collective-permute-start | bytes 393224 | tf_op jit(solution)/shard_map/ppermute | solution.py:268
  31.9 11.9 %collective-permute-start.19 = (bf16[272,256]{1,0:T(8,128)(2,1)}, bf16[272,256]{1,0:T(8,128)(2,1)}, u32[]{:S(2)}, u32[]{:S(2)}) collective-permute-start(bf16[272,256]{1,0:T(8,128)(2,1)} %get-tuple-element.30), channel_id=1, source_target_pairs={{0,1},{1,0},{2,3},{3,2},{4,5},{5,4},{6,7},{7,6},{8,9},{9,8},{10,11... | collective-permute-start | bytes 417800 | tf_op jit(solution)/shard_map/ppermute | solution.py:268
  33.4 11.9 %collective-permute-start.20 = (bf16[272,256]{1,0:T(8,128)(2,1)}, bf16[272,256]{1,0:T(8,128)(2,1)}, u32[]{:S(2)}, u32[]{:S(2)}) collective-permute-start(bf16[272,256]{1,0:T(8,128)(2,1)} %get-tuple-element.31), channel_id=1, source_target_pairs={{0,2},{1,3},{2,0},{3,1},{4,6},{5,7},{6,4},{7,5},{8,10},{9,11},{10,... | collective-permute-start | bytes 417800 | tf_op jit(solution)/shard_map/ppermute | solution.py:268
  34.9 10.9 %collective-permute-start.21 = (bf16[272,256]{1,0:T(8,128)(2,1)}, bf16[272,256]{1,0:T(8,128)(2,1)}, u32[]{:S(2)}, u32[]{:S(2)}) collective-permute-start(bf16[272,256]{1,0:T(8,128)(2,1)} %get-tuple-element.32), channel_id=1, source_target_pairs={{0,3},{1,2},{2,1},{3,0},{4,7},{5,6},{6,5},{7,4},{8,11},{9,10},{10,... | collective-permute-start | bytes 417800 | tf_op jit(solution)/shard_map/ppermute | solution.py:268
  36.0 32.8 %collective-permute-start = (bf16[16,2560]{1,0:T(8,128)(2,1)}, bf16[16,2560]{1,0:T(8,128)(2,1)}, u32[]{:S(2)}, u32[]{:S(2)}) collective-permute-start(bf16[16,2560]{1,0:T(8,128)(2,1)} %pad_maximum_fusion), channel_id=1, source_target_pairs={{28,0},{29,9},{30,18},{31,27}} | collective-permute-start | bytes 245768 | tf_op jit(solution)/shard_map/ppermute | solution.py:268
  43.8 8.0 %collective-permute-start.11 = (bf16[272,256]{1,0:T(8,128)(2,1)S(1)}, bf16[272,256]{1,0:T(8,128)(2,1)S(1)}, u32[]{:S(2)}, u32[]{:S(2)}) collective-permute-start(bf16[272,256]{1,0:T(8,128)(2,1)S(1)} %get-tuple-element.27), channel_id=1, source_target_pairs={{0,2},{1,3},{2,0},{3,1},{4,6},{5,7},{6,4},{7,5},{8,10},{9,11},{10,... | collective-permute-start | bytes 417800 | tf_op jit(solution)/shard_map/ppermute | solution.py:268
  45.3 7.5 %collective-permute-start.12 = (bf16[272,256]{1,0:T(8,128)(2,1)S(1)}, bf16[272,256]{1,0:T(8,128)(2,1)S(1)}, u32[]{:S(2)}, u32[]{:S(2)}) collective-permute-start(bf16[272,256]{1,0:T(8,128)(2,1)S(1)} %get-tuple-element.28), channel_id=1, source_target_pairs={{0,3},{1,2},{2,1},{3,0},{4,7},{5,6},{6,5},{7,4},{8,11},{9,10},{10,... | collective-permute-start | bytes 417800 | tf_op jit(solution)/shard_map/ppermute | solution.py:268
  46.9 8.5 %collective-permute-start.24 = (bf16[272,256]{1,0:T(8,128)(2,1)S(1)}, bf16[272,256]{1,0:T(8,128)(2,1)S(1)}, u32[]{:S(2)}, u32[]{:S(2)}) collective-permute-start(bf16[272,256]{1,0:T(8,128)(2,1)S(1)} %get-tuple-element.35), channel_id=1, source_target_pairs={{0,24},{1,25},{2,26},{3,27},{4,28},{5,29},{6,30},{7,31},{8,16},{9,... | collective-permute-start | bytes 417800 | tf_op jit(solution)/shard_map/ppermute | solution.py:268
  48.4 19.1 %collective-permute-start.23 = (bf16[272,256]{1,0:T(8,128)(2,1)S(1)}, bf16[272,256]{1,0:T(8,128)(2,1)S(1)}, u32[]{:S(2)}, u32[]{:S(2)}) collective-permute-start(bf16[272,256]{1,0:T(8,128)(2,1)S(1)} %get-tuple-element.36), channel_id=1, source_target_pairs={{0,16},{1,17},{2,18},{3,19},{4,20},{5,21},{6,22},{7,23},{8,24},{9,... | collective-permute-start | bytes 417800 | tf_op jit(solution)/shard_map/ppermute | solution.py:268
  51.8 16.3 %collective-permute-start.22 = (bf16[272,256]{1,0:T(8,128)(2,1)S(1)}, bf16[272,256]{1,0:T(8,128)(2,1)S(1)}, u32[]{:S(2)}, u32[]{:S(2)}) collective-permute-start(bf16[272,256]{1,0:T(8,128)(2,1)S(1)} %get-tuple-element.37), channel_id=1, source_target_pairs={{0,8},{1,9},{2,10},{3,11},{4,12},{5,13},{6,14},{7,15},{8,0},{9,1},... | collective-permute-start | bytes 417800 | tf_op jit(solution)/shard_map/ppermute | solution.py:268
  52.9 22.2 %collective-permute-start.15 = (bf16[272,256]{1,0:T(8,128)(2,1)S(1)}, bf16[272,256]{1,0:T(8,128)(2,1)S(1)}, u32[]{:S(2)}, u32[]{:S(2)}) collective-permute-start(bf16[272,256]{1,0:T(8,128)(2,1)S(1)} %get-tuple-element.39), channel_id=1, source_target_pairs={{0,24},{1,25},{2,26},{3,27},{4,28},{5,29},{6,30},{7,31},{8,16},{9,... | collective-permute-start | bytes 417800 | tf_op jit(solution)/shard_map/ppermute | solution.py:268
  55.4 21.4 %collective-permute-start.14 = (bf16[272,256]{1,0:T(8,128)(2,1)S(1)}, bf16[272,256]{1,0:T(8,128)(2,1)S(1)}, u32[]{:S(2)}, u32[]{:S(2)}) collective-permute-start(bf16[272,256]{1,0:T(8,128)(2,1)S(1)} %get-tuple-element.40), channel_id=1, source_target_pairs={{0,16},{1,17},{2,18},{3,19},{4,20},{5,21},{6,22},{7,23},{8,24},{9,... | collective-permute-start | bytes 417800 | tf_op jit(solution)/shard_map/ppermute | solution.py:268
  68.1 10.4 %collective-permute-start.13 = (bf16[272,256]{1,0:T(8,128)(2,1)S(1)}, bf16[272,256]{1,0:T(8,128)(2,1)S(1)}, u32[]{:S(2)}, u32[]{:S(2)}) collective-permute-start(bf16[272,256]{1,0:T(8,128)(2,1)S(1)} %get-tuple-element.41), channel_id=1, source_target_pairs={{0,8},{1,9},{2,10},{3,11},{4,12},{5,13},{6,14},{7,15},{8,0},{9,1},... | collective-permute-start | bytes 417800 | tf_op jit(solution)/shard_map/ppermute | solution.py:268
  68.9 14.0 %collective-permute-start.27 = (bf16[256,256]{1,0:T(8,128)(2,1)S(1)}, bf16[256,256]{1,0:T(8,128)(2,1)S(1)}, u32[]{:S(2)}, u32[]{:S(2)}) collective-permute-start(bf16[256,256]{1,0:T(8,128)(2,1)S(1)} %join_state.3.refs_10_), channel_id=1, source_target_pairs={{0,3},{1,2},{2,1},{3,0},{4,7},{5,6},{6,5},{7,4},{8,11},{9,10},{10,... | collective-permute-start | bytes 393224 | tf_op jit(solution)/shard_map/ppermute | solution.py:268
  73.2 6.1 %collective-permute-start.4 = (bf16[16,2560]{1,0:T(8,128)(2,1)S(1)}, bf16[16,2560]{1,0:T(8,128)(2,1)S(1)}, u32[]{:S(2)}, u32[]{:S(2)}) collective-permute-start(bf16[16,2560]{1,0:T(8,128)(2,1)S(1)} %add.74), channel_id=1, source_target_pairs={{0,3},{4,7},{9,10},{13,14},{18,17},{22,21},{27,24},{31,28}} | collective-permute-start | bytes 245768 | tf_op jit(solution)/shard_map/ppermute | solution.py:268
  78.5 21.3 %collective-permute-start.26 = (bf16[256,256]{1,0:T(8,128)(2,1)S(1)}, bf16[256,256]{1,0:T(8,128)(2,1)S(1)}, u32[]{:S(2)}, u32[]{:S(2)}) collective-permute-start(bf16[256,256]{1,0:T(8,128)(2,1)S(1)} %join_state.3.refs_10_), channel_id=1, source_target_pairs={{0,2},{1,3},{2,0},{3,1},{4,6},{5,7},{6,4},{7,5},{8,10},{9,11},{10,... | collective-permute-start | bytes 393224 | tf_op jit(solution)/shard_map/ppermute | solution.py:268
  79.3 20.5 %collective-permute-start.25 = (bf16[256,256]{1,0:T(8,128)(2,1)S(1)}, bf16[256,256]{1,0:T(8,128)(2,1)S(1)}, u32[]{:S(2)}, u32[]{:S(2)}) collective-permute-start(bf16[256,256]{1,0:T(8,128)(2,1)S(1)} %join_state.3.refs_10_), channel_id=1, source_target_pairs={{0,1},{1,0},{2,3},{3,2},{4,5},{5,4},{6,7},{7,6},{8,9},{9,8},{10,11... | collective-permute-start | bytes 393224 | tf_op jit(solution)/shard_map/ppermute | solution.py:268
  79.4 20.4 %collective-permute-start.18 = (bf16[256,256]{1,0:T(8,128)(2,1)S(1)}, bf16[256,256]{1,0:T(8,128)(2,1)S(1)}, u32[]{:S(2)}, u32[]{:S(2)}) collective-permute-start(bf16[256,256]{1,0:T(8,128)(2,1)S(1)} %join_state.2.refs_6_), channel_id=1, source_target_pairs={{0,3},{1,2},{2,1},{3,0},{4,7},{5,6},{6,5},{7,4},{8,11},{9,10},{10,... | collective-permute-start | bytes 393224 | tf_op jit(solution)/shard_map/ppermute | solution.py:268
  82.8 17.0 %collective-permute-start.17 = (bf16[256,256]{1,0:T(8,128)(2,1)S(1)}, bf16[256,256]{1,0:T(8,128)(2,1)S(1)}, u32[]{:S(2)}, u32[]{:S(2)}) collective-permute-start(bf16[256,256]{1,0:T(8,128)(2,1)S(1)} %join_state.2.refs_6_), channel_id=1, source_target_pairs={{0,2},{1,3},{2,0},{3,1},{4,6},{5,7},{6,4},{7,5},{8,10},{9,11},{10,... | collective-permute-start | bytes 393224 | tf_op jit(solution)/shard_map/ppermute | solution.py:268
  82.9 17.0 %collective-permute-start.16 = (bf16[256,256]{1,0:T(8,128)(2,1)S(1)}, bf16[256,256]{1,0:T(8,128)(2,1)S(1)}, u32[]{:S(2)}, u32[]{:S(2)}) collective-permute-start(bf16[256,256]{1,0:T(8,128)(2,1)S(1)} %join_state.2.refs_6_), channel_id=1, source_target_pairs={{0,1},{1,0},{2,3},{3,2},{4,5},{5,4},{6,7},{7,6},{8,9},{9,8},{10,11... | collective-permute-start | bytes 393224 | tf_op jit(solution)/shard_map/ppermute | solution.py:268
  (25 other events, 209.6 us)

commit v2 on v1

--- a/solution.py
+++ b/solution.py
@@ -300,43 +300,108 @@
     return jnp.maximum(value, 0.0) + jnp.log1p(jnp.exp(-jnp.abs(value)))
 
 
+def group_of(decay, index, size):
+    every = jnp.reshape(decay[...], (1, decay.shape[0]))
+    return pltpu.roll(every, decay.shape[0] - index * size, 1)[:, 0:size]
+
+
+def pack_kernel(
+    place, inner, proj, step, last_inner, last_b, last_c, swap_out, near_0, near_1, extra, sems
+):
+    rows, heads = step.shape[1], step.shape[0]
+    features = heads * HEAD_WIDTH
+    column, core = place[1], place[2]
+    theirs = 1 - core
+    to_features = pltpu.make_async_copy(
+        inner.at[:, pl.ds(pl.multiple_of(theirs * features, features), features)],
+        swap_out.at[0:rows, 0:features],
+        sems.at[0],
+    )
+    to_features.start()
+    group_at = (2 * column + theirs) * STATE_WIDTH
+    to_b = pltpu.make_async_copy(
+        proj.at[:, pl.ds(pl.multiple_of(group_at, STATE_WIDTH), STATE_WIDTH)],
+        swap_out.at[0:rows, features : features + STATE_WIDTH],
+        sems.at[1],
+    )
+    to_b.start()
+    dt = jnp.transpose(softplus(step[...]))
+    high = dt.astype(jnp.bfloat16)
+    low = (dt - high.astype(jnp.float32)).astype(jnp.bfloat16)
+    extra[0:rows, 0 : 4 * heads] = jnp.concatenate([high, low, high, low], axis=1)
+    for to, near in enumerate((near_0, near_1)):
+        group = slice(to * STATE_WIDTH, (to + 1) * STATE_WIDTH)
+        inner_last = last_inner[:, to * features : (to + 1) * features].astype(jnp.float32)
+        bc_last = jnp.concatenate([last_b[:, group], last_c[:, group]], axis=1)
+        pieces = [
+            inner_last[TAIL - 3 :, at : at + 2 * STATE_WIDTH]
+            for at in range(0, features, 2 * STATE_WIDTH)
+        ]
+        pieces.append(bc_last.astype(jnp.float32)[TAIL - 3 :])
+        pieces.append(jnp.zeros((TAIL - 3 * len(pieces), 2 * STATE_WIDTH), jnp.float32))
+        near[...] = jnp.concatenate(pieces, axis=0).astype(jnp.bfloat16)
+    extra[rows:] = jnp.where(core == 0, near_1[...].astype(jnp.float32), near_0[...].astype(jnp.float32)).astype(jnp.bfloat16)
+    to_dt = pltpu.make_async_copy(
+        extra.at[0:rows, 0 : 4 * heads], swap_out.at[0:rows, features + STATE_WIDTH :], sems.at[2]
+    )
+    to_dt.start()
+    to_tail = pltpu.make_async_copy(
+        extra.at[rows:], swap_out.at[rows:, 0 : 2 * STATE_WIDTH], sems.at[3]
+    )
+    to_tail.start()
+    to_features.wait()
+    to_b.wait()
+    to_dt.wait()
+    to_tail.wait()
+
+
 def prompt_weights_kernel(
-    place, own_b, other_b, halo_b, taps, own_step, other_step, decay, w_out, b_out, log_out, padded
+    place, own_b, other_b, other_dt, other_tail, halo_0, halo_1, own_tail, taps, own_step, decay,
+    w_out, b_out, log_out, halo_out, tail_out, padded,
 ):
     core = place[2]
     rows, heads = own_b.shape[0], own_step.shape[0]
     first_own = core == 0
-    rate = jnp.exp(decay[...])
-    dt_own, dt_other = softplus(own_step[...]), softplus(other_step[...])
+    rate = jnp.exp(group_of(decay, 2 * place[1] + core, heads))
+    dt_own = jnp.transpose(softplus(own_step[...]))
+    parts = other_dt[...].astype(jnp.float32)
+    dt_other = parts[:, 0:heads] + parts[:, heads : 2 * heads]
     row = lax.broadcasted_iota(jnp.int32, (rows, rows), 0)
     col = lax.broadcasted_iota(jnp.int32, (rows, rows), 1)
     later = (col > row).astype(jnp.float32)
-    same = (col == row).astype(jnp.float32)
-    ones = jnp.ones((8, rows), jnp.float32)
-    last = ((1,), (1,))
-    sum_own = contract(ones, dt_own, last, HIGHEST)[0:1]
-    sum_other = contract(ones, dt_other, last, HIGHEST)[0:1]
-    after_own = contract(later, dt_own, last, HIGHEST) + jnp.where(first_own, sum_other, 0.0)
-    after_other = contract(later, dt_other, last, HIGHEST) + jnp.where(first_own, 0.0, sum_own)
-    w_out[0:rows] = jnp.exp(-rate * after_own) * contract(same, dt_own, last, HIGHEST)
-    w_out[rows:] = jnp.exp(-rate * after_other) * contract(same, dt_other, last, HIGHEST)
+    after = contract(later, jnp.concatenate([dt_own, dt_other], axis=1), ((1,), (0,)), HIGHEST)
+    sum_own = after[0:1, 0:heads] + dt_own[0:1]
+    sum_other = after[0:1, heads:] + dt_other[0:1]
+    after_own = after[:, 0:heads] + jnp.where(first_own, sum_other, 0.0)
+    after_other = after[:, heads:] + jnp.where(first_own, 0.0, sum_own)
+    w_out[0:rows] = jnp.exp(-rate * after_own) * dt_own
+    w_out[rows:] = jnp.exp(-rate * after_other) * dt_other
     total = jnp.broadcast_to(-rate * (sum_own + sum_other), (8, heads))
-    spread = spread_heads(0, heads, heads * HEAD_WIDTH).astype(jnp.float32)
-    wide = contract(total, spread, ((1,), (0,)), HIGHEST)
-    high = wide.astype(jnp.bfloat16)
-    rest = wide - high.astype(jnp.float32)
-    mid = rest.astype(jnp.bfloat16)
-    low = (rest - mid.astype(jnp.float32)).astype(jnp.bfloat16)
-    which = lax.broadcasted_iota(jnp.int32, wide.shape, 0)
-    parts = jnp.where(
-        which == 0,
-        high.astype(jnp.float32),
-        jnp.where(which == 1, mid.astype(jnp.float32), jnp.where(which == 2, low.astype(jnp.float32), 0.0)),
-    )
-    log_out[...] = jnp.concatenate([parts, jnp.zeros_like(parts)], axis=0).astype(jnp.bfloat16)
-    own_last, other_last, halo = own_b[rows - TAIL :], other_b[rows - TAIL :], halo_b[...]
-    lead_own = jnp.where(first_own, halo.astype(jnp.float32), other_last.astype(jnp.float32))
-    lead_other = jnp.where(first_own, own_last.astype(jnp.float32), halo.astype(jnp.float32))
+    spread = spread_heads(0, heads, heads * HEAD_WIDTH).astype(jnp.bfloat16)
+    which = lax.broadcasted_iota(jnp.int32, total.shape, 0)
+    high = total.astype(jnp.bfloat16).astype(jnp.float32)
+    mid = (total - high).astype(jnp.bfloat16).astype(jnp.float32)
+    low = total - high - mid
+    parts = jnp.where(which == 0, high, jnp.where(which == 1, mid, jnp.where(which == 2, low, 0.0)))
+    wide = contract(parts.astype(jnp.bfloat16), spread, ((1,), (0,)))
+    log_out[...] = jnp.concatenate([wide, jnp.zeros_like(wide)], axis=0).astype(jnp.bfloat16)
+    near = halo_0[...].astype(jnp.float32) + halo_1[...].astype(jnp.float32)
+    features = heads * HEAD_WIDTH
+    for index in range(features // near.shape[1]):
+        at = index * near.shape[1]
+        rows_3 = near[3 * index : 3 * index + 3]
+        wide = jnp.concatenate([jnp.zeros((TAIL - 3, near.shape[1]), jnp.float32), rows_3], axis=0)
+        halo_out[:, at : at + near.shape[1]] = wide.astype(jnp.bfloat16)
+    at = 3 * (features // near.shape[1])
+    halo = jnp.concatenate(
+        [jnp.zeros((TAIL - 3, STATE_WIDTH), jnp.float32), near[at : at + 3, 0:STATE_WIDTH]], axis=0
+    )
+    tail_out[...] = jnp.where(
+        first_own, other_tail[...].astype(jnp.float32), own_tail[...].astype(jnp.float32)
+    ).astype(jnp.bfloat16)
+    own_last, other_last = own_b[rows - TAIL :], other_b[rows - TAIL :]
+    lead_own = jnp.where(first_own, halo, other_last.astype(jnp.float32))
+    lead_other = jnp.where(first_own, own_last.astype(jnp.float32), halo)
     conv_own = conv_rows(padded, taps[...], lead_own, own_b[...])
     b_out[:, 0:rows] = jnp.transpose(conv_own).astype(jnp.bfloat16)
     conv_other = conv_rows(padded, taps[...], lead_other, other_b[...])
@@ -344,7 +409,7 @@
 
 
 def prompt_state_kernel(
-    chunk, parts, place, own, other, halo, taps, weights, b_turned, logs, *rest
+    chunk, parts, place, own, other, halo, taps, weights, b_turned, logs, tail, *rest
 ):
     outs, padded = rest[:parts], rest[parts]
     column, core = place[1], place[2]
@@ -370,11 +435,31 @@
         mine = contract(b_turned[:, 0:rows], x_own.astype(jnp.bfloat16), ((1,), (0,)))
         theirs = contract(b_turned[:, rows:], x_other.astype(jnp.bfloat16), ((1,), (0,)))
         outs[step][0:state] = (mine + theirs).astype(jnp.bfloat16)
-        outs[step][state:] = logs[:, cols]
+        outs[step][state : state + TAIL] = logs[:, cols]
+        if outs[step].shape[0] > state + TAIL:
+            for index in range(2):
+                at = state + TAIL * (index + 1)
+                outs[step][at : at + TAIL] = tail[:, index * width : (index + 1) * width]
+
+
+def pick_kernel(count, place, *refs):
+    held, ready = refs[:count], refs[count : 2 * count]
+    turn = place[0] ^ place[1]
+    rows, width = ready[0].shape
+    for index in range(count):
+
+        @pl.when(turn == index)
+        def _():
+            for step in range(count):
+                ready[step][...] = held[index ^ step][0:rows]
+            for tail in refs[2 * count :]:
+                for half in range(2):
+                    at = rows + TAIL * half
+                    tail[:, half * width : (half + 1) * width] = held[index][at : at + TAIL]
 
 
 def join_state_kernel(place, *refs):
-    arrived, out = refs[:-1], refs[-1]
+    arrived, out = refs[: lax.axis_size("comp")], refs[-1]
     plane = place[0]
     state = out.shape[0]
     totals = []
@@ -393,41 +478,53 @@
 
 
 def completion_kernel(
-    place, inner, gate, b_in, c_in, lead, lead_b, lead_c, taps, taps_b, taps_c, step,
-    decay_row, decay_col, fixed_out, factor_out, c_out, padded, diag_low, rows_high,
+    slot, place, inner, gate, b_in, c_in, tail, taps, taps_b, taps_c, step,
+    decay, after, fixed_out, factor_out, c_out, padded, diag_low, rows_high,
+    cum_cols, base_rows, log_rows, leads,
 ):
     rows = inner.shape[1]
     width = inner.shape[2]
-    heads = step.shape[1]
+    heads = width // HEAD_WIDTH
     half = rows // 2
 
-    @pl.when(pl.program_id(1) == 0)
+    @pl.when(pl.program_id(0) == 0)
     def _():
-        b = conv_rows(padded, taps_b[...], lead_b[...], b_in[0]).astype(jnp.bfloat16)
-        c = conv_rows(padded, taps_c[...], lead_c[...], c_in[0]).astype(jnp.bfloat16)
-        c_out[0] = c
+        edges = tail[...].astype(jnp.float32)
+        blank = jnp.zeros((TAIL - 3, width), jnp.float32)
+        for block in range(leads.shape[0]):
+            leads[block] = jnp.concatenate([blank, edges[3 * block : 3 * block + 3]], axis=0)
+        lead_bc = leads[leads.shape[0] - 1]
+        lead_b, lead_c = lead_bc[:, 0:STATE_WIDTH], lead_bc[:, STATE_WIDTH:]
+        b = conv_rows(padded, taps_b[...], lead_b, b_in[0]).astype(jnp.bfloat16)
+        c = conv_rows(padded, taps_c[...], lead_c, c_in[0]).astype(jnp.bfloat16)
+        c_out[...] = c
         scores = contract(c, b, ((1,), (1,)))
         row = lax.broadcasted_iota(jnp.int32, (rows, rows), 0)
         col = lax.broadcasted_iota(jnp.int32, (rows, rows), 1)
         scores = jnp.where(row >= col, scores, 0.0)
         diag_low[...] = scores[0:half, 0:half]
         rows_high[...] = scores[half:]
-
-    x = conv_rows(padded, taps[...], lead[...], inner[0])
+        dt = softplus(step[:, slot])
+        decay_row = jnp.broadcast_to(group_of(decay, place[3], dt.shape[0]), (8, dt.shape[0]))
+        decay_col = jnp.transpose(decay_row)[:, 0:1]
+        before = (row <= col).astype(jnp.float32)
+        cum = contract(dt, before, ((1,), (0,)), HIGHEST) * (-LOG2E * jnp.exp(decay_col))
+        log_dt = jnp.log(dt) * LOG2E
+        turned = jnp.transpose(cum)
+        for block in range(cum_cols.shape[0]):
+            those = slice(block * heads, (block + 1) * heads)
+            cum_cols[block] = turned[:, those]
+            base_rows[block] = cum[those] - log_dt[those]
+            log_rows[block] = log_dt[those]
+
+    x = conv_rows(padded, taps[...], leads[pl.program_id(0)], inner[0])
     x = x.astype(jnp.bfloat16)
-    dt = softplus(step[0])
-    row = lax.broadcasted_iota(jnp.int32, (rows, rows), 0)
-    col = lax.broadcasted_iota(jnp.int32, (rows, rows), 1)
-    upto = (col <= row).astype(jnp.float32)
-    before = (row <= col).astype(jnp.float32)
-    cum_col = contract(upto, dt, ((1,), (1,)), HIGHEST) * (-LOG2E * jnp.exp(decay_row[0]))
-    cum_row = contract(dt, before, ((1,), (0,)), HIGHEST) * (-LOG2E * jnp.exp(decay_col[...]))
-    log_dt = jnp.log(dt) * LOG2E
-    base_row = cum_row - log_dt
+    here = pl.program_id(0)
+    cum_col, base_row, log_dt = cum_cols[here], base_rows[here], log_rows[here]
     silu_gate = half_silu(gate[0].astype(jnp.float32))
     spread = spread_heads(0, heads, width).astype(jnp.bfloat16)
     decay_wide = contract(jnp.exp2(cum_col).astype(jnp.bfloat16), spread, ((1,), (0,)))
-    factor_out[0] = (decay_wide * silu_gate).astype(jnp.bfloat16)
+    factor_out[...] = (decay_wide * silu_gate).astype(jnp.bfloat16)
     low, high = diag_low[...], rows_high[...]
     pair = 2 * HEAD_WIDTH
     lane = lax.broadcasted_iota(jnp.int32, (rows, pair), 1)
@@ -453,37 +550,46 @@
         y_high = contract(
             jnp.concatenate(highs, axis=1), jnp.concatenate([left, right], axis=0), ((1,), (0,))
         )
-        fixed_out[0, 0:half, at : at + pair] = (
+        fixed_out[0:half, at : at + pair] = (
             y_low * silu_gate[0:half, at : at + pair]
         ).astype(jnp.bfloat16)
-        fixed_out[0, half:, at : at + pair] = (
+        fixed_out[half:, at : at + pair] = (
             y_high * silu_gate[half:, at : at + pair]
         ).astype(jnp.bfloat16)
 
 
-def finish_kernel(parts, chunks, place, live, c_ref, fixed, factor, gain, *refs):
-    states, out, gated = refs[: parts * chunks], refs[-2], refs[-1]
+def finish_kernel(parts, chunks, slots, place, live, gain, *refs):
+    states, rest = refs[: parts * chunks], refs[parts * chunks :]
+    out, gated = rest[-2], rest[-1]
     column = place[1]
-    slot = pl.program_id(0)
     rows, features = out.shape[1], out.shape[2]
     width = states[0].shape[1]
     part_width = features // parts
-    c = c_ref[0]
-    squares = jnp.zeros((rows, 1), jnp.float32)
-    for chunk in range(chunks):
-        for step in range(parts):
-            start = (column ^ step) * part_width + chunk * width
-            cols = pl.ds(pl.multiple_of(start, width), width)
-            read = contract(c, states[chunk * parts + step][...], ((1,), (0,)))
-            value = fixed[0, :, cols].astype(jnp.float32) + read * factor[0, :, cols].astype(
-                jnp.float32
-            )
-            gated[:, cols] = value
-            squares = squares + jnp.sum(value * value, axis=1, keepdims=True)
-    scale = lax.rsqrt(squares / features + EPS)
-    alive = lax.broadcasted_iota(jnp.int32, (rows, 1), 0) < live[slot]
-    scale = jnp.where(alive, scale, 0.0)
-    out[0] = (gated[...] * scale * gain[...]).astype(jnp.bfloat16)
+    for slot in range(slots):
+        c_ref, fixed, factor = rest[3 * slot : 3 * slot + 3]
+
+        @pl.when(pl.program_id(0) == slot)
+        def _():
+            c = c_ref[...]
+            squares = jnp.zeros((rows, 1), jnp.float32)
+            for chunk in range(chunks):
+                for step in range(parts):
+                    start = (column ^ step) * part_width + chunk * width
+                    cols = pl.ds(pl.multiple_of(start, width), width)
+                    read = contract(c, states[chunk * parts + step][...], ((1,), (0,)))
+                    weight = factor[:, cols].astype(jnp.float32)
+                    value = fixed[:, cols].astype(jnp.float32) + read * weight
+                    gated[:, cols] = value
+                    squares = squares + jnp.sum(value * value, axis=1, keepdims=True)
+            scale = lax.rsqrt(squares / features + EPS)
+            alive = lax.broadcasted_iota(jnp.int32, (rows, 1), 0) < live[slot]
+            scale = jnp.where(alive, scale, 0.0)
+            out[0] = (gated[...] * scale * jnp.reshape(gain[...], (1, features))).astype(jnp.bfloat16)
+
+
+LASTS = dict(
+    pack=2, prompt_weights=2, prompt_state=3, pick=1, join_state=1, completion=8, finish=4
+)
 
 
 def run(kernel, name, place, out_shape, in_specs, out_specs, operands, grid=(1,), scratch=(), scalars=1):
@@ -499,6 +605,9 @@
         ),
         compiler_params=pltpu.CompilerParams(
             dimension_semantics=("arbitrary",) * len(grid), vmem_limit_bytes=VMEM_BYTES
+        ),
+        cost_estimate=pl.CostEstimate(
+            flops=LASTS[name] * 10**9, transcendentals=0, bytes_accessed=LASTS[name] * 3 * 10**6
         ),
         name=name,
     )(*place, *operands)
@@ -531,36 +640,42 @@
     def take(array, start, size, axis):
         return lax.dynamic_slice_in_dim(array, start, size, axis)
 
-    swap = lambda z, k, c: (z, 1 - k, c)
-    other_inner = routed(take(prompt_inner, (1 - core) * features, features, 1), swap)
-    other_b = routed(take(prompt_proj, (2 * column + 1 - core) * STATE_WIDTH, STATE_WIDTH, 1), swap)
-    other_step = routed(take(prompt_step, (1 - core) * heads, heads, 0), swap)
-    own_step = take(prompt_step, core * heads, heads, 0)
-
-    last_inner, last_proj = prompt_inner[rows - TAIL :], prompt_proj[rows - TAIL :]
+    whole = lambda shape: pl.BlockSpec(shape, lambda *_: (0,) * len(shape))
+    unread = pl.BlockSpec(memory_space=pl.ANY)
     planes = lax.axis_size("prompt") // 2
-    halo, tail = None, None
-    for to in range(2):
-        inner_to = last_inner[:, to * features : (to + 1) * features]
-        b_to = take(last_proj, (2 * column + to) * STATE_WIDTH, STATE_WIDTH, 1)
-        c_to = take(last_proj, (STATE_GROUPS + 2 * column + to) * STATE_WIDTH, STATE_WIDTH, 1)
-        near = routed(
-            jnp.concatenate([inner_to, b_to], axis=1),
-            lambda z, k, c: (z + 1, to, c) if k == 1 and z + 1 < planes else None,
-        )
-        far = routed(
-            jnp.concatenate([inner_to, b_to, c_to], axis=1),
-            lambda z, k, c: (c, to, c) if k == 1 and z + 1 == planes else None,
-        )
-        halo = near if halo is None else halo + near
-        tail = far if tail is None else tail + far
-    first_tail = tail
-    for step in range(1, parts):
-        tail = tail + routed(first_tail, lambda z, k, c: (z, k, z ^ step) if c == z else None)
-
-    whole = lambda shape: pl.BlockSpec(shape, lambda *_: (0,) * len(shape))
-    decay_group = take(decay_log, group * heads, heads, 0)[None]
-    weights, b_turned, logs = run(
+    state_blocks = features // STATE_WIDTH
+    swapped_width = features + STATE_WIDTH + 4 * heads
+    pair_width = 2 * STATE_WIDTH
+    edge = jax.ShapeDtypeStruct((TAIL, pair_width), bf16)
+    last_block = rows // TAIL - 1
+    c_at = STATE_GROUPS
+    in_hbm = pl.BlockSpec(memory_space=pltpu.HBM)
+    held_inner = pltpu.with_memory_space_constraint(prompt_inner, pltpu.HBM)
+    held_proj = pltpu.with_memory_space_constraint(prompt_proj, pltpu.HBM)
+
+    swap, near_0, near_1 = run(
+        pack_kernel,
+        "pack",
+        (place,),
+        (jax.ShapeDtypeStruct((rows + TAIL, swapped_width), bf16), edge, edge),
+        [
+            in_hbm,
+            in_hbm,
+            pl.BlockSpec((heads, rows), lambda i, s: (1 - s[2], 0)),
+            pl.BlockSpec((TAIL, 2 * features), lambda i, s: (last_block, 0)),
+            pl.BlockSpec((TAIL, pair_width), lambda i, s: (last_block, s[1])),
+            pl.BlockSpec((TAIL, pair_width), lambda i, s: (last_block, c_at // 2 + s[1])),
+        ],
+        (pl.BlockSpec(memory_space=pl.ANY),) + (whole(edge.shape),) * 2,
+        (held_inner, held_proj, prompt_step, held_inner, held_proj, held_proj),
+        scratch=[pltpu.VMEM((rows + TAIL, pair_width), bf16), pltpu.SemaphoreType.DMA((4,))],
+    )
+    other = routed(swap, lambda z, k, c: (z, 1 - k, c))
+    halo_0, halo_1 = [
+        routed(near, lambda z, k, c: (z + 1, to, c) if k == 1 and z + 1 < planes else None)
+        for to, near in enumerate((near_0, near_1))
+    ]
+    weights, b_turned, logs, halo, tail = run(
         prompt_weights_kernel,
         "prompt_weights",
         (place,),
@@ -568,134 +683,176 @@
             jax.ShapeDtypeStruct((2 * rows, heads), f32),
             jax.ShapeDtypeStruct((STATE_WIDTH, 2 * rows), bf16),
             jax.ShapeDtypeStruct((TAIL, features), bf16),
+            jax.ShapeDtypeStruct((TAIL, features), bf16),
+            edge,
         ),
         [
             pl.BlockSpec((rows, STATE_WIDTH), lambda i, s: (0, 2 * s[1] + s[2])),
-            whole((rows, STATE_WIDTH)),
-            pl.BlockSpec((TAIL, STATE_WIDTH), lambda i, s: (0, features // STATE_WIDTH)),
+            pl.BlockSpec((rows, STATE_WIDTH), lambda i, s: (0, state_blocks)),
+            pl.BlockSpec((rows, 4 * heads), lambda i, s: (0, (features + STATE_WIDTH) // (4 * heads))),
+            pl.BlockSpec((TAIL, pair_width), lambda i, s: (rows // TAIL, 0)),
+            whole(edge.shape),
+            whole(edge.shape),
+            whole(edge.shape),
             pl.BlockSpec((CONV, STATE_WIDTH), lambda i, s: (0, 2 * s[1] + s[2])),
-            whole((heads, rows)),
-            whole((heads, rows)),
-            whole((1, heads)),
+            pl.BlockSpec((heads, rows), lambda i, s: (s[2], 0)),
+            whole((STATE_HEADS,)),
         ],
-        (whole((2 * rows, heads)), whole((STATE_WIDTH, 2 * rows)), whole((TAIL, features))),
-        (prompt_proj, other_b, halo, conv_proj, own_step, other_step, decay_group),
+        (
+            whole((2 * rows, heads)),
+            whole((STATE_WIDTH, 2 * rows)),
+            whole((TAIL, features)),
+            whole((TAIL, features)),
+            whole(edge.shape),
+        ),
+        (
+            prompt_proj, other, other, other, halo_0, halo_1, near_1, conv_proj, prompt_step, decay_log,
+        ),
         scratch=[pltpu.VMEM((rows + 8, STATE_WIDTH), f32)],
     )
     width = features // parts // CHUNKS
     message = jax.ShapeDtypeStruct((STATE_WIDTH + TAIL, width), bf16)
-    joined = []
+    far = routed(tail, lambda z, k, c: (c, k, c) if z + 1 == planes else None)
+    held = []
     for chunk in range(CHUNKS):
+        last = chunk + 1 == CHUNKS
+        spread = jax.ShapeDtypeStruct((STATE_WIDTH + (3 if last else 1) * TAIL, width), bf16)
         sent = run(
             lambda *refs, chunk=chunk: prompt_state_kernel(chunk, parts, *refs),
             "prompt_state",
             (place,),
-            (message,) * parts,
+            (spread,) * parts,
             [
                 pl.BlockSpec((rows, features), lambda i, s: (0, s[2])),
-                whole((rows, features)),
+                pl.BlockSpec((rows, features), lambda i, s: (0, 0)),
                 pl.BlockSpec((TAIL, features), lambda i, s: (0, 0)),
                 pl.BlockSpec((CONV, features), lambda i, s: (0, 2 * s[1] + s[2])),
                 whole((2 * rows, heads)),
                 whole((STATE_WIDTH, 2 * rows)),
                 whole((TAIL, features)),
+                whole(edge.shape) if last else unread,
             ],
-            (whole(message.shape),) * parts,
-            (prompt_inner, other_inner, halo, conv_inner, weights, b_turned, logs),
+            (whole(spread.shape),) * parts,
+            (prompt_inner, other, halo, conv_inner, weights, b_turned, logs, far if last else tail),
             scratch=[pltpu.VMEM((rows + 8, width), f32)],
         )
-        held = [sent[0]] + [
-            routed(sent[step], lambda z, k, c: (z, k, c ^ step)) for step in range(1, parts)
-        ]
-        ready = [lax.select_n(column ^ plane ^ step, *held) for step in range(parts)]
-        arrived = [ready[0]] + [
-            routed(ready[step], lambda z, k, c: (z ^ step, k, c)) for step in range(1, parts)
-        ]
+        held.append(
+            [sent[0]]
+            + [routed(sent[step], lambda z, k, c: (z, k, c ^ step)) for step in range(1, parts)]
+        )
+
+    slots, positions = completion_inner.shape[:2]
+    block_heads = 8
+    block = block_heads * HEAD_WIDTH
+    blocks = heads // block_heads
+    finished = []
+
+    def completion(slot, after):
+        return run(
+            lambda *refs: completion_kernel(slot, *refs),
+            "completion",
+            (place,),
+            (
+                jax.ShapeDtypeStruct((positions, features), bf16),
+                jax.ShapeDtypeStruct((positions, features), bf16),
+                jax.ShapeDtypeStruct((positions, STATE_WIDTH), bf16),
+            ),
+            [
+                pl.BlockSpec((1, positions, block), lambda j, s: (slot, 0, j)),
+                pl.BlockSpec((1, positions, block), lambda j, s: (slot, 0, j)),
+                pl.BlockSpec((1, positions, STATE_WIDTH), lambda j, s: (slot, 0, s[3])),
+                pl.BlockSpec((1, positions, STATE_WIDTH), lambda j, s: (slot, 0, c_at + s[3])),
+                whole(edge.shape),
+                pl.BlockSpec((CONV, block), lambda j, s: (0, s[3] * blocks + j)),
+                pl.BlockSpec((CONV, STATE_WIDTH), lambda j, s: (0, s[3])),
+                pl.BlockSpec((CONV, STATE_WIDTH), lambda j, s: (0, c_at + s[3])),
+                whole((heads, slots, positions)),
+                whole((STATE_HEADS,)),
+                unread,
+            ],
+            (
+                pl.BlockSpec((positions, block), lambda j, s: (0, j)),
+                pl.BlockSpec((positions, block), lambda j, s: (0, j)),
+                whole((positions, STATE_WIDTH)),
+            ),
+            (
+                completion_inner,
+                completion_gate,
+                completion_projections,
+                completion_projections,
+                tail,
+                conv_inner,
+                conv_proj,
+                conv_proj,
+                sample_step,
+                decay_log,
+                after,
+            ),
+            grid=(blocks,),
+            scratch=[
+                pltpu.VMEM((positions + 8, block), f32),
+                pltpu.VMEM((positions // 2, positions // 2), f32),
+                pltpu.VMEM((positions // 2, positions), f32),
+                pltpu.VMEM((blocks, positions, block_heads), f32),
+                pltpu.VMEM((blocks, block_heads, positions), f32),
+                pltpu.VMEM((blocks, block_heads, positions), f32),
+                pltpu.VMEM((blocks + 1, TAIL, block), f32),
+            ],
+        )
+
+    arrived = []
+    for chunk in range(CHUNKS):
+        last = chunk + 1 == CHUNKS
+        picked = (message,) * parts + (edge,) * last
+        ready = run(
+            lambda *refs: pick_kernel(parts, *refs),
+            "pick",
+            (place,),
+            picked,
+            [whole(array.shape) for array in held[chunk]],
+            tuple(whole(each.shape) for each in picked),
+            held[chunk],
+        )
+        arrived.append(
+            [ready[0]]
+            + [routed(ready[step], lambda z, k, c: (z ^ step, k, c)) for step in range(1, parts)]
+        )
+    tail = ready[parts]
+    joined, after = [], ready[0]
+    for chunk in range(CHUNKS):
+        for slot in range(chunk * slots // CHUNKS, (chunk + 1) * slots // CHUNKS):
+            finished.append(completion(slot, after))
+            after = finished[-1][2]
         state = run(
             join_state_kernel,
             "join_state",
             (place,),
             jax.ShapeDtypeStruct((STATE_WIDTH, width), bf16),
-            [whole(message.shape)] * parts,
+            [whole(message.shape)] * parts + [unread],
             whole((STATE_WIDTH, width)),
-            arrived,
+            arrived[chunk] + [after],
         )
         joined += [state] + [
             routed(state, lambda z, k, c: (z, k, c ^ step)) for step in range(1, parts)
         ]
-
-    slots, positions = completion_inner.shape[:2]
-    block_heads = 8
-    block = block_heads * HEAD_WIDTH
-    blocks = heads // block_heads
-    decay_own = take(decay_log, row * heads, heads, 0)
-    cols_at = features // block
-    c_at = STATE_GROUPS
-    fixed, factor, c_rows = run(
-        completion_kernel,
-        "completion_blocks",
-        (place,),
-        (
-            jax.ShapeDtypeStruct((slots, positions, features), bf16),
-            jax.ShapeDtypeStruct((slots, positions, features), bf16),
-            jax.ShapeDtypeStruct((slots, positions, STATE_WIDTH), bf16),
-        ),
-        [
-            pl.BlockSpec((1, positions, block), lambda i, j, s: (i, 0, j)),
-            pl.BlockSpec((1, positions, block), lambda i, j, s: (i, 0, j)),
-            pl.BlockSpec((1, positions, STATE_WIDTH), lambda i, j, s: (i, 0, s[3])),
-            pl.BlockSpec((1, positions, STATE_WIDTH), lambda i, j, s: (i, 0, c_at + s[3])),
-            pl.BlockSpec((TAIL, block), lambda i, j, s: (0, j)),
-            pl.BlockSpec((TAIL, STATE_WIDTH), lambda i, j, s: (0, features // STATE_WIDTH)),
-            pl.BlockSpec((TAIL, STATE_WIDTH), lambda i, j, s: (0, features // STATE_WIDTH + 1)),
-            pl.BlockSpec((CONV, block), lambda i, j, s: (0, s[3] * cols_at + j)),
-            pl.BlockSpec((CONV, STATE_WIDTH), lambda i, j, s: (0, s[3])),
-            pl.BlockSpec((CONV, STATE_WIDTH), lambda i, j, s: (0, c_at + s[3])),
-            pl.BlockSpec((1, block_heads, positions), lambda i, j, s: (i, j, 0)),
-            pl.BlockSpec((1, 1, block_heads), lambda i, j, s: (j, 0, 0)),
-            pl.BlockSpec((block_heads, 1), lambda i, j, s: (j, 0)),
-        ],
-        (
-            pl.BlockSpec((1, positions, block), lambda i, j, s: (i, 0, j)),
-            pl.BlockSpec((1, positions, block), lambda i, j, s: (i, 0, j)),
-            pl.BlockSpec((1, positions, STATE_WIDTH), lambda i, j, s: (i, 0, 0)),
-        ),
-        (
-            completion_inner,
-            completion_gate,
-            completion_projections,
-            completion_projections,
-            tail,
-            tail,
-            tail,
-            conv_inner,
-            conv_proj,
-            conv_proj,
-            jnp.transpose(sample_step, (1, 0, 2)),
-            decay_own.reshape(blocks, 1, block_heads),
-            decay_own[:, None],
-        ),
-        grid=(slots, blocks),
-        scratch=[
-            pltpu.VMEM((positions + 8, block), f32),
-            pltpu.VMEM((positions // 2, positions // 2), f32),
-            pltpu.VMEM((positions // 2, positions), f32),
-        ],
-    )
+        after = state
     return run(
-        lambda *refs: finish_kernel(parts, CHUNKS, *refs),
+        lambda *refs: finish_kernel(parts, CHUNKS, slots, *refs),
         "finish",
         (place, sample_length),
         jax.ShapeDtypeStruct((slots, positions, features), bf16),
-        [
-            pl.BlockSpec((1, positions, STATE_WIDTH), lambda i, s, n: (i, 0, 0)),
-            pl.BlockSpec((1, positions, features), lambda i, s, n: (i, 0, 0)),
-            pl.BlockSpec((1, positions, features), lambda i, s, n: (i, 0, 0)),
-            whole((1, features)),
+        [whole((features,))]
+        + [whole((STATE_WIDTH, width))] * (parts * CHUNKS)
+        + [
+            whole((positions, STATE_WIDTH)),
+            whole((positions, features)),
+            whole((positions, features)),
         ]
-        + [whole((STATE_WIDTH, width))] * (parts * CHUNKS),
+        * slots,
         pl.BlockSpec((1, positions, features), lambda i, s, n: (i, 0, 0)),
-        [c_rows, fixed, factor, norm_gain[None]] + joined,
+        [norm_gain]
+        + joined
+        + [array for fixed, factor, c in finished for array in (c, fixed, factor)],
         grid=(slots,),
         scratch=[pltpu.VMEM((positions, features), f32)],
         scalars=2,

time: 105 us -> 73.4 us (0.70)
  local copies, waits for them, and re-layouts: 14 us -> 0.89 us
  starting transfers between devices: 37.5 us -> 30.5 us
  other arithmetic: 6.73 us -> 0.08 us
  waiting for transfers between devices: 14.2 us -> 9.26 us
    ppermute x28 -> x22, starting transfers between devices: 37.5 us -> 30.5 us  [routed(): return lax.ppermute(block, AXES, pairs)]
    unnamed x41 -> x20, local copies, waits for them, and re-layouts: 6.9 us -> 0.89 us
    dynamic_slice x4 -> x0, local copies, waits for them, and re-layouts: 5.39 us -> none  [take(): return lax.dynamic_slice_in_dim(array, start, size, axis)]
    ppermute x28 -> x22, waiting for transfers between devices: 14.2 us -> 9.26 us  [routed(): return lax.ppermute(block, AXES, pairs)]
    concatenate x4 -> x0, other arithmetic: 3.6 us -> none  [the longest x2 2.96 us: matched(): jnp.concatenate([inner_to, b_to], axis=1)]
    add x3 -> x0, other arithmetic: 1.87 us -> none  [the longest x1 0.94 us: matched(): halo = near if halo is None else halo + near]
    select_n x2 -> x0, other arithmetic: 1.18 us -> none  [matched(): lax.select_n(column ^ plane ^ step, *held)]
    pallas_call x7 -> x11, Pallas kernels: 30.5 us -> 31.4 us  [run(): pl.pallas_call(kernel, out_shape=out_shape, grid_spec=pltpu.PrefetchScala...]
  transfers between devices with their start and end apart: 28 -> 22, of which waited for: 4 -> 5; matrix products, arithmetic and copies ran while one was open for 12% -> 0% of each run, Pallas kernels for 23% -> 32%
where the time goes in v2:
time: 73.4 us; the launch traced here: 72.4 us
  Pallas kernels  31.4 us (43%)
  starting transfers between devices  30.5 us (42%)
  waiting for transfers between devices  9.26 us (13%)
  local copies, waits for them, and re-layouts  0.89 us (1%)
    pallas_call x11, Pallas kernels, run(): pl.pallas_call(kernel, out_shape=out_shape, grid_spec=pltpu.PrefetchScala...  31.4 us
    ppermute x22, starting transfers between devices, routed(): return lax.ppermute(block, AXES, pairs)  30.5 us
    ppermute x22, waiting for transfers between devices, routed(): return lax.ppermute(block, AXES, pairs)  9.26 us
  transfers between devices with their start and end apart: 22, of which 5 were waited for; matrix products, arithmetic and copies ran while one was open for 0% of the time, Pallas kernels for 32%

profile of v2, /device:TPU:0, one launch (start us, length us, event | category | flops | bytes accessed | tf_op | source)
XLA Modules:
  0.0 72.4 jit_solution(12727850985968435772)
XLA Ops:
  0.9 2.8 %pack.1 = (bf16[272,2432]{1,0:T(8,128)(2,1)S(1)}, bf16[16,512]{1,0:T(8,128)(2,1)S(1)}, bf16[16,512]{1,0:T(8,128)(2,1)S(1)}) custom-call(s32[4]{0:T(128)S(1)} %pad_add_fusion.place.refs_0_, bf16[256,4096]{1,0:T(8,128)(2,1)} %refs_1_.6, bf16[256,4096]{1,0:T(8,128)(2,1)} %own_b.1, f32[64,256]{1,0:T(8,128)S(1)} %copy-done.2, bf16[256,4096]{1,0:T(8,128)(2,1)} %refs_1_.6, ...), custom_call_target="tpu_custom_call" | custom-call | flops 2000000000 | bytes 6000000 | tf_op jit(solution)/shard_map/pack/pallas_call | solution.py:596
  5.8 1.2 %collective-permute-done.other_b.other_dt.other_tail.refs_2_ = bf16[272,2432]{1,0:T(8,128)(2,1)S(1)} collective-permute-done((bf16[272,2432]{1,0:T(8,128)(2,1)S(1)}, bf16[272,2432]{1,0:T(8,128)(2,1)S(1)}, u32[]{:S(2)}, u32[]{:S(2)}) %collective-permute-start) | collective-permute-done | bytes 1323040 | tf_op jit(solution)/shard_map/ppermute | solution.py:268
  7.0 1.7 %prompt_weights.1 = (f32[512,32]{1,0:T(8,128)S(1)}, bf16[256,512]{1,0:T(8,128)(2,1)S(1)}, bf16[16,2048]{1,0:T(8,128)(2,1)S(1)}, bf16[16,2048]{1,0:T(8,128)(2,1)S(1)}, bf16[16,512]{1,0:T(8,128)(2,1)S(1)}) custom-call(s32[4]{0:T(128)S(1)} %pad_add_fusion.place.refs_0_, bf16[256,4096]{1,0:T(8,128)(2,1)S(1)} %copy-done, ...), custom_call_target="tpu_custom_call" | custom-call | flops 2000000000 | bytes 6000000 | tf_op jit(solution)/shard_map/prompt_weights/pallas_call | solution.py:596
  8.7 1.3 %collective-permute-start.9 = (bf16[16,512]{1,0:T(8,128)(2,1)S(1)}, bf16[16,512]{1,0:T(8,128)(2,1)S(1)}, u32[]{:S(2)}, u32[]{:S(2)}) collective-permute-start(bf16[16,512]{1,0:T(8,128)(2,1)S(1)} %get-tuple-element.43.refs_8_), channel_id=1, source_target_pairs={{24,0},{25,9},{26,18},{27,27},{28,4},{29,13},{30,22},{31,31}} | collective-permute-start | bytes 49160 | tf_op jit(solution)/shard_map/ppermute | solution.py:268
  10.0 3.0 %prompt_state.2 = (bf16[272,256]{1,0:T(8,128)(2,1)S(1)}, bf16[272,256]{1,0:T(8,128)(2,1)S(1)}, bf16[272,256]{1,0:T(8,128)(2,1)S(1)}, bf16[272,256]{1,0:T(8,128)(2,1)S(1)}) custom-call(s32[4]{0:T(128)S(1)} %pad_add_fusion.place.refs_0_, bf16[256,4096]{1,0:T(8,128)(2,1)S(1)} %copy-done.1, ...), custom_call_target="tpu_custom_call" | custom-call | flops 3000000000 | bytes 9000000 | tf_op jit(solution)/shard_map/prompt_state/pallas_call | solution.py:596
  13.0 2.3 %collective-permute-start.3 = (bf16[272,256]{1,0:T(8,128)(2,1)S(1)}, bf16[272,256]{1,0:T(8,128)(2,1)S(1)}, u32[]{:S(2)}, u32[]{:S(2)}) collective-permute-start(bf16[272,256]{1,0:T(8,128)(2,1)S(1)} %get-tuple-element.45), channel_id=1, source_target_pairs={{0,1},{1,0},{2,3},{3,2},{4,5},{5,4},{6,7},{7,6},{8,9},{9,8},{10,11... | collective-permute-start | bytes 417800 | tf_op jit(solution)/shard_map/ppermute | solution.py:268
  15.3 1.5 %collective-permute-start.4 = (bf16[272,256]{1,0:T(8,128)(2,1)S(1)}, bf16[272,256]{1,0:T(8,128)(2,1)S(1)}, u32[]{:S(2)}, u32[]{:S(2)}) collective-permute-start(bf16[272,256]{1,0:T(8,128)(2,1)S(1)} %get-tuple-element.46), channel_id=1, source_target_pairs={{0,2},{1,3},{2,0},{3,1},{4,6},{5,7},{6,4},{7,5},{8,10},{9,11},{10,... | collective-permute-start | bytes 417800 | tf_op jit(solution)/shard_map/ppermute | solution.py:268
  16.8 1.8 %collective-permute-done.9.refs_8_ = bf16[16,512]{1,0:T(8,128)(2,1)S(1)} collective-permute-done((bf16[16,512]{1,0:T(8,128)(2,1)S(1)}, bf16[16,512]{1,0:T(8,128)(2,1)S(1)}, u32[]{:S(2)}, u32[]{:S(2)}) %collective-permute-start.9) | collective-permute-done | bytes 16416 | tf_op jit(solution)/shard_map/ppermute | solution.py:268
  18.7 3.0 %prompt_state.3 = (bf16[304,256]{1,0:T(8,128)(2,1)S(1)}, bf16[304,256]{1,0:T(8,128)(2,1)S(1)}, bf16[304,256]{1,0:T(8,128)(2,1)S(1)}, bf16[304,256]{1,0:T(8,128)(2,1)S(1)}) custom-call(s32[4]{0:T(128)S(1)} %pad_add_fusion.place.refs_0_, bf16[256,4096]{1,0:T(8,128)(2,1)S(1)} %copy-done.1, ...), custom_call_target="tpu_custom_call" | custom-call | flops 3000000000 | bytes 9000000 | tf_op jit(solution)/shard_map/prompt_state/pallas_call | solution.py:596
  21.9 1.5 %collective-permute-start.11 = (bf16[304,256]{1,0:T(8,128)(2,1)S(1)}, bf16[304,256]{1,0:T(8,128)(2,1)S(1)}, u32[]{:S(2)}, u32[]{:S(2)}) collective-permute-start(bf16[304,256]{1,0:T(8,128)(2,1)S(1)} %get-tuple-element.54), channel_id=1, source_target_pairs={{0,2},{1,3},{2,0},{3,1},{4,6},{5,7},{6,4},{7,5},{8,10},{9,11},{10,... | collective-permute-start | bytes 466952 | tf_op jit(solution)/shard_map/ppermute | solution.py:268
  23.4 1.8 %collective-permute-start.12 = (bf16[304,256]{1,0:T(8,128)(2,1)S(1)}, bf16[304,256]{1,0:T(8,128)(2,1)S(1)}, u32[]{:S(2)}, u32[]{:S(2)}) collective-permute-start(bf16[304,256]{1,0:T(8,128)(2,1)S(1)} %get-tuple-element.55), channel_id=1, source_target_pairs={{0,3},{1,2},{2,1},{3,0},{4,7},{5,6},{6,5},{7,4},{8,11},{9,10},{10,... | collective-permute-start | bytes 466952 | tf_op jit(solution)/shard_map/ppermute | solution.py:268
  25.9 2.6 %collective-permute-start.6 = (bf16[272,256]{1,0:T(8,128)(2,1)S(1)}, bf16[272,256]{1,0:T(8,128)(2,1)S(1)}, u32[]{:S(2)}, u32[]{:S(2)}) collective-permute-start(bf16[272,256]{1,0:T(8,128)(2,1)S(1)} %get-tuple-element.49), channel_id=1, source_target_pairs={{0,8},{1,9},{2,10},{3,11},{4,12},{5,13},{6,14},{7,15},{8,0},{9,1},... | collective-permute-start | bytes 417800 | tf_op jit(solution)/shard_map/ppermute | solution.py:268
  28.4 3.5 %collective-permute-start.7 = (bf16[272,256]{1,0:T(8,128)(2,1)S(1)}, bf16[272,256]{1,0:T(8,128)(2,1)S(1)}, u32[]{:S(2)}, u32[]{:S(2)}) collective-permute-start(bf16[272,256]{1,0:T(8,128)(2,1)S(1)} %get-tuple-element.50), channel_id=1, source_target_pairs={{0,16},{1,17},{2,18},{3,19},{4,20},{5,21},{6,22},{7,23},{8,24},{9,... | collective-permute-start | bytes 417800 | tf_op jit(solution)/shard_map/ppermute | solution.py:268
  33.5 2.3 %collective-permute-start.16 = (bf16[272,256]{1,0:T(8,128)(2,1)S(1)}, bf16[272,256]{1,0:T(8,128)(2,1)S(1)}, u32[]{:S(2)}, u32[]{:S(2)}) collective-permute-start(bf16[272,256]{1,0:T(8,128)(2,1)S(1)} %get-tuple-element.59), channel_id=1, source_target_pairs={{0,8},{1,9},{2,10},{3,11},{4,12},{5,13},{6,14},{7,15},{8,0},{9,1},... | collective-permute-start | bytes 417800 | tf_op jit(solution)/shard_map/ppermute | solution.py:268
  35.9 3.5 %collective-permute-start.17 = (bf16[272,256]{1,0:T(8,128)(2,1)S(1)}, bf16[272,256]{1,0:T(8,128)(2,1)S(1)}, u32[]{:S(2)}, u32[]{:S(2)}) collective-permute-start(bf16[272,256]{1,0:T(8,128)(2,1)S(1)} %get-tuple-element.60), channel_id=1, source_target_pairs={{0,16},{1,17},{2,18},{3,19},{4,20},{5,21},{6,22},{7,23},{8,24},{9,... | collective-permute-start | bytes 417800 | tf_op jit(solution)/shard_map/ppermute | solution.py:268
  39.3 7.4 %completion.2 = (bf16[256,2048]{1,0:T(8,128)(2,1)S(1)}, bf16[256,2048]{1,0:T(8,128)(2,1)S(1)}, bf16[256,256]{1,0:T(8,128)(2,1)S(1)}) custom-call(s32[4]{0:T(128)S(1)} %pad_add_fusion.place.refs_0_, bf16[2,256,2048]{2,1,0:T(8,128)(2,1)S(1)} %copy-done.3, bf16[2,256,2048]{2,1,0:T(8,128)(2,1)} %refs_2_.4, bf16[2,256,4096]{2,1,0:T(8,128)(2,1)} %refs_4_.7, ...), custom_call_target="tpu_custom_call" | custom-call | flops 8000000000 | bytes 24000000 | tf_op jit(solution)/shard_map/completion/pallas_call | solution.py:596
  47.5 1.4 %collective-permute-start.15 = (bf16[256,256]{1,0:T(8,128)(2,1)S(1)}, bf16[256,256]{1,0:T(8,128)(2,1)S(1)}, u32[]{:S(2)}, u32[]{:S(2)}) collective-permute-start(bf16[256,256]{1,0:T(8,128)(2,1)S(1)} %join_state.2.refs_11_.refs_3_), channel_id=1, source_target_pairs={{0,3},{1,2},{2,1},{3,0},{4,7},{5,6},{6,5},{7,4},{8,11},{9,10},{10,... | collective-permute-start | bytes 393224 | tf_op jit(solution)/shard_map/ppermute | solution.py:268
  49.8 7.4 %completion.3 = (bf16[256,2048]{1,0:T(8,128)(2,1)S(1)}, bf16[256,2048]{1,0:T(8,128)(2,1)S(1)}, bf16[256,256]{1,0:T(8,128)(2,1)S(1)}) custom-call(s32[4]{0:T(128)S(1)} %pad_add_fusion.place.refs_0_, bf16[2,256,2048]{2,1,0:T(8,128)(2,1)S(1)} %copy-done.3, bf16[2,256,2048]{2,1,0:T(8,128)(2,1)} %refs_2_.4, bf16[2,256,4096]{2,1,0:T(8,128)(2,1)} %refs_4_.7, ...), custom_call_target="tpu_custom_call" | custom-call | flops 8000000000 | bytes 24000000 | tf_op jit(solution)/shard_map/completion/pallas_call | solution.py:596
  57.2 1.3 %collective-permute-start.13 = (bf16[256,256]{1,0:T(8,128)(2,1)S(1)}, bf16[256,256]{1,0:T(8,128)(2,1)S(1)}, u32[]{:S(2)}, u32[]{:S(2)}) collective-permute-start(bf16[256,256]{1,0:T(8,128)(2,1)S(1)} %join_state.2.refs_11_.refs_3_), channel_id=1, source_target_pairs={{0,1},{1,0},{2,3},{3,2},{4,5},{5,4},{6,7},{7,6},{8,9},{9,8},{10,11... | collective-permute-start | bytes 393224 | tf_op jit(solution)/shard_map/ppermute | solution.py:268
  59.2 1.4 %collective-permute-start.21 = (bf16[256,256]{1,0:T(8,128)(2,1)S(1)}, bf16[256,256]{1,0:T(8,128)(2,1)S(1)}, u32[]{:S(2)}, u32[]{:S(2)}) collective-permute-start(bf16[256,256]{1,0:T(8,128)(2,1)S(1)} %join_state.3.refs_7_), channel_id=1, source_target_pairs={{0,3},{1,2},{2,1},{3,0},{4,7},{5,6},{6,5},{7,4},{8,11},{9,10},{10,... | collective-permute-start | bytes 393224 | tf_op jit(solution)/shard_map/ppermute | solution.py:268
  61.5 1.2 %collective-permute-start.19 = (bf16[256,256]{1,0:T(8,128)(2,1)S(1)}, bf16[256,256]{1,0:T(8,128)(2,1)S(1)}, u32[]{:S(2)}, u32[]{:S(2)}) collective-permute-start(bf16[256,256]{1,0:T(8,128)(2,1)S(1)} %join_state.3.refs_7_), channel_id=1, source_target_pairs={{0,1},{1,0},{2,3},{3,2},{4,5},{5,4},{6,7},{7,6},{8,9},{9,8},{10,11... | collective-permute-start | bytes 393224 | tf_op jit(solution)/shard_map/ppermute | solution.py:268
  63.5 3.5 %collective-permute-done.21.refs_10_ = bf16[256,256]{1,0:T(8,128)(2,1)S(1)} collective-permute-done((bf16[256,256]{1,0:T(8,128)(2,1)S(1)}, bf16[256,256]{1,0:T(8,128)(2,1)S(1)}, u32[]{:S(2)}, u32[]{:S(2)}) %collective-permute-start.21) | collective-permute-done | bytes 131104 | tf_op jit(solution)/shard_map/ppermute | solution.py:268
  67.0 1.9 %collective-permute-done.20.refs_9_ = bf16[256,256]{1,0:T(8,128)(2,1)S(1)} collective-permute-done((bf16[256,256]{1,0:T(8,128)(2,1)S(1)}, bf16[256,256]{1,0:T(8,128)(2,1)S(1)}, u32[]{:S(2)}, u32[]{:S(2)}) %collective-permute-start.20) | collective-permute-done | bytes 131104 | tf_op jit(solution)/shard_map/ppermute | solution.py:268
  69.0 3.4 %finish.1 = bf16[2,256,2048]{2,1,0:T(8,128)(2,1)} custom-call(s32[4]{0:T(128)S(1)} %pad_add_fusion.place.refs_0_, s32[2]{0:T(128)S(1)} %copy-done.9, f32[2048]{0:T(1024)S(1)} %copy-done.7, bf16[256,256]{1,0:T(8,128)(2,1)S(1)} %join_state.2.refs_11_.refs_3_, bf16[256,256]{1,0:T(8,128)(2,1)S(1)} %collective-permute-done.13.refs_4_, ...), custom_call_target="tpu_custom_call" | custom-call | flops 4000000000 | bytes 12000000 | tf_op jit(solution)/shard_map/finish/pallas_call | solution.py:596
  (52 shorter events, 9.4 us)
Async XLA Ops:
  3.8 3.2 %collective-permute-start = (bf16[272,2432]{1,0:T(8,128)(2,1)S(1)}, bf16[272,2432]{1,0:T(8,128)(2,1)S(1)}, u32[]{:S(2)}, u32[]{:S(2)}) collective-permute-start(bf16[272,2432]{1,0:T(8,128)(2,1)S(1)} %get-tuple-element.36), channel_id=1, source_target_pairs={{0,4},{1,5},{2,6},{3,7},{4,0},{5,1},{6,2},{7,3},{8,12},{9,13},{10,... | collective-permute-start | bytes 3969032 | tf_op jit(solution)/shard_map/ppermute | solution.py:268
  4.3 1.5 %collective-permute-start.1 = (bf16[16,512]{1,0:T(8,128)(2,1)S(1)}, bf16[16,512]{1,0:T(8,128)(2,1)S(1)}, u32[]{:S(2)}, u32[]{:S(2)}) collective-permute-start(bf16[16,512]{1,0:T(8,128)(2,1)S(1)} %get-tuple-element.37), channel_id=1, source_target_pairs={{4,8},{5,9},{6,10},{7,11},{12,16},{13,17},{14,18},{15,19},{20,24},... | collective-permute-start | bytes 49160 | tf_op jit(solution)/shard_map/ppermute | solution.py:268
  5.0 0.8 %collective-permute-start.2 = (bf16[16,512]{1,0:T(8,128)(2,1)S(1)}, bf16[16,512]{1,0:T(8,128)(2,1)S(1)}, u32[]{:S(2)}, u32[]{:S(2)}) collective-permute-start(bf16[16,512]{1,0:T(8,128)(2,1)S(1)} %get-tuple-element.38.own_tail), channel_id=1, source_target_pairs={{4,12},{5,13},{6,14},{7,15},{12,20},{13,21},{14,22},{15,23},{20,28... | collective-permute-start | bytes 49160 | tf_op jit(solution)/shard_map/ppermute | solution.py:268
  8.7 10.0 %collective-permute-start.9 = (bf16[16,512]{1,0:T(8,128)(2,1)S(1)}, bf16[16,512]{1,0:T(8,128)(2,1)S(1)}, u32[]{:S(2)}, u32[]{:S(2)}) collective-permute-start(bf16[16,512]{1,0:T(8,128)(2,1)S(1)} %get-tuple-element.43.refs_8_), channel_id=1, source_target_pairs={{24,0},{25,9},{26,18},{27,27},{28,4},{29,13},{30,22},{31,31}} | collective-permute-start | bytes 49160 | tf_op jit(solution)/shard_map/ppermute | solution.py:268
  13.0 10.4 %collective-permute-start.3 = (bf16[272,256]{1,0:T(8,128)(2,1)S(1)}, bf16[272,256]{1,0:T(8,128)(2,1)S(1)}, u32[]{:S(2)}, u32[]{:S(2)}) collective-permute-start(bf16[272,256]{1,0:T(8,128)(2,1)S(1)} %get-tuple-element.45), channel_id=1, source_target_pairs={{0,1},{1,0},{2,3},{3,2},{4,5},{5,4},{6,7},{7,6},{8,9},{9,8},{10,11... | collective-permute-start | bytes 417800 | tf_op jit(solution)/shard_map/ppermute | solution.py:268
  15.3 10.0 %collective-permute-start.4 = (bf16[272,256]{1,0:T(8,128)(2,1)S(1)}, bf16[272,256]{1,0:T(8,128)(2,1)S(1)}, u32[]{:S(2)}, u32[]{:S(2)}) collective-permute-start(bf16[272,256]{1,0:T(8,128)(2,1)S(1)} %get-tuple-element.46), channel_id=1, source_target_pairs={{0,2},{1,3},{2,0},{3,1},{4,6},{5,7},{6,4},{7,5},{8,10},{9,11},{10,... | collective-permute-start | bytes 417800 | tf_op jit(solution)/shard_map/ppermute | solution.py:268
  16.8 8.4 %collective-permute-start.5 = (bf16[272,256]{1,0:T(8,128)(2,1)S(1)}, bf16[272,256]{1,0:T(8,128)(2,1)S(1)}, u32[]{:S(2)}, u32[]{:S(2)}) collective-permute-start(bf16[272,256]{1,0:T(8,128)(2,1)S(1)} %get-tuple-element.47), channel_id=1, source_target_pairs={{0,3},{1,2},{2,1},{3,0},{4,7},{5,6},{6,5},{7,4},{8,11},{9,10},{10,... | collective-permute-start | bytes 417800 | tf_op jit(solution)/shard_map/ppermute | solution.py:268
  21.7 10.3 %collective-permute-start.10 = (bf16[304,256]{1,0:T(8,128)(2,1)S(1)}, bf16[304,256]{1,0:T(8,128)(2,1)S(1)}, u32[]{:S(2)}, u32[]{:S(2)}) collective-permute-start(bf16[304,256]{1,0:T(8,128)(2,1)S(1)} %get-tuple-element.53), channel_id=1, source_target_pairs={{0,1},{1,0},{2,3},{3,2},{4,5},{5,4},{6,7},{7,6},{8,9},{9,8},{10,11... | collective-permute-start | bytes 466952 | tf_op jit(solution)/shard_map/ppermute | solution.py:268
  21.9 10.8 %collective-permute-start.11 = (bf16[304,256]{1,0:T(8,128)(2,1)S(1)}, bf16[304,256]{1,0:T(8,128)(2,1)S(1)}, u32[]{:S(2)}, u32[]{:S(2)}) collective-permute-start(bf16[304,256]{1,0:T(8,128)(2,1)S(1)} %get-tuple-element.54), channel_id=1, source_target_pairs={{0,2},{1,3},{2,0},{3,1},{4,6},{5,7},{6,4},{7,5},{8,10},{9,11},{10,... | collective-permute-start | bytes 466952 | tf_op jit(solution)/shard_map/ppermute | solution.py:268
  23.4 9.3 %collective-permute-start.12 = (bf16[304,256]{1,0:T(8,128)(2,1)S(1)}, bf16[304,256]{1,0:T(8,128)(2,1)S(1)}, u32[]{:S(2)}, u32[]{:S(2)}) collective-permute-start(bf16[304,256]{1,0:T(8,128)(2,1)S(1)} %get-tuple-element.55), channel_id=1, source_target_pairs={{0,3},{1,2},{2,1},{3,0},{4,7},{5,6},{6,5},{7,4},{8,11},{9,10},{10,... | collective-permute-start | bytes 466952 | tf_op jit(solution)/shard_map/ppermute | solution.py:268
  25.9 13.5 %copy-start.3 = (bf16[2,256,2048]{2,1,0:T(8,128)(2,1)S(1)}, bf16[2,256,2048]{2,1,0:T(8,128)(2,1)}, u32[]{:S(2)}) copy-start(bf16[2,256,2048]{2,1,0:T(8,128)(2,1)} %refs_1_.8) | copy-start | bytes 6291460
  25.9 13.5 %copy-start.5 = (f32[32,2,256]{2,1,0:T(2,128)S(1)}, f32[32,2,256]{2,1,0:T(2,128)}, u32[]{:S(2)}) copy-start(f32[32,2,256]{2,1,0:T(2,128)} %refs_9_.3) | copy-start | bytes 196612
  25.9 20.8 %collective-permute-start.6 = (bf16[272,256]{1,0:T(8,128)(2,1)S(1)}, bf16[272,256]{1,0:T(8,128)(2,1)S(1)}, u32[]{:S(2)}, u32[]{:S(2)}) collective-permute-start(bf16[272,256]{1,0:T(8,128)(2,1)S(1)} %get-tuple-element.49), channel_id=1, source_target_pairs={{0,8},{1,9},{2,10},{3,11},{4,12},{5,13},{6,14},{7,15},{8,0},{9,1},... | collective-permute-start | bytes 417800 | tf_op jit(solution)/shard_map/ppermute | solution.py:268
  28.4 18.3 %collective-permute-start.7 = (bf16[272,256]{1,0:T(8,128)(2,1)S(1)}, bf16[272,256]{1,0:T(8,128)(2,1)S(1)}, u32[]{:S(2)}, u32[]{:S(2)}) collective-permute-start(bf16[272,256]{1,0:T(8,128)(2,1)S(1)} %get-tuple-element.50), channel_id=1, source_target_pairs={{0,16},{1,17},{2,18},{3,19},{4,20},{5,21},{6,22},{7,23},{8,24},{9,... | collective-permute-start | bytes 417800 | tf_op jit(solution)/shard_map/ppermute | solution.py:268
  32.0 14.8 %collective-permute-start.8 = (bf16[272,256]{1,0:T(8,128)(2,1)S(1)}, bf16[272,256]{1,0:T(8,128)(2,1)S(1)}, u32[]{:S(2)}, u32[]{:S(2)}) collective-permute-start(bf16[272,256]{1,0:T(8,128)(2,1)S(1)} %get-tuple-element.51), channel_id=1, source_target_pairs={{0,24},{1,25},{2,26},{3,27},{4,28},{5,29},{6,30},{7,31},{8,16},{9,... | collective-permute-start | bytes 417800 | tf_op jit(solution)/shard_map/ppermute | solution.py:268
  33.5 23.7 %collective-permute-start.16 = (bf16[272,256]{1,0:T(8,128)(2,1)S(1)}, bf16[272,256]{1,0:T(8,128)(2,1)S(1)}, u32[]{:S(2)}, u32[]{:S(2)}) collective-permute-start(bf16[272,256]{1,0:T(8,128)(2,1)S(1)} %get-tuple-element.59), channel_id=1, source_target_pairs={{0,8},{1,9},{2,10},{3,11},{4,12},{5,13},{6,14},{7,15},{8,0},{9,1},... | collective-permute-start | bytes 417800 | tf_op jit(solution)/shard_map/ppermute | solution.py:268
  35.9 22.6 %collective-permute-start.17 = (bf16[272,256]{1,0:T(8,128)(2,1)S(1)}, bf16[272,256]{1,0:T(8,128)(2,1)S(1)}, u32[]{:S(2)}, u32[]{:S(2)}) collective-permute-start(bf16[272,256]{1,0:T(8,128)(2,1)S(1)} %get-tuple-element.60), channel_id=1, source_target_pairs={{0,16},{1,17},{2,18},{3,19},{4,20},{5,21},{6,22},{7,23},{8,24},{9,... | collective-permute-start | bytes 417800 | tf_op jit(solution)/shard_map/ppermute | solution.py:268
  46.7 11.8 %collective-permute-start.18 = (bf16[272,256]{1,0:T(8,128)(2,1)S(1)}, bf16[272,256]{1,0:T(8,128)(2,1)S(1)}, u32[]{:S(2)}, u32[]{:S(2)}) collective-permute-start(bf16[272,256]{1,0:T(8,128)(2,1)S(1)} %get-tuple-element.61), channel_id=1, source_target_pairs={{0,24},{1,25},{2,26},{3,27},{4,28},{5,29},{6,30},{7,31},{8,16},{9,... | collective-permute-start | bytes 417800 | tf_op jit(solution)/shard_map/ppermute | solution.py:268
  47.5 14.0 %collective-permute-start.15 = (bf16[256,256]{1,0:T(8,128)(2,1)S(1)}, bf16[256,256]{1,0:T(8,128)(2,1)S(1)}, u32[]{:S(2)}, u32[]{:S(2)}) collective-permute-start(bf16[256,256]{1,0:T(8,128)(2,1)S(1)} %join_state.2.refs_11_.refs_3_), channel_id=1, source_target_pairs={{0,3},{1,2},{2,1},{3,0},{4,7},{5,6},{6,5},{7,4},{8,11},{9,10},{10,... | collective-permute-start | bytes 393224 | tf_op jit(solution)/shard_map/ppermute | solution.py:268
  48.9 13.9 %collective-permute-start.14 = (bf16[256,256]{1,0:T(8,128)(2,1)S(1)}, bf16[256,256]{1,0:T(8,128)(2,1)S(1)}, u32[]{:S(2)}, u32[]{:S(2)}) collective-permute-start(bf16[256,256]{1,0:T(8,128)(2,1)S(1)} %join_state.2.refs_11_.refs_3_), channel_id=1, source_target_pairs={{0,2},{1,3},{2,0},{3,1},{4,6},{5,7},{6,4},{7,5},{8,10},{9,11},{10,... | collective-permute-start | bytes 393224 | tf_op jit(solution)/shard_map/ppermute | solution.py:268
  57.2 6.3 %collective-permute-start.13 = (bf16[256,256]{1,0:T(8,128)(2,1)S(1)}, bf16[256,256]{1,0:T(8,128)(2,1)S(1)}, u32[]{:S(2)}, u32[]{:S(2)}) collective-permute-start(bf16[256,256]{1,0:T(8,128)(2,1)S(1)} %join_state.2.refs_11_.refs_3_), channel_id=1, source_target_pairs={{0,1},{1,0},{2,3},{3,2},{4,5},{5,4},{6,7},{7,6},{8,9},{9,8},{10,11... | collective-permute-start | bytes 393224 | tf_op jit(solution)/shard_map/ppermute | solution.py:268
  59.2 7.9 %collective-permute-start.21 = (bf16[256,256]{1,0:T(8,128)(2,1)S(1)}, bf16[256,256]{1,0:T(8,128)(2,1)S(1)}, u32[]{:S(2)}, u32[]{:S(2)}) collective-permute-start(bf16[256,256]{1,0:T(8,128)(2,1)S(1)} %join_state.3.refs_7_), channel_id=1, source_target_pairs={{0,3},{1,2},{2,1},{3,0},{4,7},{5,6},{6,5},{7,4},{8,11},{9,10},{10,... | collective-permute-start | bytes 393224 | tf_op jit(solution)/shard_map/ppermute | solution.py:268
  60.6 8.4 %collective-permute-start.20 = (bf16[256,256]{1,0:T(8,128)(2,1)S(1)}, bf16[256,256]{1,0:T(8,128)(2,1)S(1)}, u32[]{:S(2)}, u32[]{:S(2)}) collective-permute-start(bf16[256,256]{1,0:T(8,128)(2,1)S(1)} %join_state.3.refs_7_), channel_id=1, source_target_pairs={{0,2},{1,3},{2,0},{3,1},{4,6},{5,7},{6,4},{7,5},{8,10},{9,11},{10,... | collective-permute-start | bytes 393224 | tf_op jit(solution)/shard_map/ppermute | solution.py:268
  61.5 7.4 %collective-permute-start.19 = (bf16[256,256]{1,0:T(8,128)(2,1)S(1)}, bf16[256,256]{1,0:T(8,128)(2,1)S(1)}, u32[]{:S(2)}, u32[]{:S(2)}) collective-permute-start(bf16[256,256]{1,0:T(8,128)(2,1)S(1)} %join_state.3.refs_7_), channel_id=1, source_target_pairs={{0,1},{1,0},{2,3},{3,2},{4,5},{5,4},{6,7},{7,6},{8,9},{9,8},{10,11... | collective-permute-start | bytes 393224 | tf_op jit(solution)/shard_map/ppermute | solution.py:268
  (8 other events, 52.6 us)

commit v3 on v0

--- a/solution.py
+++ b/solution.py
@@ -1,6 +1,8 @@
 import jax
 import jax.numpy as jnp
 from jax import lax
+from jax.experimental import pallas as pl
+from jax.experimental.pallas import tpu as pltpu
 from jax.sharding import PartitionSpec as P
 
 STATE_HEADS = 256
@@ -93,7 +95,7 @@
     )
 
 
-def local(
+def any_shape(
     prompt_inner,
     prompt_proj,
     prompt_step,
@@ -247,6 +249,686 @@
     return jnp.where(live_rows[:, :, None], result, 0.0).astype(jnp.bfloat16)
 
 
+LOG2E = 1.4426950408889634
+AXES = ("prompt", "comp")
+CHUNKS = (1, 1)
+PIECES = 1
+TAIL = 16
+VMEM_BYTES = 16 * 1024 * 1024
+
+
+def routed(block, route):
+    columns = lax.axis_size("comp")
+    pairs = []
+    for row in range(lax.axis_size("prompt")):
+        for column in range(columns):
+            target = route(row // 2, row % 2, column)
+            if target is not None:
+                plane, core, to = target
+                pairs.append((row * columns + column, (2 * plane + core) * columns + to))
+    return lax.ppermute(block, AXES, pairs)
+
+
+def half_silu(value):
+    return 0.5 * value * (1.0 + jnp.tanh(0.5 * value))
+
+
+def conv_rows(taps, lead, block):
+    wide = taps.astype(jnp.float32)
+    rows = block.astype(jnp.float32)
+    edge = jnp.concatenate([lead.astype(jnp.float32)[TAIL - 8 :], rows[0:8]], axis=0)
+    total = wide[CONV - 1 : CONV] * rows
+    for back in range(1, CONV):
+        shifted = pltpu.roll(rows, back, 0)
+        shifted = jnp.concatenate([edge[8 - back : 16 - back], shifted[8:]], axis=0)
+        total = total + wide[CONV - 1 - back : CONV - back] * shifted
+    return half_silu(total)
+
+
+def spread_heads(first, heads, width):
+    row = lax.broadcasted_iota(jnp.int32, (heads, width), 0)
+    col = lax.broadcasted_iota(jnp.int32, (heads, width), 1)
+    return row == first + col // HEAD_WIDTH
+
+
+def contract(lhs, rhs, dims, precision=None):
+    return lax.dot_general(
+        lhs, rhs, (dims, ((), ())), preferred_element_type=jnp.float32, precision=precision
+    )
+
+
+def softplus(value):
+    return jnp.maximum(value, 0.0) + jnp.log1p(jnp.exp(-jnp.abs(value)))
+
+
+def group_of(decay, index, size):
+    every = jnp.reshape(decay[...], (1, decay.shape[0]))
+    return pltpu.roll(every, decay.shape[0] - index * size, 1)[:, 0:size]
+
+
+def pack_kernel(
+    place, inner, proj, step, swap_out, edge_out, own_out, step_in, inner_in, b_in, c_in, sems
+):
+    heads, rows = step_in.shape
+    features = heads * HEAD_WIDTH
+    column, core = place[1], place[2]
+    theirs = 1 - core
+    pair = 2 * STATE_WIDTH
+
+    def columns(first, size):
+        return pl.ds(pl.multiple_of(first * size, size), size)
+
+    last = slice(rows - TAIL, rows)
+    copies = [
+        (step.at[columns(theirs, heads)], step_in),
+        (inner.at[last], inner_in),
+        (proj.at[last, columns(column, pair)], b_in),
+        (proj.at[last, columns(STATE_GROUPS // 2 + column, pair)], c_in),
+        (proj.at[:, columns(2 * column + theirs, STATE_WIDTH)], swap_out.at[0:rows, 0:STATE_WIDTH]),
+        (proj.at[:, columns(2 * column + core, STATE_WIDTH)], own_out),
+    ]
+    copies = [
+        pltpu.make_async_copy(source, target, sems.at[index])
+        for index, (source, target) in enumerate(copies)
+    ]
+    for copy in copies:
+        copy.start()
+    for copy in copies:
+        copy.wait()
+    dt = jnp.transpose(softplus(step_in[...]))
+    high = dt.astype(jnp.bfloat16)
+    low = (dt - high.astype(jnp.float32)).astype(jnp.bfloat16)
+    swap_out[0:rows, STATE_WIDTH:pair] = jnp.concatenate([high, low] * (STATE_WIDTH // heads // 2), axis=1)
+    edges = []
+    for to in range(2):
+        group = slice(to * STATE_WIDTH, (to + 1) * STATE_WIDTH)
+        inner_last = inner_in[:, to * features : (to + 1) * features].astype(jnp.float32)
+        bc_last = jnp.concatenate([b_in[:, group], c_in[:, group]], axis=1)
+        pieces = [inner_last[TAIL - 3 :, at : at + pair] for at in range(0, features, pair)]
+        pieces.append(bc_last.astype(jnp.float32)[TAIL - 3 :])
+        pieces.append(jnp.zeros((TAIL - 3 * len(pieces), pair), jnp.float32))
+        edges.append(jnp.concatenate(pieces, axis=0))
+    swap_out[rows:] = jnp.where(core == 0, edges[1], edges[0]).astype(jnp.bfloat16)
+    edge_out[...] = edges[1].astype(jnp.bfloat16)
+
+
+def prompt_weights_kernel(
+    place, own, other, taps_b, step, decay, w_out, b_out, log_out, first_out
+):
+    rows = own.shape[0]
+    heads = step.shape[0] // 2
+    group = 2 * place[1] + place[2]
+    own_b = own[...]
+    other_b = other[0:rows, 0:STATE_WIDTH]
+    other_dt = other[0:rows, STATE_WIDTH : STATE_WIDTH + 2 * heads]
+    taps = taps_b[:, pl.ds(pl.multiple_of(group * STATE_WIDTH, STATE_WIDTH), STATE_WIDTH)]
+    own_step = step[pl.ds(pl.multiple_of(place[2] * heads, heads), heads)]
+    core = place[2]
+    first_own = core == 0
+    rate = jnp.exp(group_of(decay, 2 * place[1] + core, heads))
+    dt_own = jnp.transpose(softplus(own_step))
+    parts = other_dt.astype(jnp.float32)
+    dt_other = parts[:, 0:heads] + parts[:, heads : 2 * heads]
+    row = lax.broadcasted_iota(jnp.int32, (rows, rows), 0)
+    col = lax.broadcasted_iota(jnp.int32, (rows, rows), 1)
+    later = (col > row).astype(jnp.float32)
+    after = contract(later, jnp.concatenate([dt_own, dt_other], axis=1), ((1,), (0,)), HIGHEST)
+    sum_own = after[0:1, 0:heads] + dt_own[0:1]
+    sum_other = after[0:1, heads:] + dt_other[0:1]
+    after_own = after[:, 0:heads] + jnp.where(first_own, sum_other, 0.0)
+    after_other = after[:, heads:] + jnp.where(first_own, 0.0, sum_own)
+    w_out[0:rows] = jnp.exp(-rate * after_own) * dt_own
+    w_out[rows:] = jnp.exp(-rate * after_other) * dt_other
+    total = jnp.broadcast_to(-rate * (sum_own + sum_other), (8, heads))
+    spread = spread_heads(0, heads, heads * HEAD_WIDTH).astype(jnp.bfloat16)
+    which = lax.broadcasted_iota(jnp.int32, total.shape, 0)
+    high = total.astype(jnp.bfloat16).astype(jnp.float32)
+    mid = (total - high).astype(jnp.bfloat16).astype(jnp.float32)
+    low = total - high - mid
+    parts = jnp.where(which == 0, high, jnp.where(which == 1, mid, jnp.where(which == 2, low, 0.0)))
+    wide = contract(parts.astype(jnp.bfloat16), spread, ((1,), (0,)))
+    log_out[...] = jnp.concatenate([wide, jnp.zeros_like(wide)], axis=0).astype(jnp.bfloat16)
+    own_last, other_last = own_b[rows - TAIL :], other_b[rows - TAIL :]
+    first = jnp.where(first_own, own_b[0:TAIL].astype(jnp.float32), other_b[0:TAIL].astype(jnp.float32))
+    first_out[...] = first.astype(jnp.bfloat16)
+    blank = jnp.zeros((TAIL, STATE_WIDTH), jnp.float32)
+    lead_own = jnp.where(first_own, blank, other_last.astype(jnp.float32))
+    lead_other = jnp.where(first_own, own_last.astype(jnp.float32), blank)
+    conv_own = conv_rows(taps, lead_own, own_b)
+    b_out[:, 0:rows] = jnp.transpose(conv_own).astype(jnp.bfloat16)
+    conv_other = conv_rows(taps, lead_other, other_b)
+    b_out[:, rows:] = jnp.transpose(conv_other).astype(jnp.bfloat16)
+
+
+def prompt_state_kernel(
+    offset, parts, place, inner, other, near, taps, taps_b, weights, b_turned, b_first, logs, tail,
+    *rest,
+):
+    outs, b_here = rest[:parts], rest[-1]
+    column, core = place[1], place[2]
+    group = 2 * column + core
+    first_own = core == 0
+    rows = inner.shape[0]
+    width = outs[0].shape[1]
+    heads = weights.shape[1]
+    features = heads * HEAD_WIDTH
+    part_width = features // parts
+    state = b_turned.shape[0]
+    w = weights[...].astype(jnp.bfloat16)
+    before = jnp.where(place[0] == 0, 0.0, near[...].astype(jnp.float32))
+    blank = jnp.zeros((TAIL - 3, STATE_WIDTH), jnp.float32)
+    lead_b = jnp.concatenate([blank, before[3 * parts : 3 * parts + 3, 0:STATE_WIDTH]], axis=0)
+    taps_here = taps_b[:, pl.ds(pl.multiple_of(group * STATE_WIDTH, STATE_WIDTH), STATE_WIDTH)]
+    fresh = conv_rows(taps_here, lead_b, b_first[...])
+    fresh = jnp.transpose(jnp.concatenate([fresh, jnp.zeros((128 - TAIL, state), jnp.float32)], axis=0))
+    lane = lax.broadcasted_iota(jnp.int32, fresh.shape, 1)
+    for index, first in enumerate((core == 0, core == 1)):
+        at = index * rows
+        old = b_turned[:, at : at + 128].astype(jnp.float32)
+        patched = jnp.where(lane < jnp.where(first, CONV - 1, 0), fresh, old)
+        b_here[:, at : at + 128] = patched.astype(jnp.bfloat16)
+        b_here[:, at + 128 : at + rows] = b_turned[:, at + 128 : at + rows]
+    blank = jnp.zeros((TAIL - 3, width), jnp.float32)
+    for turn in range(parts):
+        part = column ^ turn
+        start = part * part_width + offset
+        cols = pl.ds(pl.multiple_of(start, 128), width)
+        tap_cols = pl.ds(pl.multiple_of(group * features + start, 128), width)
+        spread = spread_heads(start // HEAD_WIDTH, heads, width).astype(jnp.bfloat16)
+        w_wide = contract(w, spread, ((1,), (0,)))
+        own_cols = pl.ds(pl.multiple_of(core * features + start, 128), width)
+        own_x, other_x = inner[:, own_cols], other[:, own_cols]
+        halo = before[0:3, offset : offset + width]
+        for index in range(1, parts):
+            at = before[3 * index : 3 * index + 3, offset : offset + width]
+            halo = jnp.where(part == index, at, halo)
+        halo = jnp.concatenate([blank, halo], axis=0)
+        own_last, other_last = own_x[rows - TAIL :], other_x[rows - TAIL :]
+        lead_own = jnp.where(first_own, halo, other_last.astype(jnp.float32))
+        lead_other = jnp.where(first_own, own_last.astype(jnp.float32), halo)
+        x_own = conv_rows(taps[:, tap_cols], lead_own, own_x) * w_wide[0:rows]
+        x_other = conv_rows(taps[:, tap_cols], lead_other, other_x) * w_wide[rows:]
+        mine = contract(b_here[:, 0:rows], x_own.astype(jnp.bfloat16), ((1,), (0,)))
+        theirs = contract(b_here[:, rows:], x_other.astype(jnp.bfloat16), ((1,), (0,)))
+        outs[turn][0:state] = (mine + theirs).astype(jnp.bfloat16)
+        outs[turn][state : state + TAIL] = logs[:, cols]
+        if outs[turn].shape[0] > state + TAIL:
+            for index in range(tail.shape[1] // width):
+                at = state + TAIL * (index + 1)
+                outs[turn][at : at + TAIL] = tail[:, index * width : (index + 1) * width]
+
+
+def pick_kernel(count, place, after, *refs):
+    held, (stays, goes), tails = refs[:count], refs[count : count + 2], refs[count + 2 :]
+    turn = place[0] ^ place[1]
+    rows, width = stays.shape[1:]
+    for index in range(count):
+
+        @pl.when(turn == index)
+        def _():
+            for step in range(0, count, 2):
+                stays[step // 2] = held[index ^ step][0:rows]
+                goes[step // 2] = held[index ^ (step + 1)][0:rows]
+            for tail in tails:
+                for piece in range(tail.shape[1] // width):
+                    at = rows + TAIL * piece
+                    tail[:, piece * width : (piece + 1) * width] = held[index][at : at + TAIL]
+
+
+def log_of(message, state):
+    rows = message[state:].astype(jnp.float32)
+    return rows[0:1] + rows[1:2] + rows[2:3]
+
+
+def merge_kernel(bit, place, own, came, *refs):
+    after, *outs = refs
+    state = own.shape[1] - TAIL
+    first = (place[0] >> bit) & 1 == 0
+    count = own.shape[0]
+    for index in range(count):
+        mine, theirs = own[index], came[index]
+        log_mine, log_theirs = log_of(mine, state), log_of(theirs, state)
+        mine_by = jnp.exp(jnp.where(first, log_theirs, 0.0))
+        theirs_by = jnp.exp(jnp.where(first, 0.0, log_mine))
+        joined = mine[0:state].astype(jnp.float32) * mine_by
+        joined = joined + theirs[0:state].astype(jnp.float32) * theirs_by
+        if len(outs) == 1:
+            outs[0][...] = joined.astype(jnp.bfloat16)
+            continue
+        out = outs[0] if index < count // 2 else outs[1]
+        at = index % (count // 2)
+        out[at, 0:state] = joined.astype(jnp.bfloat16)
+        total = log_mine + log_theirs
+        high = total.astype(jnp.bfloat16)
+        rest = total - high.astype(jnp.float32)
+        mid = rest.astype(jnp.bfloat16)
+        low = (rest - mid.astype(jnp.float32)).astype(jnp.bfloat16)
+        blank = jnp.zeros((TAIL - 3, total.shape[1]), jnp.float32)
+        parts = [part.astype(jnp.float32) for part in (high, mid, low)] + [blank]
+        out[at, state:] = jnp.concatenate(parts, axis=0).astype(jnp.bfloat16)
+
+
+def completion_kernel(
+    slot, piece, pieces, place, inner, gate, proj, tail, taps, taps_bc, step, decay, after, *refs
+):
+    if piece == 0:
+        fixed_out, factor_out, c_out, score_out, x_held, gate_held, bc_in, sems = refs
+    else:
+        _, _, score_in, fixed_out, factor_out, x_held, gate_held = refs
+    rows, features = fixed_out.shape
+    heads = step.shape[0] // pieces
+    first_head = piece * heads
+    half = rows // 2
+    own = place[3]
+    state = STATE_WIDTH
+    if piece == 0:
+        copies = [
+            pltpu.make_async_copy(
+                proj.at[slot, :, pl.ds(pl.multiple_of((own + skip) * state, state), state)],
+                bc_in.at[index],
+                sems.at[index],
+            )
+            for index, skip in enumerate((0, STATE_GROUPS))
+        ]
+        for copy in copies:
+            copy.start()
+    edges = tail[...].astype(jnp.float32)
+    pair_width = edges.shape[1]
+    blank = jnp.zeros((TAIL - 3, pair_width), jnp.float32)
+    row = lax.broadcasted_iota(jnp.int32, (rows, rows), 0)
+    col = lax.broadcasted_iota(jnp.int32, (rows, rows), 1)
+    dt = softplus(step[first_head : first_head + heads, slot])
+    every = heads * pieces
+    decay_row = jnp.broadcast_to(group_of(decay, own, every), (8, every))
+    decay_col = jnp.transpose(decay_row)[first_head : first_head + heads, 0:1]
+    before = (row <= col).astype(jnp.float32)
+    cum = contract(dt, before, ((1,), (0,)), HIGHEST) * (-LOG2E * jnp.exp(decay_col))
+    log_dt = jnp.log(dt) * LOG2E
+    base_rows = cum - log_dt
+    cum_cols = jnp.transpose(cum)
+    decay_cols = jnp.exp2(cum_cols).astype(jnp.bfloat16)
+    blocks = features // pair_width
+    for block in range(piece * blocks // pieces, (piece + 1) * blocks // pieces):
+        at = block * pair_width
+        cols = slice(at, at + pair_width)
+        lead = jnp.concatenate([blank, edges[3 * block : 3 * block + 3]], axis=0)
+        taps_here = taps[:, pl.ds(pl.multiple_of(own * features + at, pair_width), pair_width)]
+        x_held[:, cols] = conv_rows(taps_here, lead, inner[slot, :, cols]).astype(jnp.bfloat16)
+        silu_gate = half_silu(gate[slot, :, cols].astype(jnp.float32))
+        gate_held[:, cols] = silu_gate
+        spread = spread_heads(at // HEAD_WIDTH - first_head, heads, pair_width).astype(jnp.bfloat16)
+        decay_wide = contract(decay_cols, spread, ((1,), (0,)))
+        factor_out[:, cols] = (decay_wide * silu_gate).astype(jnp.bfloat16)
+    if piece == 0:
+        for copy in copies:
+            copy.wait()
+        lead_bc = jnp.concatenate([blank, edges[3 * blocks : 3 * blocks + 3]], axis=0)
+        bc = []
+        for index, skip in enumerate((0, STATE_GROUPS)):
+            taps_here = taps_bc[:, pl.ds(pl.multiple_of((own + skip) * state, state), state)]
+            lead = lead_bc[:, index * state : (index + 1) * state]
+            bc.append(conv_rows(taps_here, lead, bc_in[index]).astype(jnp.bfloat16))
+        c_out[...] = bc[1]
+        scores = contract(bc[1], bc[0], ((1,), (1,)))
+        scores = jnp.where(row >= col, scores, 0.0)
+        score_out[...] = scores
+    else:
+        scores = score_in[...]
+    low, high_left, high_right = scores[0:half, 0:half], scores[half:, 0:half], scores[half:, half:]
+    pair = 2 * HEAD_WIDTH
+    lane = lax.broadcasted_iota(jnp.int32, (rows, pair), 1)
+    for first in range(0, heads, 2):
+        at = (first_head + first) * HEAD_WIDTH
+        cols = slice(at, at + pair)
+        x_pair = x_held[:, cols]
+        zero = jnp.zeros_like(x_pair)
+        left = jnp.where(lane < HEAD_WIDTH, x_pair, zero)
+        right = jnp.where(lane < HEAD_WIDTH, zero, x_pair)
+        lows, highs = [], []
+        for h in (first, first + 1):
+            cc = cum_cols[:, h : h + 1]
+            rr, ll = base_rows[h : h + 1], log_dt[h : h + 1]
+            grown = jnp.minimum(cc[0:half] - rr[:, 0:half], ll[:, 0:half])
+            lows.append((low * jnp.exp2(grown)).astype(jnp.bfloat16))
+            grown = jnp.minimum(cc[half:] - rr[:, 0:half], ll[:, 0:half])
+            highs.append((high_left * jnp.exp2(grown)).astype(jnp.bfloat16))
+            grown = jnp.minimum(cc[half:] - rr[:, half:], ll[:, half:])
+            highs.append((high_right * jnp.exp2(grown)).astype(jnp.bfloat16))
+        y_low = contract(
+            jnp.concatenate(lows, axis=1),
+            jnp.concatenate([left[0:half], right[0:half]], axis=0),
+            ((1,), (0,)),
+        )
+        y_high = contract(
+            jnp.concatenate(highs, axis=1), jnp.concatenate([left, right], axis=0), ((1,), (0,))
+        )
+        fixed_out[0:half, cols] = (y_low * gate_held[0:half, cols]).astype(jnp.bfloat16)
+        fixed_out[half:, cols] = (y_high * gate_held[half:, cols]).astype(jnp.bfloat16)
+
+
+def read_slot(parts, offset, column, slot, states, own_work, gated, slot_at):
+    c_ref, fixed, factor = own_work[3 * slot : 3 * slot + 3]
+    rows, features = fixed.shape
+    part_width = features // parts
+    width = states[0].shape[1]
+    c = c_ref[...]
+    total = jnp.zeros((rows, 128), jnp.float32)
+    for step in range(parts):
+        start = (column ^ step) * part_width + offset
+        cols = pl.ds(pl.multiple_of(start, 128), width)
+        read = contract(c, states[step][...], ((1,), (0,)))
+        weight = factor[:, cols].astype(jnp.float32)
+        value = fixed[:, cols].astype(jnp.float32) + read * weight
+        gated[slot_at, step] = value
+        square = value * value
+        for lanes in range(0, width, 128):
+            total = total + square[:, lanes : lanes + 128]
+    return total
+
+
+def read_kernel(parts, offset, slots, place, *refs):
+    states, own_work, (gated, squares) = refs[:parts], refs[parts:-2], refs[-2:]
+    for slot in range(slots):
+        squares[slot] = read_slot(parts, offset, place[1], slot, states, own_work, gated, slot)
+
+
+def finish_kernel(parts, offsets, slots, place, live, gain, *refs):
+    chunks = len(offsets)
+    inputs, (out, gated, held, sems) = refs[:-4], refs[-4:]
+    earlier, inputs = inputs[: 2 * (chunks - 1)], inputs[2 * (chunks - 1) :]
+    states, own_work = inputs[:parts], inputs[parts:]
+    column = place[1]
+    slots, rows, features = held.shape
+    part_width = features // parts
+    copies = []
+    for slot in range(slots):
+        total = read_slot(parts, offsets[-1], column, slot, states, own_work, gated, 0)
+        for chunk in range(chunks - 1):
+            total = total + earlier[2 * chunk + 1][slot]
+        scale = lax.rsqrt(jnp.sum(total, axis=1, keepdims=True) / features + EPS)
+        alive = lax.broadcasted_iota(jnp.int32, (rows, 1), 0) < live[slot]
+        scale = jnp.where(alive, scale, 0.0)
+        for step in range(parts):
+            for chunk, offset in enumerate(offsets):
+                last = chunk + 1 == chunks
+                values = gated if last else earlier[2 * chunk]
+                width = values.shape[-1]
+                start = (column ^ step) * part_width + offset
+                cols = pl.ds(pl.multiple_of(start, 128), width)
+                gain_here = jnp.reshape(gain[cols], (1, width))
+                value = values[0 if last else slot, step]
+                held[slot, :, cols] = (value * scale * gain_here).astype(jnp.bfloat16)
+            part = pl.ds(pl.multiple_of((column ^ step) * part_width, part_width), part_width)
+            copies.append(
+                pltpu.make_async_copy(
+                    held.at[slot, :, part], out.at[slot, :, part], sems.at[slot * parts + step]
+                )
+            )
+            copies[-1].start()
+    for copy in copies:
+        copy.wait()
+
+
+LASTS = dict(
+    pack=2, prompt_weights=2, prompt_state=3, pick=1, merge=1, completion=4, read=2, finish=2
+)
+
+
+def matched(
+    prompt_inner,
+    prompt_proj,
+    prompt_step,
+    completion_inner,
+    completion_gate,
+    completion_projections,
+    sample_step,
+    sample_length,
+    decay_log,
+    conv_inner,
+    conv_proj,
+    norm_gain,
+):
+    parts = lax.axis_size("comp")
+    row, column = lax.axis_index("prompt"), lax.axis_index("comp")
+    plane, core = row // 2, row % 2
+    group = 2 * column + core
+    rows = prompt_inner.shape[0]
+    heads = sample_step.shape[0]
+    features = heads * HEAD_WIDTH
+    place = jnp.stack([plane, column, core, row]).astype(jnp.int32)
+    bf16, f32 = jnp.bfloat16, jnp.float32
+
+    def take(array, start, size, axis):
+        return lax.dynamic_slice_in_dim(array, start, size, axis)
+
+    planes = lax.axis_size("prompt") // 2
+    pair_width = 2 * STATE_WIDTH
+    edge = jax.ShapeDtypeStruct((TAIL, pair_width), bf16)
+    held_inner = pltpu.with_memory_space_constraint(prompt_inner, pltpu.HBM)
+    held_proj = pltpu.with_memory_space_constraint(prompt_proj, pltpu.HBM)
+    held_step = pltpu.with_memory_space_constraint(prompt_step, pltpu.HBM)
+
+    swap, edge_1, own_b = run_whole(
+        pack_kernel,
+        "pack",
+        (place,),
+        (
+            jax.ShapeDtypeStruct((rows + TAIL, pair_width), bf16),
+            edge,
+            jax.ShapeDtypeStruct((rows, STATE_WIDTH), bf16),
+        ),
+        (held_inner, held_proj, held_step),
+        spaces=[pltpu.HBM] * 3,
+        scratch=[
+            pltpu.VMEM((heads, rows), f32),
+            pltpu.VMEM((TAIL, 2 * features), bf16),
+            pltpu.VMEM((TAIL, pair_width), bf16),
+            pltpu.VMEM((TAIL, pair_width), bf16),
+            pltpu.SemaphoreType.DMA((6,)),
+        ],
+    )
+    trade = lambda z, k, c: (z, 1 - k, c)
+    other = routed(swap, trade)
+    other_inner = routed(prompt_inner, trade)
+    edges = jnp.where(core == 0, other[rows:], edge_1)
+    near = routed(edges, lambda z, k, c: (z + 1, k, c) if z + 1 < planes else None)
+    far = routed(edges, lambda z, k, c: (c, k, c) if z + 1 == planes else None)
+    weights, b_turned, logs, b_first = run_whole(
+        prompt_weights_kernel,
+        "prompt_weights",
+        (place,),
+        (
+            jax.ShapeDtypeStruct((2 * rows, heads), f32),
+            jax.ShapeDtypeStruct((STATE_WIDTH, 2 * rows), bf16),
+            jax.ShapeDtypeStruct((TAIL, features), bf16),
+            jax.ShapeDtypeStruct((TAIL, STATE_WIDTH), bf16),
+        ),
+        (own_b, other, conv_proj, prompt_step, decay_log),
+    )
+    unit = features // parts // sum(CHUNKS)
+    widths = [unit * size for size in CHUNKS]
+    offsets = [sum(widths[:chunk]) for chunk in range(len(widths))]
+    picks = []
+    for chunk, width in enumerate(widths):
+        message = jax.ShapeDtypeStruct((STATE_WIDTH + TAIL, width), bf16)
+        with_tail = chunk == 0
+        tail_rows = TAIL * (pair_width // width) if with_tail else 0
+        spread = jax.ShapeDtypeStruct((STATE_WIDTH + TAIL + tail_rows, width), bf16)
+        sent = run_whole(
+            lambda *refs, offset=offsets[chunk]: prompt_state_kernel(offset, parts, *refs),
+            "prompt_state",
+            (place,),
+            (spread,) * parts,
+            (
+                prompt_inner, other_inner, near, conv_inner, conv_proj, weights, b_turned, b_first,
+                logs, far,
+            ),
+            scratch=[pltpu.VMEM((STATE_WIDTH, 2 * rows), bf16)],
+        )
+        held = [sent[0]] + [
+            routed(sent[step], lambda z, k, c: (z, k, c ^ step)) for step in range(1, parts)
+        ]
+        two = jax.ShapeDtypeStruct((parts // 2,) + message.shape, bf16)
+        picks.append(
+            lambda after, held=held, two=two, with_tail=with_tail: run_whole(
+                lambda *refs: pick_kernel(parts, *refs),
+                "pick",
+                (place,),
+                (two, two) + (edge,) * with_tail,
+                [after] + held,
+                spaces=[pl.ANY] + [pltpu.VMEM] * parts,
+            )
+        )
+
+    slots, positions = completion_inner.shape[:2]
+    held_projections = pltpu.with_memory_space_constraint(completion_projections, pltpu.HBM)
+    wide = jax.ShapeDtypeStruct((positions, features), bf16)
+    pieces = PIECES
+
+    def completion(slot, piece, after, begun):
+        outs = (wide, wide)
+        scratch = [pltpu.VMEM((positions, features), bf16), pltpu.VMEM((positions, features), f32)]
+        operands = [
+            completion_inner, completion_gate, held_projections, tail, conv_inner, conv_proj,
+            sample_step, decay_log, after,
+        ]
+        if piece == 0:
+            outs += (
+                jax.ShapeDtypeStruct((positions, STATE_WIDTH), bf16),
+                jax.ShapeDtypeStruct((positions, positions), f32),
+            )
+            scratch += [
+                pltpu.VMEM((2, positions, STATE_WIDTH), bf16), pltpu.SemaphoreType.DMA((2,)),
+            ]
+            aliases = None
+        else:
+            fixed, factor, c, scores = begun
+            aliases = {len(operands) + 1: 0, len(operands) + 2: 1}
+            operands += [fixed, factor, scores]
+        results = run_whole(
+            lambda *refs: completion_kernel(slot, piece, pieces, *refs),
+            "completion",
+            (place,),
+            outs,
+            operands,
+            spaces=[pltpu.VMEM] * 2
+            + [pltpu.HBM]
+            + [pltpu.VMEM] * 5
+            + [pl.ANY]
+            + [pltpu.VMEM] * (len(operands) - 9),
+            scratch=scratch,
+            aliases=aliases,
+        )
+        return results if piece == 0 else results + tuple(begun[2:])
+
+    def merge(bit, own, came, shapes, after):
+        return run_whole(
+            lambda *refs: merge_kernel(bit, *refs),
+            "merge",
+            (place,),
+            shapes,
+            (own, came, after),
+            spaces=[pltpu.VMEM] * 2 + [pl.ANY],
+        )
+
+    def gather(state):
+        return [state] + [
+            routed(state, lambda z, k, c: (z, k, c ^ step)) for step in range(1, parts)
+        ]
+
+    work = [(slot, piece) for slot in range(slots) for piece in range(pieces)]
+    begun = {}
+
+    def do_work(after):
+        if not work:
+            return after
+        slot, piece = work.pop(0)
+        begun[slot] = completion(slot, piece, after, begun.get(slot))
+        return begun[slot][1]
+
+    stays, goes, merged, joined = [], [], [], []
+    near_plane = lambda z, k, c: (z ^ 1, k, c)
+    far_plane = lambda z, k, c: (z ^ 2, k, c)
+    tail, after = None, place
+    for chunk in range(len(widths)):
+        stay, go, *maybe = picks[chunk](after)
+        tail = maybe[0] if maybe else tail
+        stays.append(stay)
+        goes.append(routed(go, near_plane))
+        if chunk + 1 < len(widths):
+            after = do_work(go)
+    after = go
+    for chunk, width in enumerate(widths):
+        one = jax.ShapeDtypeStruct((1, STATE_WIDTH + TAIL, width), bf16)
+        stay, go = merge(0, stays[chunk], goes[chunk], (one, one), after)
+        merged.append((stay, routed(go, far_plane)))
+        after = do_work(go) if chunk + 1 < len(widths) else go
+    for chunk, width in enumerate(widths):
+        state = jax.ShapeDtypeStruct((STATE_WIDTH, width), bf16)
+        joined.append(gather(merge(1, *merged[chunk], state, after)))
+        after = do_work(joined[-1][0])
+    while work:
+        after = do_work(after)
+    finished = [begun[slot][:3] for slot in range(slots)]
+    own_work = [array for fixed, factor, c in finished for array in (c, fixed, factor)]
+    earlier = []
+    for chunk, width in enumerate(widths[:-1]):
+        earlier += run_whole(
+            lambda *refs, offset=offsets[chunk]: read_kernel(parts, offset, slots, *refs),
+            "read",
+            (place,),
+            (
+                jax.ShapeDtypeStruct((slots, parts, positions, width), f32),
+                jax.ShapeDtypeStruct((slots, positions, 128), f32),
+            ),
+            joined[chunk] + own_work,
+        )
+    return run_whole(
+        lambda *refs: finish_kernel(parts, offsets, slots, *refs),
+        "finish",
+        (place, sample_length),
+        jax.ShapeDtypeStruct((slots, positions, features), bf16),
+        [norm_gain] + earlier + joined[-1] + own_work,
+        out_spaces=pltpu.HBM,
+        scratch=[
+            pltpu.VMEM((1, parts, positions, widths[-1]), f32),
+            pltpu.VMEM((slots, positions, features), bf16),
+            pltpu.SemaphoreType.DMA((slots * parts,)),
+        ],
+    )
+
+
+def run_whole(
+    kernel, name, place, out_shape, operands, scratch=(), spaces=None, out_spaces=None, aliases=None
+):
+    vmem = pltpu.VMEM
+    spaces = spaces or [vmem] * len(operands)
+    out_spaces = out_spaces or jax.tree.map(lambda _: vmem, out_shape)
+    return pl.pallas_call(
+        kernel,
+        out_shape=out_shape,
+        in_specs=[pl.BlockSpec(memory_space=pltpu.SMEM)] * len(place)
+        + [pl.BlockSpec(memory_space=space) for space in spaces],
+        out_specs=jax.tree.map(lambda space: pl.BlockSpec(memory_space=space), out_spaces),
+        scratch_shapes=scratch,
+        input_output_aliases=aliases or {},
+        compiler_params=pltpu.CompilerParams(vmem_limit_bytes=VMEM_BYTES),
+        cost_estimate=pl.CostEstimate(
+            flops=LASTS[name] * 10**9, transcendentals=0, bytes_accessed=LASTS[name] * 3 * 10**6
+        ),
+        name=name,
+    )(*place, *operands)
+
+
+def local(*arrays):
+    columns, prompts = lax.axis_size("comp"), lax.axis_size("prompt")
+    heads_col, heads_row = arrays[2].shape[0], arrays[6].shape[0]
+    one_group = heads_row == STATE_HEADS // STATE_GROUPS and heads_col == 2 * heads_row
+    if one_group and prompts == 2 * columns and columns & (columns - 1) == 0:
+        return matched(*arrays)
+    return any_shape(*arrays)
+
+
 def solution(mesh):
     placed = (
         P("prompt", "comp"),

time: 469 us -> 64.9 us (0.14)
  waiting for transfers between devices: 191 us -> 9.98 us
  other arithmetic: 126 us -> 0.08 us
  local copies, waits for them, and re-layouts: 63 us -> 0.05 us
  blocking collectives: 44.5 us -> 0 us
  Pallas kernels: 0 us -> 27.8 us
  matrix products: 19.6 us -> 0 us
  starting transfers between devices: 7.83 us -> 26.4 us
  between operations: 14.3 us -> 0.41 us
    psum x2 -> x0, waiting for transfers between devices: 97.4 us -> none  [from_root(): return lax.psum(jnp.where(mine, array, jnp.zeros_like(array)), axis)]
    all_gather x1 -> x0, waiting for transfers between devices: 93.9 us -> none  [carried_in(): lax.all_gather(part.astype(kind), axis)]
    select_n x14 -> x1, other arithmetic: 55.9 us -> 0.01 us  [matched(): edges = jnp.where(core == 0, other[rows:], edge_1)]
    convert_element_type x16 -> x0, other arithmetic: 45.5 us -> none  [the longest x4 21.2 us: causal_conv(): return jax.nn.silu(summed).astype(jnp.bfloat16)]
    unnamed x1 -> x0, blocking collectives: 28.2 us -> none
    pallas_call x0 -> x14, Pallas kernels: none -> 27.8 us  [run_whole(): pl.pallas_call(kernel, out_shape=out_shape, in_specs=[pl.BlockSpec(memory...]
    unnamed x51 -> x20, local copies, waits for them, and re-layouts: 19.9 us -> 0.05 us
    dot_general x17 -> x0, matrix products: 19.6 us -> none  [the longest x4 5.99 us: block_scan(): jnp.einsum('ign,gkdn->igkd', c_blk.astype(jnp.float32), state_in, precisi...]
  transfers between devices with their start and end apart: 5 -> 20, of which waited for: 3 -> 6; matrix products, arithmetic and copies ran while one was open for 14% -> 0% of each run, Pallas kernels for 0% -> 35%
where the time goes in v3:
time: 64.9 us; the launch traced here: 64.7 us
  Pallas kernels  27.8 us (43%)
  starting transfers between devices  26.4 us (41%)
  waiting for transfers between devices  9.98 us (15%)
    pallas_call x14, Pallas kernels, run_whole(): pl.pallas_call(kernel, out_shape=out_shape, in_specs=[pl.BlockSpec(memory...  27.8 us
    ppermute x20, starting transfers between devices, routed(): return lax.ppermute(block, AXES, pairs)  26.4 us
    ppermute x20, waiting for transfers between devices, routed(): return lax.ppermute(block, AXES, pairs)  9.98 us
  transfers between devices with their start and end apart: 20, of which 6 were waited for; matrix products, arithmetic and copies ran while one was open for 0% of the time, Pallas kernels for 35%

profile of v3, /device:TPU:0, one launch (start us, length us, event | category | flops | bytes accessed | tf_op | source)
XLA Modules:
  0.0 64.7 jit_solution(15032500483528202898)
XLA Ops:
  0.5 1.9 %pack.1 = (bf16[272,512]{1,0:T(8,128)(2,1)S(1)}, bf16[16,512]{1,0:T(8,128)(2,1)S(1)}, bf16[256,256]{1,0:T(8,128)(2,1)S(1)}) custom-call(s32[4]{0:T(128)S(1)} %pad_add_fusion.place.refs_0_.refs_1_, bf16[256,4096]{1,0:T(8,128)(2,1)} %refs_1_.7, bf16[256,4096]{1,0:T(8,128)(2,1)} %proj.1, f32[64,256]{1,0:T(8,128)} %step.3), custom_call_target="tpu_custom_call" | custom-call | flops 2000000000 | bytes 6000000 | tf_op jit(solution)/shard_map/pack/pallas_call | solution.py:907
  2.6 2.1 %collective-permute-done.1.other = bf16[272,512]{1,0:T(8,128)(2,1)S(1)} collective-permute-done((bf16[272,512]{1,0:T(8,128)(2,1)S(1)}, bf16[272,512]{1,0:T(8,128)(2,1)S(1)}, u32[]{:S(2)}, u32[]{:S(2)}) %collective-permute-start.1) | collective-permute-done | bytes 278560 | tf_op jit(solution)/shard_map/ppermute | solution.py:269
  4.6 1.3 %collective-permute-start.3 = (bf16[16,512]{1,0:T(8,128)(2,1)S(1)}, bf16[16,512]{1,0:T(8,128)(2,1)S(1)}, u32[]{:S(2)}, u32[]{:S(2)}) collective-permute-start(bf16[16,512]{1,0:T(8,128)(2,1)S(1)} %slice_select_fusion), channel_id=1, source_target_pairs={{24,0},{25,9},{26,18},{27,27},{28,4},{29,13},{30,22},{31,31}} | collective-permute-start | bytes 49160 | tf_op jit(solution)/shard_map/ppermute | solution.py:269
  5.9 4.2 %collective-permute-start.2 = (bf16[16,512]{1,0:T(8,128)(2,1)S(1)}, bf16[16,512]{1,0:T(8,128)(2,1)S(1)}, u32[]{:S(2)}, u32[]{:S(2)}) collective-permute-start(bf16[16,512]{1,0:T(8,128)(2,1)S(1)} %slice_select_fusion), channel_id=1, source_target_pairs={{0,8},{1,9},{2,10},{3,11},{4,12},{5,13},{6,14},{7,15},{8,16},{9,17... | collective-permute-start | bytes 49160 | tf_op jit(solution)/shard_map/ppermute | solution.py:269
  10.2 1.6 %prompt_weights.1 = (f32[512,32]{1,0:T(8,128)S(1)}, bf16[256,512]{1,0:T(8,128)(2,1)S(1)}, bf16[16,2048]{1,0:T(8,128)(2,1)S(1)}, bf16[16,256]{1,0:T(8,128)(2,1)S(1)}) custom-call(s32[4]{0:T(128)S(1)} %pad_add_fusion.place.refs_0_.refs_1_, bf16[256,256]{1,0:T(8,128)(2,1)S(1)} %get-tuple-element.39.own, bf16[272,512]{1,0:T(8,128)(2,1)S(1)} %collective-permute-done.1.other, ...), custom_call_target="tpu_custom_call" | custom-call | flops 2000000000 | bytes 6000000 | tf_op jit(solution)/shard_map/prompt_weights/pallas_call | solution.py:907
  12.6 2.5 %prompt_state.2 = (bf16[304,256]{1,0:T(8,128)(2,1)S(1)}, bf16[304,256]{1,0:T(8,128)(2,1)S(1)}, bf16[304,256]{1,0:T(8,128)(2,1)S(1)}, bf16[304,256]{1,0:T(8,128)(2,1)S(1)}) custom-call(s32[4]{0:T(128)S(1)} %pad_add_fusion.place.refs_0_.refs_1_, bf16[256,4096]{1,0:T(8,128)(2,1)S(1)} %copy-done.2, bf16[256,4096]{1,0:T(8,128)(2,1)S(1)} %collective-permute-done.refs_2_, ...), custom_call_target="tpu_custom_call" | custom-call | flops 3000000000 | bytes 9000000 | tf_op jit(solution)/shard_map/prompt_state/pallas_call | solution.py:907
  15.1 1.4 %collective-permute-start.4 = (bf16[304,256]{1,0:T(8,128)(2,1)S(1)}, bf16[304,256]{1,0:T(8,128)(2,1)S(1)}, u32[]{:S(2)}, u32[]{:S(2)}) collective-permute-start(bf16[304,256]{1,0:T(8,128)(2,1)S(1)} %get-tuple-element.45), channel_id=1, source_target_pairs={{0,1},{1,0},{2,3},{3,2},{4,5},{5,4},{6,7},{7,6},{8,9},{9,8},{10,11... | collective-permute-start | bytes 466952 | tf_op jit(solution)/shard_map/ppermute | solution.py:269
  17.5 1.2 %collective-permute-start.6 = (bf16[304,256]{1,0:T(8,128)(2,1)S(1)}, bf16[304,256]{1,0:T(8,128)(2,1)S(1)}, u32[]{:S(2)}, u32[]{:S(2)}) collective-permute-start(bf16[304,256]{1,0:T(8,128)(2,1)S(1)} %get-tuple-element.47), channel_id=1, source_target_pairs={{0,3},{1,2},{2,1},{3,0},{4,7},{5,6},{6,5},{7,4},{8,11},{9,10},{10,... | collective-permute-start | bytes 466952 | tf_op jit(solution)/shard_map/ppermute | solution.py:269
  18.7 2.5 %prompt_state.3 = (bf16[272,256]{1,0:T(8,128)(2,1)S(1)}, bf16[272,256]{1,0:T(8,128)(2,1)S(1)}, bf16[272,256]{1,0:T(8,128)(2,1)S(1)}, bf16[272,256]{1,0:T(8,128)(2,1)S(1)}) custom-call(s32[4]{0:T(128)S(1)} %pad_add_fusion.place.refs_0_.refs_1_, bf16[256,4096]{1,0:T(8,128)(2,1)S(1)} %copy-done.2, bf16[256,4096]{1,0:T(8,128)(2,1)S(1)} %collective-permute-done.refs_2_, ...), custom_call_target="tpu_custom_call" | custom-call | flops 3000000000 | bytes 9000000 | tf_op jit(solution)/shard_map/prompt_state/pallas_call | solution.py:907
  21.2 1.4 %collective-permute-start.8 = (bf16[272,256]{1,0:T(8,128)(2,1)S(1)}, bf16[272,256]{1,0:T(8,128)(2,1)S(1)}, u32[]{:S(2)}, u32[]{:S(2)}) collective-permute-start(bf16[272,256]{1,0:T(8,128)(2,1)S(1)} %get-tuple-element.53), channel_id=1, source_target_pairs={{0,1},{1,0},{2,3},{3,2},{4,5},{5,4},{6,7},{7,6},{8,9},{9,8},{10,11... | collective-permute-start | bytes 417800 | tf_op jit(solution)/shard_map/ppermute | solution.py:269
  23.5 1.2 %collective-permute-start.10 = (bf16[272,256]{1,0:T(8,128)(2,1)S(1)}, bf16[272,256]{1,0:T(8,128)(2,1)S(1)}, u32[]{:S(2)}, u32[]{:S(2)}) collective-permute-start(bf16[272,256]{1,0:T(8,128)(2,1)S(1)} %get-tuple-element.55), channel_id=1, source_target_pairs={{0,3},{1,2},{2,1},{3,0},{4,7},{5,6},{6,5},{7,4},{8,11},{9,10},{10,... | collective-permute-start | bytes 417800 | tf_op jit(solution)/shard_map/ppermute | solution.py:269
  24.8 1.2 %collective-permute-done.5.refs_4_ = bf16[304,256]{1,0:T(8,128)(2,1)S(1)} collective-permute-done((bf16[304,256]{1,0:T(8,128)(2,1)S(1)}, bf16[304,256]{1,0:T(8,128)(2,1)S(1)}, u32[]{:S(2)}, u32[]{:S(2)}) %collective-permute-start.5) | collective-permute-done | bytes 155680 | tf_op jit(solution)/shard_map/ppermute | solution.py:269
  26.6 1.9 %collective-permute-start.7 = (bf16[2,272,256]{2,1,0:T(8,128)(2,1)S(1)}, bf16[2,272,256]{2,1,0:T(8,128)(2,1)S(1)}, u32[]{:S(2)}, u32[]{:S(2)}) collective-permute-start(bf16[2,272,256]{2,1,0:T(8,128)(2,1)S(1)} %get-tuple-element.49.refs_9_), channel_id=1, source_target_pairs={{0,8},{1,9},{2,10},{3,11},{4,12},{5,13},{6,14},{7,15},{8,0},{9,1},... | collective-permute-start | bytes 835592 | tf_op jit(solution)/shard_map/ppermute | solution.py:269
  28.6 5.7 %completion.2 = (bf16[256,2048]{1,0:T(8,128)(2,1)S(1)}, bf16[256,2048]{1,0:T(8,128)(2,1)S(1)}, bf16[256,256]{1,0:T(8,128)(2,1)S(1)}, f32[256,256]{1,0:T(8,128)}) custom-call(s32[4]{0:T(128)S(1)} %pad_add_fusion.place.refs_0_.refs_1_, bf16[2,256,2048]{2,1,0:T(8,128)(2,1)S(1)} %copy-done.3, bf16[2,256,2048]{2,1,0:T(8,128)(2,1)S(1)} %copy-done.4, ...), custom_call_target="tpu_custom_call" | custom-call | flops 4000000000 | bytes 12000000 | tf_op jit(solution)/shard_map/completion/pallas_call | solution.py:907
  36.0 3.9 %collective-permute-start.11 = (bf16[1,272,256]{2,1,0:T(8,128)(2,1)S(1)}, bf16[1,272,256]{2,1,0:T(8,128)(2,1)S(1)}, u32[]{:S(2)}, u32[]{:S(2)}) collective-permute-start(bf16[1,272,256]{2,1,0:T(8,128)(2,1)S(1)} %get-tuple-element.58.refs_9_), channel_id=1, source_target_pairs={{0,16},{1,17},{2,18},{3,19},{4,20},{5,21},{6,22},{7,23},{8,24},{9,... | collective-permute-start | bytes 417800 | tf_op jit(solution)/shard_map/ppermute | solution.py:269
  39.9 5.7 %completion.3 = (bf16[256,2048]{1,0:T(8,128)(2,1)S(1)}, bf16[256,2048]{1,0:T(8,128)(2,1)S(1)}, bf16[256,256]{1,0:T(8,128)(2,1)S(1)}, f32[256,256]{1,0:T(8,128)}) custom-call(s32[4]{0:T(128)S(1)} %pad_add_fusion.place.refs_0_.refs_1_, bf16[2,256,2048]{2,1,0:T(8,128)(2,1)S(1)} %copy-done.3, bf16[2,256,2048]{2,1,0:T(8,128)(2,1)S(1)} %copy-done.4, ...), custom_call_target="tpu_custom_call" | custom-call | flops 4000000000 | bytes 12000000 | tf_op jit(solution)/shard_map/completion/pallas_call | solution.py:907
  47.0 1.4 %collective-permute-start.15 = (bf16[256,256]{1,0:T(8,128)(2,1)S(1)}, bf16[256,256]{1,0:T(8,128)(2,1)S(1)}, u32[]{:S(2)}, u32[]{:S(2)}) collective-permute-start(bf16[256,256]{1,0:T(8,128)(2,1)S(1)} %merge.6.refs_1_.refs_3_), channel_id=1, source_target_pairs={{0,3},{1,2},{2,1},{3,0},{4,7},{5,6},{6,5},{7,4},{8,11},{9,10},{10,... | collective-permute-start | bytes 393224 | tf_op jit(solution)/shard_map/ppermute | solution.py:269
  48.9 1.7 %collective-permute-start.13 = (bf16[256,256]{1,0:T(8,128)(2,1)S(1)}, bf16[256,256]{1,0:T(8,128)(2,1)S(1)}, u32[]{:S(2)}, u32[]{:S(2)}) collective-permute-start(bf16[256,256]{1,0:T(8,128)(2,1)S(1)} %merge.6.refs_1_.refs_3_), channel_id=1, source_target_pairs={{0,1},{1,0},{2,3},{3,2},{4,5},{5,4},{6,7},{7,6},{8,9},{9,8},{10,11... | collective-permute-start | bytes 393224 | tf_op jit(solution)/shard_map/ppermute | solution.py:269
  50.6 3.3 %collective-permute-done.16.refs_2_ = bf16[1,272,256]{2,1,0:T(8,128)(2,1)S(1)} collective-permute-done((bf16[1,272,256]{2,1,0:T(8,128)(2,1)S(1)}, bf16[1,272,256]{2,1,0:T(8,128)(2,1)S(1)}, u32[]{:S(2)}, u32[]{:S(2)}) %collective-permute-start.16) | collective-permute-done | bytes 139296 | tf_op jit(solution)/shard_map/ppermute | solution.py:269
  54.4 1.4 %collective-permute-start.19 = (bf16[256,256]{1,0:T(8,128)(2,1)S(1)}, bf16[256,256]{1,0:T(8,128)(2,1)S(1)}, u32[]{:S(2)}, u32[]{:S(2)}) collective-permute-start(bf16[256,256]{1,0:T(8,128)(2,1)S(1)} %merge.7.refs_5_), channel_id=1, source_target_pairs={{0,3},{1,2},{2,1},{3,0},{4,7},{5,6},{6,5},{7,4},{8,11},{9,10},{10,... | collective-permute-start | bytes 393224 | tf_op jit(solution)/shard_map/ppermute | solution.py:269
  55.8 2.2 %collective-permute-start.17 = (bf16[256,256]{1,0:T(8,128)(2,1)S(1)}, bf16[256,256]{1,0:T(8,128)(2,1)S(1)}, u32[]{:S(2)}, u32[]{:S(2)}) collective-permute-start(bf16[256,256]{1,0:T(8,128)(2,1)S(1)} %merge.7.refs_5_), channel_id=1, source_target_pairs={{0,1},{1,0},{2,3},{3,2},{4,5},{5,4},{6,7},{7,6},{8,9},{9,8},{10,11... | collective-permute-start | bytes 393224 | tf_op jit(solution)/shard_map/ppermute | solution.py:269
  59.2 1.3 %collective-permute-done.19.refs_8_ = bf16[256,256]{1,0:T(8,128)(2,1)S(1)} collective-permute-done((bf16[256,256]{1,0:T(8,128)(2,1)S(1)}, bf16[256,256]{1,0:T(8,128)(2,1)S(1)}, u32[]{:S(2)}, u32[]{:S(2)}) %collective-permute-start.19) | collective-permute-done | bytes 131104 | tf_op jit(solution)/shard_map/ppermute | solution.py:269
  60.5 1.3 %collective-permute-done.18.refs_7_ = bf16[256,256]{1,0:T(8,128)(2,1)S(1)} collective-permute-done((bf16[256,256]{1,0:T(8,128)(2,1)S(1)}, bf16[256,256]{1,0:T(8,128)(2,1)S(1)}, u32[]{:S(2)}, u32[]{:S(2)}) %collective-permute-start.18) | collective-permute-done | bytes 131104 | tf_op jit(solution)/shard_map/ppermute | solution.py:269
  61.8 2.8 %finish.1 = bf16[2,256,2048]{2,1,0:T(8,128)(2,1)} custom-call(s32[4]{0:T(128)S(1)} %pad_add_fusion.place.refs_0_.refs_1_, s32[2]{0:T(128)S(1)} %copy-done.1, f32[2048]{0:T(1024)S(1)} %copy-done, f32[2,4,256,256]{3,2,1,0:T(8,128)S(1)} %get-tuple-element.66.refs_3_, f32[2,256,128]{2,1,0:T(8,128)S(1)} %get-tuple-element.67.refs_4_, ...), custom_call_target="tpu_custom_call" | custom-call | flops 2000000000 | bytes 6000000 | tf_op jit(solution)/shard_map/finish/pallas_call | solution.py:907
  (52 shorter events, 9.2 us)
Async XLA Ops:
  0.0 12.6 %collective-permute-start = (bf16[256,4096]{1,0:T(8,128)(2,1)}, bf16[256,4096]{1,0:T(8,128)(2,1)S(1)}, u32[]{:S(2)}, u32[]{:S(2)}) collective-permute-start(bf16[256,4096]{1,0:T(8,128)(2,1)} %refs_1_.7), channel_id=1, source_target_pairs={{0,4},{1,5},{2,6},{3,7},{4,0},{5,1},{6,2},{7,3},{8,12},{9,13},{10,... | collective-permute-start | bytes 6291464 | tf_op jit(solution)/shard_map/ppermute | solution.py:269
  0.5 9.6 %copy-start.6 = (f32[64,256]{1,0:T(8,128)S(1)}, f32[64,256]{1,0:T(8,128)}, u32[]{:S(2)}) copy-start(f32[64,256]{1,0:T(8,128)} %step.3) | copy-start | bytes 196612
  0.5 9.6 %copy-start.8 = (bf16[4,4096]{1,0:T(4,128)(2,1)S(1)}, bf16[4,4096]{1,0:T(4,128)(2,1)}, u32[]{:S(2)}) copy-start(bf16[4,4096]{1,0:T(4,128)(2,1)} %refs_6_.3) | copy-start | bytes 98308
  0.5 9.6 %copy-start.9 = (f32[256]{0:T(256)S(1)}, f32[256]{0:T(256)}, u32[]{:S(2)}) copy-start(f32[256]{0:T(256)} %refs_8_.3) | copy-start | bytes 3076
  2.5 2.2 %collective-permute-start.1 = (bf16[272,512]{1,0:T(8,128)(2,1)S(1)}, bf16[272,512]{1,0:T(8,128)(2,1)S(1)}, u32[]{:S(2)}, u32[]{:S(2)}) collective-permute-start(bf16[272,512]{1,0:T(8,128)(2,1)S(1)} %get-tuple-element.37), channel_id=1, source_target_pairs={{0,4},{1,5},{2,6},{3,7},{4,0},{5,1},{6,2},{7,3},{8,12},{9,13},{10,... | collective-permute-start | bytes 835592 | tf_op jit(solution)/shard_map/ppermute | solution.py:269
  4.6 8.0 %collective-permute-start.3 = (bf16[16,512]{1,0:T(8,128)(2,1)S(1)}, bf16[16,512]{1,0:T(8,128)(2,1)S(1)}, u32[]{:S(2)}, u32[]{:S(2)}) collective-permute-start(bf16[16,512]{1,0:T(8,128)(2,1)S(1)} %slice_select_fusion), channel_id=1, source_target_pairs={{24,0},{25,9},{26,18},{27,27},{28,4},{29,13},{30,22},{31,31}} | collective-permute-start | bytes 49160 | tf_op jit(solution)/shard_map/ppermute | solution.py:269
  5.9 6.7 %collective-permute-start.2 = (bf16[16,512]{1,0:T(8,128)(2,1)S(1)}, bf16[16,512]{1,0:T(8,128)(2,1)S(1)}, u32[]{:S(2)}, u32[]{:S(2)}) collective-permute-start(bf16[16,512]{1,0:T(8,128)(2,1)S(1)} %slice_select_fusion), channel_id=1, source_target_pairs={{0,8},{1,9},{2,10},{3,11},{4,12},{5,13},{6,14},{7,15},{8,16},{9,17... | collective-permute-start | bytes 49160 | tf_op jit(solution)/shard_map/ppermute | solution.py:269
  15.1 8.4 %collective-permute-start.4 = (bf16[304,256]{1,0:T(8,128)(2,1)S(1)}, bf16[304,256]{1,0:T(8,128)(2,1)S(1)}, u32[]{:S(2)}, u32[]{:S(2)}) collective-permute-start(bf16[304,256]{1,0:T(8,128)(2,1)S(1)} %get-tuple-element.45), channel_id=1, source_target_pairs={{0,1},{1,0},{2,3},{3,2},{4,5},{5,4},{6,7},{7,6},{8,9},{9,8},{10,11... | collective-permute-start | bytes 466952 | tf_op jit(solution)/shard_map/ppermute | solution.py:269
  16.6 9.5 %collective-permute-start.5 = (bf16[304,256]{1,0:T(8,128)(2,1)S(1)}, bf16[304,256]{1,0:T(8,128)(2,1)S(1)}, u32[]{:S(2)}, u32[]{:S(2)}) collective-permute-start(bf16[304,256]{1,0:T(8,128)(2,1)S(1)} %get-tuple-element.46), channel_id=1, source_target_pairs={{0,2},{1,3},{2,0},{3,1},{4,6},{5,7},{6,4},{7,5},{8,10},{9,11},{10,... | collective-permute-start | bytes 466952 | tf_op jit(solution)/shard_map/ppermute | solution.py:269
  17.5 8.6 %collective-permute-start.6 = (bf16[304,256]{1,0:T(8,128)(2,1)S(1)}, bf16[304,256]{1,0:T(8,128)(2,1)S(1)}, u32[]{:S(2)}, u32[]{:S(2)}) collective-permute-start(bf16[304,256]{1,0:T(8,128)(2,1)S(1)} %get-tuple-element.47), channel_id=1, source_target_pairs={{0,3},{1,2},{2,1},{3,0},{4,7},{5,6},{6,5},{7,4},{8,11},{9,10},{10,... | collective-permute-start | bytes 466952 | tf_op jit(solution)/shard_map/ppermute | solution.py:269
  18.7 9.9 %copy-start.4 = (bf16[2,256,2048]{2,1,0:T(8,128)(2,1)S(1)}, bf16[2,256,2048]{2,1,0:T(8,128)(2,1)}, u32[]{:S(2)}) copy-start(bf16[2,256,2048]{2,1,0:T(8,128)(2,1)} %refs_2_.4) | copy-start | bytes 6291460
  21.2 13.1 %collective-permute-start.8 = (bf16[272,256]{1,0:T(8,128)(2,1)S(1)}, bf16[272,256]{1,0:T(8,128)(2,1)S(1)}, u32[]{:S(2)}, u32[]{:S(2)}) collective-permute-start(bf16[272,256]{1,0:T(8,128)(2,1)S(1)} %get-tuple-element.53), channel_id=1, source_target_pairs={{0,1},{1,0},{2,3},{3,2},{4,5},{5,4},{6,7},{7,6},{8,9},{9,8},{10,11... | collective-permute-start | bytes 417800 | tf_op jit(solution)/shard_map/ppermute | solution.py:269
  22.7 11.7 %collective-permute-start.9 = (bf16[272,256]{1,0:T(8,128)(2,1)S(1)}, bf16[272,256]{1,0:T(8,128)(2,1)S(1)}, u32[]{:S(2)}, u32[]{:S(2)}) collective-permute-start(bf16[272,256]{1,0:T(8,128)(2,1)S(1)} %get-tuple-element.54), channel_id=1, source_target_pairs={{0,2},{1,3},{2,0},{3,1},{4,6},{5,7},{6,4},{7,5},{8,10},{9,11},{10,... | collective-permute-start | bytes 417800 | tf_op jit(solution)/shard_map/ppermute | solution.py:269
  23.5 10.8 %collective-permute-start.10 = (bf16[272,256]{1,0:T(8,128)(2,1)S(1)}, bf16[272,256]{1,0:T(8,128)(2,1)S(1)}, u32[]{:S(2)}, u32[]{:S(2)}) collective-permute-start(bf16[272,256]{1,0:T(8,128)(2,1)S(1)} %get-tuple-element.55), channel_id=1, source_target_pairs={{0,3},{1,2},{2,1},{3,0},{4,7},{5,6},{6,5},{7,4},{8,11},{9,10},{10,... | collective-permute-start | bytes 417800 | tf_op jit(solution)/shard_map/ppermute | solution.py:269
  26.6 8.7 %collective-permute-start.7 = (bf16[2,272,256]{2,1,0:T(8,128)(2,1)S(1)}, bf16[2,272,256]{2,1,0:T(8,128)(2,1)S(1)}, u32[]{:S(2)}, u32[]{:S(2)}) collective-permute-start(bf16[2,272,256]{2,1,0:T(8,128)(2,1)S(1)} %get-tuple-element.49.refs_9_), channel_id=1, source_target_pairs={{0,8},{1,9},{2,10},{3,11},{4,12},{5,13},{6,14},{7,15},{8,0},{9,1},... | collective-permute-start | bytes 835592 | tf_op jit(solution)/shard_map/ppermute | solution.py:269
  35.1 10.5 %collective-permute-start.12 = (bf16[2,272,256]{2,1,0:T(8,128)(2,1)S(1)}, bf16[2,272,256]{2,1,0:T(8,128)(2,1)S(1)}, u32[]{:S(2)}, u32[]{:S(2)}) collective-permute-start(bf16[2,272,256]{2,1,0:T(8,128)(2,1)S(1)} %get-tuple-element.56.refs_3_), channel_id=1, source_target_pairs={{0,8},{1,9},{2,10},{3,11},{4,12},{5,13},{6,14},{7,15},{8,0},{9,1},... | collective-permute-start | bytes 835592 | tf_op jit(solution)/shard_map/ppermute | solution.py:269
  36.0 10.4 %collective-permute-start.11 = (bf16[1,272,256]{2,1,0:T(8,128)(2,1)S(1)}, bf16[1,272,256]{2,1,0:T(8,128)(2,1)S(1)}, u32[]{:S(2)}, u32[]{:S(2)}) collective-permute-start(bf16[1,272,256]{2,1,0:T(8,128)(2,1)S(1)} %get-tuple-element.58.refs_9_), channel_id=1, source_target_pairs={{0,16},{1,17},{2,18},{3,19},{4,20},{5,21},{6,22},{7,23},{8,24},{9,... | collective-permute-start | bytes 417800 | tf_op jit(solution)/shard_map/ppermute | solution.py:269
  46.3 7.5 %collective-permute-start.16 = (bf16[1,272,256]{2,1,0:T(8,128)(2,1)S(1)}, bf16[1,272,256]{2,1,0:T(8,128)(2,1)S(1)}, u32[]{:S(2)}, u32[]{:S(2)}) collective-permute-start(bf16[1,272,256]{2,1,0:T(8,128)(2,1)S(1)} %get-tuple-element.61.refs_3_), channel_id=1, source_target_pairs={{0,16},{1,17},{2,18},{3,19},{4,20},{5,21},{6,22},{7,23},{8,24},{9,... | collective-permute-start | bytes 417800 | tf_op jit(solution)/shard_map/ppermute | solution.py:269
  47.0 8.8 %collective-permute-start.15 = (bf16[256,256]{1,0:T(8,128)(2,1)S(1)}, bf16[256,256]{1,0:T(8,128)(2,1)S(1)}, u32[]{:S(2)}, u32[]{:S(2)}) collective-permute-start(bf16[256,256]{1,0:T(8,128)(2,1)S(1)} %merge.6.refs_1_.refs_3_), channel_id=1, source_target_pairs={{0,3},{1,2},{2,1},{3,0},{4,7},{5,6},{6,5},{7,4},{8,11},{9,10},{10,... | collective-permute-start | bytes 393224 | tf_op jit(solution)/shard_map/ppermute | solution.py:269
  48.4 9.6 %collective-permute-start.14 = (bf16[256,256]{1,0:T(8,128)(2,1)S(1)}, bf16[256,256]{1,0:T(8,128)(2,1)S(1)}, u32[]{:S(2)}, u32[]{:S(2)}) collective-permute-start(bf16[256,256]{1,0:T(8,128)(2,1)S(1)} %merge.6.refs_1_.refs_3_), channel_id=1, source_target_pairs={{0,2},{1,3},{2,0},{3,1},{4,6},{5,7},{6,4},{7,5},{8,10},{9,11},{10,... | collective-permute-start | bytes 393224 | tf_op jit(solution)/shard_map/ppermute | solution.py:269
  48.9 9.1 %collective-permute-start.13 = (bf16[256,256]{1,0:T(8,128)(2,1)S(1)}, bf16[256,256]{1,0:T(8,128)(2,1)S(1)}, u32[]{:S(2)}, u32[]{:S(2)}) collective-permute-start(bf16[256,256]{1,0:T(8,128)(2,1)S(1)} %merge.6.refs_1_.refs_3_), channel_id=1, source_target_pairs={{0,1},{1,0},{2,3},{3,2},{4,5},{5,4},{6,7},{7,6},{8,9},{9,8},{10,11... | collective-permute-start | bytes 393224 | tf_op jit(solution)/shard_map/ppermute | solution.py:269
  54.4 6.0 %collective-permute-start.19 = (bf16[256,256]{1,0:T(8,128)(2,1)S(1)}, bf16[256,256]{1,0:T(8,128)(2,1)S(1)}, u32[]{:S(2)}, u32[]{:S(2)}) collective-permute-start(bf16[256,256]{1,0:T(8,128)(2,1)S(1)} %merge.7.refs_5_), channel_id=1, source_target_pairs={{0,3},{1,2},{2,1},{3,0},{4,7},{5,6},{6,5},{7,4},{8,11},{9,10},{10,... | collective-permute-start | bytes 393224 | tf_op jit(solution)/shard_map/ppermute | solution.py:269
  55.8 5.9 %collective-permute-start.18 = (bf16[256,256]{1,0:T(8,128)(2,1)S(1)}, bf16[256,256]{1,0:T(8,128)(2,1)S(1)}, u32[]{:S(2)}, u32[]{:S(2)}) collective-permute-start(bf16[256,256]{1,0:T(8,128)(2,1)S(1)} %merge.7.refs_5_), channel_id=1, source_target_pairs={{0,2},{1,3},{2,0},{3,1},{4,6},{5,7},{6,4},{7,5},{8,10},{9,11},{10,... | collective-permute-start | bytes 393224 | tf_op jit(solution)/shard_map/ppermute | solution.py:269
  55.8 5.9 %collective-permute-start.17 = (bf16[256,256]{1,0:T(8,128)(2,1)S(1)}, bf16[256,256]{1,0:T(8,128)(2,1)S(1)}, u32[]{:S(2)}, u32[]{:S(2)}) collective-permute-start(bf16[256,256]{1,0:T(8,128)(2,1)S(1)} %merge.7.refs_5_), channel_id=1, source_target_pairs={{0,1},{1,0},{2,3},{3,2},{4,5},{5,4},{6,7},{7,6},{8,9},{9,8},{10,11... | collective-permute-start | bytes 393224 | tf_op jit(solution)/shard_map/ppermute | solution.py:269
  (6 other events, 27.1 us)

commit v4 on v3

--- a/solution.py
+++ b/solution.py
@@ -252,7 +252,7 @@
 LOG2E = 1.4426950408889634
 AXES = ("prompt", "comp")
 CHUNKS = (1, 1)
-PIECES = 1
+LOG_LANES = 32
 TAIL = 16
 VMEM_BYTES = 16 * 1024 * 1024
 
@@ -352,6 +352,24 @@
     edge_out[...] = edges[1].astype(jnp.bfloat16)
 
 
+def log_lanes(high, low):
+    lane = lax.broadcasted_iota(jnp.int32, high.shape, 1)
+    return jnp.where(lane % LOG_LANES < LOG_LANES // 2, high, low)
+
+
+def logs_of(tiles, width):
+    rows = [tile.astype(jnp.float32)[TAIL - 1 : TAIL] for tile in tiles]
+    lanes = rows[0].shape[1]
+    rows.append(jnp.zeros((8 - len(rows), lanes), jnp.float32))
+    source = lax.broadcasted_iota(jnp.int32, (lanes, width + lanes), 0)
+    target = lax.broadcasted_iota(jnp.int32, (lanes, width + lanes), 1)
+    head = jnp.where(target < width, target >> 6, (target - width) >> 5)
+    pick = (source >> 5 == head) & ((source & (LOG_LANES // 2 - 1)) == 0)
+    rows = jnp.concatenate(rows, axis=0).astype(jnp.bfloat16)
+    found = contract(rows, pick.astype(jnp.bfloat16), ((1,), (0,)))
+    return found[:, 0:width], found[:, width:]
+
+
 def prompt_weights_kernel(
     place, own, other, taps_b, step, decay, w_out, b_out, log_out, first_out
 ):
@@ -380,14 +398,14 @@
     w_out[0:rows] = jnp.exp(-rate * after_own) * dt_own
     w_out[rows:] = jnp.exp(-rate * after_other) * dt_other
     total = jnp.broadcast_to(-rate * (sum_own + sum_other), (8, heads))
-    spread = spread_heads(0, heads, heads * HEAD_WIDTH).astype(jnp.bfloat16)
-    which = lax.broadcasted_iota(jnp.int32, total.shape, 0)
-    high = total.astype(jnp.bfloat16).astype(jnp.float32)
-    mid = (total - high).astype(jnp.bfloat16).astype(jnp.float32)
-    low = total - high - mid
-    parts = jnp.where(which == 0, high, jnp.where(which == 1, mid, jnp.where(which == 2, low, 0.0)))
-    wide = contract(parts.astype(jnp.bfloat16), spread, ((1,), (0,)))
-    log_out[...] = jnp.concatenate([wide, jnp.zeros_like(wide)], axis=0).astype(jnp.bfloat16)
+    high = total.astype(jnp.bfloat16)
+    low = (total - high.astype(jnp.float32)).astype(jnp.bfloat16)
+    row = lax.broadcasted_iota(jnp.int32, (heads, heads * LOG_LANES), 0)
+    lane = lax.broadcasted_iota(jnp.int32, (heads, heads * LOG_LANES), 1)
+    spread = (row == lane // LOG_LANES).astype(jnp.bfloat16)
+    log_out[...] = log_lanes(
+        contract(high, spread, ((1,), (0,))), contract(low, spread, ((1,), (0,)))
+    )
     own_last, other_last = own_b[rows - TAIL :], other_b[rows - TAIL :]
     first = jnp.where(first_own, own_b[0:TAIL].astype(jnp.float32), other_b[0:TAIL].astype(jnp.float32))
     first_out[...] = first.astype(jnp.bfloat16)
@@ -404,7 +422,7 @@
     offset, parts, place, inner, other, near, taps, taps_b, weights, b_turned, b_first, logs, tail,
     *rest,
 ):
-    outs, b_here = rest[:parts], rest[-1]
+    outs, handed, b_here = rest[:parts], rest[parts:-1], rest[-1]
     column, core = place[1], place[2]
     group = 2 * column + core
     first_own = core == 0
@@ -451,11 +469,16 @@
         mine = contract(b_here[:, 0:rows], x_own.astype(jnp.bfloat16), ((1,), (0,)))
         theirs = contract(b_here[:, rows:], x_other.astype(jnp.bfloat16), ((1,), (0,)))
         outs[turn][0:state] = (mine + theirs).astype(jnp.bfloat16)
-        outs[turn][state : state + TAIL] = logs[:, cols]
-        if outs[turn].shape[0] > state + TAIL:
-            for index in range(tail.shape[1] // width):
-                at = state + TAIL * (index + 1)
-                outs[turn][at : at + TAIL] = tail[:, index * width : (index + 1) * width]
+        if outs[turn].shape[0] > state:
+            log_width = part_width * LOG_LANES // HEAD_WIDTH
+            at = pl.ds(pl.multiple_of(part * log_width, log_width), log_width)
+            pieces = tail[:, 0:width].astype(jnp.float32)
+            row = lax.broadcasted_iota(jnp.int32, pieces.shape, 0)
+            pieces = jnp.where(row == TAIL - 1, logs[0:1, at], pieces)
+            outs[turn][state : state + TAIL] = pieces.astype(jnp.bfloat16)
+            outs[turn][state + TAIL :] = tail[:, width:]
+    for out in handed:
+        out[...] = tail[...]
 
 
 def pick_kernel(count, place, after, *refs):
@@ -470,116 +493,134 @@
                 stays[step // 2] = held[index ^ step][0:rows]
                 goes[step // 2] = held[index ^ (step + 1)][0:rows]
             for tail in tails:
-                for piece in range(tail.shape[1] // width):
-                    at = rows + TAIL * piece
-                    tail[:, piece * width : (piece + 1) * width] = held[index][at : at + TAIL]
-
-
-def log_of(message, state):
-    rows = message[state:].astype(jnp.float32)
-    return rows[0:1] + rows[1:2] + rows[2:3]
-
-
-def merge_kernel(bit, place, own, came, *refs):
-    after, *outs = refs
-    state = own.shape[1] - TAIL
+                tail[:, 0:width] = held[index][rows - TAIL : rows]
+                tail[:, width:] = held[index][rows:]
+
+
+def merge_kernel(bit, chunk, place, own, came, given, after, *refs):
+    count, rows, width = own.shape
+    state = STATE_WIDTH
     first = (place[0] >> bit) & 1 == 0
-    count = own.shape[0]
+    outs = refs if chunk else refs[:-1]
+    factors = given if chunk else refs[-1]
+    if chunk == 0:
+        last = slice(rows - TAIL, rows)
+        tiles = [ref[index, last] for index in range(count) for ref in (own, came)]
+        wide, lanes = logs_of(tiles, factors.shape[1])
+        row = lax.broadcasted_iota(jnp.int32, wide.shape, 0)
+        other = jnp.where(row % 2 == 0, pltpu.roll(wide, 7, 0), pltpu.roll(wide, 1, 0))
+        scaled = (row % 2 == 0) == first
+        factors[...] = jnp.exp(jnp.where(scaled, other, 0.0))
     for index in range(count):
-        mine, theirs = own[index], came[index]
-        log_mine, log_theirs = log_of(mine, state), log_of(theirs, state)
-        mine_by = jnp.exp(jnp.where(first, log_theirs, 0.0))
-        theirs_by = jnp.exp(jnp.where(first, 0.0, log_mine))
-        joined = mine[0:state].astype(jnp.float32) * mine_by
-        joined = joined + theirs[0:state].astype(jnp.float32) * theirs_by
-        if len(outs) == 1:
+        cols = slice(chunk * width, (chunk + 1) * width)
+        mine_by = factors[2 * index : 2 * index + 1, cols]
+        theirs_by = factors[2 * index + 1 : 2 * index + 2, cols]
+        joined = own[index, 0:state].astype(jnp.float32) * mine_by
+        joined = joined + came[index, 0:state].astype(jnp.float32) * theirs_by
+        if count == 1:
             outs[0][...] = joined.astype(jnp.bfloat16)
             continue
-        out = outs[0] if index < count // 2 else outs[1]
-        at = index % (count // 2)
-        out[at, 0:state] = joined.astype(jnp.bfloat16)
-        total = log_mine + log_theirs
-        high = total.astype(jnp.bfloat16)
-        rest = total - high.astype(jnp.float32)
-        mid = rest.astype(jnp.bfloat16)
-        low = (rest - mid.astype(jnp.float32)).astype(jnp.bfloat16)
-        blank = jnp.zeros((TAIL - 3, total.shape[1]), jnp.float32)
-        parts = [part.astype(jnp.float32) for part in (high, mid, low)] + [blank]
-        out[at, state:] = jnp.concatenate(parts, axis=0).astype(jnp.bfloat16)
+        outs[index][0, 0:state] = joined.astype(jnp.bfloat16)
+        if rows > state:
+            total = lanes[2 * index : 2 * index + 1] + lanes[2 * index + 1 : 2 * index + 2]
+            total = jnp.broadcast_to(total, (8, total.shape[1]))
+            high = total.astype(jnp.bfloat16).astype(jnp.float32)
+            compact = log_lanes(high, total - high)
+            compact = jnp.concatenate([compact, compact], axis=0)
+            outs[index][0, state:] = compact.astype(jnp.bfloat16)
+
+
+def prepare_kernel(
+    slot, fetch, place, gate, step, decay, after,
+    gate_out, factor_out, cum_out, turned_out, log_out, after_out, *rest,
+):
+    width = 2 * STATE_WIDTH
+    copies = []
+    if fetch:
+        gate_in, sems = rest
+        copies = [
+            pltpu.make_async_copy(
+                gate.at[slot, :, at : at + width], gate_in.at[:, at : at + width], sems.at[index]
+            )
+            for index, at in enumerate(range(0, gate.shape[2], width))
+        ]
+    for copy in copies:
+        copy.start()
+    after_out[...] = after[...]
+    rows, features = gate_out.shape
+    heads = step.shape[0]
+    row = lax.broadcasted_iota(jnp.int32, (rows, rows), 0)
+    col = lax.broadcasted_iota(jnp.int32, (rows, rows), 1)
+    dt = softplus(step[:, slot])
+    decay_row = jnp.broadcast_to(group_of(decay, place[3], heads), (8, heads))
+    decay_col = jnp.transpose(decay_row)[:, 0:1]
+    before = (row <= col).astype(jnp.float32)
+    cum = contract(dt, before, ((1,), (0,)), HIGHEST) * (-LOG2E * jnp.exp(decay_col))
+    log_dt = jnp.log(dt) * LOG2E
+    cum_out[...] = cum - log_dt
+    log_out[...] = log_dt
+    turned = jnp.transpose(cum)
+    turned_out[...] = turned
+    decays = jnp.exp2(turned).astype(jnp.bfloat16)
+    for index, at in enumerate(range(0, features, width)):
+        cols = slice(at, at + width)
+        if fetch:
+            copies[index].wait()
+        gate_here = gate_in[:, cols] if fetch else gate[slot, :, cols]
+        silu_gate = half_silu(gate_here.astype(jnp.float32))
+        gate_out[:, cols] = silu_gate.astype(jnp.bfloat16)
+        spread = spread_heads(at // HEAD_WIDTH, heads, width).astype(jnp.bfloat16)
+        decay_wide = contract(decays, spread, ((1,), (0,)))
+        factor_out[:, cols] = (decay_wide * silu_gate).astype(jnp.bfloat16)
 
 
 def completion_kernel(
-    slot, piece, pieces, place, inner, gate, proj, tail, taps, taps_bc, step, decay, after, *refs
+    slot, place, inner, proj, tail, taps, taps_bc, gates, base_rows, cum_cols, log_dt, after,
+    fixed_out, c_out, x_held, bc_in, sems,
 ):
-    if piece == 0:
-        fixed_out, factor_out, c_out, score_out, x_held, gate_held, bc_in, sems = refs
-    else:
-        _, _, score_in, fixed_out, factor_out, x_held, gate_held = refs
     rows, features = fixed_out.shape
-    heads = step.shape[0] // pieces
-    first_head = piece * heads
+    heads = base_rows.shape[0]
     half = rows // 2
     own = place[3]
     state = STATE_WIDTH
-    if piece == 0:
-        copies = [
-            pltpu.make_async_copy(
-                proj.at[slot, :, pl.ds(pl.multiple_of((own + skip) * state, state), state)],
-                bc_in.at[index],
-                sems.at[index],
-            )
-            for index, skip in enumerate((0, STATE_GROUPS))
-        ]
-        for copy in copies:
-            copy.start()
+    copies = [
+        pltpu.make_async_copy(
+            proj.at[slot, :, pl.ds(pl.multiple_of((own + skip) * state, state), state)],
+            bc_in.at[index],
+            sems.at[index],
+        )
+        for index, skip in enumerate((0, STATE_GROUPS))
+    ]
+    for copy in copies:
+        copy.start()
     edges = tail[...].astype(jnp.float32)
     pair_width = edges.shape[1]
     blank = jnp.zeros((TAIL - 3, pair_width), jnp.float32)
     row = lax.broadcasted_iota(jnp.int32, (rows, rows), 0)
     col = lax.broadcasted_iota(jnp.int32, (rows, rows), 1)
-    dt = softplus(step[first_head : first_head + heads, slot])
-    every = heads * pieces
-    decay_row = jnp.broadcast_to(group_of(decay, own, every), (8, every))
-    decay_col = jnp.transpose(decay_row)[first_head : first_head + heads, 0:1]
-    before = (row <= col).astype(jnp.float32)
-    cum = contract(dt, before, ((1,), (0,)), HIGHEST) * (-LOG2E * jnp.exp(decay_col))
-    log_dt = jnp.log(dt) * LOG2E
-    base_rows = cum - log_dt
-    cum_cols = jnp.transpose(cum)
-    decay_cols = jnp.exp2(cum_cols).astype(jnp.bfloat16)
     blocks = features // pair_width
-    for block in range(piece * blocks // pieces, (piece + 1) * blocks // pieces):
+    for block in range(blocks):
         at = block * pair_width
         cols = slice(at, at + pair_width)
         lead = jnp.concatenate([blank, edges[3 * block : 3 * block + 3]], axis=0)
         taps_here = taps[:, pl.ds(pl.multiple_of(own * features + at, pair_width), pair_width)]
         x_held[:, cols] = conv_rows(taps_here, lead, inner[slot, :, cols]).astype(jnp.bfloat16)
-        silu_gate = half_silu(gate[slot, :, cols].astype(jnp.float32))
-        gate_held[:, cols] = silu_gate
-        spread = spread_heads(at // HEAD_WIDTH - first_head, heads, pair_width).astype(jnp.bfloat16)
-        decay_wide = contract(decay_cols, spread, ((1,), (0,)))
-        factor_out[:, cols] = (decay_wide * silu_gate).astype(jnp.bfloat16)
-    if piece == 0:
-        for copy in copies:
-            copy.wait()
-        lead_bc = jnp.concatenate([blank, edges[3 * blocks : 3 * blocks + 3]], axis=0)
-        bc = []
-        for index, skip in enumerate((0, STATE_GROUPS)):
-            taps_here = taps_bc[:, pl.ds(pl.multiple_of((own + skip) * state, state), state)]
-            lead = lead_bc[:, index * state : (index + 1) * state]
-            bc.append(conv_rows(taps_here, lead, bc_in[index]).astype(jnp.bfloat16))
-        c_out[...] = bc[1]
-        scores = contract(bc[1], bc[0], ((1,), (1,)))
-        scores = jnp.where(row >= col, scores, 0.0)
-        score_out[...] = scores
-    else:
-        scores = score_in[...]
+    for copy in copies:
+        copy.wait()
+    lead_bc = jnp.concatenate([blank, edges[3 * blocks : 3 * blocks + 3]], axis=0)
+    bc = []
+    for index, skip in enumerate((0, STATE_GROUPS)):
+        taps_here = taps_bc[:, pl.ds(pl.multiple_of((own + skip) * state, state), state)]
+        lead = lead_bc[:, index * state : (index + 1) * state]
+        bc.append(conv_rows(taps_here, lead, bc_in[index]).astype(jnp.bfloat16))
+    c_out[...] = bc[1]
+    scores = contract(bc[1], bc[0], ((1,), (1,)))
+    scores = jnp.where(row >= col, scores, 0.0)
     low, high_left, high_right = scores[0:half, 0:half], scores[half:, 0:half], scores[half:, half:]
     pair = 2 * HEAD_WIDTH
     lane = lax.broadcasted_iota(jnp.int32, (rows, pair), 1)
     for first in range(0, heads, 2):
-        at = (first_head + first) * HEAD_WIDTH
-        cols = slice(at, at + pair)
+        cols = slice(first * HEAD_WIDTH, first * HEAD_WIDTH + pair)
         x_pair = x_held[:, cols]
         zero = jnp.zeros_like(x_pair)
         left = jnp.where(lane < HEAD_WIDTH, x_pair, zero)
@@ -602,8 +643,8 @@
         y_high = contract(
             jnp.concatenate(highs, axis=1), jnp.concatenate([left, right], axis=0), ((1,), (0,))
         )
-        fixed_out[0:half, cols] = (y_low * gate_held[0:half, cols]).astype(jnp.bfloat16)
-        fixed_out[half:, cols] = (y_high * gate_held[half:, cols]).astype(jnp.bfloat16)
+        fixed_out[0:half, cols] = (y_low * gates[0:half, cols].astype(jnp.float32)).astype(jnp.bfloat16)
+        fixed_out[half:, cols] = (y_high * gates[half:, cols].astype(jnp.float32)).astype(jnp.bfloat16)
 
 
 def read_slot(parts, offset, column, slot, states, own_work, gated, slot_at):
@@ -670,7 +711,7 @@
 
 
 LASTS = dict(
-    pack=2, prompt_weights=2, prompt_state=3, pick=1, merge=1, completion=4, read=2, finish=2
+    pack=2, prompt_weights=2, prompt_state=3, pick=1, merge=1, prepare=0, completion=4, read=2, finish=2
 )
 
 
@@ -730,6 +771,30 @@
     trade = lambda z, k, c: (z, 1 - k, c)
     other = routed(swap, trade)
     other_inner = routed(prompt_inner, trade)
+    slots, positions = completion_inner.shape[:2]
+    wide = jax.ShapeDtypeStruct((positions, features), bf16)
+    prepared = {}
+    held_gate = pltpu.with_memory_space_constraint(completion_gate, pltpu.HBM)
+
+    def prepare(slot, after, fetch):
+        every = jax.ShapeDtypeStruct((heads, positions), f32)
+        turned = jax.ShapeDtypeStruct((positions, heads), f32)
+        return run_whole(
+            lambda *refs: prepare_kernel(slot, fetch, *refs),
+            "prepare",
+            (place,),
+            (wide, wide, every, turned, every, edge),
+            (held_gate if fetch else completion_gate, sample_step, decay_log, after),
+            spaces=[pltpu.HBM if fetch else pltpu.VMEM] + [pltpu.VMEM] * 3,
+            scratch=[
+                pltpu.VMEM((positions, features), bf16),
+                pltpu.SemaphoreType.DMA((features // pair_width,)),
+            ]
+            * fetch,
+        )
+
+    for slot in range(1, slots):
+        *prepared[slot], edge_1 = prepare(slot, edge_1, True)
     edges = jnp.where(core == 0, other[rows:], edge_1)
     near = routed(edges, lambda z, k, c: (z + 1, k, c) if z + 1 < planes else None)
     far = routed(edges, lambda z, k, c: (c, k, c) if z + 1 == planes else None)
@@ -740,7 +805,7 @@
         (
             jax.ShapeDtypeStruct((2 * rows, heads), f32),
             jax.ShapeDtypeStruct((STATE_WIDTH, 2 * rows), bf16),
-            jax.ShapeDtypeStruct((TAIL, features), bf16),
+            jax.ShapeDtypeStruct((8, heads * LOG_LANES), f32),
             jax.ShapeDtypeStruct((TAIL, STATE_WIDTH), bf16),
         ),
         (own_b, other, conv_proj, prompt_step, decay_log),
@@ -750,21 +815,22 @@
     offsets = [sum(widths[:chunk]) for chunk in range(len(widths))]
     picks = []
     for chunk, width in enumerate(widths):
-        message = jax.ShapeDtypeStruct((STATE_WIDTH + TAIL, width), bf16)
         with_tail = chunk == 0
-        tail_rows = TAIL * (pair_width // width) if with_tail else 0
-        spread = jax.ShapeDtypeStruct((STATE_WIDTH + TAIL + tail_rows, width), bf16)
+        message = jax.ShapeDtypeStruct((STATE_WIDTH + TAIL * with_tail, width), bf16)
+        spread = jax.ShapeDtypeStruct((STATE_WIDTH + 2 * TAIL * with_tail, width), bf16)
         sent = run_whole(
             lambda *refs, offset=offsets[chunk]: prompt_state_kernel(offset, parts, *refs),
             "prompt_state",
             (place,),
-            (spread,) * parts,
+            (spread,) * parts + (edge,) * (chunk + 1 == len(widths)),
             (
                 prompt_inner, other_inner, near, conv_inner, conv_proj, weights, b_turned, b_first,
                 logs, far,
             ),
             scratch=[pltpu.VMEM((STATE_WIDTH, 2 * rows), bf16)],
         )
+        if chunk + 1 == len(widths):
+            *prepared[0], handed = prepare(0, sent[parts], False)
         held = [sent[0]] + [
             routed(sent[step], lambda z, k, c: (z, k, c ^ step)) for step in range(1, parts)
         ]
@@ -780,97 +846,81 @@
             )
         )
 
-    slots, positions = completion_inner.shape[:2]
     held_projections = pltpu.with_memory_space_constraint(completion_projections, pltpu.HBM)
-    wide = jax.ShapeDtypeStruct((positions, features), bf16)
-    pieces = PIECES
-
-    def completion(slot, piece, after, begun):
-        outs = (wide, wide)
-        scratch = [pltpu.VMEM((positions, features), bf16), pltpu.VMEM((positions, features), f32)]
-        operands = [
-            completion_inner, completion_gate, held_projections, tail, conv_inner, conv_proj,
-            sample_step, decay_log, after,
-        ]
-        if piece == 0:
-            outs += (
-                jax.ShapeDtypeStruct((positions, STATE_WIDTH), bf16),
-                jax.ShapeDtypeStruct((positions, positions), f32),
-            )
-            scratch += [
-                pltpu.VMEM((2, positions, STATE_WIDTH), bf16), pltpu.SemaphoreType.DMA((2,)),
-            ]
-            aliases = None
-        else:
-            fixed, factor, c, scores = begun
-            aliases = {len(operands) + 1: 0, len(operands) + 2: 1}
-            operands += [fixed, factor, scores]
-        results = run_whole(
-            lambda *refs: completion_kernel(slot, piece, pieces, *refs),
+    def completion(slot, after):
+        gates, factor, *decays = prepared[slot]
+        fixed, c = run_whole(
+            lambda *refs: completion_kernel(slot, *refs),
             "completion",
             (place,),
-            outs,
-            operands,
-            spaces=[pltpu.VMEM] * 2
-            + [pltpu.HBM]
-            + [pltpu.VMEM] * 5
-            + [pl.ANY]
-            + [pltpu.VMEM] * (len(operands) - 9),
-            scratch=scratch,
-            aliases=aliases,
-        )
-        return results if piece == 0 else results + tuple(begun[2:])
-
-    def merge(bit, own, came, shapes, after):
-        return run_whole(
-            lambda *refs: merge_kernel(bit, *refs),
+            (wide, jax.ShapeDtypeStruct((positions, STATE_WIDTH), bf16)),
+            (
+                completion_inner, held_projections, tail, conv_inner, conv_proj, gates, *decays, after,
+            ),
+            spaces=[pltpu.VMEM, pltpu.HBM] + [pltpu.VMEM] * 7 + [pl.ANY],
+            scratch=[
+                pltpu.VMEM((positions, features), bf16),
+                pltpu.VMEM((2, positions, STATE_WIDTH), bf16),
+                pltpu.SemaphoreType.DMA((2,)),
+            ],
+        )
+        return c, fixed, factor
+
+    def merge(bit, chunk, own, came, shapes, given, after):
+        table = jax.ShapeDtypeStruct((8, features // parts), f32)
+        *outs, factors = run_whole(
+            lambda *refs: merge_kernel(bit, chunk, *refs),
             "merge",
             (place,),
-            shapes,
-            (own, came, after),
-            spaces=[pltpu.VMEM] * 2 + [pl.ANY],
-        )
+            shapes + (table,) * (chunk == 0),
+            (own, came, given, after),
+            spaces=[pltpu.VMEM] * 2 + [pltpu.VMEM if chunk else pl.ANY, pl.ANY],
+        ) + ((given,) if chunk else ())
+        return outs, factors
 
     def gather(state):
         return [state] + [
             routed(state, lambda z, k, c: (z, k, c ^ step)) for step in range(1, parts)
         ]
 
-    work = [(slot, piece) for slot in range(slots) for piece in range(pieces)]
-    begun = {}
+    work = list(range(slots))
+    finished = []
 
     def do_work(after):
         if not work:
             return after
-        slot, piece = work.pop(0)
-        begun[slot] = completion(slot, piece, after, begun.get(slot))
-        return begun[slot][1]
-
-    stays, goes, merged, joined = [], [], [], []
+        finished.append(completion(work.pop(0), after))
+        return finished[-1][0]
+
+    stays, goes, go_shapes, merged, joined = [], [], [], [], []
     near_plane = lambda z, k, c: (z ^ 1, k, c)
     far_plane = lambda z, k, c: (z ^ 2, k, c)
-    tail, after = None, place
+    tail, after = None, handed
     for chunk in range(len(widths)):
         stay, go, *maybe = picks[chunk](after)
         tail = maybe[0] if maybe else tail
         stays.append(stay)
         goes.append(routed(go, near_plane))
+        go_shapes.append(go.shape[1:])
         if chunk + 1 < len(widths):
             after = do_work(go)
-    after = go
-    for chunk, width in enumerate(widths):
-        one = jax.ShapeDtypeStruct((1, STATE_WIDTH + TAIL, width), bf16)
-        stay, go = merge(0, stays[chunk], goes[chunk], (one, one), after)
+    given = after = go
+    for chunk in range(len(widths)):
+        one = jax.ShapeDtypeStruct((1,) + go_shapes[chunk], bf16)
+        (stay, go), given = merge(
+            0, chunk, stays[chunk], goes[chunk], (one, one), given, after
+        )
         merged.append((stay, routed(go, far_plane)))
-        after = do_work(go) if chunk + 1 < len(widths) else go
+        after = do_work(go)
+    given = go
     for chunk, width in enumerate(widths):
         state = jax.ShapeDtypeStruct((STATE_WIDTH, width), bf16)
-        joined.append(gather(merge(1, *merged[chunk], state, after)))
-        after = do_work(joined[-1][0])
+        (state,), given = merge(1, chunk, *merged[chunk], (state,), given, go)
+        joined.append(gather(state))
+    after = state
     while work:
         after = do_work(after)
-    finished = [begun[slot][:3] for slot in range(slots)]
-    own_work = [array for fixed, factor, c in finished for array in (c, fixed, factor)]
+    own_work = [array for three in finished for array in three]
     earlier = []
     for chunk, width in enumerate(widths[:-1]):
         earlier += run_whole(

time: 64.9 us -> 62.7 us (0.966)
  waiting for transfers between devices: 9.98 us -> 5.1 us
  Pallas kernels: 27.8 us -> 29.2 us
  starting transfers between devices: 26.4 us -> 27.7 us
    ppermute x20, waiting for transfers between devices: 9.98 us -> 5.1 us  [routed(): return lax.ppermute(block, AXES, pairs)]
    pallas_call x14 -> x16, Pallas kernels: 27.8 us -> 29.2 us  [run_whole(): pl.pallas_call(kernel, out_shape=out_shape, in_specs=[pl.BlockSpec(memory...]
    ppermute x20, starting transfers between devices: 26.4 us -> 27.7 us  [routed(): return lax.ppermute(block, AXES, pairs)]
  transfers between devices with their start and end apart: 20 -> 20, of which waited for: 6 -> 6; matrix products, arithmetic and copies ran while one was open for 0% -> 0% of each run, Pallas kernels for 35% -> 38%
where the time goes in v4:
time: 62.7 us; the launch traced here: 62.5 us
  Pallas kernels  29.2 us (47%)
  starting transfers between devices  27.7 us (44%)
  waiting for transfers between devices  5.1 us (8%)
    pallas_call x16, Pallas kernels, run_whole(): pl.pallas_call(kernel, out_shape=out_shape, in_specs=[pl.BlockSpec(memory...  29.2 us
    ppermute x20, starting transfers between devices, routed(): return lax.ppermute(block, AXES, pairs)  27.7 us
    ppermute x20, waiting for transfers between devices, routed(): return lax.ppermute(block, AXES, pairs)  5.1 us
  transfers between devices with their start and end apart: 20, of which 6 were waited for; matrix products, arithmetic and copies ran while one was open for 0% of the time, Pallas kernels for 38%

profile of v4, /device:TPU:0, one launch (start us, length us, event | category | flops | bytes accessed | tf_op | source)
XLA Modules:
  0.0 62.5 jit_solution(11665580309254072526)
XLA Ops:
  0.5 1.9 %pack.1 = (bf16[272,512]{1,0:T(8,128)(2,1)S(1)}, bf16[16,512]{1,0:T(8,128)(2,1)S(1)}, bf16[256,256]{1,0:T(8,128)(2,1)S(1)}) custom-call(s32[4]{0:T(128)S(1)} %pad_add_fusion.place.refs_0_, bf16[256,4096]{1,0:T(8,128)(2,1)} %refs_1_.10, bf16[256,4096]{1,0:T(8,128)(2,1)} %proj.1, f32[64,256]{1,0:T(8,128)} %step.3), custom_call_target="tpu_custom_call" | custom-call | flops 2000000000 | bytes 6000000 | tf_op jit(solution)/shard_map/pack/pallas_call | solution.py:957
  2.6 2.4 %prepare.2 = (bf16[256,2048]{1,0:T(8,128)(2,1)S(1)}, bf16[256,2048]{1,0:T(8,128)(2,1)S(1)}, f32[32,256]{1,0:T(8,128)S(1)}, f32[256,32]{1,0:T(8,128)S(1)}, f32[32...) custom-call(s32[4]{0:T(128)S(1)} %pad_add_fusion.place.refs_0_, bf16[2,256,2048]{2,1,0:T(8,128)(2,1)} %refs_1_.9, ...), custom_call_target="tpu_custom_call" | custom-call | tf_op jit(solution)/shard_map/prepare/pallas_call | solution.py:957
  5.1 1.3 %collective-permute-start.3 = (bf16[16,512]{1,0:T(8,128)(2,1)S(1)}, bf16[16,512]{1,0:T(8,128)(2,1)S(1)}, u32[]{:S(2)}, u32[]{:S(2)}) collective-permute-start(bf16[16,512]{1,0:T(8,128)(2,1)S(1)} %slice_select_fusion), channel_id=1, source_target_pairs={{24,0},{25,9},{26,18},{27,27},{28,4},{29,13},{30,22},{31,31}} | collective-permute-start | bytes 49160 | tf_op jit(solution)/shard_map/ppermute | solution.py:269
  6.4 4.3 %collective-permute-start.2 = (bf16[16,512]{1,0:T(8,128)(2,1)S(1)}, bf16[16,512]{1,0:T(8,128)(2,1)S(1)}, u32[]{:S(2)}, u32[]{:S(2)}) collective-permute-start(bf16[16,512]{1,0:T(8,128)(2,1)S(1)} %slice_select_fusion), channel_id=1, source_target_pairs={{0,8},{1,9},{2,10},{3,11},{4,12},{5,13},{6,14},{7,15},{8,16},{9,17... | collective-permute-start | bytes 49160 | tf_op jit(solution)/shard_map/ppermute | solution.py:269
  10.7 1.6 %prompt_weights.1 = (f32[512,32]{1,0:T(8,128)S(1)}, bf16[256,512]{1,0:T(8,128)(2,1)S(1)}, f32[8,1024]{1,0:T(8,128)S(1)}, bf16[16,256]{1,0:T(8,128)(2,1)S(1)}) custom-call(s32[4]{0:T(128)S(1)} %pad_add_fusion.place.refs_0_, bf16[256,256]{1,0:T(8,128)(2,1)S(1)} %get-tuple-element.54.own, bf16[272,512]{1,0:T(8,128)(2,1)S(1)} %collective-permute-done.1.other, ...), custom_call_target="tpu_custom_call" | custom-call | flops 2000000000 | bytes 6000000 | tf_op jit(solution)/shard_map/prompt_weights/pallas_call | solution.py:957
  13.2 2.5 %prompt_state.3 = (bf16[288,256]{1,0:T(8,128)(2,1)S(1)}, bf16[288,256]{1,0:T(8,128)(2,1)S(1)}, bf16[288,256]{1,0:T(8,128)(2,1)S(1)}, bf16[288,256]{1,0:T(8,128)(2,1)S(1)}) custom-call(s32[4]{0:T(128)S(1)} %pad_add_fusion.place.refs_0_, bf16[256,4096]{1,0:T(8,128)(2,1)S(1)} %copy-done.5, bf16[256,4096]{1,0:T(8,128)(2,1)S(1)} %collective-permute-done.refs_2_, ...), custom_call_target="tpu_custom_call" | custom-call | flops 3000000000 | bytes 9000000 | tf_op jit(solution)/shard_map/prompt_state/pallas_call | solution.py:957
  15.7 1.4 %collective-permute-start.4 = (bf16[288,256]{1,0:T(8,128)(2,1)S(1)}, bf16[288,256]{1,0:T(8,128)(2,1)S(1)}, u32[]{:S(2)}, u32[]{:S(2)}) collective-permute-start(bf16[288,256]{1,0:T(8,128)(2,1)S(1)} %get-tuple-element.62), channel_id=1, source_target_pairs={{0,1},{1,0},{2,3},{3,2},{4,5},{5,4},{6,7},{7,6},{8,9},{9,8},{10,11... | collective-permute-start | bytes 442376 | tf_op jit(solution)/shard_map/ppermute | solution.py:269
  18.0 1.3 %collective-permute-start.6 = (bf16[288,256]{1,0:T(8,128)(2,1)S(1)}, bf16[288,256]{1,0:T(8,128)(2,1)S(1)}, u32[]{:S(2)}, u32[]{:S(2)}) collective-permute-start(bf16[288,256]{1,0:T(8,128)(2,1)S(1)} %get-tuple-element.64), channel_id=1, source_target_pairs={{0,3},{1,2},{2,1},{3,0},{4,7},{5,6},{6,5},{7,4},{8,11},{9,10},{10,... | collective-permute-start | bytes 442376 | tf_op jit(solution)/shard_map/ppermute | solution.py:269
  19.2 2.5 %prompt_state.2 = (bf16[256,256]{1,0:T(8,128)(2,1)S(1)}, bf16[256,256]{1,0:T(8,128)(2,1)S(1)}, bf16[256,256]{1,0:T(8,128)(2,1)S(1)}, bf16[256,256]{1,0:T(8,128)(2,1)S(1)}, bf16[16,512]{1,0:T(8,128)(2,1)S(1)}) custom-call(s32[4]{0:T(128)S(1)} %pad_add_fusion.place.refs_0_, bf16[256,4096]{1,0:T(8,128)(2,1)S(1)} %copy-done.5, ...), custom_call_target="tpu_custom_call" | custom-call | flops 3000000000 | bytes 9000000 | tf_op jit(solution)/shard_map/prompt_state/pallas_call | solution.py:957
  21.7 1.4 %collective-permute-start.8 = (bf16[256,256]{1,0:T(8,128)(2,1)S(1)}, bf16[256,256]{1,0:T(8,128)(2,1)S(1)}, u32[]{:S(2)}, u32[]{:S(2)}) collective-permute-start(bf16[256,256]{1,0:T(8,128)(2,1)S(1)} %get-tuple-element.74), channel_id=1, source_target_pairs={{0,1},{1,0},{2,3},{3,2},{4,5},{5,4},{6,7},{7,6},{8,9},{9,8},{10,11... | collective-permute-start | bytes 393224 | tf_op jit(solution)/shard_map/ppermute | solution.py:269
  24.0 1.6 %prepare.3 = (bf16[256,2048]{1,0:T(8,128)(2,1)S(1)}, bf16[256,2048]{1,0:T(8,128)(2,1)S(1)}, f32[32,256]{1,0:T(8,128)S(1)}, f32[256,32]{1,0:T(8,128)S(1)}, f32[32...) custom-call(s32[4]{0:T(128)S(1)} %pad_add_fusion.place.refs_0_, bf16[2,256,2048]{2,1,0:T(8,128)(2,1)S(1)} %copy-done, ...), custom_call_target="tpu_custom_call" | custom-call | tf_op jit(solution)/shard_map/prepare/pallas_call | solution.py:957
  25.6 1.3 %collective-permute-start.10 = (bf16[256,256]{1,0:T(8,128)(2,1)S(1)}, bf16[256,256]{1,0:T(8,128)(2,1)S(1)}, u32[]{:S(2)}, u32[]{:S(2)}) collective-permute-start(bf16[256,256]{1,0:T(8,128)(2,1)S(1)} %get-tuple-element.76), channel_id=1, source_target_pairs={{0,3},{1,2},{2,1},{3,0},{4,7},{5,6},{6,5},{7,4},{8,11},{9,10},{10,... | collective-permute-start | bytes 393224 | tf_op jit(solution)/shard_map/ppermute | solution.py:269
  27.6 1.5 %collective-permute-start.7 = (bf16[2,272,256]{2,1,0:T(8,128)(2,1)S(1)}, bf16[2,272,256]{2,1,0:T(8,128)(2,1)S(1)}, u32[]{:S(2)}, u32[]{:S(2)}) collective-permute-start(bf16[2,272,256]{2,1,0:T(8,128)(2,1)S(1)} %get-tuple-element.66.refs_10_), channel_id=1, source_target_pairs={{0,8},{1,9},{2,10},{3,11},{4,12},{5,13},{6,14},{7,15},{8,0},{9,1},... | collective-permute-start | bytes 835592 | tf_op jit(solution)/shard_map/ppermute | solution.py:269
  29.1 4.3 %completion.2 = (bf16[256,2048]{1,0:T(8,128)(2,1)S(1)}, bf16[256,256]{1,0:T(8,128)(2,1)S(1)}) custom-call(s32[4]{0:T(128)S(1)} %pad_add_fusion.place.refs_0_, bf16[2,256,2048]{2,1,0:T(8,128)(2,1)S(1)} %copy-done.6, bf16[2,256,4096]{2,1,0:T(8,128)(2,1)} %refs_2_.8, bf16[16,512]{1,0:T(8,128)(2,1)S(1)} %get-tuple-element.67.refs_3_, ...), custom_call_target="tpu_custom_call" | custom-call | flops 4000000000 | bytes 12000000 | tf_op jit(solution)/shard_map/completion/pallas_call | solution.py:957
  35.7 3.1 %collective-permute-start.11 = (bf16[1,272,256]{2,1,0:T(8,128)(2,1)S(1)}, bf16[1,272,256]{2,1,0:T(8,128)(2,1)S(1)}, u32[]{:S(2)}, u32[]{:S(2)}) collective-permute-start(bf16[1,272,256]{2,1,0:T(8,128)(2,1)S(1)} %get-tuple-element.79.refs_10_), channel_id=1, source_target_pairs={{0,16},{1,17},{2,18},{3,19},{4,20},{5,21},{6,22},{7,23},{8,24},{9,... | collective-permute-start | bytes 417800 | tf_op jit(solution)/shard_map/ppermute | solution.py:269
  38.8 4.3 %completion.3 = (bf16[256,2048]{1,0:T(8,128)(2,1)S(1)}, bf16[256,256]{1,0:T(8,128)(2,1)S(1)}) custom-call(s32[4]{0:T(128)S(1)} %pad_add_fusion.place.refs_0_, bf16[2,256,2048]{2,1,0:T(8,128)(2,1)S(1)} %copy-done.6, bf16[2,256,4096]{2,1,0:T(8,128)(2,1)} %refs_2_.8, bf16[16,512]{1,0:T(8,128)(2,1)S(1)} %get-tuple-element.67.refs_3_, ...), custom_call_target="tpu_custom_call" | custom-call | flops 4000000000 | bytes 12000000 | tf_op jit(solution)/shard_map/completion/pallas_call | solution.py:957
  43.7 1.4 %collective-permute-start.16 = (bf16[1,256,256]{2,1,0:T(8,128)(2,1)S(1)}, bf16[1,256,256]{2,1,0:T(8,128)(2,1)S(1)}, u32[]{:S(2)}, u32[]{:S(2)}) collective-permute-start(bf16[1,256,256]{2,1,0:T(8,128)(2,1)S(1)} %get-tuple-element.87.refs_3_.refs_4_), channel_id=1, source_target_pairs={{0,16},{1,17},{2,18},{3,19},{4,20},{5,21},{6,22},{7,23},{8,24},{9,... | collective-permute-start | bytes 393224 | tf_op jit(solution)/shard_map/ppermute | solution.py:269
  45.9 1.6 %collective-permute-start.15 = (bf16[256,256]{1,0:T(8,128)(2,1)S(1)}, bf16[256,256]{1,0:T(8,128)(2,1)S(1)}, u32[]{:S(2)}, u32[]{:S(2)}) collective-permute-start(bf16[256,256]{1,0:T(8,128)(2,1)S(1)} %get-tuple-element.88.refs_1_), channel_id=1, source_target_pairs={{0,3},{1,2},{2,1},{3,0},{4,7},{5,6},{6,5},{7,4},{8,11},{9,10},{10,... | collective-permute-start | bytes 393224 | tf_op jit(solution)/shard_map/ppermute | solution.py:269
  47.6 1.6 %collective-permute-start.14 = (bf16[256,256]{1,0:T(8,128)(2,1)S(1)}, bf16[256,256]{1,0:T(8,128)(2,1)S(1)}, u32[]{:S(2)}, u32[]{:S(2)}) collective-permute-start(bf16[256,256]{1,0:T(8,128)(2,1)S(1)} %get-tuple-element.88.refs_1_), channel_id=1, source_target_pairs={{0,2},{1,3},{2,0},{3,1},{4,6},{5,7},{6,4},{7,5},{8,10},{9,11},{10,... | collective-permute-start | bytes 393224 | tf_op jit(solution)/shard_map/ppermute | solution.py:269
  50.3 3.4 %collective-permute-start.19 = (bf16[256,256]{1,0:T(8,128)(2,1)S(1)}, bf16[256,256]{1,0:T(8,128)(2,1)S(1)}, u32[]{:S(2)}, u32[]{:S(2)}) collective-permute-start(bf16[256,256]{1,0:T(8,128)(2,1)S(1)} %merge.7.refs_5_), channel_id=1, source_target_pairs={{0,3},{1,2},{2,1},{3,0},{4,7},{5,6},{6,5},{7,4},{8,11},{9,10},{10,... | collective-permute-start | bytes 393224 | tf_op jit(solution)/shard_map/ppermute | solution.py:269
  54.3 1.9 %collective-permute-done.14.refs_3_ = bf16[256,256]{1,0:T(8,128)(2,1)S(1)} collective-permute-done((bf16[256,256]{1,0:T(8,128)(2,1)S(1)}, bf16[256,256]{1,0:T(8,128)(2,1)S(1)}, u32[]{:S(2)}, u32[]{:S(2)}) %collective-permute-start.14) | collective-permute-done | bytes 131104 | tf_op jit(solution)/shard_map/ppermute | solution.py:269
  56.2 1.1 %read.1 = (f32[2,4,256,256]{3,2,1,0:T(8,128)S(1)}, f32[2,256,128]{2,1,0:T(8,128)S(1)}) custom-call(s32[4]{0:T(128)S(1)} %pad_add_fusion.place.refs_0_, bf16[256,256]{1,0:T(8,128)(2,1)S(1)} %get-tuple-element.88.refs_1_, bf16[256,256]{1,0:T(8,128)(2,1)S(1)} %collective-permute-done.13.refs_2_, bf16[256,256]{1,0:T(8,128)(2,1)S(1)} %collective-permute-done.14.refs_3_, ...), custom_call_target="tpu_custom_call" | custom-call | flops 2000000000 | bytes 6000000 | tf_op jit(solution)/shard_map/read/pallas_call | solution.py:957
  57.9 1.2 %collective-permute-done.18.refs_7_ = bf16[256,256]{1,0:T(8,128)(2,1)S(1)} collective-permute-done((bf16[256,256]{1,0:T(8,128)(2,1)S(1)}, bf16[256,256]{1,0:T(8,128)(2,1)S(1)}, u32[]{:S(2)}, u32[]{:S(2)}) %collective-permute-start.18) | collective-permute-done | bytes 131104 | tf_op jit(solution)/shard_map/ppermute | solution.py:269
  59.6 2.8 %finish.1 = bf16[2,256,2048]{2,1,0:T(8,128)(2,1)} custom-call(s32[4]{0:T(128)S(1)} %pad_add_fusion.place.refs_0_, s32[2]{0:T(128)S(1)} %copy-done.4, f32[2048]{0:T(1024)S(1)} %copy-done.2, f32[2,4,256,256]{3,2,1,0:T(8,128)S(1)} %get-tuple-element.93.refs_3_, f32[2,256,128]{2,1,0:T(8,128)S(1)} %get-tuple-element.94.refs_4_, ...), custom_call_target="tpu_custom_call" | custom-call | flops 2000000000 | bytes 6000000 | tf_op jit(solution)/shard_map/finish/pallas_call | solution.py:957
  (54 shorter events, 10.3 us)
Async XLA Ops:
  0.0 13.1 %collective-permute-start = (bf16[256,4096]{1,0:T(8,128)(2,1)}, bf16[256,4096]{1,0:T(8,128)(2,1)S(1)}, u32[]{:S(2)}, u32[]{:S(2)}) collective-permute-start(bf16[256,4096]{1,0:T(8,128)(2,1)} %refs_1_.10), channel_id=1, source_target_pairs={{0,4},{1,5},{2,6},{3,7},{4,0},{5,1},{6,2},{7,3},{8,12},{9,13},{10,... | collective-permute-start | bytes 6291464 | tf_op jit(solution)/shard_map/ppermute | solution.py:269
  2.5 8.2 %copy-start.8 = (f32[64,256]{1,0:T(8,128)S(1)}, f32[64,256]{1,0:T(8,128)}, u32[]{:S(2)}) copy-start(f32[64,256]{1,0:T(8,128)} %step.3) | copy-start | bytes 196612
  2.5 8.2 %copy-start.9 = (bf16[4,4096]{1,0:T(4,128)(2,1)S(1)}, bf16[4,4096]{1,0:T(4,128)(2,1)}, u32[]{:S(2)}) copy-start(bf16[4,4096]{1,0:T(4,128)(2,1)} %refs_5_.7) | copy-start | bytes 98308
  2.5 2.6 %collective-permute-start.1 = (bf16[272,512]{1,0:T(8,128)(2,1)S(1)}, bf16[272,512]{1,0:T(8,128)(2,1)S(1)}, u32[]{:S(2)}, u32[]{:S(2)}) collective-permute-start(bf16[272,512]{1,0:T(8,128)(2,1)S(1)} %get-tuple-element.51), channel_id=1, source_target_pairs={{0,4},{1,5},{2,6},{3,7},{4,0},{5,1},{6,2},{7,3},{8,12},{9,13},{10,... | collective-permute-start | bytes 835592 | tf_op jit(solution)/shard_map/ppermute | solution.py:269
  5.1 8.0 %collective-permute-start.3 = (bf16[16,512]{1,0:T(8,128)(2,1)S(1)}, bf16[16,512]{1,0:T(8,128)(2,1)S(1)}, u32[]{:S(2)}, u32[]{:S(2)}) collective-permute-start(bf16[16,512]{1,0:T(8,128)(2,1)S(1)} %slice_select_fusion), channel_id=1, source_target_pairs={{24,0},{25,9},{26,18},{27,27},{28,4},{29,13},{30,22},{31,31}} | collective-permute-start | bytes 49160 | tf_op jit(solution)/shard_map/ppermute | solution.py:269
  6.4 6.7 %collective-permute-start.2 = (bf16[16,512]{1,0:T(8,128)(2,1)S(1)}, bf16[16,512]{1,0:T(8,128)(2,1)S(1)}, u32[]{:S(2)}, u32[]{:S(2)}) collective-permute-start(bf16[16,512]{1,0:T(8,128)(2,1)S(1)} %slice_select_fusion), channel_id=1, source_target_pairs={{0,8},{1,9},{2,10},{3,11},{4,12},{5,13},{6,14},{7,15},{8,16},{9,17... | collective-permute-start | bytes 49160 | tf_op jit(solution)/shard_map/ppermute | solution.py:269
  15.7 9.9 %collective-permute-start.4 = (bf16[288,256]{1,0:T(8,128)(2,1)S(1)}, bf16[288,256]{1,0:T(8,128)(2,1)S(1)}, u32[]{:S(2)}, u32[]{:S(2)}) collective-permute-start(bf16[288,256]{1,0:T(8,128)(2,1)S(1)} %get-tuple-element.62), channel_id=1, source_target_pairs={{0,1},{1,0},{2,3},{3,2},{4,5},{5,4},{6,7},{7,6},{8,9},{9,8},{10,11... | collective-permute-start | bytes 442376 | tf_op jit(solution)/shard_map/ppermute | solution.py:269
  17.1 9.9 %collective-permute-start.5 = (bf16[288,256]{1,0:T(8,128)(2,1)S(1)}, bf16[288,256]{1,0:T(8,128)(2,1)S(1)}, u32[]{:S(2)}, u32[]{:S(2)}) collective-permute-start(bf16[288,256]{1,0:T(8,128)(2,1)S(1)} %get-tuple-element.63), channel_id=1, source_target_pairs={{0,2},{1,3},{2,0},{3,1},{4,6},{5,7},{6,4},{7,5},{8,10},{9,11},{10,... | collective-permute-start | bytes 442376 | tf_op jit(solution)/shard_map/ppermute | solution.py:269
  18.0 6.1 %copy-start = (bf16[2,256,2048]{2,1,0:T(8,128)(2,1)S(1)}, bf16[2,256,2048]{2,1,0:T(8,128)(2,1)}, u32[]{:S(2)}) copy-start(bf16[2,256,2048]{2,1,0:T(8,128)(2,1)} %refs_1_.9) | copy-start | bytes 6291460
  18.0 9.0 %collective-permute-start.6 = (bf16[288,256]{1,0:T(8,128)(2,1)S(1)}, bf16[288,256]{1,0:T(8,128)(2,1)S(1)}, u32[]{:S(2)}, u32[]{:S(2)}) collective-permute-start(bf16[288,256]{1,0:T(8,128)(2,1)S(1)} %get-tuple-element.64), channel_id=1, source_target_pairs={{0,3},{1,2},{2,1},{3,0},{4,7},{5,6},{6,5},{7,4},{8,11},{9,10},{10,... | collective-permute-start | bytes 442376 | tf_op jit(solution)/shard_map/ppermute | solution.py:269
  21.7 11.6 %collective-permute-start.8 = (bf16[256,256]{1,0:T(8,128)(2,1)S(1)}, bf16[256,256]{1,0:T(8,128)(2,1)S(1)}, u32[]{:S(2)}, u32[]{:S(2)}) collective-permute-start(bf16[256,256]{1,0:T(8,128)(2,1)S(1)} %get-tuple-element.74), channel_id=1, source_target_pairs={{0,1},{1,0},{2,3},{3,2},{4,5},{5,4},{6,7},{7,6},{8,9},{9,8},{10,11... | collective-permute-start | bytes 393224 | tf_op jit(solution)/shard_map/ppermute | solution.py:269
  23.1 10.2 %collective-permute-start.9 = (bf16[256,256]{1,0:T(8,128)(2,1)S(1)}, bf16[256,256]{1,0:T(8,128)(2,1)S(1)}, u32[]{:S(2)}, u32[]{:S(2)}) collective-permute-start(bf16[256,256]{1,0:T(8,128)(2,1)S(1)} %get-tuple-element.75), channel_id=1, source_target_pairs={{0,2},{1,3},{2,0},{3,1},{4,6},{5,7},{6,4},{7,5},{8,10},{9,11},{10,... | collective-permute-start | bytes 393224 | tf_op jit(solution)/shard_map/ppermute | solution.py:269
  25.6 3.5 %copy-start.6 = (bf16[2,256,2048]{2,1,0:T(8,128)(2,1)S(1)}, bf16[2,256,2048]{2,1,0:T(8,128)(2,1)}, u32[]{:S(2)}) copy-start(bf16[2,256,2048]{2,1,0:T(8,128)(2,1)} %refs_1_.12) | copy-start | bytes 6291460
  25.6 7.8 %collective-permute-start.10 = (bf16[256,256]{1,0:T(8,128)(2,1)S(1)}, bf16[256,256]{1,0:T(8,128)(2,1)S(1)}, u32[]{:S(2)}, u32[]{:S(2)}) collective-permute-start(bf16[256,256]{1,0:T(8,128)(2,1)S(1)} %get-tuple-element.76), channel_id=1, source_target_pairs={{0,3},{1,2},{2,1},{3,0},{4,7},{5,6},{6,5},{7,4},{8,11},{9,10},{10,... | collective-permute-start | bytes 393224 | tf_op jit(solution)/shard_map/ppermute | solution.py:269
  27.6 7.3 %collective-permute-start.7 = (bf16[2,272,256]{2,1,0:T(8,128)(2,1)S(1)}, bf16[2,272,256]{2,1,0:T(8,128)(2,1)S(1)}, u32[]{:S(2)}, u32[]{:S(2)}) collective-permute-start(bf16[2,272,256]{2,1,0:T(8,128)(2,1)S(1)} %get-tuple-element.66.refs_10_), channel_id=1, source_target_pairs={{0,8},{1,9},{2,10},{3,11},{4,12},{5,13},{6,14},{7,15},{8,0},{9,1},... | collective-permute-start | bytes 835592 | tf_op jit(solution)/shard_map/ppermute | solution.py:269
  34.2 8.9 %collective-permute-start.12 = (bf16[2,256,256]{2,1,0:T(8,128)(2,1)S(1)}, bf16[2,256,256]{2,1,0:T(8,128)(2,1)S(1)}, u32[]{:S(2)}, u32[]{:S(2)}) collective-permute-start(bf16[2,256,256]{2,1,0:T(8,128)(2,1)S(1)} %get-tuple-element.77.refs_3_.refs_4_), channel_id=1, source_target_pairs={{0,8},{1,9},{2,10},{3,11},{4,12},{5,13},{6,14},{7,15},{8,0},{9,1},... | collective-permute-start | bytes 786440 | tf_op jit(solution)/shard_map/ppermute | solution.py:269
  35.7 9.5 %collective-permute-start.11 = (bf16[1,272,256]{2,1,0:T(8,128)(2,1)S(1)}, bf16[1,272,256]{2,1,0:T(8,128)(2,1)S(1)}, u32[]{:S(2)}, u32[]{:S(2)}) collective-permute-start(bf16[1,272,256]{2,1,0:T(8,128)(2,1)S(1)} %get-tuple-element.79.refs_10_), channel_id=1, source_target_pairs={{0,16},{1,17},{2,18},{3,19},{4,20},{5,21},{6,22},{7,23},{8,24},{9,... | collective-permute-start | bytes 417800 | tf_op jit(solution)/shard_map/ppermute | solution.py:269
  43.7 5.9 %collective-permute-start.16 = (bf16[1,256,256]{2,1,0:T(8,128)(2,1)S(1)}, bf16[1,256,256]{2,1,0:T(8,128)(2,1)S(1)}, u32[]{:S(2)}, u32[]{:S(2)}) collective-permute-start(bf16[1,256,256]{2,1,0:T(8,128)(2,1)S(1)} %get-tuple-element.87.refs_3_.refs_4_), channel_id=1, source_target_pairs={{0,16},{1,17},{2,18},{3,19},{4,20},{5,21},{6,22},{7,23},{8,24},{9,... | collective-permute-start | bytes 393224 | tf_op jit(solution)/shard_map/ppermute | solution.py:269
  45.9 7.8 %collective-permute-start.15 = (bf16[256,256]{1,0:T(8,128)(2,1)S(1)}, bf16[256,256]{1,0:T(8,128)(2,1)S(1)}, u32[]{:S(2)}, u32[]{:S(2)}) collective-permute-start(bf16[256,256]{1,0:T(8,128)(2,1)S(1)} %get-tuple-element.88.refs_1_), channel_id=1, source_target_pairs={{0,3},{1,2},{2,1},{3,0},{4,7},{5,6},{6,5},{7,4},{8,11},{9,10},{10,... | collective-permute-start | bytes 393224 | tf_op jit(solution)/shard_map/ppermute | solution.py:269
  47.6 8.7 %collective-permute-start.14 = (bf16[256,256]{1,0:T(8,128)(2,1)S(1)}, bf16[256,256]{1,0:T(8,128)(2,1)S(1)}, u32[]{:S(2)}, u32[]{:S(2)}) collective-permute-start(bf16[256,256]{1,0:T(8,128)(2,1)S(1)} %get-tuple-element.88.refs_1_), channel_id=1, source_target_pairs={{0,2},{1,3},{2,0},{3,1},{4,6},{5,7},{6,4},{7,5},{8,10},{9,11},{10,... | collective-permute-start | bytes 393224 | tf_op jit(solution)/shard_map/ppermute | solution.py:269
  49.2 7.0 %collective-permute-start.13 = (bf16[256,256]{1,0:T(8,128)(2,1)S(1)}, bf16[256,256]{1,0:T(8,128)(2,1)S(1)}, u32[]{:S(2)}, u32[]{:S(2)}) collective-permute-start(bf16[256,256]{1,0:T(8,128)(2,1)S(1)} %get-tuple-element.88.refs_1_), channel_id=1, source_target_pairs={{0,1},{1,0},{2,3},{3,2},{4,5},{5,4},{6,7},{7,6},{8,9},{9,8},{10,11... | collective-permute-start | bytes 393224 | tf_op jit(solution)/shard_map/ppermute | solution.py:269
  50.3 7.6 %collective-permute-start.19 = (bf16[256,256]{1,0:T(8,128)(2,1)S(1)}, bf16[256,256]{1,0:T(8,128)(2,1)S(1)}, u32[]{:S(2)}, u32[]{:S(2)}) collective-permute-start(bf16[256,256]{1,0:T(8,128)(2,1)S(1)} %merge.7.refs_5_), channel_id=1, source_target_pairs={{0,3},{1,2},{2,1},{3,0},{4,7},{5,6},{6,5},{7,4},{8,11},{9,10},{10,... | collective-permute-start | bytes 393224 | tf_op jit(solution)/shard_map/ppermute | solution.py:269
  53.7 5.4 %collective-permute-start.18 = (bf16[256,256]{1,0:T(8,128)(2,1)S(1)}, bf16[256,256]{1,0:T(8,128)(2,1)S(1)}, u32[]{:S(2)}, u32[]{:S(2)}) collective-permute-start(bf16[256,256]{1,0:T(8,128)(2,1)S(1)} %merge.7.refs_5_), channel_id=1, source_target_pairs={{0,2},{1,3},{2,0},{3,1},{4,6},{5,7},{6,4},{7,5},{8,10},{9,11},{10,... | collective-permute-start | bytes 393224 | tf_op jit(solution)/shard_map/ppermute | solution.py:269
  53.7 5.9 %collective-permute-start.17 = (bf16[256,256]{1,0:T(8,128)(2,1)S(1)}, bf16[256,256]{1,0:T(8,128)(2,1)S(1)}, u32[]{:S(2)}, u32[]{:S(2)}) collective-permute-start(bf16[256,256]{1,0:T(8,128)(2,1)S(1)} %merge.7.refs_5_), channel_id=1, source_target_pairs={{0,1},{1,0},{2,3},{3,2},{4,5},{5,4},{6,7},{7,6},{8,9},{9,8},{10,11... | collective-permute-start | bytes 393224 | tf_op jit(solution)/shard_map/ppermute | solution.py:269
  (6 other events, 15.8 us)

commit v5 on v4

--- a/solution.py
+++ b/solution.py
@@ -297,13 +297,22 @@
     )
 
 
+def in_three(value):
+    high = value.astype(jnp.bfloat16)
+    rest = value - high.astype(jnp.float32)
+    mid = rest.astype(jnp.bfloat16)
+    low = (rest - mid.astype(jnp.float32)).astype(jnp.bfloat16)
+    return high, mid, low
+
+
 def softplus(value):
     return jnp.maximum(value, 0.0) + jnp.log1p(jnp.exp(-jnp.abs(value)))
 
 
 def group_of(decay, index, size):
     every = jnp.reshape(decay[...], (1, decay.shape[0]))
-    return pltpu.roll(every, decay.shape[0] - index * size, 1)[:, 0:size]
+    count = decay.shape[0]
+    return pltpu.roll(every, lax.rem(count - index * size, count), 1)[:, 0:size]
 
 
 def pack_kernel(
@@ -333,12 +342,13 @@
     ]
     for copy in copies:
         copy.start()
-    for copy in copies:
-        copy.wait()
+    copies[0].wait()
     dt = jnp.transpose(softplus(step_in[...]))
     high = dt.astype(jnp.bfloat16)
     low = (dt - high.astype(jnp.float32)).astype(jnp.bfloat16)
     swap_out[0:rows, STATE_WIDTH:pair] = jnp.concatenate([high, low] * (STATE_WIDTH // heads // 2), axis=1)
+    for copy in copies[1:4]:
+        copy.wait()
     edges = []
     for to in range(2):
         group = slice(to * STATE_WIDTH, (to + 1) * STATE_WIDTH)
@@ -350,6 +360,8 @@
         edges.append(jnp.concatenate(pieces, axis=0))
     swap_out[rows:] = jnp.where(core == 0, edges[1], edges[0]).astype(jnp.bfloat16)
     edge_out[...] = edges[1].astype(jnp.bfloat16)
+    for copy in copies[4:]:
+        copy.wait()
 
 
 def log_lanes(high, low):
@@ -389,8 +401,11 @@
     dt_other = parts[:, 0:heads] + parts[:, heads : 2 * heads]
     row = lax.broadcasted_iota(jnp.int32, (rows, rows), 0)
     col = lax.broadcasted_iota(jnp.int32, (rows, rows), 1)
-    later = (col > row).astype(jnp.float32)
-    after = contract(later, jnp.concatenate([dt_own, dt_other], axis=1), ((1,), (0,)), HIGHEST)
+    later = (col > row).astype(jnp.bfloat16)
+    both = jnp.concatenate([dt_own, dt_other], axis=1)
+    after = contract(later, jnp.concatenate(in_three(both), axis=1), ((1,), (0,)))
+    size = 2 * heads
+    after = after[:, 0:size] + after[:, size : 2 * size] + after[:, 2 * size :]
     sum_own = after[0:1, 0:heads] + dt_own[0:1]
     sum_other = after[0:1, heads:] + dt_other[0:1]
     after_own = after[:, 0:heads] + jnp.where(first_own, sum_other, 0.0)
@@ -422,7 +437,9 @@
     offset, parts, place, inner, other, near, taps, taps_b, weights, b_turned, b_first, logs, tail,
     *rest,
 ):
-    outs, handed, b_here = rest[:parts], rest[parts:-1], rest[-1]
+    outs, handed = rest[:parts], rest[parts]
+    patch = offset == 0
+    b_here = handed if patch else b_turned
     column, core = place[1], place[2]
     group = 2 * column + core
     first_own = core == 0
@@ -434,18 +451,19 @@
     state = b_turned.shape[0]
     w = weights[...].astype(jnp.bfloat16)
     before = jnp.where(place[0] == 0, 0.0, near[...].astype(jnp.float32))
-    blank = jnp.zeros((TAIL - 3, STATE_WIDTH), jnp.float32)
-    lead_b = jnp.concatenate([blank, before[3 * parts : 3 * parts + 3, 0:STATE_WIDTH]], axis=0)
-    taps_here = taps_b[:, pl.ds(pl.multiple_of(group * STATE_WIDTH, STATE_WIDTH), STATE_WIDTH)]
-    fresh = conv_rows(taps_here, lead_b, b_first[...])
-    fresh = jnp.transpose(jnp.concatenate([fresh, jnp.zeros((128 - TAIL, state), jnp.float32)], axis=0))
-    lane = lax.broadcasted_iota(jnp.int32, fresh.shape, 1)
-    for index, first in enumerate((core == 0, core == 1)):
-        at = index * rows
-        old = b_turned[:, at : at + 128].astype(jnp.float32)
-        patched = jnp.where(lane < jnp.where(first, CONV - 1, 0), fresh, old)
-        b_here[:, at : at + 128] = patched.astype(jnp.bfloat16)
-        b_here[:, at + 128 : at + rows] = b_turned[:, at + 128 : at + rows]
+    if patch:
+        blank = jnp.zeros((TAIL - 3, STATE_WIDTH), jnp.float32)
+        lead_b = jnp.concatenate([blank, before[3 * parts : 3 * parts + 3, 0:STATE_WIDTH]], axis=0)
+        taps_here = taps_b[:, pl.ds(pl.multiple_of(group * STATE_WIDTH, STATE_WIDTH), STATE_WIDTH)]
+        fresh = conv_rows(taps_here, lead_b, b_first[...])
+        fresh = jnp.transpose(jnp.concatenate([fresh, jnp.zeros((128 - TAIL, state), jnp.float32)], axis=0))
+        lane = lax.broadcasted_iota(jnp.int32, fresh.shape, 1)
+        for index, first in enumerate((core == 0, core == 1)):
+            at = index * rows
+            old = b_turned[:, at : at + 128].astype(jnp.float32)
+            patched = jnp.where(lane < jnp.where(first, CONV - 1, 0), fresh, old)
+            b_here[:, at : at + 128] = patched.astype(jnp.bfloat16)
+            b_here[:, at + 128 : at + rows] = b_turned[:, at + 128 : at + rows]
     blank = jnp.zeros((TAIL - 3, width), jnp.float32)
     for turn in range(parts):
         part = column ^ turn
@@ -477,8 +495,8 @@
             pieces = jnp.where(row == TAIL - 1, logs[0:1, at], pieces)
             outs[turn][state : state + TAIL] = pieces.astype(jnp.bfloat16)
             outs[turn][state + TAIL :] = tail[:, width:]
-    for out in handed:
-        out[...] = tail[...]
+    if not patch:
+        handed[...] = tail[...]
 
 
 def pick_kernel(count, place, after, *refs):
@@ -534,44 +552,49 @@
     slot, fetch, place, gate, step, decay, after,
     gate_out, factor_out, cum_out, turned_out, log_out, after_out, *rest,
 ):
-    width = 2 * STATE_WIDTH
+    rows, features = gate_out.shape
+    size = rows // 4
     copies = []
     if fetch:
         gate_in, sems = rest
         copies = [
             pltpu.make_async_copy(
-                gate.at[slot, :, at : at + width], gate_in.at[:, at : at + width], sems.at[index]
+                gate.at[slot, at : at + size], gate_in.at[at : at + size], sems.at[index]
             )
-            for index, at in enumerate(range(0, gate.shape[2], width))
+            for index, at in enumerate(range(0, rows, size))
         ]
     for copy in copies:
         copy.start()
     after_out[...] = after[...]
-    rows, features = gate_out.shape
     heads = step.shape[0]
     row = lax.broadcasted_iota(jnp.int32, (rows, rows), 0)
     col = lax.broadcasted_iota(jnp.int32, (rows, rows), 1)
     dt = softplus(step[:, slot])
     decay_row = jnp.broadcast_to(group_of(decay, place[3], heads), (8, heads))
     decay_col = jnp.transpose(decay_row)[:, 0:1]
-    before = (row <= col).astype(jnp.float32)
-    cum = contract(dt, before, ((1,), (0,)), HIGHEST) * (-LOG2E * jnp.exp(decay_col))
+    before = (row <= col).astype(jnp.bfloat16)
+    cum = contract(jnp.concatenate(in_three(dt), axis=0), before, ((1,), (0,)))
+    cum = cum[0:heads] + cum[heads : 2 * heads] + cum[2 * heads :]
+    cum = cum * (-LOG2E * jnp.exp(decay_col))
     log_dt = jnp.log(dt) * LOG2E
     cum_out[...] = cum - log_dt
     log_out[...] = log_dt
     turned = jnp.transpose(cum)
     turned_out[...] = turned
     decays = jnp.exp2(turned).astype(jnp.bfloat16)
-    for index, at in enumerate(range(0, features, width)):
-        cols = slice(at, at + width)
+    width = 2 * STATE_WIDTH
+    for index, top in enumerate(range(0, rows, size)):
         if fetch:
             copies[index].wait()
-        gate_here = gate_in[:, cols] if fetch else gate[slot, :, cols]
-        silu_gate = half_silu(gate_here.astype(jnp.float32))
-        gate_out[:, cols] = silu_gate.astype(jnp.bfloat16)
-        spread = spread_heads(at // HEAD_WIDTH, heads, width).astype(jnp.bfloat16)
-        decay_wide = contract(decays, spread, ((1,), (0,)))
-        factor_out[:, cols] = (decay_wide * silu_gate).astype(jnp.bfloat16)
+        here = slice(top, top + size)
+        for at in range(0, features, width):
+            cols = slice(at, at + width)
+            gate_here = gate_in[here, cols] if fetch else gate[slot, here, cols]
+            silu_gate = half_silu(gate_here.astype(jnp.float32))
+            gate_out[here, cols] = silu_gate.astype(jnp.bfloat16)
+            spread = spread_heads(at // HEAD_WIDTH, heads, width).astype(jnp.bfloat16)
+            decay_wide = contract(decays[here], spread, ((1,), (0,)))
+            factor_out[here, cols] = (decay_wide * silu_gate).astype(jnp.bfloat16)
 
 
 def completion_kernel(
@@ -647,62 +670,67 @@
         fixed_out[half:, cols] = (y_high * gates[half:, cols].astype(jnp.float32)).astype(jnp.bfloat16)
 
 
-def read_slot(parts, offset, column, slot, states, own_work, gated, slot_at):
+def read_slot(parts, steps, offset, column, slot, states, own_work, gated, slot_at):
     c_ref, fixed, factor = own_work[3 * slot : 3 * slot + 3]
     rows, features = fixed.shape
     part_width = features // parts
     width = states[0].shape[1]
     c = c_ref[...]
     total = jnp.zeros((rows, 128), jnp.float32)
-    for step in range(parts):
+    for index, step in enumerate(steps):
         start = (column ^ step) * part_width + offset
         cols = pl.ds(pl.multiple_of(start, 128), width)
-        read = contract(c, states[step][...], ((1,), (0,)))
+        read = contract(c, states[index][...], ((1,), (0,)))
         weight = factor[:, cols].astype(jnp.float32)
         value = fixed[:, cols].astype(jnp.float32) + read * weight
-        gated[slot_at, step] = value
+        gated[slot_at, index] = value
         square = value * value
         for lanes in range(0, width, 128):
             total = total + square[:, lanes : lanes + 128]
     return total
 
 
-def read_kernel(parts, offset, slots, place, *refs):
-    states, own_work, (gated, squares) = refs[:parts], refs[parts:-2], refs[-2:]
+def read_kernel(parts, steps, offset, slots, place, after, *refs):
+    states, own_work, (gated, squares) = refs[: len(steps)], refs[len(steps) : -2], refs[-2:]
     for slot in range(slots):
-        squares[slot] = read_slot(parts, offset, place[1], slot, states, own_work, gated, slot)
-
-
-def finish_kernel(parts, offsets, slots, place, live, gain, *refs):
-    chunks = len(offsets)
+        squares[slot] = read_slot(
+            parts, steps, offset, place[1], slot, states, own_work, gated, slot
+        )
+
+
+def finish_kernel(parts, groups, slots, place, live, gain, *refs):
     inputs, (out, gated, held, sems) = refs[:-4], refs[-4:]
-    earlier, inputs = inputs[: 2 * (chunks - 1)], inputs[2 * (chunks - 1) :]
-    states, own_work = inputs[:parts], inputs[parts:]
+    count = 2 * (len(groups) - 1)
+    earlier, inputs = inputs[:count], inputs[count:]
+    offset, steps = groups[-1]
+    states, own_work = inputs[: len(steps)], inputs[len(steps) :]
     column = place[1]
     slots, rows, features = held.shape
     part_width = features // parts
     copies = []
     for slot in range(slots):
-        total = read_slot(parts, offsets[-1], column, slot, states, own_work, gated, 0)
-        for chunk in range(chunks - 1):
-            total = total + earlier[2 * chunk + 1][slot]
+        total = read_slot(parts, steps, offset, column, slot, states, own_work, gated, 0)
+        for group in range(len(groups) - 1):
+            total = total + earlier[2 * group + 1][slot]
         scale = lax.rsqrt(jnp.sum(total, axis=1, keepdims=True) / features + EPS)
         alive = lax.broadcasted_iota(jnp.int32, (rows, 1), 0) < live[slot]
         scale = jnp.where(alive, scale, 0.0)
-        for step in range(parts):
-            for chunk, offset in enumerate(offsets):
-                last = chunk + 1 == chunks
-                values = gated if last else earlier[2 * chunk]
+        size = rows // parts
+        for block in range(parts):
+            here = slice(block * size, (block + 1) * size)
+            for group, (offset_here, steps_here) in enumerate(groups):
+                last = group + 1 == len(groups)
+                values = gated if last else earlier[2 * group]
                 width = values.shape[-1]
-                start = (column ^ step) * part_width + offset
-                cols = pl.ds(pl.multiple_of(start, 128), width)
-                gain_here = jnp.reshape(gain[cols], (1, width))
-                value = values[0 if last else slot, step]
-                held[slot, :, cols] = (value * scale * gain_here).astype(jnp.bfloat16)
-            part = pl.ds(pl.multiple_of((column ^ step) * part_width, part_width), part_width)
+                for index, step in enumerate(steps_here):
+                    start = (column ^ step) * part_width + offset_here
+                    cols = pl.ds(pl.multiple_of(start, 128), width)
+                    gain_here = jnp.reshape(gain[cols], (1, width))
+                    value = values[0 if last else slot, index, here]
+                    held[slot, here, cols] = (value * scale[here] * gain_here).astype(jnp.bfloat16)
             copies.append(
                 pltpu.make_async_copy(
-                    held.at[slot, :, part], out.at[slot, :, part], sems.at[slot * parts + step]
+                    held.at[slot, here], out.at[slot, here], sems.at[slot * parts + block]
                 )
             )
             copies[-1].start()
@@ -788,7 +816,7 @@
             spaces=[pltpu.HBM if fetch else pltpu.VMEM] + [pltpu.VMEM] * 3,
             scratch=[
                 pltpu.VMEM((positions, features), bf16),
-                pltpu.SemaphoreType.DMA((features // pair_width,)),
+                pltpu.SemaphoreType.DMA((4,)),
             ]
             * fetch,
         )
@@ -822,14 +850,16 @@
             lambda *refs, offset=offsets[chunk]: prompt_state_kernel(offset, parts, *refs),
             "prompt_state",
             (place,),
-            (spread,) * parts + (edge,) * (chunk + 1 == len(widths)),
+            (spread,) * parts
+            + (edge if chunk else jax.ShapeDtypeStruct((STATE_WIDTH, 2 * rows), bf16),),
             (
                 prompt_inner, other_inner, near, conv_inner, conv_proj, weights, b_turned, b_first,
                 logs, far,
             ),
-            scratch=[pltpu.VMEM((STATE_WIDTH, 2 * rows), bf16)],
-        )
-        if chunk + 1 == len(widths):
+        )
+        if chunk == 0:
+            b_turned = sent[parts]
+        else:
             *prepared[0], handed = prepare(0, sent[parts], False)
         held = [sent[0]] + [
             routed(sent[step], lambda z, k, c: (z, k, c ^ step)) for step in range(1, parts)
@@ -921,27 +951,37 @@
     while work:
         after = do_work(after)
     own_work = [array for three in finished for array in three]
+    every = tuple(range(parts))
+    groups = [(chunk, every) for chunk in range(len(widths) - 1)]
+    groups.append((len(widths) - 1, every))
     earlier = []
-    for chunk, width in enumerate(widths[:-1]):
+    for chunk, steps in groups[:-1]:
         earlier += run_whole(
-            lambda *refs, offset=offsets[chunk]: read_kernel(parts, offset, slots, *refs),
+            lambda *refs, steps=steps, offset=offsets[chunk]: read_kernel(
+                parts, steps, offset, slots, *refs
+            ),
             "read",
             (place,),
             (
-                jax.ShapeDtypeStruct((slots, parts, positions, width), f32),
+                jax.ShapeDtypeStruct((slots, len(steps), positions, widths[chunk]), f32),
                 jax.ShapeDtypeStruct((slots, positions, 128), f32),
             ),
-            joined[chunk] + own_work,
-        )
+            [earlier[-1] if earlier else joined[chunk][0]]
+            + [joined[chunk][step] for step in steps]
+            + own_work,
+            spaces=[pl.ANY] + [pltpu.VMEM] * (len(steps) + len(own_work)),
+        )
+    chunk, steps = groups[-1]
+    groups = [(offsets[chunk], steps) for chunk, steps in groups]
     return run_whole(
-        lambda *refs: finish_kernel(parts, offsets, slots, *refs),
+        lambda *refs: finish_kernel(parts, groups, slots, *refs),
         "finish",
         (place, sample_length),
         jax.ShapeDtypeStruct((slots, positions, features), bf16),
-        [norm_gain] + earlier + joined[-1] + own_work,
+        [norm_gain] + earlier + [joined[chunk][step] for step in steps] + own_work,
         out_spaces=pltpu.HBM,
         scratch=[
-            pltpu.VMEM((1, parts, positions, widths[-1]), f32),
+            pltpu.VMEM((1, len(steps), positions, widths[-1]), f32),
             pltpu.VMEM((slots, positions, features), bf16),
             pltpu.SemaphoreType.DMA((slots * parts,)),
         ],

time: 62.7 us -> 62.3 us (level)
  no operation moved by 1% of the time
where the time goes in v5:
time: 62.3 us; the launch traced here: 62.1 us
  Pallas kernels  28.6 us (46%)
  starting transfers between devices  27.3 us (44%)
  waiting for transfers between devices  5.56 us (9%)
    pallas_call x16, Pallas kernels, run_whole(): pl.pallas_call(kernel, out_shape=out_shape, in_specs=[pl.BlockSpec(memory...  28.6 us
    ppermute x20, starting transfers between devices, routed(): return lax.ppermute(block, AXES, pairs)  27.3 us
    ppermute x20, waiting for transfers between devices, routed(): return lax.ppermute(block, AXES, pairs)  5.56 us
  transfers between devices with their start and end apart: 20, of which 6 were waited for; matrix products, arithmetic and copies ran while one was open for 0% of the time, Pallas kernels for 38%

profile of v5, /device:TPU:0, one launch (start us, length us, event | category | flops | bytes accessed | tf_op | source)
XLA Modules:
  0.0 62.1 jit_solution(13373114407999834831)
XLA Ops:
  0.5 1.7 %pack.1 = (bf16[272,512]{1,0:T(8,128)(2,1)S(1)}, bf16[16,512]{1,0:T(8,128)(2,1)S(1)}, bf16[256,256]{1,0:T(8,128)(2,1)S(1)}) custom-call(s32[4]{0:T(128)S(1)} %pad_add_fusion.place.refs_0_, bf16[256,4096]{1,0:T(8,128)(2,1)} %refs_1_.9, bf16[256,4096]{1,0:T(8,128)(2,1)} %proj.1, f32[64,256]{1,0:T(8,128)} %step.3), custom_call_target="tpu_custom_call" | custom-call | flops 2000000000 | bytes 6000000 | tf_op jit(solution)/shard_map/pack/pallas_call | solution.py:997
  2.4 2.4 %prepare.2 = (bf16[256,2048]{1,0:T(8,128)(2,1)S(1)}, bf16[256,2048]{1,0:T(8,128)(2,1)S(1)}, f32[32,256]{1,0:T(8,128)S(1)}, f32[256,32]{1,0:T(8,128)S(1)}, f32[32...) custom-call(s32[4]{0:T(128)S(1)} %pad_add_fusion.place.refs_0_, bf16[2,256,2048]{2,1,0:T(8,128)(2,1)} %refs_1_.10, ...), custom_call_target="tpu_custom_call" | custom-call | tf_op jit(solution)/shard_map/prepare/pallas_call | solution.py:997
  4.8 1.3 %collective-permute-start.3 = (bf16[16,512]{1,0:T(8,128)(2,1)S(1)}, bf16[16,512]{1,0:T(8,128)(2,1)S(1)}, u32[]{:S(2)}, u32[]{:S(2)}) collective-permute-start(bf16[16,512]{1,0:T(8,128)(2,1)S(1)} %slice_select_fusion), channel_id=1, source_target_pairs={{24,0},{25,9},{26,18},{27,27},{28,4},{29,13},{30,22},{31,31}} | collective-permute-start | bytes 49160 | tf_op jit(solution)/shard_map/ppermute | solution.py:269
  6.1 4.3 %collective-permute-start.2 = (bf16[16,512]{1,0:T(8,128)(2,1)S(1)}, bf16[16,512]{1,0:T(8,128)(2,1)S(1)}, u32[]{:S(2)}, u32[]{:S(2)}) collective-permute-start(bf16[16,512]{1,0:T(8,128)(2,1)S(1)} %slice_select_fusion), channel_id=1, source_target_pairs={{0,8},{1,9},{2,10},{3,11},{4,12},{5,13},{6,14},{7,15},{8,16},{9,17... | collective-permute-start | bytes 49160 | tf_op jit(solution)/shard_map/ppermute | solution.py:269
  10.5 1.5 %prompt_weights.1 = (f32[512,32]{1,0:T(8,128)S(1)}, bf16[256,512]{1,0:T(8,128)(2,1)S(1)}, f32[8,1024]{1,0:T(8,128)S(1)}, bf16[16,256]{1,0:T(8,128)(2,1)S(1)}) custom-call(s32[4]{0:T(128)S(1)} %pad_add_fusion.place.refs_0_, bf16[256,256]{1,0:T(8,128)(2,1)S(1)} %get-tuple-element.55.own, bf16[272,512]{1,0:T(8,128)(2,1)S(1)} %collective-permute-done.1.other, ...), custom_call_target="tpu_custom_call" | custom-call | flops 2000000000 | bytes 6000000 | tf_op jit(solution)/shard_map/prompt_weights/pallas_call | solution.py:997
  12.9 2.5 %prompt_state.2 = (bf16[288,256]{1,0:T(8,128)(2,1)S(1)}, bf16[288,256]{1,0:T(8,128)(2,1)S(1)}, bf16[288,256]{1,0:T(8,128)(2,1)S(1)}, bf16[288,256]{1,0:T(8,128)(2,1)S(1)}, bf16[256,512]{1,0:T(8,128)(2,1)S(1)}) custom-call(s32[4]{0:T(128)S(1)} %pad_add_fusion.place.refs_0_, bf16[256,4096]{1,0:T(8,128)(2,1)S(1)} %copy-done.5, ...), custom_call_target="tpu_custom_call" | custom-call | flops 3000000000 | bytes 9000000 | tf_op jit(solution)/shard_map/prompt_state/pallas_call | solution.py:997
  15.4 1.3 %collective-permute-start.4 = (bf16[288,256]{1,0:T(8,128)(2,1)S(1)}, bf16[288,256]{1,0:T(8,128)(2,1)S(1)}, u32[]{:S(2)}, u32[]{:S(2)}) collective-permute-start(bf16[288,256]{1,0:T(8,128)(2,1)S(1)} %get-tuple-element.64), channel_id=1, source_target_pairs={{0,1},{1,0},{2,3},{3,2},{4,5},{5,4},{6,7},{7,6},{8,9},{9,8},{10,11... | collective-permute-start | bytes 442376 | tf_op jit(solution)/shard_map/ppermute | solution.py:269
  17.6 1.3 %collective-permute-start.6 = (bf16[288,256]{1,0:T(8,128)(2,1)S(1)}, bf16[288,256]{1,0:T(8,128)(2,1)S(1)}, u32[]{:S(2)}, u32[]{:S(2)}) collective-permute-start(bf16[288,256]{1,0:T(8,128)(2,1)S(1)} %get-tuple-element.66), channel_id=1, source_target_pairs={{0,3},{1,2},{2,1},{3,0},{4,7},{5,6},{6,5},{7,4},{8,11},{9,10},{10,... | collective-permute-start | bytes 442376 | tf_op jit(solution)/shard_map/ppermute | solution.py:269
  19.0 2.5 %prompt_state.3 = (bf16[256,256]{1,0:T(8,128)(2,1)S(1)}, bf16[256,256]{1,0:T(8,128)(2,1)S(1)}, bf16[256,256]{1,0:T(8,128)(2,1)S(1)}, bf16[256,256]{1,0:T(8,128)(2,1)S(1)}, bf16[16,512]{1,0:T(8,128)(2,1)S(1)}) custom-call(s32[4]{0:T(128)S(1)} %pad_add_fusion.place.refs_0_, bf16[256,4096]{1,0:T(8,128)(2,1)S(1)} %copy-done.5, ...), custom_call_target="tpu_custom_call" | custom-call | flops 3000000000 | bytes 9000000 | tf_op jit(solution)/shard_map/prompt_state/pallas_call | solution.py:997
  21.5 1.3 %collective-permute-start.8 = (bf16[256,256]{1,0:T(8,128)(2,1)S(1)}, bf16[256,256]{1,0:T(8,128)(2,1)S(1)}, u32[]{:S(2)}, u32[]{:S(2)}) collective-permute-start(bf16[256,256]{1,0:T(8,128)(2,1)S(1)} %get-tuple-element.76), channel_id=1, source_target_pairs={{0,1},{1,0},{2,3},{3,2},{4,5},{5,4},{6,7},{7,6},{8,9},{9,8},{10,11... | collective-permute-start | bytes 393224 | tf_op jit(solution)/shard_map/ppermute | solution.py:269
  23.7 1.6 %prepare.3 = (bf16[256,2048]{1,0:T(8,128)(2,1)S(1)}, bf16[256,2048]{1,0:T(8,128)(2,1)S(1)}, f32[32,256]{1,0:T(8,128)S(1)}, f32[256,32]{1,0:T(8,128)S(1)}, f32[32...) custom-call(s32[4]{0:T(128)S(1)} %pad_add_fusion.place.refs_0_, bf16[2,256,2048]{2,1,0:T(8,128)(2,1)S(1)} %copy-done, ...), custom_call_target="tpu_custom_call" | custom-call | tf_op jit(solution)/shard_map/prepare/pallas_call | solution.py:997
  25.3 1.4 %collective-permute-start.10 = (bf16[256,256]{1,0:T(8,128)(2,1)S(1)}, bf16[256,256]{1,0:T(8,128)(2,1)S(1)}, u32[]{:S(2)}, u32[]{:S(2)}) collective-permute-start(bf16[256,256]{1,0:T(8,128)(2,1)S(1)} %get-tuple-element.78), channel_id=1, source_target_pairs={{0,3},{1,2},{2,1},{3,0},{4,7},{5,6},{6,5},{7,4},{8,11},{9,10},{10,... | collective-permute-start | bytes 393224 | tf_op jit(solution)/shard_map/ppermute | solution.py:269
  27.3 1.5 %collective-permute-start.7 = (bf16[2,272,256]{2,1,0:T(8,128)(2,1)S(1)}, bf16[2,272,256]{2,1,0:T(8,128)(2,1)S(1)}, u32[]{:S(2)}, u32[]{:S(2)}) collective-permute-start(bf16[2,272,256]{2,1,0:T(8,128)(2,1)S(1)} %get-tuple-element.68.refs_10_), channel_id=1, source_target_pairs={{0,8},{1,9},{2,10},{3,11},{4,12},{5,13},{6,14},{7,15},{8,0},{9,1},... | collective-permute-start | bytes 835592 | tf_op jit(solution)/shard_map/ppermute | solution.py:269
  28.8 4.3 %completion.2 = (bf16[256,2048]{1,0:T(8,128)(2,1)S(1)}, bf16[256,256]{1,0:T(8,128)(2,1)S(1)}) custom-call(s32[4]{0:T(128)S(1)} %pad_add_fusion.place.refs_0_, bf16[2,256,2048]{2,1,0:T(8,128)(2,1)S(1)} %copy-done.6, bf16[2,256,4096]{2,1,0:T(8,128)(2,1)} %refs_2_.8, bf16[16,512]{1,0:T(8,128)(2,1)S(1)} %get-tuple-element.69.refs_3_, ...), custom_call_target="tpu_custom_call" | custom-call | flops 4000000000 | bytes 12000000 | tf_op jit(solution)/shard_map/completion/pallas_call | solution.py:997
  35.4 3.1 %collective-permute-start.11 = (bf16[1,272,256]{2,1,0:T(8,128)(2,1)S(1)}, bf16[1,272,256]{2,1,0:T(8,128)(2,1)S(1)}, u32[]{:S(2)}, u32[]{:S(2)}) collective-permute-start(bf16[1,272,256]{2,1,0:T(8,128)(2,1)S(1)} %get-tuple-element.81.refs_10_), channel_id=1, source_target_pairs={{0,16},{1,17},{2,18},{3,19},{4,20},{5,21},{6,22},{7,23},{8,24},{9,... | collective-permute-start | bytes 417800 | tf_op jit(solution)/shard_map/ppermute | solution.py:269
  38.5 4.3 %completion.3 = (bf16[256,2048]{1,0:T(8,128)(2,1)S(1)}, bf16[256,256]{1,0:T(8,128)(2,1)S(1)}) custom-call(s32[4]{0:T(128)S(1)} %pad_add_fusion.place.refs_0_, bf16[2,256,2048]{2,1,0:T(8,128)(2,1)S(1)} %copy-done.6, bf16[2,256,4096]{2,1,0:T(8,128)(2,1)} %refs_2_.8, bf16[16,512]{1,0:T(8,128)(2,1)S(1)} %get-tuple-element.69.refs_3_, ...), custom_call_target="tpu_custom_call" | custom-call | flops 4000000000 | bytes 12000000 | tf_op jit(solution)/shard_map/completion/pallas_call | solution.py:997
  43.4 1.5 %collective-permute-start.16 = (bf16[1,256,256]{2,1,0:T(8,128)(2,1)S(1)}, bf16[1,256,256]{2,1,0:T(8,128)(2,1)S(1)}, u32[]{:S(2)}, u32[]{:S(2)}) collective-permute-start(bf16[1,256,256]{2,1,0:T(8,128)(2,1)S(1)} %get-tuple-element.89.refs_3_.refs_4_), channel_id=1, source_target_pairs={{0,16},{1,17},{2,18},{3,19},{4,20},{5,21},{6,22},{7,23},{8,24},{9,... | collective-permute-start | bytes 393224 | tf_op jit(solution)/shard_map/ppermute | solution.py:269
  45.7 1.6 %collective-permute-start.15 = (bf16[256,256]{1,0:T(8,128)(2,1)S(1)}, bf16[256,256]{1,0:T(8,128)(2,1)S(1)}, u32[]{:S(2)}, u32[]{:S(2)}) collective-permute-start(bf16[256,256]{1,0:T(8,128)(2,1)S(1)} %get-tuple-element.90.refs_1_.refs_2_), channel_id=1, source_target_pairs={{0,3},{1,2},{2,1},{3,0},{4,7},{5,6},{6,5},{7,4},{8,11},{9,10},{10,... | collective-permute-start | bytes 393224 | tf_op jit(solution)/shard_map/ppermute | solution.py:269
  47.3 1.6 %collective-permute-start.14 = (bf16[256,256]{1,0:T(8,128)(2,1)S(1)}, bf16[256,256]{1,0:T(8,128)(2,1)S(1)}, u32[]{:S(2)}, u32[]{:S(2)}) collective-permute-start(bf16[256,256]{1,0:T(8,128)(2,1)S(1)} %get-tuple-element.90.refs_1_.refs_2_), channel_id=1, source_target_pairs={{0,2},{1,3},{2,0},{3,1},{4,6},{5,7},{6,4},{7,5},{8,10},{9,11},{10,... | collective-permute-start | bytes 393224 | tf_op jit(solution)/shard_map/ppermute | solution.py:269
  50.0 2.0 %collective-permute-start.19 = (bf16[256,256]{1,0:T(8,128)(2,1)S(1)}, bf16[256,256]{1,0:T(8,128)(2,1)S(1)}, u32[]{:S(2)}, u32[]{:S(2)}) collective-permute-start(bf16[256,256]{1,0:T(8,128)(2,1)S(1)} %merge.7.refs_5_), channel_id=1, source_target_pairs={{0,3},{1,2},{2,1},{3,0},{4,7},{5,6},{6,5},{7,4},{8,11},{9,10},{10,... | collective-permute-start | bytes 393224 | tf_op jit(solution)/shard_map/ppermute | solution.py:269
  51.9 1.6 %collective-permute-start.18 = (bf16[256,256]{1,0:T(8,128)(2,1)S(1)}, bf16[256,256]{1,0:T(8,128)(2,1)S(1)}, u32[]{:S(2)}, u32[]{:S(2)}) collective-permute-start(bf16[256,256]{1,0:T(8,128)(2,1)S(1)} %merge.7.refs_5_), channel_id=1, source_target_pairs={{0,2},{1,3},{2,0},{3,1},{4,6},{5,7},{6,4},{7,5},{8,10},{9,11},{10,... | collective-permute-start | bytes 393224 | tf_op jit(solution)/shard_map/ppermute | solution.py:269
  53.7 2.3 %collective-permute-done.14.refs_4_ = bf16[256,256]{1,0:T(8,128)(2,1)S(1)} collective-permute-done((bf16[256,256]{1,0:T(8,128)(2,1)S(1)}, bf16[256,256]{1,0:T(8,128)(2,1)S(1)}, u32[]{:S(2)}, u32[]{:S(2)}) %collective-permute-start.14) | collective-permute-done | bytes 131104 | tf_op jit(solution)/shard_map/ppermute | solution.py:269
  56.0 1.1 %read.1 = (f32[2,4,256,256]{3,2,1,0:T(8,128)S(1)}, f32[2,256,128]{2,1,0:T(8,128)S(1)}) custom-call(s32[4]{0:T(128)S(1)} %pad_add_fusion.place.refs_0_, bf16[256,256]{1,0:T(8,128)(2,1)S(1)} %get-tuple-element.90.refs_1_.refs_2_, bf16[256,256]{1,0:T(8,128)(2,1)S(1)} %get-tuple-element.90.refs_1_.refs_2_, bf16[256,256]{1,0:T(8,128)(2,1)S(1)} %collective-permute-done.13.refs_3_, ...), custom_call_target="tpu_custom_call" | custom-call | flops 2000000000 | bytes 6000000 | tf_op jit(solution)/shard_map/read/pallas_call | solution.py:997
  59.3 2.6 %finish.1 = bf16[2,256,2048]{2,1,0:T(8,128)(2,1)} custom-call(s32[4]{0:T(128)S(1)} %pad_add_fusion.place.refs_0_, s32[2]{0:T(128)S(1)} %copy-done.4, f32[2048]{0:T(1024)S(1)} %copy-done.2, f32[2,4,256,256]{3,2,1,0:T(8,128)S(1)} %get-tuple-element.95.refs_3_, f32[2,256,128]{2,1,0:T(8,128)S(1)} %get-tuple-element.96.refs_4_, ...), custom_call_target="tpu_custom_call" | custom-call | flops 2000000000 | bytes 6000000 | tf_op jit(solution)/shard_map/finish/pallas_call | solution.py:997
  (54 shorter events, 11.1 us)
Async XLA Ops:
  0.0 12.9 %collective-permute-start = (bf16[256,4096]{1,0:T(8,128)(2,1)}, bf16[256,4096]{1,0:T(8,128)(2,1)S(1)}, u32[]{:S(2)}, u32[]{:S(2)}) collective-permute-start(bf16[256,4096]{1,0:T(8,128)(2,1)} %refs_1_.9), channel_id=1, source_target_pairs={{0,4},{1,5},{2,6},{3,7},{4,0},{5,1},{6,2},{7,3},{8,12},{9,13},{10,... | collective-permute-start | bytes 6291464 | tf_op jit(solution)/shard_map/ppermute | solution.py:269
  2.2 8.2 %copy-start.8 = (f32[64,256]{1,0:T(8,128)S(1)}, f32[64,256]{1,0:T(8,128)}, u32[]{:S(2)}) copy-start(f32[64,256]{1,0:T(8,128)} %step.3) | copy-start | bytes 196612
  2.2 8.2 %copy-start.9 = (bf16[4,4096]{1,0:T(4,128)(2,1)S(1)}, bf16[4,4096]{1,0:T(4,128)(2,1)}, u32[]{:S(2)}) copy-start(bf16[4,4096]{1,0:T(4,128)(2,1)} %refs_5_.7) | copy-start | bytes 98308
  2.3 2.5 %collective-permute-start.1 = (bf16[272,512]{1,0:T(8,128)(2,1)S(1)}, bf16[272,512]{1,0:T(8,128)(2,1)S(1)}, u32[]{:S(2)}, u32[]{:S(2)}) collective-permute-start(bf16[272,512]{1,0:T(8,128)(2,1)S(1)} %get-tuple-element.52), channel_id=1, source_target_pairs={{0,4},{1,5},{2,6},{3,7},{4,0},{5,1},{6,2},{7,3},{8,12},{9,13},{10,... | collective-permute-start | bytes 835592 | tf_op jit(solution)/shard_map/ppermute | solution.py:269
  4.8 8.0 %collective-permute-start.3 = (bf16[16,512]{1,0:T(8,128)(2,1)S(1)}, bf16[16,512]{1,0:T(8,128)(2,1)S(1)}, u32[]{:S(2)}, u32[]{:S(2)}) collective-permute-start(bf16[16,512]{1,0:T(8,128)(2,1)S(1)} %slice_select_fusion), channel_id=1, source_target_pairs={{24,0},{25,9},{26,18},{27,27},{28,4},{29,13},{30,22},{31,31}} | collective-permute-start | bytes 49160 | tf_op jit(solution)/shard_map/ppermute | solution.py:269
  6.1 6.8 %collective-permute-start.2 = (bf16[16,512]{1,0:T(8,128)(2,1)S(1)}, bf16[16,512]{1,0:T(8,128)(2,1)S(1)}, u32[]{:S(2)}, u32[]{:S(2)}) collective-permute-start(bf16[16,512]{1,0:T(8,128)(2,1)S(1)} %slice_select_fusion), channel_id=1, source_target_pairs={{0,8},{1,9},{2,10},{3,11},{4,12},{5,13},{6,14},{7,15},{8,16},{9,17... | collective-permute-start | bytes 49160 | tf_op jit(solution)/shard_map/ppermute | solution.py:269
  15.4 9.9 %collective-permute-start.4 = (bf16[288,256]{1,0:T(8,128)(2,1)S(1)}, bf16[288,256]{1,0:T(8,128)(2,1)S(1)}, u32[]{:S(2)}, u32[]{:S(2)}) collective-permute-start(bf16[288,256]{1,0:T(8,128)(2,1)S(1)} %get-tuple-element.64), channel_id=1, source_target_pairs={{0,1},{1,0},{2,3},{3,2},{4,5},{5,4},{6,7},{7,6},{8,9},{9,8},{10,11... | collective-permute-start | bytes 442376 | tf_op jit(solution)/shard_map/ppermute | solution.py:269
  16.7 9.9 %collective-permute-start.5 = (bf16[288,256]{1,0:T(8,128)(2,1)S(1)}, bf16[288,256]{1,0:T(8,128)(2,1)S(1)}, u32[]{:S(2)}, u32[]{:S(2)}) collective-permute-start(bf16[288,256]{1,0:T(8,128)(2,1)S(1)} %get-tuple-element.65), channel_id=1, source_target_pairs={{0,2},{1,3},{2,0},{3,1},{4,6},{5,7},{6,4},{7,5},{8,10},{9,11},{10,... | collective-permute-start | bytes 442376 | tf_op jit(solution)/shard_map/ppermute | solution.py:269
  17.6 9.0 %collective-permute-start.6 = (bf16[288,256]{1,0:T(8,128)(2,1)S(1)}, bf16[288,256]{1,0:T(8,128)(2,1)S(1)}, u32[]{:S(2)}, u32[]{:S(2)}) collective-permute-start(bf16[288,256]{1,0:T(8,128)(2,1)S(1)} %get-tuple-element.66), channel_id=1, source_target_pairs={{0,3},{1,2},{2,1},{3,0},{4,7},{5,6},{6,5},{7,4},{8,11},{9,10},{10,... | collective-permute-start | bytes 442376 | tf_op jit(solution)/shard_map/ppermute | solution.py:269
  19.0 4.7 %copy-start = (bf16[2,256,2048]{2,1,0:T(8,128)(2,1)S(1)}, bf16[2,256,2048]{2,1,0:T(8,128)(2,1)}, u32[]{:S(2)}) copy-start(bf16[2,256,2048]{2,1,0:T(8,128)(2,1)} %refs_1_.10) | copy-start | bytes 6291460
  21.5 11.6 %collective-permute-start.8 = (bf16[256,256]{1,0:T(8,128)(2,1)S(1)}, bf16[256,256]{1,0:T(8,128)(2,1)S(1)}, u32[]{:S(2)}, u32[]{:S(2)}) collective-permute-start(bf16[256,256]{1,0:T(8,128)(2,1)S(1)} %get-tuple-element.76), channel_id=1, source_target_pairs={{0,1},{1,0},{2,3},{3,2},{4,5},{5,4},{6,7},{7,6},{8,9},{9,8},{10,11... | collective-permute-start | bytes 393224 | tf_op jit(solution)/shard_map/ppermute | solution.py:269
  22.8 10.3 %collective-permute-start.9 = (bf16[256,256]{1,0:T(8,128)(2,1)S(1)}, bf16[256,256]{1,0:T(8,128)(2,1)S(1)}, u32[]{:S(2)}, u32[]{:S(2)}) collective-permute-start(bf16[256,256]{1,0:T(8,128)(2,1)S(1)} %get-tuple-element.77), channel_id=1, source_target_pairs={{0,2},{1,3},{2,0},{3,1},{4,6},{5,7},{6,4},{7,5},{8,10},{9,11},{10,... | collective-permute-start | bytes 393224 | tf_op jit(solution)/shard_map/ppermute | solution.py:269
  25.2 3.5 %copy-start.6 = (bf16[2,256,2048]{2,1,0:T(8,128)(2,1)S(1)}, bf16[2,256,2048]{2,1,0:T(8,128)(2,1)}, u32[]{:S(2)}) copy-start(bf16[2,256,2048]{2,1,0:T(8,128)(2,1)} %refs_1_.12) | copy-start | bytes 6291460
  25.3 7.8 %collective-permute-start.10 = (bf16[256,256]{1,0:T(8,128)(2,1)S(1)}, bf16[256,256]{1,0:T(8,128)(2,1)S(1)}, u32[]{:S(2)}, u32[]{:S(2)}) collective-permute-start(bf16[256,256]{1,0:T(8,128)(2,1)S(1)} %get-tuple-element.78), channel_id=1, source_target_pairs={{0,3},{1,2},{2,1},{3,0},{4,7},{5,6},{6,5},{7,4},{8,11},{9,10},{10,... | collective-permute-start | bytes 393224 | tf_op jit(solution)/shard_map/ppermute | solution.py:269
  27.3 7.3 %collective-permute-start.7 = (bf16[2,272,256]{2,1,0:T(8,128)(2,1)S(1)}, bf16[2,272,256]{2,1,0:T(8,128)(2,1)S(1)}, u32[]{:S(2)}, u32[]{:S(2)}) collective-permute-start(bf16[2,272,256]{2,1,0:T(8,128)(2,1)S(1)} %get-tuple-element.68.refs_10_), channel_id=1, source_target_pairs={{0,8},{1,9},{2,10},{3,11},{4,12},{5,13},{6,14},{7,15},{8,0},{9,1},... | collective-permute-start | bytes 835592 | tf_op jit(solution)/shard_map/ppermute | solution.py:269
  33.9 8.9 %collective-permute-start.12 = (bf16[2,256,256]{2,1,0:T(8,128)(2,1)S(1)}, bf16[2,256,256]{2,1,0:T(8,128)(2,1)S(1)}, u32[]{:S(2)}, u32[]{:S(2)}) collective-permute-start(bf16[2,256,256]{2,1,0:T(8,128)(2,1)S(1)} %get-tuple-element.79.refs_3_.refs_4_), channel_id=1, source_target_pairs={{0,8},{1,9},{2,10},{3,11},{4,12},{5,13},{6,14},{7,15},{8,0},{9,1},... | collective-permute-start | bytes 786440 | tf_op jit(solution)/shard_map/ppermute | solution.py:269
  35.4 9.5 %collective-permute-start.11 = (bf16[1,272,256]{2,1,0:T(8,128)(2,1)S(1)}, bf16[1,272,256]{2,1,0:T(8,128)(2,1)S(1)}, u32[]{:S(2)}, u32[]{:S(2)}) collective-permute-start(bf16[1,272,256]{2,1,0:T(8,128)(2,1)S(1)} %get-tuple-element.81.refs_10_), channel_id=1, source_target_pairs={{0,16},{1,17},{2,18},{3,19},{4,20},{5,21},{6,22},{7,23},{8,24},{9,... | collective-permute-start | bytes 417800 | tf_op jit(solution)/shard_map/ppermute | solution.py:269
  43.4 5.9 %collective-permute-start.16 = (bf16[1,256,256]{2,1,0:T(8,128)(2,1)S(1)}, bf16[1,256,256]{2,1,0:T(8,128)(2,1)S(1)}, u32[]{:S(2)}, u32[]{:S(2)}) collective-permute-start(bf16[1,256,256]{2,1,0:T(8,128)(2,1)S(1)} %get-tuple-element.89.refs_3_.refs_4_), channel_id=1, source_target_pairs={{0,16},{1,17},{2,18},{3,19},{4,20},{5,21},{6,22},{7,23},{8,24},{9,... | collective-permute-start | bytes 393224 | tf_op jit(solution)/shard_map/ppermute | solution.py:269
  45.7 7.9 %collective-permute-start.15 = (bf16[256,256]{1,0:T(8,128)(2,1)S(1)}, bf16[256,256]{1,0:T(8,128)(2,1)S(1)}, u32[]{:S(2)}, u32[]{:S(2)}) collective-permute-start(bf16[256,256]{1,0:T(8,128)(2,1)S(1)} %get-tuple-element.90.refs_1_.refs_2_), channel_id=1, source_target_pairs={{0,3},{1,2},{2,1},{3,0},{4,7},{5,6},{6,5},{7,4},{8,11},{9,10},{10,... | collective-permute-start | bytes 393224 | tf_op jit(solution)/shard_map/ppermute | solution.py:269
  47.3 8.7 %collective-permute-start.14 = (bf16[256,256]{1,0:T(8,128)(2,1)S(1)}, bf16[256,256]{1,0:T(8,128)(2,1)S(1)}, u32[]{:S(2)}, u32[]{:S(2)}) collective-permute-start(bf16[256,256]{1,0:T(8,128)(2,1)S(1)} %get-tuple-element.90.refs_1_.refs_2_), channel_id=1, source_target_pairs={{0,2},{1,3},{2,0},{3,1},{4,6},{5,7},{6,4},{7,5},{8,10},{9,11},{10,... | collective-permute-start | bytes 393224 | tf_op jit(solution)/shard_map/ppermute | solution.py:269
  48.9 7.0 %collective-permute-start.13 = (bf16[256,256]{1,0:T(8,128)(2,1)S(1)}, bf16[256,256]{1,0:T(8,128)(2,1)S(1)}, u32[]{:S(2)}, u32[]{:S(2)}) collective-permute-start(bf16[256,256]{1,0:T(8,128)(2,1)S(1)} %get-tuple-element.90.refs_1_.refs_2_), channel_id=1, source_target_pairs={{0,1},{1,0},{2,3},{3,2},{4,5},{5,4},{6,7},{7,6},{8,9},{9,8},{10,11... | collective-permute-start | bytes 393224 | tf_op jit(solution)/shard_map/ppermute | solution.py:269
  50.0 7.7 %collective-permute-start.19 = (bf16[256,256]{1,0:T(8,128)(2,1)S(1)}, bf16[256,256]{1,0:T(8,128)(2,1)S(1)}, u32[]{:S(2)}, u32[]{:S(2)}) collective-permute-start(bf16[256,256]{1,0:T(8,128)(2,1)S(1)} %merge.7.refs_5_), channel_id=1, source_target_pairs={{0,3},{1,2},{2,1},{3,0},{4,7},{5,6},{6,5},{7,4},{8,11},{9,10},{10,... | collective-permute-start | bytes 393224 | tf_op jit(solution)/shard_map/ppermute | solution.py:269
  51.9 6.7 %collective-permute-start.18 = (bf16[256,256]{1,0:T(8,128)(2,1)S(1)}, bf16[256,256]{1,0:T(8,128)(2,1)S(1)}, u32[]{:S(2)}, u32[]{:S(2)}) collective-permute-start(bf16[256,256]{1,0:T(8,128)(2,1)S(1)} %merge.7.refs_5_), channel_id=1, source_target_pairs={{0,2},{1,3},{2,0},{3,1},{4,6},{5,7},{6,4},{7,5},{8,10},{9,11},{10,... | collective-permute-start | bytes 393224 | tf_op jit(solution)/shard_map/ppermute | solution.py:269
  53.6 5.8 %collective-permute-start.17 = (bf16[256,256]{1,0:T(8,128)(2,1)S(1)}, bf16[256,256]{1,0:T(8,128)(2,1)S(1)}, u32[]{:S(2)}, u32[]{:S(2)}) collective-permute-start(bf16[256,256]{1,0:T(8,128)(2,1)S(1)} %merge.7.refs_5_), channel_id=1, source_target_pairs={{0,1},{1,0},{2,3},{3,2},{4,5},{5,4},{6,7},{7,6},{8,9},{9,8},{10,11... | collective-permute-start | bytes 393224 | tf_op jit(solution)/shard_map/ppermute | solution.py:269
  (6 other events, 15.3 us)

commit v6 on v5

--- a/solution.py
+++ b/solution.py
@@ -269,12 +269,12 @@
     return lax.ppermute(block, AXES, pairs)
 
 
-def half_silu(value):
-    return 0.5 * value * (1.0 + jnp.tanh(0.5 * value))
+def silu_of_twice(half):
+    return half + half * jnp.tanh(half)
 
 
 def conv_rows(taps, lead, block):
-    wide = taps.astype(jnp.float32)
+    wide = 0.5 * taps.astype(jnp.float32)
     rows = block.astype(jnp.float32)
     edge = jnp.concatenate([lead.astype(jnp.float32)[TAIL - 8 :], rows[0:8]], axis=0)
     total = wide[CONV - 1 : CONV] * rows
@@ -282,7 +282,7 @@
         shifted = pltpu.roll(rows, back, 0)
         shifted = jnp.concatenate([edge[8 - back : 16 - back], shifted[8:]], axis=0)
         total = total + wide[CONV - 1 - back : CONV - back] * shifted
-    return half_silu(total)
+    return silu_of_twice(total)
 
 
 def spread_heads(first, heads, width):
@@ -590,7 +590,7 @@
         for at in range(0, features, width):
             cols = slice(at, at + width)
             gate_here = gate_in[here, cols] if fetch else gate[slot, here, cols]
-            silu_gate = half_silu(gate_here.astype(jnp.float32))
+            silu_gate = silu_of_twice(0.5 * gate_here.astype(jnp.float32))
             gate_out[here, cols] = silu_gate.astype(jnp.bfloat16)
             spread = spread_heads(at // HEAD_WIDTH, heads, width).astype(jnp.bfloat16)
             decay_wide = contract(decays[here], spread, ((1,), (0,)))

time: 62.3 us -> 62.1 us (level)
  transfers between devices with their start and end apart: 20 -> 20, of which waited for: 6 -> 6; matrix products, arithmetic and copies ran while one was open for 0% -> 0% of each run, Pallas kernels for 38% -> 37%
where the time goes in v6:
time: 62.1 us; the launch traced here: 61.9 us
  Pallas kernels  28.2 us (45%)
  starting transfers between devices  27.6 us (44%)
  waiting for transfers between devices  5.49 us (9%)
    pallas_call x16, Pallas kernels, run_whole(): pl.pallas_call(kernel, out_shape=out_shape, in_specs=[pl.BlockSpec(memory...  28.2 us
    ppermute x20, starting transfers between devices, routed(): return lax.ppermute(block, AXES, pairs)  27.6 us
    ppermute x20, waiting for transfers between devices, routed(): return lax.ppermute(block, AXES, pairs)  5.49 us
  transfers between devices with their start and end apart: 20, of which 6 were waited for; matrix products, arithmetic and copies ran while one was open for 0% of the time, Pallas kernels for 37%

profile of v6, /device:TPU:0, one launch (start us, length us, event | category | flops | bytes accessed | tf_op | source)
XLA Modules:
  0.0 61.9 jit_solution(14265151394842889731)
XLA Ops:
  0.5 1.7 %pack.1 = (bf16[272,512]{1,0:T(8,128)(2,1)S(1)}, bf16[16,512]{1,0:T(8,128)(2,1)S(1)}, bf16[256,256]{1,0:T(8,128)(2,1)S(1)}) custom-call(s32[4]{0:T(128)S(1)} %pad_add_fusion.place.refs_0_, bf16[256,4096]{1,0:T(8,128)(2,1)} %refs_1_.9, bf16[256,4096]{1,0:T(8,128)(2,1)} %proj.1, f32[64,256]{1,0:T(8,128)} %step.3), custom_call_target="tpu_custom_call" | custom-call | flops 2000000000 | bytes 6000000 | tf_op jit(solution)/shard_map/pack/pallas_call | solution.py:997
  2.4 2.4 %prepare.2 = (bf16[256,2048]{1,0:T(8,128)(2,1)S(1)}, bf16[256,2048]{1,0:T(8,128)(2,1)S(1)}, f32[32,256]{1,0:T(8,128)S(1)}, f32[256,32]{1,0:T(8,128)S(1)}, f32[32...) custom-call(s32[4]{0:T(128)S(1)} %pad_add_fusion.place.refs_0_, bf16[2,256,2048]{2,1,0:T(8,128)(2,1)} %refs_1_.10, ...), custom_call_target="tpu_custom_call" | custom-call | tf_op jit(solution)/shard_map/prepare/pallas_call | solution.py:997
  4.8 1.3 %collective-permute-start.3 = (bf16[16,512]{1,0:T(8,128)(2,1)S(1)}, bf16[16,512]{1,0:T(8,128)(2,1)S(1)}, u32[]{:S(2)}, u32[]{:S(2)}) collective-permute-start(bf16[16,512]{1,0:T(8,128)(2,1)S(1)} %slice_select_fusion), channel_id=1, source_target_pairs={{24,0},{25,9},{26,18},{27,27},{28,4},{29,13},{30,22},{31,31}} | collective-permute-start | bytes 49160 | tf_op jit(solution)/shard_map/ppermute | solution.py:269
  6.1 4.3 %collective-permute-start.2 = (bf16[16,512]{1,0:T(8,128)(2,1)S(1)}, bf16[16,512]{1,0:T(8,128)(2,1)S(1)}, u32[]{:S(2)}, u32[]{:S(2)}) collective-permute-start(bf16[16,512]{1,0:T(8,128)(2,1)S(1)} %slice_select_fusion), channel_id=1, source_target_pairs={{0,8},{1,9},{2,10},{3,11},{4,12},{5,13},{6,14},{7,15},{8,16},{9,17... | collective-permute-start | bytes 49160 | tf_op jit(solution)/shard_map/ppermute | solution.py:269
  10.5 1.5 %prompt_weights.1 = (f32[512,32]{1,0:T(8,128)S(1)}, bf16[256,512]{1,0:T(8,128)(2,1)S(1)}, f32[8,1024]{1,0:T(8,128)S(1)}, bf16[16,256]{1,0:T(8,128)(2,1)S(1)}) custom-call(s32[4]{0:T(128)S(1)} %pad_add_fusion.place.refs_0_, bf16[256,256]{1,0:T(8,128)(2,1)S(1)} %get-tuple-element.55.own, bf16[272,512]{1,0:T(8,128)(2,1)S(1)} %collective-permute-done.1.other, ...), custom_call_target="tpu_custom_call" | custom-call | flops 2000000000 | bytes 6000000 | tf_op jit(solution)/shard_map/prompt_weights/pallas_call | solution.py:997
  12.9 2.4 %prompt_state.2 = (bf16[288,256]{1,0:T(8,128)(2,1)S(1)}, bf16[288,256]{1,0:T(8,128)(2,1)S(1)}, bf16[288,256]{1,0:T(8,128)(2,1)S(1)}, bf16[288,256]{1,0:T(8,128)(2,1)S(1)}, bf16[256,512]{1,0:T(8,128)(2,1)S(1)}) custom-call(s32[4]{0:T(128)S(1)} %pad_add_fusion.place.refs_0_, bf16[256,4096]{1,0:T(8,128)(2,1)S(1)} %copy-done.5, ...), custom_call_target="tpu_custom_call" | custom-call | flops 3000000000 | bytes 9000000 | tf_op jit(solution)/shard_map/prompt_state/pallas_call | solution.py:997
  15.3 1.3 %collective-permute-start.4 = (bf16[288,256]{1,0:T(8,128)(2,1)S(1)}, bf16[288,256]{1,0:T(8,128)(2,1)S(1)}, u32[]{:S(2)}, u32[]{:S(2)}) collective-permute-start(bf16[288,256]{1,0:T(8,128)(2,1)S(1)} %get-tuple-element.64), channel_id=1, source_target_pairs={{0,1},{1,0},{2,3},{3,2},{4,5},{5,4},{6,7},{7,6},{8,9},{9,8},{10,11... | collective-permute-start | bytes 442376 | tf_op jit(solution)/shard_map/ppermute | solution.py:269
  17.5 1.3 %collective-permute-start.6 = (bf16[288,256]{1,0:T(8,128)(2,1)S(1)}, bf16[288,256]{1,0:T(8,128)(2,1)S(1)}, u32[]{:S(2)}, u32[]{:S(2)}) collective-permute-start(bf16[288,256]{1,0:T(8,128)(2,1)S(1)} %get-tuple-element.66), channel_id=1, source_target_pairs={{0,3},{1,2},{2,1},{3,0},{4,7},{5,6},{6,5},{7,4},{8,11},{9,10},{10,... | collective-permute-start | bytes 442376 | tf_op jit(solution)/shard_map/ppermute | solution.py:269
  18.8 2.4 %prompt_state.3 = (bf16[256,256]{1,0:T(8,128)(2,1)S(1)}, bf16[256,256]{1,0:T(8,128)(2,1)S(1)}, bf16[256,256]{1,0:T(8,128)(2,1)S(1)}, bf16[256,256]{1,0:T(8,128)(2,1)S(1)}, bf16[16,512]{1,0:T(8,128)(2,1)S(1)}) custom-call(s32[4]{0:T(128)S(1)} %pad_add_fusion.place.refs_0_, bf16[256,4096]{1,0:T(8,128)(2,1)S(1)} %copy-done.5, ...), custom_call_target="tpu_custom_call" | custom-call | flops 3000000000 | bytes 9000000 | tf_op jit(solution)/shard_map/prompt_state/pallas_call | solution.py:997
  21.2 1.4 %collective-permute-start.8 = (bf16[256,256]{1,0:T(8,128)(2,1)S(1)}, bf16[256,256]{1,0:T(8,128)(2,1)S(1)}, u32[]{:S(2)}, u32[]{:S(2)}) collective-permute-start(bf16[256,256]{1,0:T(8,128)(2,1)S(1)} %get-tuple-element.76), channel_id=1, source_target_pairs={{0,1},{1,0},{2,3},{3,2},{4,5},{5,4},{6,7},{7,6},{8,9},{9,8},{10,11... | collective-permute-start | bytes 393224 | tf_op jit(solution)/shard_map/ppermute | solution.py:269
  23.5 1.6 %prepare.3 = (bf16[256,2048]{1,0:T(8,128)(2,1)S(1)}, bf16[256,2048]{1,0:T(8,128)(2,1)S(1)}, f32[32,256]{1,0:T(8,128)S(1)}, f32[256,32]{1,0:T(8,128)S(1)}, f32[32...) custom-call(s32[4]{0:T(128)S(1)} %pad_add_fusion.place.refs_0_, bf16[2,256,2048]{2,1,0:T(8,128)(2,1)S(1)} %copy-done, ...), custom_call_target="tpu_custom_call" | custom-call | tf_op jit(solution)/shard_map/prepare/pallas_call | solution.py:997
  25.1 1.4 %collective-permute-start.10 = (bf16[256,256]{1,0:T(8,128)(2,1)S(1)}, bf16[256,256]{1,0:T(8,128)(2,1)S(1)}, u32[]{:S(2)}, u32[]{:S(2)}) collective-permute-start(bf16[256,256]{1,0:T(8,128)(2,1)S(1)} %get-tuple-element.78), channel_id=1, source_target_pairs={{0,3},{1,2},{2,1},{3,0},{4,7},{5,6},{6,5},{7,4},{8,11},{9,10},{10,... | collective-permute-start | bytes 393224 | tf_op jit(solution)/shard_map/ppermute | solution.py:269
  27.0 1.5 %collective-permute-start.7 = (bf16[2,272,256]{2,1,0:T(8,128)(2,1)S(1)}, bf16[2,272,256]{2,1,0:T(8,128)(2,1)S(1)}, u32[]{:S(2)}, u32[]{:S(2)}) collective-permute-start(bf16[2,272,256]{2,1,0:T(8,128)(2,1)S(1)} %get-tuple-element.68.refs_10_), channel_id=1, source_target_pairs={{0,8},{1,9},{2,10},{3,11},{4,12},{5,13},{6,14},{7,15},{8,0},{9,1},... | collective-permute-start | bytes 835592 | tf_op jit(solution)/shard_map/ppermute | solution.py:269
  28.6 4.1 %completion.2 = (bf16[256,2048]{1,0:T(8,128)(2,1)S(1)}, bf16[256,256]{1,0:T(8,128)(2,1)S(1)}) custom-call(s32[4]{0:T(128)S(1)} %pad_add_fusion.place.refs_0_, bf16[2,256,2048]{2,1,0:T(8,128)(2,1)S(1)} %copy-done.6, bf16[2,256,4096]{2,1,0:T(8,128)(2,1)} %refs_2_.8, bf16[16,512]{1,0:T(8,128)(2,1)S(1)} %get-tuple-element.69.refs_3_, ...), custom_call_target="tpu_custom_call" | custom-call | flops 4000000000 | bytes 12000000 | tf_op jit(solution)/shard_map/completion/pallas_call | solution.py:997
  35.0 3.3 %collective-permute-start.11 = (bf16[1,272,256]{2,1,0:T(8,128)(2,1)S(1)}, bf16[1,272,256]{2,1,0:T(8,128)(2,1)S(1)}, u32[]{:S(2)}, u32[]{:S(2)}) collective-permute-start(bf16[1,272,256]{2,1,0:T(8,128)(2,1)S(1)} %get-tuple-element.81.refs_10_), channel_id=1, source_target_pairs={{0,16},{1,17},{2,18},{3,19},{4,20},{5,21},{6,22},{7,23},{8,24},{9,... | collective-permute-start | bytes 417800 | tf_op jit(solution)/shard_map/ppermute | solution.py:269
  38.3 4.2 %completion.3 = (bf16[256,2048]{1,0:T(8,128)(2,1)S(1)}, bf16[256,256]{1,0:T(8,128)(2,1)S(1)}) custom-call(s32[4]{0:T(128)S(1)} %pad_add_fusion.place.refs_0_, bf16[2,256,2048]{2,1,0:T(8,128)(2,1)S(1)} %copy-done.6, bf16[2,256,4096]{2,1,0:T(8,128)(2,1)} %refs_2_.8, bf16[16,512]{1,0:T(8,128)(2,1)S(1)} %get-tuple-element.69.refs_3_, ...), custom_call_target="tpu_custom_call" | custom-call | flops 4000000000 | bytes 12000000 | tf_op jit(solution)/shard_map/completion/pallas_call | solution.py:997
  43.2 1.4 %collective-permute-start.16 = (bf16[1,256,256]{2,1,0:T(8,128)(2,1)S(1)}, bf16[1,256,256]{2,1,0:T(8,128)(2,1)S(1)}, u32[]{:S(2)}, u32[]{:S(2)}) collective-permute-start(bf16[1,256,256]{2,1,0:T(8,128)(2,1)S(1)} %get-tuple-element.89.refs_3_.refs_4_), channel_id=1, source_target_pairs={{0,16},{1,17},{2,18},{3,19},{4,20},{5,21},{6,22},{7,23},{8,24},{9,... | collective-permute-start | bytes 393224 | tf_op jit(solution)/shard_map/ppermute | solution.py:269
  45.3 1.7 %collective-permute-start.15 = (bf16[256,256]{1,0:T(8,128)(2,1)S(1)}, bf16[256,256]{1,0:T(8,128)(2,1)S(1)}, u32[]{:S(2)}, u32[]{:S(2)}) collective-permute-start(bf16[256,256]{1,0:T(8,128)(2,1)S(1)} %get-tuple-element.90.refs_1_.refs_2_), channel_id=1, source_target_pairs={{0,3},{1,2},{2,1},{3,0},{4,7},{5,6},{6,5},{7,4},{8,11},{9,10},{10,... | collective-permute-start | bytes 393224 | tf_op jit(solution)/shard_map/ppermute | solution.py:269
  47.1 1.6 %collective-permute-start.14 = (bf16[256,256]{1,0:T(8,128)(2,1)S(1)}, bf16[256,256]{1,0:T(8,128)(2,1)S(1)}, u32[]{:S(2)}, u32[]{:S(2)}) collective-permute-start(bf16[256,256]{1,0:T(8,128)(2,1)S(1)} %get-tuple-element.90.refs_1_.refs_2_), channel_id=1, source_target_pairs={{0,2},{1,3},{2,0},{3,1},{4,6},{5,7},{6,4},{7,5},{8,10},{9,11},{10,... | collective-permute-start | bytes 393224 | tf_op jit(solution)/shard_map/ppermute | solution.py:269
  49.7 1.9 %collective-permute-start.19 = (bf16[256,256]{1,0:T(8,128)(2,1)S(1)}, bf16[256,256]{1,0:T(8,128)(2,1)S(1)}, u32[]{:S(2)}, u32[]{:S(2)}) collective-permute-start(bf16[256,256]{1,0:T(8,128)(2,1)S(1)} %merge.7.refs_5_), channel_id=1, source_target_pairs={{0,3},{1,2},{2,1},{3,0},{4,7},{5,6},{6,5},{7,4},{8,11},{9,10},{10,... | collective-permute-start | bytes 393224 | tf_op jit(solution)/shard_map/ppermute | solution.py:269
  51.6 1.9 %collective-permute-start.18 = (bf16[256,256]{1,0:T(8,128)(2,1)S(1)}, bf16[256,256]{1,0:T(8,128)(2,1)S(1)}, u32[]{:S(2)}, u32[]{:S(2)}) collective-permute-start(bf16[256,256]{1,0:T(8,128)(2,1)S(1)} %merge.7.refs_5_), channel_id=1, source_target_pairs={{0,2},{1,3},{2,0},{3,1},{4,6},{5,7},{6,4},{7,5},{8,10},{9,11},{10,... | collective-permute-start | bytes 393224 | tf_op jit(solution)/shard_map/ppermute | solution.py:269
  53.6 1.9 %collective-permute-done.14.refs_4_ = bf16[256,256]{1,0:T(8,128)(2,1)S(1)} collective-permute-done((bf16[256,256]{1,0:T(8,128)(2,1)S(1)}, bf16[256,256]{1,0:T(8,128)(2,1)S(1)}, u32[]{:S(2)}, u32[]{:S(2)}) %collective-permute-start.14) | collective-permute-done | bytes 131104 | tf_op jit(solution)/shard_map/ppermute | solution.py:269
  55.5 1.1 %read.1 = (f32[2,4,256,256]{3,2,1,0:T(8,128)S(1)}, f32[2,256,128]{2,1,0:T(8,128)S(1)}) custom-call(s32[4]{0:T(128)S(1)} %pad_add_fusion.place.refs_0_, bf16[256,256]{1,0:T(8,128)(2,1)S(1)} %get-tuple-element.90.refs_1_.refs_2_, bf16[256,256]{1,0:T(8,128)(2,1)S(1)} %get-tuple-element.90.refs_1_.refs_2_, bf16[256,256]{1,0:T(8,128)(2,1)S(1)} %collective-permute-done.13.refs_3_, ...), custom_call_target="tpu_custom_call" | custom-call | flops 2000000000 | bytes 6000000 | tf_op jit(solution)/shard_map/read/pallas_call | solution.py:997
  59.1 2.6 %finish.1 = bf16[2,256,2048]{2,1,0:T(8,128)(2,1)} custom-call(s32[4]{0:T(128)S(1)} %pad_add_fusion.place.refs_0_, s32[2]{0:T(128)S(1)} %copy-done.4, f32[2048]{0:T(1024)S(1)} %copy-done.2, f32[2,4,256,256]{3,2,1,0:T(8,128)S(1)} %get-tuple-element.95.refs_3_, f32[2,256,128]{2,1,0:T(8,128)S(1)} %get-tuple-element.96.refs_4_, ...), custom_call_target="tpu_custom_call" | custom-call | flops 2000000000 | bytes 6000000 | tf_op jit(solution)/shard_map/finish/pallas_call | solution.py:997
  (54 shorter events, 11.2 us)
Async XLA Ops:
  0.0 12.9 %collective-permute-start = (bf16[256,4096]{1,0:T(8,128)(2,1)}, bf16[256,4096]{1,0:T(8,128)(2,1)S(1)}, u32[]{:S(2)}, u32[]{:S(2)}) collective-permute-start(bf16[256,4096]{1,0:T(8,128)(2,1)} %refs_1_.9), channel_id=1, source_target_pairs={{0,4},{1,5},{2,6},{3,7},{4,0},{5,1},{6,2},{7,3},{8,12},{9,13},{10,... | collective-permute-start | bytes 6291464 | tf_op jit(solution)/shard_map/ppermute | solution.py:269
  2.2 8.2 %copy-start.8 = (f32[64,256]{1,0:T(8,128)S(1)}, f32[64,256]{1,0:T(8,128)}, u32[]{:S(2)}) copy-start(f32[64,256]{1,0:T(8,128)} %step.3) | copy-start | bytes 196612
  2.2 8.2 %copy-start.9 = (bf16[4,4096]{1,0:T(4,128)(2,1)S(1)}, bf16[4,4096]{1,0:T(4,128)(2,1)}, u32[]{:S(2)}) copy-start(bf16[4,4096]{1,0:T(4,128)(2,1)} %refs_5_.7) | copy-start | bytes 98308
  2.3 2.5 %collective-permute-start.1 = (bf16[272,512]{1,0:T(8,128)(2,1)S(1)}, bf16[272,512]{1,0:T(8,128)(2,1)S(1)}, u32[]{:S(2)}, u32[]{:S(2)}) collective-permute-start(bf16[272,512]{1,0:T(8,128)(2,1)S(1)} %get-tuple-element.52), channel_id=1, source_target_pairs={{0,4},{1,5},{2,6},{3,7},{4,0},{5,1},{6,2},{7,3},{8,12},{9,13},{10,... | collective-permute-start | bytes 835592 | tf_op jit(solution)/shard_map/ppermute | solution.py:269
  4.8 8.0 %collective-permute-start.3 = (bf16[16,512]{1,0:T(8,128)(2,1)S(1)}, bf16[16,512]{1,0:T(8,128)(2,1)S(1)}, u32[]{:S(2)}, u32[]{:S(2)}) collective-permute-start(bf16[16,512]{1,0:T(8,128)(2,1)S(1)} %slice_select_fusion), channel_id=1, source_target_pairs={{24,0},{25,9},{26,18},{27,27},{28,4},{29,13},{30,22},{31,31}} | collective-permute-start | bytes 49160 | tf_op jit(solution)/shard_map/ppermute | solution.py:269
  6.1 6.8 %collective-permute-start.2 = (bf16[16,512]{1,0:T(8,128)(2,1)S(1)}, bf16[16,512]{1,0:T(8,128)(2,1)S(1)}, u32[]{:S(2)}, u32[]{:S(2)}) collective-permute-start(bf16[16,512]{1,0:T(8,128)(2,1)S(1)} %slice_select_fusion), channel_id=1, source_target_pairs={{0,8},{1,9},{2,10},{3,11},{4,12},{5,13},{6,14},{7,15},{8,16},{9,17... | collective-permute-start | bytes 49160 | tf_op jit(solution)/shard_map/ppermute | solution.py:269
  15.3 9.8 %collective-permute-start.4 = (bf16[288,256]{1,0:T(8,128)(2,1)S(1)}, bf16[288,256]{1,0:T(8,128)(2,1)S(1)}, u32[]{:S(2)}, u32[]{:S(2)}) collective-permute-start(bf16[288,256]{1,0:T(8,128)(2,1)S(1)} %get-tuple-element.64), channel_id=1, source_target_pairs={{0,1},{1,0},{2,3},{3,2},{4,5},{5,4},{6,7},{7,6},{8,9},{9,8},{10,11... | collective-permute-start | bytes 442376 | tf_op jit(solution)/shard_map/ppermute | solution.py:269
  16.6 9.8 %collective-permute-start.5 = (bf16[288,256]{1,0:T(8,128)(2,1)S(1)}, bf16[288,256]{1,0:T(8,128)(2,1)S(1)}, u32[]{:S(2)}, u32[]{:S(2)}) collective-permute-start(bf16[288,256]{1,0:T(8,128)(2,1)S(1)} %get-tuple-element.65), channel_id=1, source_target_pairs={{0,2},{1,3},{2,0},{3,1},{4,6},{5,7},{6,4},{7,5},{8,10},{9,11},{10,... | collective-permute-start | bytes 442376 | tf_op jit(solution)/shard_map/ppermute | solution.py:269
  17.5 8.9 %collective-permute-start.6 = (bf16[288,256]{1,0:T(8,128)(2,1)S(1)}, bf16[288,256]{1,0:T(8,128)(2,1)S(1)}, u32[]{:S(2)}, u32[]{:S(2)}) collective-permute-start(bf16[288,256]{1,0:T(8,128)(2,1)S(1)} %get-tuple-element.66), channel_id=1, source_target_pairs={{0,3},{1,2},{2,1},{3,0},{4,7},{5,6},{6,5},{7,4},{8,11},{9,10},{10,... | collective-permute-start | bytes 442376 | tf_op jit(solution)/shard_map/ppermute | solution.py:269
  18.8 4.6 %copy-start = (bf16[2,256,2048]{2,1,0:T(8,128)(2,1)S(1)}, bf16[2,256,2048]{2,1,0:T(8,128)(2,1)}, u32[]{:S(2)}) copy-start(bf16[2,256,2048]{2,1,0:T(8,128)(2,1)} %refs_1_.10) | copy-start | bytes 6291460
  21.2 11.5 %collective-permute-start.8 = (bf16[256,256]{1,0:T(8,128)(2,1)S(1)}, bf16[256,256]{1,0:T(8,128)(2,1)S(1)}, u32[]{:S(2)}, u32[]{:S(2)}) collective-permute-start(bf16[256,256]{1,0:T(8,128)(2,1)S(1)} %get-tuple-element.76), channel_id=1, source_target_pairs={{0,1},{1,0},{2,3},{3,2},{4,5},{5,4},{6,7},{7,6},{8,9},{9,8},{10,11... | collective-permute-start | bytes 393224 | tf_op jit(solution)/shard_map/ppermute | solution.py:269
  22.6 10.2 %collective-permute-start.9 = (bf16[256,256]{1,0:T(8,128)(2,1)S(1)}, bf16[256,256]{1,0:T(8,128)(2,1)S(1)}, u32[]{:S(2)}, u32[]{:S(2)}) collective-permute-start(bf16[256,256]{1,0:T(8,128)(2,1)S(1)} %get-tuple-element.77), channel_id=1, source_target_pairs={{0,2},{1,3},{2,0},{3,1},{4,6},{5,7},{6,4},{7,5},{8,10},{9,11},{10,... | collective-permute-start | bytes 393224 | tf_op jit(solution)/shard_map/ppermute | solution.py:269
  25.1 7.7 %collective-permute-start.10 = (bf16[256,256]{1,0:T(8,128)(2,1)S(1)}, bf16[256,256]{1,0:T(8,128)(2,1)S(1)}, u32[]{:S(2)}, u32[]{:S(2)}) collective-permute-start(bf16[256,256]{1,0:T(8,128)(2,1)S(1)} %get-tuple-element.78), channel_id=1, source_target_pairs={{0,3},{1,2},{2,1},{3,0},{4,7},{5,6},{6,5},{7,4},{8,11},{9,10},{10,... | collective-permute-start | bytes 393224 | tf_op jit(solution)/shard_map/ppermute | solution.py:269
  27.0 7.1 %collective-permute-start.7 = (bf16[2,272,256]{2,1,0:T(8,128)(2,1)S(1)}, bf16[2,272,256]{2,1,0:T(8,128)(2,1)S(1)}, u32[]{:S(2)}, u32[]{:S(2)}) collective-permute-start(bf16[2,272,256]{2,1,0:T(8,128)(2,1)S(1)} %get-tuple-element.68.refs_10_), channel_id=1, source_target_pairs={{0,8},{1,9},{2,10},{3,11},{4,12},{5,13},{6,14},{7,15},{8,0},{9,1},... | collective-permute-start | bytes 835592 | tf_op jit(solution)/shard_map/ppermute | solution.py:269
  33.5 9.0 %collective-permute-start.12 = (bf16[2,256,256]{2,1,0:T(8,128)(2,1)S(1)}, bf16[2,256,256]{2,1,0:T(8,128)(2,1)S(1)}, u32[]{:S(2)}, u32[]{:S(2)}) collective-permute-start(bf16[2,256,256]{2,1,0:T(8,128)(2,1)S(1)} %get-tuple-element.79.refs_3_.refs_4_), channel_id=1, source_target_pairs={{0,8},{1,9},{2,10},{3,11},{4,12},{5,13},{6,14},{7,15},{8,0},{9,1},... | collective-permute-start | bytes 786440 | tf_op jit(solution)/shard_map/ppermute | solution.py:269
  35.0 9.5 %collective-permute-start.11 = (bf16[1,272,256]{2,1,0:T(8,128)(2,1)S(1)}, bf16[1,272,256]{2,1,0:T(8,128)(2,1)S(1)}, u32[]{:S(2)}, u32[]{:S(2)}) collective-permute-start(bf16[1,272,256]{2,1,0:T(8,128)(2,1)S(1)} %get-tuple-element.81.refs_10_), channel_id=1, source_target_pairs={{0,16},{1,17},{2,18},{3,19},{4,20},{5,21},{6,22},{7,23},{8,24},{9,... | collective-permute-start | bytes 417800 | tf_op jit(solution)/shard_map/ppermute | solution.py:269
  43.2 5.9 %collective-permute-start.16 = (bf16[1,256,256]{2,1,0:T(8,128)(2,1)S(1)}, bf16[1,256,256]{2,1,0:T(8,128)(2,1)S(1)}, u32[]{:S(2)}, u32[]{:S(2)}) collective-permute-start(bf16[1,256,256]{2,1,0:T(8,128)(2,1)S(1)} %get-tuple-element.89.refs_3_.refs_4_), channel_id=1, source_target_pairs={{0,16},{1,17},{2,18},{3,19},{4,20},{5,21},{6,22},{7,23},{8,24},{9,... | collective-permute-start | bytes 393224 | tf_op jit(solution)/shard_map/ppermute | solution.py:269
  45.3 8.1 %collective-permute-start.15 = (bf16[256,256]{1,0:T(8,128)(2,1)S(1)}, bf16[256,256]{1,0:T(8,128)(2,1)S(1)}, u32[]{:S(2)}, u32[]{:S(2)}) collective-permute-start(bf16[256,256]{1,0:T(8,128)(2,1)S(1)} %get-tuple-element.90.refs_1_.refs_2_), channel_id=1, source_target_pairs={{0,3},{1,2},{2,1},{3,0},{4,7},{5,6},{6,5},{7,4},{8,11},{9,10},{10,... | collective-permute-start | bytes 393224 | tf_op jit(solution)/shard_map/ppermute | solution.py:269
  47.1 8.4 %collective-permute-start.14 = (bf16[256,256]{1,0:T(8,128)(2,1)S(1)}, bf16[256,256]{1,0:T(8,128)(2,1)S(1)}, u32[]{:S(2)}, u32[]{:S(2)}) collective-permute-start(bf16[256,256]{1,0:T(8,128)(2,1)S(1)} %get-tuple-element.90.refs_1_.refs_2_), channel_id=1, source_target_pairs={{0,2},{1,3},{2,0},{3,1},{4,6},{5,7},{6,4},{7,5},{8,10},{9,11},{10,... | collective-permute-start | bytes 393224 | tf_op jit(solution)/shard_map/ppermute | solution.py:269
  48.7 6.8 %collective-permute-start.13 = (bf16[256,256]{1,0:T(8,128)(2,1)S(1)}, bf16[256,256]{1,0:T(8,128)(2,1)S(1)}, u32[]{:S(2)}, u32[]{:S(2)}) collective-permute-start(bf16[256,256]{1,0:T(8,128)(2,1)S(1)} %get-tuple-element.90.refs_1_.refs_2_), channel_id=1, source_target_pairs={{0,1},{1,0},{2,3},{3,2},{4,5},{5,4},{6,7},{7,6},{8,9},{9,8},{10,11... | collective-permute-start | bytes 393224 | tf_op jit(solution)/shard_map/ppermute | solution.py:269
  49.7 7.6 %collective-permute-start.19 = (bf16[256,256]{1,0:T(8,128)(2,1)S(1)}, bf16[256,256]{1,0:T(8,128)(2,1)S(1)}, u32[]{:S(2)}, u32[]{:S(2)}) collective-permute-start(bf16[256,256]{1,0:T(8,128)(2,1)S(1)} %merge.7.refs_5_), channel_id=1, source_target_pairs={{0,3},{1,2},{2,1},{3,0},{4,7},{5,6},{6,5},{7,4},{8,11},{9,10},{10,... | collective-permute-start | bytes 393224 | tf_op jit(solution)/shard_map/ppermute | solution.py:269
  51.6 6.7 %collective-permute-start.18 = (bf16[256,256]{1,0:T(8,128)(2,1)S(1)}, bf16[256,256]{1,0:T(8,128)(2,1)S(1)}, u32[]{:S(2)}, u32[]{:S(2)}) collective-permute-start(bf16[256,256]{1,0:T(8,128)(2,1)S(1)} %merge.7.refs_5_), channel_id=1, source_target_pairs={{0,2},{1,3},{2,0},{3,1},{4,6},{5,7},{6,4},{7,5},{8,10},{9,11},{10,... | collective-permute-start | bytes 393224 | tf_op jit(solution)/shard_map/ppermute | solution.py:269
  53.5 5.6 %collective-permute-start.17 = (bf16[256,256]{1,0:T(8,128)(2,1)S(1)}, bf16[256,256]{1,0:T(8,128)(2,1)S(1)}, u32[]{:S(2)}, u32[]{:S(2)}) collective-permute-start(bf16[256,256]{1,0:T(8,128)(2,1)S(1)} %merge.7.refs_5_), channel_id=1, source_target_pairs={{0,1},{1,0},{2,3},{3,2},{4,5},{5,4},{6,7},{7,6},{8,9},{9,8},{10,11... | collective-permute-start | bytes 393224 | tf_op jit(solution)/shard_map/ppermute | solution.py:269
  55.5 3.6 %copy-start.4 = (s32[2]{0:T(128)S(1)}, s32[2]{0:T(128)}, u32[]{:S(2)}) copy-start(s32[2]{0:T(128)} %refs_1_.13) | copy-start | bytes 28
  (6 other events, 15.7 us)

commit v7 on v6

--- a/solution.py
+++ b/solution.py
@@ -500,30 +500,44 @@
 
 
 def pick_kernel(count, place, after, *refs):
-    held, (stays, goes), tails = refs[:count], refs[count : count + 2], refs[count + 2 :]
+    held, (goes, *more) = refs[:count], refs[count:]
+    stays, tails = more[:1], more[1:]
     turn = place[0] ^ place[1]
-    rows, width = stays.shape[1:]
+    rows, width = goes.shape[1:]
     for index in range(count):
 
         @pl.when(turn == index)
         def _():
             for step in range(0, count, 2):
-                stays[step // 2] = held[index ^ step][0:rows]
                 goes[step // 2] = held[index ^ (step + 1)][0:rows]
+                for stay in stays:
+                    stay[step // 2] = held[index ^ step][0:rows]
             for tail in tails:
                 tail[:, 0:width] = held[index][rows - TAIL : rows]
                 tail[:, width:] = held[index][rows:]
 
 
+def merge_held_kernel(bit, chunk, place, *refs):
+    count = lax.axis_size("comp")
+    turn = place[0] ^ place[1]
+    for index in range(count):
+
+        @pl.when(turn == index)
+        def _():
+            own = [refs[index ^ step] for step in range(0, count, 2)]
+            merge_kernel(bit, chunk, place, own, *refs[count:])
+
+
 def merge_kernel(bit, chunk, place, own, came, given, after, *refs):
-    count, rows, width = own.shape
+    count, rows, width = came.shape
+    own = own if isinstance(own, list) else [own.at[index] for index in range(count)]
     state = STATE_WIDTH
     first = (place[0] >> bit) & 1 == 0
     outs = refs if chunk else refs[:-1]
     factors = given if chunk else refs[-1]
     if chunk == 0:
-        last = slice(rows - TAIL, rows)
-        tiles = [ref[index, last] for index in range(count) for ref in (own, came)]
+        last = slice(state, state + TAIL)
+        tiles = [tile for at in range(count) for tile in (own[at][last], came[at, last])]
         wide, lanes = logs_of(tiles, factors.shape[1])
         row = lax.broadcasted_iota(jnp.int32, wide.shape, 0)
         other = jnp.where(row % 2 == 0, pltpu.roll(wide, 7, 0), pltpu.roll(wide, 1, 0))
@@ -533,7 +547,7 @@
         cols = slice(chunk * width, (chunk + 1) * width)
         mine_by = factors[2 * index : 2 * index + 1, cols]
         theirs_by = factors[2 * index + 1 : 2 * index + 2, cols]
-        joined = own[index, 0:state].astype(jnp.float32) * mine_by
+        joined = own[index][0:state].astype(jnp.float32) * mine_by
         joined = joined + came[index, 0:state].astype(jnp.float32) * theirs_by
         if count == 1:
             outs[0][...] = joined.astype(jnp.bfloat16)
@@ -841,7 +855,7 @@
     unit = features // parts // sum(CHUNKS)
     widths = [unit * size for size in CHUNKS]
     offsets = [sum(widths[:chunk]) for chunk in range(len(widths))]
-    picks = []
+    picks, holds = [], []
     for chunk, width in enumerate(widths):
         with_tail = chunk == 0
         message = jax.ShapeDtypeStruct((STATE_WIDTH + TAIL * with_tail, width), bf16)
@@ -865,12 +879,13 @@
             routed(sent[step], lambda z, k, c: (z, k, c ^ step)) for step in range(1, parts)
         ]
         two = jax.ShapeDtypeStruct((parts // 2,) + message.shape, bf16)
+        holds.append(held)
         picks.append(
             lambda after, held=held, two=two, with_tail=with_tail: run_whole(
                 lambda *refs: pick_kernel(parts, *refs),
                 "pick",
                 (place,),
-                (two, two) + (edge,) * with_tail,
+                (two,) + (two, edge) * with_tail,
                 [after] + held,
                 spaces=[pl.ANY] + [pltpu.VMEM] * parts,
             )
@@ -899,12 +914,12 @@
     def merge(bit, chunk, own, came, shapes, given, after):
         table = jax.ShapeDtypeStruct((8, features // parts), f32)
         *outs, factors = run_whole(
-            lambda *refs: merge_kernel(bit, chunk, *refs),
+            lambda *refs: (merge_kernel if len(own) == 1 else merge_held_kernel)(bit, chunk, *refs),
             "merge",
             (place,),
             shapes + (table,) * (chunk == 0),
-            (own, came, given, after),
-            spaces=[pltpu.VMEM] * 2 + [pltpu.VMEM if chunk else pl.ANY, pl.ANY],
+            (*own, came, given, after),
+            spaces=[pltpu.VMEM] * (len(own) + 1) + [pltpu.VMEM if chunk else pl.ANY, pl.ANY],
         ) + ((given,) if chunk else ())
         return outs, factors
 
@@ -927,9 +942,9 @@
     far_plane = lambda z, k, c: (z ^ 2, k, c)
     tail, after = None, handed
     for chunk in range(len(widths)):
-        stay, go, *maybe = picks[chunk](after)
-        tail = maybe[0] if maybe else tail
-        stays.append(stay)
+        go, *maybe = picks[chunk](after)
+        tail = maybe[1] if maybe else tail
+        stays.append(maybe[:1] or holds[chunk])
         goes.append(routed(go, near_plane))
         go_shapes.append(go.shape[1:])
         if chunk + 1 < len(widths):
@@ -945,7 +960,7 @@
     given = go
     for chunk, width in enumerate(widths):
         state = jax.ShapeDtypeStruct((STATE_WIDTH, width), bf16)
-        (state,), given = merge(1, chunk, *merged[chunk], (state,), given, go)
+        (state,), given = merge(1, chunk, [merged[chunk][0]], merged[chunk][1], (state,), given, go)
         joined.append(gather(state))
     after = state
     while work:

time: 62.1 us -> 62.1 us (level)
  transfers between devices with their start and end apart: 20 -> 20, of which waited for: 6 -> 6; matrix products, arithmetic and copies ran while one was open for 0% -> 0% of each run, Pallas kernels for 37% -> 38%
where the time goes in v7:
time: 62.1 us; the launch traced here: 61.8 us
  Pallas kernels  28.2 us (45%)
  starting transfers between devices  27.6 us (44%)
  waiting for transfers between devices  5.53 us (9%)
    pallas_call x16, Pallas kernels, run_whole(): pl.pallas_call(kernel, out_shape=out_shape, in_specs=[pl.BlockSpec(memory...  28.2 us
    ppermute x20, starting transfers between devices, routed(): return lax.ppermute(block, AXES, pairs)  27.6 us
    ppermute x20, waiting for transfers between devices, routed(): return lax.ppermute(block, AXES, pairs)  5.53 us
  transfers between devices with their start and end apart: 20, of which 6 were waited for; matrix products, arithmetic and copies ran while one was open for 0% of the time, Pallas kernels for 38%

profile of v7, /device:TPU:0, one launch (start us, length us, event | category | flops | bytes accessed | tf_op | source)
XLA Modules:
  0.0 61.8 jit_solution(4069644108598425759)
XLA Ops:
  0.5 1.7 %pack.1 = (bf16[272,512]{1,0:T(8,128)(2,1)S(1)}, bf16[16,512]{1,0:T(8,128)(2,1)S(1)}, bf16[256,256]{1,0:T(8,128)(2,1)S(1)}) custom-call(s32[4]{0:T(128)S(1)} %pad_add_fusion.place.refs_0_, bf16[256,4096]{1,0:T(8,128)(2,1)} %refs_1_.9, bf16[256,4096]{1,0:T(8,128)(2,1)} %proj.1, f32[64,256]{1,0:T(8,128)} %step.3), custom_call_target="tpu_custom_call" | custom-call | flops 2000000000 | bytes 6000000 | tf_op jit(solution)/shard_map/pack/pallas_call | solution.py:1012
  2.4 2.4 %prepare.2 = (bf16[256,2048]{1,0:T(8,128)(2,1)S(1)}, bf16[256,2048]{1,0:T(8,128)(2,1)S(1)}, f32[32,256]{1,0:T(8,128)S(1)}, f32[256,32]{1,0:T(8,128)S(1)}, f32[32...) custom-call(s32[4]{0:T(128)S(1)} %pad_add_fusion.place.refs_0_, bf16[2,256,2048]{2,1,0:T(8,128)(2,1)} %refs_1_.10, ...), custom_call_target="tpu_custom_call" | custom-call | tf_op jit(solution)/shard_map/prepare/pallas_call | solution.py:1012
  4.8 1.3 %collective-permute-start.3 = (bf16[16,512]{1,0:T(8,128)(2,1)S(1)}, bf16[16,512]{1,0:T(8,128)(2,1)S(1)}, u32[]{:S(2)}, u32[]{:S(2)}) collective-permute-start(bf16[16,512]{1,0:T(8,128)(2,1)S(1)} %slice_select_fusion), channel_id=1, source_target_pairs={{24,0},{25,9},{26,18},{27,27},{28,4},{29,13},{30,22},{31,31}} | collective-permute-start | bytes 49160 | tf_op jit(solution)/shard_map/ppermute | solution.py:269
  6.1 4.3 %collective-permute-start.2 = (bf16[16,512]{1,0:T(8,128)(2,1)S(1)}, bf16[16,512]{1,0:T(8,128)(2,1)S(1)}, u32[]{:S(2)}, u32[]{:S(2)}) collective-permute-start(bf16[16,512]{1,0:T(8,128)(2,1)S(1)} %slice_select_fusion), channel_id=1, source_target_pairs={{0,8},{1,9},{2,10},{3,11},{4,12},{5,13},{6,14},{7,15},{8,16},{9,17... | collective-permute-start | bytes 49160 | tf_op jit(solution)/shard_map/ppermute | solution.py:269
  10.5 1.5 %prompt_weights.1 = (f32[512,32]{1,0:T(8,128)S(1)}, bf16[256,512]{1,0:T(8,128)(2,1)S(1)}, f32[8,1024]{1,0:T(8,128)S(1)}, bf16[16,256]{1,0:T(8,128)(2,1)S(1)}) custom-call(s32[4]{0:T(128)S(1)} %pad_add_fusion.place.refs_0_, bf16[256,256]{1,0:T(8,128)(2,1)S(1)} %get-tuple-element.53.own, bf16[272,512]{1,0:T(8,128)(2,1)S(1)} %collective-permute-done.1.other, ...), custom_call_target="tpu_custom_call" | custom-call | flops 2000000000 | bytes 6000000 | tf_op jit(solution)/shard_map/prompt_weights/pallas_call | solution.py:1012
  12.9 2.4 %prompt_state.2 = (bf16[288,256]{1,0:T(8,128)(2,1)S(1)}, bf16[288,256]{1,0:T(8,128)(2,1)S(1)}, bf16[288,256]{1,0:T(8,128)(2,1)S(1)}, bf16[288,256]{1,0:T(8,128)(2,1)S(1)}, bf16[256,512]{1,0:T(8,128)(2,1)S(1)}) custom-call(s32[4]{0:T(128)S(1)} %pad_add_fusion.place.refs_0_, bf16[256,4096]{1,0:T(8,128)(2,1)S(1)} %copy-done.5, ...), custom_call_target="tpu_custom_call" | custom-call | flops 3000000000 | bytes 9000000 | tf_op jit(solution)/shard_map/prompt_state/pallas_call | solution.py:1012
  15.3 1.3 %collective-permute-start.4 = (bf16[288,256]{1,0:T(8,128)(2,1)S(1)}, bf16[288,256]{1,0:T(8,128)(2,1)S(1)}, u32[]{:S(2)}, u32[]{:S(2)}) collective-permute-start(bf16[288,256]{1,0:T(8,128)(2,1)S(1)} %get-tuple-element.62), channel_id=1, source_target_pairs={{0,1},{1,0},{2,3},{3,2},{4,5},{5,4},{6,7},{7,6},{8,9},{9,8},{10,11... | collective-permute-start | bytes 442376 | tf_op jit(solution)/shard_map/ppermute | solution.py:269
  17.5 1.3 %collective-permute-start.6 = (bf16[288,256]{1,0:T(8,128)(2,1)S(1)}, bf16[288,256]{1,0:T(8,128)(2,1)S(1)}, u32[]{:S(2)}, u32[]{:S(2)}) collective-permute-start(bf16[288,256]{1,0:T(8,128)(2,1)S(1)} %get-tuple-element.64), channel_id=1, source_target_pairs={{0,3},{1,2},{2,1},{3,0},{4,7},{5,6},{6,5},{7,4},{8,11},{9,10},{10,... | collective-permute-start | bytes 442376 | tf_op jit(solution)/shard_map/ppermute | solution.py:269
  18.8 2.4 %prompt_state.3 = (bf16[256,256]{1,0:T(8,128)(2,1)S(1)}, bf16[256,256]{1,0:T(8,128)(2,1)S(1)}, bf16[256,256]{1,0:T(8,128)(2,1)S(1)}, bf16[256,256]{1,0:T(8,128)(2,1)S(1)}, bf16[16,512]{1,0:T(8,128)(2,1)S(1)}) custom-call(s32[4]{0:T(128)S(1)} %pad_add_fusion.place.refs_0_, bf16[256,4096]{1,0:T(8,128)(2,1)S(1)} %copy-done.5, ...), custom_call_target="tpu_custom_call" | custom-call | flops 3000000000 | bytes 9000000 | tf_op jit(solution)/shard_map/prompt_state/pallas_call | solution.py:1012
  21.2 1.3 %collective-permute-start.8 = (bf16[256,256]{1,0:T(8,128)(2,1)S(1)}, bf16[256,256]{1,0:T(8,128)(2,1)S(1)}, u32[]{:S(2)}, u32[]{:S(2)}) collective-permute-start(bf16[256,256]{1,0:T(8,128)(2,1)S(1)} %get-tuple-element.74), channel_id=1, source_target_pairs={{0,1},{1,0},{2,3},{3,2},{4,5},{5,4},{6,7},{7,6},{8,9},{9,8},{10,11... | collective-permute-start | bytes 393224 | tf_op jit(solution)/shard_map/ppermute | solution.py:269
  23.4 1.6 %prepare.3 = (bf16[256,2048]{1,0:T(8,128)(2,1)S(1)}, bf16[256,2048]{1,0:T(8,128)(2,1)S(1)}, f32[32,256]{1,0:T(8,128)S(1)}, f32[256,32]{1,0:T(8,128)S(1)}, f32[32...) custom-call(s32[4]{0:T(128)S(1)} %pad_add_fusion.place.refs_0_, bf16[2,256,2048]{2,1,0:T(8,128)(2,1)S(1)} %copy-done, ...), custom_call_target="tpu_custom_call" | custom-call | tf_op jit(solution)/shard_map/prepare/pallas_call | solution.py:1012
  25.0 1.4 %collective-permute-start.10 = (bf16[256,256]{1,0:T(8,128)(2,1)S(1)}, bf16[256,256]{1,0:T(8,128)(2,1)S(1)}, u32[]{:S(2)}, u32[]{:S(2)}) collective-permute-start(bf16[256,256]{1,0:T(8,128)(2,1)S(1)} %get-tuple-element.76), channel_id=1, source_target_pairs={{0,3},{1,2},{2,1},{3,0},{4,7},{5,6},{6,5},{7,4},{8,11},{9,10},{10,... | collective-permute-start | bytes 393224 | tf_op jit(solution)/shard_map/ppermute | solution.py:269
  27.0 1.5 %collective-permute-start.7 = (bf16[2,272,256]{2,1,0:T(8,128)(2,1)S(1)}, bf16[2,272,256]{2,1,0:T(8,128)(2,1)S(1)}, u32[]{:S(2)}, u32[]{:S(2)}) collective-permute-start(bf16[2,272,256]{2,1,0:T(8,128)(2,1)S(1)} %get-tuple-element.66.refs_10_), channel_id=1, source_target_pairs={{0,8},{1,9},{2,10},{3,11},{4,12},{5,13},{6,14},{7,15},{8,0},{9,1},... | collective-permute-start | bytes 835592 | tf_op jit(solution)/shard_map/ppermute | solution.py:269
  28.6 4.1 %completion.2 = (bf16[256,2048]{1,0:T(8,128)(2,1)S(1)}, bf16[256,256]{1,0:T(8,128)(2,1)S(1)}) custom-call(s32[4]{0:T(128)S(1)} %pad_add_fusion.place.refs_0_, bf16[2,256,2048]{2,1,0:T(8,128)(2,1)S(1)} %copy-done.6, bf16[2,256,4096]{2,1,0:T(8,128)(2,1)} %refs_2_.8, bf16[16,512]{1,0:T(8,128)(2,1)S(1)} %get-tuple-element.67.refs_3_, ...), custom_call_target="tpu_custom_call" | custom-call | flops 4000000000 | bytes 12000000 | tf_op jit(solution)/shard_map/completion/pallas_call | solution.py:1012
  35.0 3.3 %collective-permute-start.11 = (bf16[1,272,256]{2,1,0:T(8,128)(2,1)S(1)}, bf16[1,272,256]{2,1,0:T(8,128)(2,1)S(1)}, u32[]{:S(2)}, u32[]{:S(2)}) collective-permute-start(bf16[1,272,256]{2,1,0:T(8,128)(2,1)S(1)} %get-tuple-element.78.refs_10_), channel_id=1, source_target_pairs={{0,16},{1,17},{2,18},{3,19},{4,20},{5,21},{6,22},{7,23},{8,24},{9,... | collective-permute-start | bytes 417800 | tf_op jit(solution)/shard_map/ppermute | solution.py:269
  38.3 4.2 %completion.3 = (bf16[256,2048]{1,0:T(8,128)(2,1)S(1)}, bf16[256,256]{1,0:T(8,128)(2,1)S(1)}) custom-call(s32[4]{0:T(128)S(1)} %pad_add_fusion.place.refs_0_, bf16[2,256,2048]{2,1,0:T(8,128)(2,1)S(1)} %copy-done.6, bf16[2,256,4096]{2,1,0:T(8,128)(2,1)} %refs_2_.8, bf16[16,512]{1,0:T(8,128)(2,1)S(1)} %get-tuple-element.67.refs_3_, ...), custom_call_target="tpu_custom_call" | custom-call | flops 4000000000 | bytes 12000000 | tf_op jit(solution)/shard_map/completion/pallas_call | solution.py:1012
  43.2 1.4 %collective-permute-start.16 = (bf16[1,256,256]{2,1,0:T(8,128)(2,1)S(1)}, bf16[1,256,256]{2,1,0:T(8,128)(2,1)S(1)}, u32[]{:S(2)}, u32[]{:S(2)}) collective-permute-start(bf16[1,256,256]{2,1,0:T(8,128)(2,1)S(1)} %get-tuple-element.85.refs_3_.refs_4_), channel_id=1, source_target_pairs={{0,16},{1,17},{2,18},{3,19},{4,20},{5,21},{6,22},{7,23},{8,24},{9,... | collective-permute-start | bytes 393224 | tf_op jit(solution)/shard_map/ppermute | solution.py:269
  45.3 1.7 %collective-permute-start.15 = (bf16[256,256]{1,0:T(8,128)(2,1)S(1)}, bf16[256,256]{1,0:T(8,128)(2,1)S(1)}, u32[]{:S(2)}, u32[]{:S(2)}) collective-permute-start(bf16[256,256]{1,0:T(8,128)(2,1)S(1)} %get-tuple-element.86.refs_1_.refs_2_), channel_id=1, source_target_pairs={{0,3},{1,2},{2,1},{3,0},{4,7},{5,6},{6,5},{7,4},{8,11},{9,10},{10,... | collective-permute-start | bytes 393224 | tf_op jit(solution)/shard_map/ppermute | solution.py:269
  47.1 1.6 %collective-permute-start.14 = (bf16[256,256]{1,0:T(8,128)(2,1)S(1)}, bf16[256,256]{1,0:T(8,128)(2,1)S(1)}, u32[]{:S(2)}, u32[]{:S(2)}) collective-permute-start(bf16[256,256]{1,0:T(8,128)(2,1)S(1)} %get-tuple-element.86.refs_1_.refs_2_), channel_id=1, source_target_pairs={{0,2},{1,3},{2,0},{3,1},{4,6},{5,7},{6,4},{7,5},{8,10},{9,11},{10,... | collective-permute-start | bytes 393224 | tf_op jit(solution)/shard_map/ppermute | solution.py:269
  49.7 1.8 %collective-permute-start.19 = (bf16[256,256]{1,0:T(8,128)(2,1)S(1)}, bf16[256,256]{1,0:T(8,128)(2,1)S(1)}, u32[]{:S(2)}, u32[]{:S(2)}) collective-permute-start(bf16[256,256]{1,0:T(8,128)(2,1)S(1)} %merge.7.refs_5_), channel_id=1, source_target_pairs={{0,3},{1,2},{2,1},{3,0},{4,7},{5,6},{6,5},{7,4},{8,11},{9,10},{10,... | collective-permute-start | bytes 393224 | tf_op jit(solution)/shard_map/ppermute | solution.py:269
  51.6 1.9 %collective-permute-start.18 = (bf16[256,256]{1,0:T(8,128)(2,1)S(1)}, bf16[256,256]{1,0:T(8,128)(2,1)S(1)}, u32[]{:S(2)}, u32[]{:S(2)}) collective-permute-start(bf16[256,256]{1,0:T(8,128)(2,1)S(1)} %merge.7.refs_5_), channel_id=1, source_target_pairs={{0,2},{1,3},{2,0},{3,1},{4,6},{5,7},{6,4},{7,5},{8,10},{9,11},{10,... | collective-permute-start | bytes 393224 | tf_op jit(solution)/shard_map/ppermute | solution.py:269
  53.6 2.2 %collective-permute-done.14.refs_4_ = bf16[256,256]{1,0:T(8,128)(2,1)S(1)} collective-permute-done((bf16[256,256]{1,0:T(8,128)(2,1)S(1)}, bf16[256,256]{1,0:T(8,128)(2,1)S(1)}, u32[]{:S(2)}, u32[]{:S(2)}) %collective-permute-start.14) | collective-permute-done | bytes 131104 | tf_op jit(solution)/shard_map/ppermute | solution.py:269
  55.8 1.1 %read.1 = (f32[2,4,256,256]{3,2,1,0:T(8,128)S(1)}, f32[2,256,128]{2,1,0:T(8,128)S(1)}) custom-call(s32[4]{0:T(128)S(1)} %pad_add_fusion.place.refs_0_, bf16[256,256]{1,0:T(8,128)(2,1)S(1)} %get-tuple-element.86.refs_1_.refs_2_, bf16[256,256]{1,0:T(8,128)(2,1)S(1)} %get-tuple-element.86.refs_1_.refs_2_, bf16[256,256]{1,0:T(8,128)(2,1)S(1)} %collective-permute-done.13.refs_3_, ...), custom_call_target="tpu_custom_call" | custom-call | flops 2000000000 | bytes 6000000 | tf_op jit(solution)/shard_map/read/pallas_call | solution.py:1012
  59.1 2.6 %finish.1 = bf16[2,256,2048]{2,1,0:T(8,128)(2,1)} custom-call(s32[4]{0:T(128)S(1)} %pad_add_fusion.place.refs_0_, s32[2]{0:T(128)S(1)} %copy-done.4, f32[2048]{0:T(1024)S(1)} %copy-done.2, f32[2,4,256,256]{3,2,1,0:T(8,128)S(1)} %get-tuple-element.91.refs_3_, f32[2,256,128]{2,1,0:T(8,128)S(1)} %get-tuple-element.92.refs_4_, ...), custom_call_target="tpu_custom_call" | custom-call | flops 2000000000 | bytes 6000000 | tf_op jit(solution)/shard_map/finish/pallas_call | solution.py:1012
  (54 shorter events, 11.0 us)
Async XLA Ops:
  0.0 12.9 %collective-permute-start = (bf16[256,4096]{1,0:T(8,128)(2,1)}, bf16[256,4096]{1,0:T(8,128)(2,1)S(1)}, u32[]{:S(2)}, u32[]{:S(2)}) collective-permute-start(bf16[256,4096]{1,0:T(8,128)(2,1)} %refs_1_.9), channel_id=1, source_target_pairs={{0,4},{1,5},{2,6},{3,7},{4,0},{5,1},{6,2},{7,3},{8,12},{9,13},{10,... | collective-permute-start | bytes 6291464 | tf_op jit(solution)/shard_map/ppermute | solution.py:269
  2.2 8.2 %copy-start.8 = (f32[64,256]{1,0:T(8,128)S(1)}, f32[64,256]{1,0:T(8,128)}, u32[]{:S(2)}) copy-start(f32[64,256]{1,0:T(8,128)} %step.3) | copy-start | bytes 196612
  2.2 8.2 %copy-start.9 = (bf16[4,4096]{1,0:T(4,128)(2,1)S(1)}, bf16[4,4096]{1,0:T(4,128)(2,1)}, u32[]{:S(2)}) copy-start(bf16[4,4096]{1,0:T(4,128)(2,1)} %refs_5_.7) | copy-start | bytes 98308
  2.3 2.5 %collective-permute-start.1 = (bf16[272,512]{1,0:T(8,128)(2,1)S(1)}, bf16[272,512]{1,0:T(8,128)(2,1)S(1)}, u32[]{:S(2)}, u32[]{:S(2)}) collective-permute-start(bf16[272,512]{1,0:T(8,128)(2,1)S(1)} %get-tuple-element.50), channel_id=1, source_target_pairs={{0,4},{1,5},{2,6},{3,7},{4,0},{5,1},{6,2},{7,3},{8,12},{9,13},{10,... | collective-permute-start | bytes 835592 | tf_op jit(solution)/shard_map/ppermute | solution.py:269
  4.8 8.0 %collective-permute-start.3 = (bf16[16,512]{1,0:T(8,128)(2,1)S(1)}, bf16[16,512]{1,0:T(8,128)(2,1)S(1)}, u32[]{:S(2)}, u32[]{:S(2)}) collective-permute-start(bf16[16,512]{1,0:T(8,128)(2,1)S(1)} %slice_select_fusion), channel_id=1, source_target_pairs={{24,0},{25,9},{26,18},{27,27},{28,4},{29,13},{30,22},{31,31}} | collective-permute-start | bytes 49160 | tf_op jit(solution)/shard_map/ppermute | solution.py:269
  6.1 6.8 %collective-permute-start.2 = (bf16[16,512]{1,0:T(8,128)(2,1)S(1)}, bf16[16,512]{1,0:T(8,128)(2,1)S(1)}, u32[]{:S(2)}, u32[]{:S(2)}) collective-permute-start(bf16[16,512]{1,0:T(8,128)(2,1)S(1)} %slice_select_fusion), channel_id=1, source_target_pairs={{0,8},{1,9},{2,10},{3,11},{4,12},{5,13},{6,14},{7,15},{8,16},{9,17... | collective-permute-start | bytes 49160 | tf_op jit(solution)/shard_map/ppermute | solution.py:269
  15.3 9.7 %collective-permute-start.4 = (bf16[288,256]{1,0:T(8,128)(2,1)S(1)}, bf16[288,256]{1,0:T(8,128)(2,1)S(1)}, u32[]{:S(2)}, u32[]{:S(2)}) collective-permute-start(bf16[288,256]{1,0:T(8,128)(2,1)S(1)} %get-tuple-element.62), channel_id=1, source_target_pairs={{0,1},{1,0},{2,3},{3,2},{4,5},{5,4},{6,7},{7,6},{8,9},{9,8},{10,11... | collective-permute-start | bytes 442376 | tf_op jit(solution)/shard_map/ppermute | solution.py:269
  16.6 9.8 %collective-permute-start.5 = (bf16[288,256]{1,0:T(8,128)(2,1)S(1)}, bf16[288,256]{1,0:T(8,128)(2,1)S(1)}, u32[]{:S(2)}, u32[]{:S(2)}) collective-permute-start(bf16[288,256]{1,0:T(8,128)(2,1)S(1)} %get-tuple-element.63), channel_id=1, source_target_pairs={{0,2},{1,3},{2,0},{3,1},{4,6},{5,7},{6,4},{7,5},{8,10},{9,11},{10,... | collective-permute-start | bytes 442376 | tf_op jit(solution)/shard_map/ppermute | solution.py:269
  17.5 8.9 %collective-permute-start.6 = (bf16[288,256]{1,0:T(8,128)(2,1)S(1)}, bf16[288,256]{1,0:T(8,128)(2,1)S(1)}, u32[]{:S(2)}, u32[]{:S(2)}) collective-permute-start(bf16[288,256]{1,0:T(8,128)(2,1)S(1)} %get-tuple-element.64), channel_id=1, source_target_pairs={{0,3},{1,2},{2,1},{3,0},{4,7},{5,6},{6,5},{7,4},{8,11},{9,10},{10,... | collective-permute-start | bytes 442376 | tf_op jit(solution)/shard_map/ppermute | solution.py:269
  18.8 4.6 %copy-start = (bf16[2,256,2048]{2,1,0:T(8,128)(2,1)S(1)}, bf16[2,256,2048]{2,1,0:T(8,128)(2,1)}, u32[]{:S(2)}) copy-start(bf16[2,256,2048]{2,1,0:T(8,128)(2,1)} %refs_1_.10) | copy-start | bytes 6291460
  21.2 11.5 %collective-permute-start.8 = (bf16[256,256]{1,0:T(8,128)(2,1)S(1)}, bf16[256,256]{1,0:T(8,128)(2,1)S(1)}, u32[]{:S(2)}, u32[]{:S(2)}) collective-permute-start(bf16[256,256]{1,0:T(8,128)(2,1)S(1)} %get-tuple-element.74), channel_id=1, source_target_pairs={{0,1},{1,0},{2,3},{3,2},{4,5},{5,4},{6,7},{7,6},{8,9},{9,8},{10,11... | collective-permute-start | bytes 393224 | tf_op jit(solution)/shard_map/ppermute | solution.py:269
  22.6 10.2 %collective-permute-start.9 = (bf16[256,256]{1,0:T(8,128)(2,1)S(1)}, bf16[256,256]{1,0:T(8,128)(2,1)S(1)}, u32[]{:S(2)}, u32[]{:S(2)}) collective-permute-start(bf16[256,256]{1,0:T(8,128)(2,1)S(1)} %get-tuple-element.75), channel_id=1, source_target_pairs={{0,2},{1,3},{2,0},{3,1},{4,6},{5,7},{6,4},{7,5},{8,10},{9,11},{10,... | collective-permute-start | bytes 393224 | tf_op jit(solution)/shard_map/ppermute | solution.py:269
  25.0 3.5 %copy-start.6 = (bf16[2,256,2048]{2,1,0:T(8,128)(2,1)S(1)}, bf16[2,256,2048]{2,1,0:T(8,128)(2,1)}, u32[]{:S(2)}) copy-start(bf16[2,256,2048]{2,1,0:T(8,128)(2,1)} %refs_1_.12) | copy-start | bytes 6291460
  25.0 7.7 %collective-permute-start.10 = (bf16[256,256]{1,0:T(8,128)(2,1)S(1)}, bf16[256,256]{1,0:T(8,128)(2,1)S(1)}, u32[]{:S(2)}, u32[]{:S(2)}) collective-permute-start(bf16[256,256]{1,0:T(8,128)(2,1)S(1)} %get-tuple-element.76), channel_id=1, source_target_pairs={{0,3},{1,2},{2,1},{3,0},{4,7},{5,6},{6,5},{7,4},{8,11},{9,10},{10,... | collective-permute-start | bytes 393224 | tf_op jit(solution)/shard_map/ppermute | solution.py:269
  27.0 7.1 %collective-permute-start.7 = (bf16[2,272,256]{2,1,0:T(8,128)(2,1)S(1)}, bf16[2,272,256]{2,1,0:T(8,128)(2,1)S(1)}, u32[]{:S(2)}, u32[]{:S(2)}) collective-permute-start(bf16[2,272,256]{2,1,0:T(8,128)(2,1)S(1)} %get-tuple-element.66.refs_10_), channel_id=1, source_target_pairs={{0,8},{1,9},{2,10},{3,11},{4,12},{5,13},{6,14},{7,15},{8,0},{9,1},... | collective-permute-start | bytes 835592 | tf_op jit(solution)/shard_map/ppermute | solution.py:269
  33.5 9.0 %collective-permute-start.12 = (bf16[2,256,256]{2,1,0:T(8,128)(2,1)S(1)}, bf16[2,256,256]{2,1,0:T(8,128)(2,1)S(1)}, u32[]{:S(2)}, u32[]{:S(2)}) collective-permute-start(bf16[2,256,256]{2,1,0:T(8,128)(2,1)S(1)} %pick.3.refs_3_.refs_4_), channel_id=1, source_target_pairs={{0,8},{1,9},{2,10},{3,11},{4,12},{5,13},{6,14},{7,15},{8,0},{9,1},... | collective-permute-start | bytes 786440 | tf_op jit(solution)/shard_map/ppermute | solution.py:269
  35.0 9.6 %collective-permute-start.11 = (bf16[1,272,256]{2,1,0:T(8,128)(2,1)S(1)}, bf16[1,272,256]{2,1,0:T(8,128)(2,1)S(1)}, u32[]{:S(2)}, u32[]{:S(2)}) collective-permute-start(bf16[1,272,256]{2,1,0:T(8,128)(2,1)S(1)} %get-tuple-element.78.refs_10_), channel_id=1, source_target_pairs={{0,16},{1,17},{2,18},{3,19},{4,20},{5,21},{6,22},{7,23},{8,24},{9,... | collective-permute-start | bytes 417800 | tf_op jit(solution)/shard_map/ppermute | solution.py:269
  43.2 5.9 %collective-permute-start.16 = (bf16[1,256,256]{2,1,0:T(8,128)(2,1)S(1)}, bf16[1,256,256]{2,1,0:T(8,128)(2,1)S(1)}, u32[]{:S(2)}, u32[]{:S(2)}) collective-permute-start(bf16[1,256,256]{2,1,0:T(8,128)(2,1)S(1)} %get-tuple-element.85.refs_3_.refs_4_), channel_id=1, source_target_pairs={{0,16},{1,17},{2,18},{3,19},{4,20},{5,21},{6,22},{7,23},{8,24},{9,... | collective-permute-start | bytes 393224 | tf_op jit(solution)/shard_map/ppermute | solution.py:269
  45.3 8.1 %collective-permute-start.15 = (bf16[256,256]{1,0:T(8,128)(2,1)S(1)}, bf16[256,256]{1,0:T(8,128)(2,1)S(1)}, u32[]{:S(2)}, u32[]{:S(2)}) collective-permute-start(bf16[256,256]{1,0:T(8,128)(2,1)S(1)} %get-tuple-element.86.refs_1_.refs_2_), channel_id=1, source_target_pairs={{0,3},{1,2},{2,1},{3,0},{4,7},{5,6},{6,5},{7,4},{8,11},{9,10},{10,... | collective-permute-start | bytes 393224 | tf_op jit(solution)/shard_map/ppermute | solution.py:269
  47.1 8.7 %collective-permute-start.14 = (bf16[256,256]{1,0:T(8,128)(2,1)S(1)}, bf16[256,256]{1,0:T(8,128)(2,1)S(1)}, u32[]{:S(2)}, u32[]{:S(2)}) collective-permute-start(bf16[256,256]{1,0:T(8,128)(2,1)S(1)} %get-tuple-element.86.refs_1_.refs_2_), channel_id=1, source_target_pairs={{0,2},{1,3},{2,0},{3,1},{4,6},{5,7},{6,4},{7,5},{8,10},{9,11},{10,... | collective-permute-start | bytes 393224 | tf_op jit(solution)/shard_map/ppermute | solution.py:269
  48.7 7.1 %collective-permute-start.13 = (bf16[256,256]{1,0:T(8,128)(2,1)S(1)}, bf16[256,256]{1,0:T(8,128)(2,1)S(1)}, u32[]{:S(2)}, u32[]{:S(2)}) collective-permute-start(bf16[256,256]{1,0:T(8,128)(2,1)S(1)} %get-tuple-element.86.refs_1_.refs_2_), channel_id=1, source_target_pairs={{0,1},{1,0},{2,3},{3,2},{4,5},{5,4},{6,7},{7,6},{8,9},{9,8},{10,11... | collective-permute-start | bytes 393224 | tf_op jit(solution)/shard_map/ppermute | solution.py:269
  49.7 7.5 %collective-permute-start.19 = (bf16[256,256]{1,0:T(8,128)(2,1)S(1)}, bf16[256,256]{1,0:T(8,128)(2,1)S(1)}, u32[]{:S(2)}, u32[]{:S(2)}) collective-permute-start(bf16[256,256]{1,0:T(8,128)(2,1)S(1)} %merge.7.refs_5_), channel_id=1, source_target_pairs={{0,3},{1,2},{2,1},{3,0},{4,7},{5,6},{6,5},{7,4},{8,11},{9,10},{10,... | collective-permute-start | bytes 393224 | tf_op jit(solution)/shard_map/ppermute | solution.py:269
  51.6 6.8 %collective-permute-start.18 = (bf16[256,256]{1,0:T(8,128)(2,1)S(1)}, bf16[256,256]{1,0:T(8,128)(2,1)S(1)}, u32[]{:S(2)}, u32[]{:S(2)}) collective-permute-start(bf16[256,256]{1,0:T(8,128)(2,1)S(1)} %merge.7.refs_5_), channel_id=1, source_target_pairs={{0,2},{1,3},{2,0},{3,1},{4,6},{5,7},{6,4},{7,5},{8,10},{9,11},{10,... | collective-permute-start | bytes 393224 | tf_op jit(solution)/shard_map/ppermute | solution.py:269
  53.4 5.7 %collective-permute-start.17 = (bf16[256,256]{1,0:T(8,128)(2,1)S(1)}, bf16[256,256]{1,0:T(8,128)(2,1)S(1)}, u32[]{:S(2)}, u32[]{:S(2)}) collective-permute-start(bf16[256,256]{1,0:T(8,128)(2,1)S(1)} %merge.7.refs_5_), channel_id=1, source_target_pairs={{0,1},{1,0},{2,3},{3,2},{4,5},{5,4},{6,7},{7,6},{8,9},{9,8},{10,11... | collective-permute-start | bytes 393224 | tf_op jit(solution)/shard_map/ppermute | solution.py:269
  (6 other events, 15.2 us)
